TPU v7x, 32 devices: a whole 2x2x4 slice. The times are simulated.
32 devices in a mesh: dom: 8 (over z, x), grp: 4 (over y, core).
Axes of the slice: x: 2, y: 2, z: 4, core: 2. Of those that a mesh axis runs over, the one named last changes fastest.
Arguments:
- features: bfloat16 [16384, 128], P('dom'), may hold values from -6 to 6
- weight_self: bfloat16 [128, 1024], P(None, 'grp'), may hold values from -0.5 to 0.5
- weight_neigh: bfloat16 [128, 1024], P(None, 'grp'), may hold values from -3 to 3
- cotangent: bfloat16 [16384, 1024], P('dom', 'grp'), may hold values from -6 to 6
- inner_rows: int32 [8, 64], P('dom'), may hold values from 0 to 15
- inner_cols: int32 [8, 64], P('dom'), may hold values from 0 to 15
- inner_values: bfloat16 [8, 64, 128, 128], P('dom'), may hold values from 0 to 1, as said below
- send_blocks: int32 [8, 8, 3], P('dom'), may hold values from 0 to 15
- outer_rows: int32 [8, 24], P('dom'), may hold values from 0 to 15
- outer_values: bfloat16 [8, 24, 128, 128], P('dom'), may hold values from 0 to 1, as said below
- live_count: int32 [8, 8], P('dom'), may hold values from 0 to 3
Outputs:
- layer_out: bfloat16 [16384, 1024], P('dom', 'grp')
- feature_grad: float32 [16384, 128], P('dom')
- self_grad: float32 [128, 1024], P(None, 'grp')
- neigh_grad: float32 [128, 1024], P(None, 'grp')
Inputs may be any that keep to these rules, and one draw needn't show every extreme that they name: `inner_values`: edge weights are zero or positive; most are zero. `outer_values`: edge weights are zero or positive; most are zero.
All inputs are finite; a program needn't handle non-finite values.
Results may differ from a plain program's by a relative error of at most 0.0055.
Values may be sent and summed in bfloat16 or wider, within the bound.
No kernel may reach another device: no remote copies, remote signals or barrier semaphores. Data moves between devices by JAX's collectives and lax.ppermute only.
A program may use at most 128 MiB of HBM per device.

v0:
```python
import jax
import jax.numpy as jnp
from jax import lax
from jax.sharding import PartitionSpec as P


def block_segment(one_hot, products, block_size):
    count = products.shape[0]
    summed = jnp.dot(one_hot, products.reshape(count, -1), precision=lax.Precision.HIGHEST)
    return summed.reshape(one_hot.shape[0], block_size, -1)


def shards(
    features,
    weight_self,
    weight_neigh,
    cotangent,
    inner_rows,
    inner_cols,
    inner_values,
    send_blocks,
    outer_rows,
    outer_values,
    live_count,
):
    block_size = inner_values.shape[-1]
    node_rows, feat_width = features.shape
    loc_blocks = node_rows // block_size
    peer_count = lax.axis_size("dom")
    slot_depth = send_blocks.shape[-1]
    inner_a = inner_values[0]
    outer_a = outer_values[0]
    row_inner = inner_rows[0]
    col_inner = inner_cols[0]
    row_outer = outer_rows[0]
    targets = send_blocks[0]
    slot_limit = jnp.repeat(live_count[0], slot_depth)
    slot_index = jnp.tile(jnp.arange(slot_depth, dtype=jnp.int32), peer_count)
    live_mask = (slot_index < slot_limit).astype(jnp.float32)
    block_ids = jnp.arange(loc_blocks, dtype=jnp.int32)[:, None]
    inner_onehot = (row_inner[None, :] == block_ids).astype(jnp.float32)
    outer_onehot = (row_outer[None, :] == block_ids).astype(jnp.float32) * live_mask[None, :]
    degree = 1.0 + jnp.dot(
        inner_onehot, jnp.sum(inner_a, axis=-1, dtype=jnp.float32), precision=lax.Precision.HIGHEST
    )
    degree = degree + jnp.dot(
        outer_onehot, jnp.sum(outer_a, axis=-1, dtype=jnp.float32), precision=lax.Precision.HIGHEST
    )
    feat_blocks = features.reshape(loc_blocks, block_size, feat_width)
    outgoing = feat_blocks[targets]
    incoming = lax.all_to_all(outgoing, "dom", split_axis=0, concat_axis=0, tiled=True)
    incoming = incoming.reshape(peer_count * slot_depth, block_size, feat_width)
    inner_prod = jnp.einsum(
        "nij,njf->nif", inner_a, feat_blocks[col_inner], preferred_element_type=jnp.float32
    )
    outer_prod = jnp.einsum("nij,njf->nif", outer_a, incoming, preferred_element_type=jnp.float32)
    neighbour = block_segment(inner_onehot, inner_prod, block_size) + block_segment(
        outer_onehot, outer_prod, block_size
    )
    agg_part = ((feat_blocks.astype(jnp.float32) + neighbour) / degree[..., None]).astype(
        jnp.bfloat16
    )
    agg_part = agg_part.reshape(node_rows, feat_width)
    preact = jnp.dot(features, weight_self, preferred_element_type=jnp.float32) + jnp.dot(
        agg_part, weight_neigh, preferred_element_type=jnp.float32
    )
    layer_out = jax.nn.silu(preact).astype(jnp.bfloat16)
    sigmoid_v = jax.nn.sigmoid(preact)
    grad_pre = (
        cotangent.astype(jnp.float32) * sigmoid_v * (1.0 + preact * (1.0 - sigmoid_v))
    ).astype(jnp.bfloat16)
    first_dims = (((0,), (0,)), ((), ()))
    grad_self = lax.dot_general(features, grad_pre, first_dims, preferred_element_type=jnp.float32)
    grad_neigh = lax.dot_general(agg_part, grad_pre, first_dims, preferred_element_type=jnp.float32)
    grad_self, grad_neigh = lax.psum((grad_self, grad_neigh), "dom")
    second_dims = (((1,), (1,)), ((), ()))
    self_part = lax.dot_general(
        grad_pre, weight_self, second_dims, preferred_element_type=jnp.float32
    )
    neigh_part = lax.dot_general(
        grad_pre, weight_neigh, second_dims, preferred_element_type=jnp.float32
    )
    self_back, neigh_back = lax.psum((self_part, neigh_part), "grp")
    scaled = (neigh_back.reshape(loc_blocks, block_size, feat_width) / degree[..., None]).astype(
        jnp.bfloat16
    )
    inner_back = jnp.einsum(
        "nij,nif->njf", inner_a, scaled[row_inner], preferred_element_type=jnp.float32
    )
    outer_back = (
        jnp.einsum("nij,nif->njf", outer_a, scaled[row_outer], preferred_element_type=jnp.float32)
        * live_mask[:, None, None]
    )
    returned = lax.all_to_all(
        outer_back.reshape(peer_count, slot_depth, block_size, feat_width).astype(jnp.bfloat16),
        "dom",
        split_axis=0,
        concat_axis=0,
        tiled=True,
    ).astype(jnp.float32)
    col_onehot = (col_inner[None, :] == block_ids).astype(jnp.float32)
    target_onehot = (targets.reshape(-1)[None, :] == block_ids).astype(jnp.float32)
    pulled_back = block_segment(col_onehot, inner_back, block_size)
    pulled_back = pulled_back + block_segment(
        target_onehot, returned.reshape(peer_count * slot_depth, block_size, feat_width), block_size
    )
    grad_part = self_back + (scaled.astype(jnp.float32) + pulled_back).reshape(
        node_rows, feat_width
    )
    return (layer_out, grad_part, grad_self, grad_neigh)


def solution(mesh):
    placed = (
        P("dom", None),
        P(None, "grp"),
        P(None, "grp"),
        P("dom", "grp"),
        P("dom", None),
        P("dom", None),
        P("dom", None, None, None),
        P("dom", None, None),
        P("dom", None),
        P("dom", None, None, None),
        P("dom", None),
    )
    return jax.shard_map(
        shards,
        mesh=mesh,
        in_specs=placed,
        out_specs=(P("dom", "grp"), P("dom", None), P(None, "grp"), P(None, "grp")),
        check_vma=False,
    )
```

profile of v0, /device:TPU:0, one launch (start us, length us, event | category | flops | bytes accessed | tf_op | source)
XLA Modules:
  0.0 238.3 jit_solution(9666383319873453520)
XLA Ops:
  9.1 2.6 %gather_fusion.1 = bf16[24,128,128]{2,1,0:T(8,128)(2,1)} fusion(bf16[16,128,128]{2,1,0:T(8,128)(2,1)} %bitcast.146, s32[1024]{0:T(1024)S(1)} %pad_clamp_fusion.2), kind=kCustom, calls=%fused_computation.1 | custom fusion | bytes 1572960 | tf_op jit(solution)/shard_map/gather | solution.py:50
  11.7 7.4 %all-to-all-start = ((bf16[8,3,128,128]{3,2,1,0:T(8,128)(2,1)}), bf16[8,3,128,128]{3,2,1,0:T(8,128)(2,1)}, u32[]{:S(2)}, u32[]{:S(2)}) async-start(bf16[8,3,128,128]{3,2,1,0:T(8,128)(2,1)} %bitcast.153), calls=%async_computation | async-start | bytes 1572864 | tf_op jit(solution)/shard_map/all_to_all | solution.py:51
  21.2 2.2 gather_fusion
  23.4 5.1 %convolution_bitcast_fusion.1 = f32[64,128,128]{1,2,0:T(8,128)} fusion(bf16[64,128,128]{2,1,0:T(8,128)(2,1)} %gather_fusion, bf16[1,64,128,128]{3,2,1,0:T(8,128)(2,1)S(1)} %copy-done.2), kind=kOutput, calls=%fused_computation.15 | convolution fusion | flops 268435456 | bytes 8388608 | tf_op jit(solution)/shard_map/nij,njf->nif/dot_general | solution.py:53
  28.5 5.7 %copy.25 = f32[64,128,128]{2,1,0:T(8,128)} copy(f32[64,128,128]{1,2,0:T(8,128)} %convolution_bitcast_fusion.1) | data formatting | bytes 8388608 | tf_op jit(solution)/shard_map/nij,njf->nif/dot_general | solution.py:53
  34.2 2.6 %fusion.57 = f32[2048,256]{1,0:T(8,128)} fusion(bf16[2048,128]{1,0:T(8,128)(2,1)S(1)} %copy-done.1, bf16[128,256]{1,0:T(8,128)(2,1)} %param.12), kind=kOutput, calls=%fused_computation.79 | convolution fusion | flops 134217728 | bytes 2686976 | tf_op jit(solution)/shard_map/dot_general | solution.py:64
  36.8 6.8 %fusion.3 = f32[16,128,128]{2,0,1:T(8,128)} fusion(s32[64]{0:T(128)S(1)} %bitcast.158, f32[8,8,128,128]{3,2,1,0:T(8,128)} %bitcast.150), kind=kOutput, calls=%fused_computation.9 | convolution fusion | flops 201327616 | bytes 5243136 | tf_op jit(solution)/shard_map/dot_general | solution.py:9
  43.5 3.0 %convolution_bitcast_fusion.2 = f32[24,128,128]{1,2,0:T(8,128)} fusion(bf16[24,128,128]{2,1,0:T(8,128)(2,1)} %bitcast.34, bf16[1,24,128,128]{3,2,1,0:T(8,128)(2,1)S(1)} %copy-done.4), kind=kOutput, calls=%fused_computation.27 | convolution fusion | flops 100663296 | bytes 3145728 | tf_op jit(solution)/shard_map/nij,njf->nif/dot_general | solution.py:56
  46.5 3.0 %copy.29 = f32[24,128,128]{2,1,0:T(8,128)} copy(f32[24,128,128]{1,2,0:T(8,128)} %convolution_bitcast_fusion.2) | data formatting | bytes 3145728 | tf_op jit(solution)/shard_map/nij,njf->nif/dot_general | solution.py:56
  49.6 4.1 %fusion.26 = bf16[16,128,128]{2,0,1:T(8,128)(2,1)S(1)} fusion(f32[16,128,128]{2,0,1:T(8,128)} %fusion.3, bf16[16,128,128]{2,1,0:T(8,128)(2,1)S(1)} %bitcast.148, f32[16,128]{0,1:T(8,128)S(1)} %copy.31, f32[24]{0:T(128)S(1)} %reshape.188, s32[24]{0:T(128)S(1)} %bitcast.162, f32[3,8,128,128]{3,2,1,0:T(8,128)} %bitcast.156), kind=kOutput, calls=%fused_computation.33 | convolution fusion | flops 76808960 | bytes 3678400 | tf_op jit(solution)/shard_map/dot_general | solution.py:9
  53.9 2.2 multiply_convert_fusion
  60.0 53.1 %all-reduce.7.cloned.1.call-done = (f32[2048,128]{1,0:T(8,128)}, f32[16,128,128]{2,0,1:T(8,128)}) async-done(((f32[2048,128]{1,0:T(8,128)}, f32[16,128,128]{2,0,1:T(8,128)}), (f32[2048,128]{1,0:T(8,128)}, f32[16,128,128]{2,0,1:T(8,128)})) %all-reduce.7.cloned.1.call-update) | async-done | bytes 2097168 | tf_op jit(solution)/shard_map/psum | solution.py:83
  117.2 2.7 %multiply_convert_fusion.2 = bf16[24,128,128]{2,1,0:T(8,128)(2,1)} fusion(bf16[24,128,128]{2,1,0:T(8,128)(2,1)} %gather_fusion.3, bf16[1,24,128,128]{3,2,1,0:T(8,128)(2,1)} %param.20, f32[24]{0:T(128)S(1)} %reshape.188), kind=kOutput, calls=%fused_computation.25 | convolution fusion | flops 101449728 | bytes 2359392 | tf_op jit(solution)/shard_map/nij,nif->njf/dot_general | solution.py:91
  119.9 2.3 copy.41
  122.2 5.5 %all-to-all-start.1 = ((bf16[8,3,128,128]{3,2,1,0:T(8,128)(2,1)}), bf16[8,3,128,128]{3,2,1,0:T(8,128)(2,1)}, u32[]{:S(2)}, u32[]{:S(2)}) async-start(bf16[8,3,128,128]{3,2,1,0:T(8,128)(2,1)} %copy.41), calls=%async_computation.1 | async-start | bytes 1572864 | tf_op jit(solution)/shard_map/all_to_all | solution.py:94
  128.2 2.4 %fusion.60 = f32[128,256]{1,0:T(8,128)} fusion(bf16[2048,128]{1,0:T(8,128)(2,1)} %bitcast.155, bf16[2048,256]{1,0:T(8,128)(2,1)} %copy-done.3), kind=kOutput, calls=%fused_computation.82 | convolution fusion | flops 134217728 | bytes 1703936 | tf_op jit(solution)/shard_map/dot_general | solution.py:74
  130.6 2.4 convolution_bitcast_fusion.3
  133.0 73.3 %all-reduce.5.cloned.1.call-done = (f32[128,256]{0,1:T(8,128)}, f32[128,256]{1,0:T(8,128)}) async-done(((f32[128,256]{0,1:T(8,128)}, f32[128,256]{1,0:T(8,128)}), (f32[128,256]{0,1:T(8,128)}, f32[128,256]{1,0:T(8,128)})) %all-reduce.5.cloned.1.call-update) | async-done | bytes 262160 | tf_op jit(solution)/shard_map/psum | solution.py:75
  206.3 1.7 copy.44
  208.0 2.1 gather_fusion.2
  210.1 4.5 %convolution_bitcast_fusion = f32[64,128,128]{1,2,0:T(8,128)} fusion(bf16[64,128,128]{2,1,0:T(8,128)(2,1)} %gather_fusion.2, bf16[1,64,128,128]{3,2,1,0:T(8,128)(2,1)S(1)} %copy-done.2), kind=kOutput, calls=%fused_computation.14 | convolution fusion | flops 268435456 | bytes 8388608 | tf_op jit(solution)/shard_map/nij,nif->njf/dot_general | solution.py:87
  214.5 5.6 %copy.36 = f32[64,128,128]{2,1,0:T(8,128)} copy(f32[64,128,128]{1,2,0:T(8,128)} %convolution_bitcast_fusion) | data formatting | bytes 8388608 | tf_op jit(solution)/shard_map/nij,nif->njf/dot_general | solution.py:87
  220.2 1.9 fusion.29
  222.0 5.8 %fusion.17 = f32[16,128,128]{2,0,1:T(8,128)S(1)} fusion(f32[16,128,128]{2,0,1:T(8,128)S(1)} %fusion.29, bf16[16,128,128]{2,0,1:T(8,128)(2,1)S(1)} %copy-done.6, s32[64]{0:T(128)S(1)} %bitcast.159, f32[8,8,128,128]{3,2,1,0:T(8,128)} %bitcast.149), kind=kOutput, calls=%fused_computation.30 | convolution fusion | flops 202114048 | bytes 6816000 | tf_op jit(solution)/shard_map/dot_general | solution.py:9
  (73 shorter events, 14.7 us)
Async XLA Ops:
  8.0 45.8 %copy-start = (bf16[128,256]{1,0:T(8,128)(2,1)S(1)}, bf16[128,256]{1,0:T(8,128)(2,1)}, u32[]{:S(2)}) copy-start(bf16[128,256]{1,0:T(8,128)(2,1)} %param.13) | copy-start | bytes 196612
  8.0 11.1 %copy-start.15 = (s32[1,8]{1,0:T(1,128)S(1)}, s32[1,8]{1,0:T(1,128)}, u32[]{:S(2)}) copy-start(s32[1,8]{1,0:T(1,128)} %param.21) | copy-start | bytes 100
  8.0 11.2 %copy-start.4 = (bf16[1,24,128,128]{3,2,1,0:T(8,128)(2,1)S(1)}, bf16[1,24,128,128]{3,2,1,0:T(8,128)(2,1)}, u32[]{:S(2)}) copy-start(bf16[1,24,128,128]{3,2,1,0:T(8,128)(2,1)} %param.20) | copy-start | bytes 2359300
  8.0 11.5 %copy-start.2 = (bf16[1,64,128,128]{3,2,1,0:T(8,128)(2,1)S(1)}, bf16[1,64,128,128]{3,2,1,0:T(8,128)(2,1)}, u32[]{:S(2)}) copy-start(bf16[1,64,128,128]{3,2,1,0:T(8,128)(2,1)} %param.17) | copy-start | bytes 6291460
  11.7 8.5 %copy-start.13 = (s32[1,64]{1,0:T(1,128)S(1)}, s32[1,64]{1,0:T(1,128)}, u32[]{:S(2)}) copy-start(s32[1,64]{1,0:T(1,128)} %param.15) | copy-start | bytes 772
  11.7 8.7 %copy-start.16 = (s32[1,24]{1,0:T(1,128)S(1)}, s32[1,24]{1,0:T(1,128)}, u32[]{:S(2)}) copy-start(s32[1,24]{1,0:T(1,128)} %param.19) | copy-start | bytes 292
  11.7 9.6 %copy-start.1 = (bf16[2048,128]{1,0:T(8,128)(2,1)S(1)}, bf16[2048,128]{1,0:T(8,128)(2,1)}, u32[]{:S(2)}) copy-start(bf16[2048,128]{1,0:T(8,128)(2,1)} %param.11) | copy-start | bytes 1572868
  11.7 31.9 %all-to-all-start = ((bf16[8,3,128,128]{3,2,1,0:T(8,128)(2,1)}), bf16[8,3,128,128]{3,2,1,0:T(8,128)(2,1)}, u32[]{:S(2)}, u32[]{:S(2)}) async-start(bf16[8,3,128,128]{3,2,1,0:T(8,128)(2,1)} %bitcast.153), calls=%async_computation | async-start | bytes 1572864 | tf_op jit(solution)/shard_map/all_to_all | solution.py:51
  19.0 94.0 %all-reduce.7.cloned.1.call-start = ((), (), s32[]{:S(2)}) async-start(), calls=%async_computation.3 | async-start | bytes 4194304 | tf_op jit(solution)/shard_map/psum | solution.py:83
  46.5 3.0 %copy-start.17 = (s32[1,24]{1,0:T(1,128)S(1)}, s32[1,24]{1,0:T(1,128)}, u32[]{:S(2)}) copy-start(s32[1,24]{1,0:T(1,128)} %param.19) | copy-start | bytes 292
  49.6 4.3 %copy-start.7 = (f32[2048,256]{1,0:T(8,128)S(1)}, f32[2048,256]{1,0:T(8,128)}, u32[]{:S(2)}) copy-start(f32[2048,256]{1,0:T(8,128)} %fusion.57) | copy-start | bytes 6291460
  49.6 4.3 %copy-start.18 = (bf16[2048,256]{1,0:T(8,128)(2,1)S(1)}, bf16[2048,256]{1,0:T(8,128)(2,1)}, u32[]{:S(2)}) copy-start(bf16[2048,256]{1,0:T(8,128)(2,1)} %param.14) | copy-start | bytes 3145732
  53.8 2.2 copy-start.8
  56.1 2.3 copy-start.3
  56.1 0.9 copy-start.10
  114.7 0.8 copy-start.5
  119.9 8.1 %copy-start.12 = (s32[1,8,3]{1,0,2:T(1,128)S(1)}, s32[1,8,3]{1,0,2:T(1,128)}, u32[]{:S(2)}) copy-start(s32[1,8,3]{1,0,2:T(1,128)} %param.18) | copy-start | bytes 292
  122.2 97.9 %all-to-all-start.1 = ((bf16[8,3,128,128]{3,2,1,0:T(8,128)(2,1)}), bf16[8,3,128,128]{3,2,1,0:T(8,128)(2,1)}, u32[]{:S(2)}, u32[]{:S(2)}) async-start(bf16[8,3,128,128]{3,2,1,0:T(8,128)(2,1)} %copy.41), calls=%async_computation.1 | async-start | bytes 1572864 | tf_op jit(solution)/shard_map/all_to_all | solution.py:94
  127.7 78.6 %all-reduce.5.cloned.1.call-start = ((), (), s32[]{:S(2)}) async-start(), calls=%async_computation.2 | async-start | bytes 524288 | tf_op jit(solution)/shard_map/psum | solution.py:75
  214.5 7.5 %copy-start.14 = (s32[1,64]{1,0:T(1,128)S(1)}, s32[1,64]{1,0:T(1,128)}, u32[]{:S(2)}) copy-start(s32[1,64]{1,0:T(1,128)} %param.16) | copy-start | bytes 772
  220.2 1.9 copy-start.6
  227.9 1.2 copy-start.9
  228.2 1.9 copy-start.11
Sparse Core Ops, SparseCore 0:
  60.1 52.9 all-reduce.6
Sparse Core Ops, SparseCore 1:
  133.0 73.2 all-reduce.4
where the time goes:
time: 239 us; the launch traced here: 238 us
  waiting for transfers between devices  126 us (53%)
  matrix products  45.5 us (19%)
  local copies, waits for them, and re-layouts  32.3 us (14%)
  between operations  15.7 us (7%)
  starting transfers between devices  13.2 us (6%)
  other arithmetic  5.14 us (2%)
    psum x1, waiting for transfers between devices, shards(): grad_self, grad_neigh = lax.psum((grad_self, grad_neigh), 'dom')  73.3 us
    psum x1, waiting for transfers between devices, shards(): self_back, neigh_back = lax.psum((self_part, neigh_part), 'grp')  53.1 us
    dot_general x4, matrix products, block_segment(): jnp.dot(one_hot, products.reshape(count, -1), precision=lax.Precision.HIG...  18.6 us
    all_to_all x1, starting transfers between devices, shards(): lax.all_to_all(outgoing, 'dom', split_axis=0, concat_axis=0, tiled=True)  7.38 us
    dot_general x1, local copies, waits for them, and re-layouts, shards(): jnp.einsum('nij,njf->nif', inner_a, feat_blocks[col_inner], preferred_ele...  5.66 us
    dot_general x1, local copies, waits for them, and re-layouts, shards(): jnp.einsum('nij,nif->njf', inner_a, scaled[row_inner], preferred_element_...  5.61 us
    all_to_all x1, starting transfers between devices, shards(): lax.all_to_all(outer_back.reshape(peer_count, slot_depth, block_size, fea...  5.51 us
    dot_general x1, matrix products, shards(): jnp.einsum('nij,njf->nif', inner_a, feat_blocks[col_inner], preferred_ele...  5.14 us
  transfers between devices with their start and end apart: 4, of which 2 were waited for; matrix products, arithmetic and copies ran while one was open for 18% of the time, Pallas kernels for 0%

commit v1 on v0

v1 whole, which is shorter than its diff:
```python
import functools

import jax
import jax.numpy as jnp
from jax import lax
from jax.experimental import pallas as pl
from jax.experimental.pallas import tpu as pltpu
from jax.sharding import PartitionSpec as P

F32 = jnp.float32
BF16 = jnp.bfloat16
MIB = 1 << 20
GROUP = 8
ROWS_LAST = (((1,), (1,)), ((), ()))
ROWS_FIRST = (((0,), (0,)), ((), ()))
WHOLE = pl.BlockSpec(memory_space=pltpu.VMEM)
SCALARS = pl.BlockSpec(memory_space=pltpu.SMEM)
ANYWHERE = pl.BlockSpec(memory_space=pl.ANY)


def dot(a, b):
    return jnp.dot(a, b, preferred_element_type=F32)


def params(mib):
    return pltpu.CompilerParams(vmem_limit_bytes=int(mib * MIB))


def cost(flops, moved):
    return pl.CostEstimate(flops=int(flops), bytes_accessed=int(moved), transcendentals=0)


def gather_kernel(half, targets, feat, out, sem):
    peers, slots = targets.shape
    block = half * 2
    mine = lax.axis_index("grp") % 2
    for p in range(peers):
        for s in range(slots):
            start = pl.multiple_of(targets[p, s] * block + mine * half, half)
            pltpu.make_async_copy(feat.at[pl.ds(start, half)], out.at[p, s], sem).start()
    pltpu.make_async_copy(out, out, sem).wait()


def gather_halves(features, targets, block):
    peers, slots = targets.shape
    return pl.pallas_call(
        functools.partial(gather_kernel, block // 2),
        out_shape=jax.ShapeDtypeStruct((peers, slots, block // 2, features.shape[1]), BF16),
        in_specs=[SCALARS, ANYWHERE],
        out_specs=ANYWHERE,
        scratch_shapes=[pltpu.SemaphoreType.DMA],
        name="gather_halves",
    )(targets, features)


def inner_kernel(rows, cols, feat, a, total, wide):
    step = pl.program_id(0)
    loc, block, width = total.shape
    feat_width = width // 2

    @pl.when(step == 0)
    def _():
        x = feat[...].reshape(loc, block, feat_width)
        wide[:, :, :feat_width] = x
        wide[:, :, feat_width:] = jnp.ones((loc, block, feat_width), BF16)
        total[:, :, :feat_width] = x.astype(F32)
        total[:, :, feat_width:] = jnp.ones((loc, block, feat_width), F32)

    count = a.shape[0]
    products = [dot(a[k], wide[cols[0, step * count + k]]) for k in range(count)]
    for k in range(count):
        total[rows[0, step * count + k]] += products[k]


def inner_sums(rows, cols, features, values):
    count, block, _ = values.shape
    nodes, feat_width = features.shape
    loc = nodes // block
    return pl.pallas_call(
        inner_kernel,
        out_shape=jax.ShapeDtypeStruct((loc, block, 2 * feat_width), F32),
        grid=(count // GROUP,),
        in_specs=[
            SCALARS,
            SCALARS,
            pl.BlockSpec((nodes, feat_width), lambda i: (0, 0)),
            pl.BlockSpec((GROUP, block, block), lambda i: (i, 0, 0)),
        ],
        out_specs=pl.BlockSpec((loc, block, 2 * feat_width), lambda i: (0, 0, 0)),
        scratch_shapes=[pltpu.VMEM((loc, block, 2 * feat_width), BF16)],
        compiler_params=params(16),
        cost_estimate=cost(count * block * block * feat_width * 4, 6 * MIB),
        name="inner_sums",
    )(rows, cols, features, values)


def layer_kernel(
    chunk_blocks,
    outer_rows, live, own, other, outer, total, feat, cot, w_self, w_neigh,
    layer_out, grads, send_n, keep_n, send_s, keep_s,
    x_wide, a_all, far, weights, turned, grad_sum, sems,
):
    step = pl.program_id(0)
    peers, slots, half, feat_width = own.shape
    count, block, _ = a_all.shape
    loc = far.shape[0]
    group = lax.axis_size("grp")
    part = feat_width // group
    me = lax.axis_index("grp")

    @pl.when(step == 0)
    def _():
        mine = me % 2
        copies = [
            pltpu.make_async_copy(
                own, x_wide.at[:, :, pl.ds(pl.multiple_of(mine * half, half), half), pl.ds(0, feat_width)], sems.at[0]
            ),
            pltpu.make_async_copy(
                other,
                x_wide.at[:, :, pl.ds(pl.multiple_of((1 - mine) * half, half), half), pl.ds(0, feat_width)],
                sems.at[1],
            ),
            pltpu.make_async_copy(outer, a_all, sems.at[2]),
        ]
        for copy in copies:
            copy.start()
        x_wide[:, :, :, feat_width:] = jnp.ones((peers, slots, block, feat_width), BF16)
        far[...] = jnp.zeros_like(far)
        grad_sum[...] = jnp.zeros_like(grad_sum)
        weights[:feat_width] = w_self[...]
        weights[feat_width:] = w_neigh[...]
        for place, away in enumerate((3, 1, 2, 0)):
            start = pl.multiple_of((me ^ away) * part, part)
            turned[pl.ds(place * part, part)] = w_self[pl.ds(start, part)]
            turned[pl.ds(feat_width + place * part, part)] = w_neigh[pl.ds(start, part)]
        for copy in copies:
            copy.wait()

        def some(g, _):
            products = []
            for k in range(GROUP):
                n = g * GROUP + k
                products.append(dot(a_all[n], x_wide[n // slots, n % slots]))
            for k in range(GROUP):
                n = g * GROUP + k
                alive = (n % slots < live[0, n // slots]).astype(F32)
                far[outer_rows[0, n]] += products[k] * alive
            return 0

        lax.fori_loop(0, count // GROUP, some, 0)

    rows = chunk_blocks * block
    here = (total[...] + far[pl.ds(step * chunk_blocks, chunk_blocks)]).reshape(rows, 2 * feat_width)
    over = 1.0 / here[:, feat_width:]
    agg = (here[:, :feat_width] * over).astype(BF16)
    both = jnp.concatenate([feat[...], agg], axis=1)
    pre = dot(both, weights[...])
    sig = 0.5 * jnp.tanh(0.5 * pre) + 0.5
    smooth = pre * sig
    layer_out[...] = smooth.astype(BF16)
    grad_pre = (cot[...].astype(F32) * (sig + smooth * (1.0 - sig))).astype(BF16)
    grad_sum[...] += lax.dot_general(both, grad_pre, ROWS_FIRST, preferred_element_type=F32)
    self_t = lax.dot_general(turned[:feat_width], grad_pre, ROWS_LAST, preferred_element_type=F32).astype(BF16)
    neigh = lax.dot_general(grad_pre, turned[feat_width:], ROWS_LAST, preferred_element_type=F32)
    neigh = (neigh * over).astype(BF16)
    eye = lax.broadcasted_iota(jnp.int32, (feat_width, feat_width), 0) == lax.broadcasted_iota(
        jnp.int32, (feat_width, feat_width), 1
    )
    neigh_t = lax.dot_general(eye.astype(BF16), neigh, ROWS_LAST, preferred_element_type=F32).astype(BF16)
    for b in range(chunk_blocks):
        lanes = slice(b * block, (b + 1) * block)
        for y in range(2):
            send_n[y, b] = neigh_t[y * part : (y + 1) * part, lanes]
            keep_n[y, b] = neigh_t[(2 + y) * part : (3 + y) * part, lanes]
            send_s[y, b] = self_t[y * part : (y + 1) * part, lanes]
            keep_s[y, b] = self_t[(2 + y) * part : (3 + y) * part, lanes]

    @pl.when(step == pl.num_programs(0) - 1)
    def _():
        grads[...] = grad_sum[...].astype(BF16)


def layer(outer_rows, live, own, other, outer, total, features, cotangent, w_self, w_neigh):
    nodes, feat_width = features.shape
    hidden = cotangent.shape[1]
    loc, block, _ = total.shape
    peers, slots, half, _ = own.shape
    count = outer.shape[0]
    chunk = 4
    rows = chunk * block
    part = feat_width // lax.axis_size("grp")
    piece = jax.ShapeDtypeStruct((2, loc, part, block), BF16)
    piece_spec = pl.BlockSpec((2, chunk, part, block), lambda i: (0, i, 0, 0))
    far_bytes = count * block * (block + 2 * feat_width) * 2
    return pl.pallas_call(
        functools.partial(layer_kernel, chunk),
        out_shape=(
            jax.ShapeDtypeStruct((nodes, hidden), BF16),
            jax.ShapeDtypeStruct((2 * feat_width, hidden), BF16),
            piece, piece, piece, piece,
        ),
        grid=(loc // chunk,),
        in_specs=[
            SCALARS, SCALARS, ANYWHERE, ANYWHERE, ANYWHERE,
            pl.BlockSpec((chunk, block, 2 * feat_width), lambda i: (i, 0, 0)),
            pl.BlockSpec((rows, feat_width), lambda i: (i, 0)),
            pl.BlockSpec((rows, hidden), lambda i: (i, 0)),
            pl.BlockSpec((feat_width, hidden), lambda i: (0, 0)),
            pl.BlockSpec((feat_width, hidden), lambda i: (0, 0)),
        ],
        out_specs=(
            pl.BlockSpec((rows, hidden), lambda i: (i, 0)),
            pl.BlockSpec((2 * feat_width, hidden), lambda i: (0, 0)),
            piece_spec, piece_spec, piece_spec, piece_spec,
        ),
        scratch_shapes=[
            pltpu.VMEM((peers, slots, block, 2 * feat_width), BF16),
            pltpu.VMEM((count, block, block), BF16),
            pltpu.VMEM((loc, block, 2 * feat_width), F32),
            pltpu.VMEM((2 * feat_width, hidden), BF16),
            pltpu.VMEM((2 * feat_width, hidden), BF16),
            pltpu.VMEM((2 * feat_width, hidden), F32),
            pltpu.SemaphoreType.DMA((3,)),
        ],
        compiler_params=params(20 + far_bytes / MIB),
        cost_estimate=cost(1.2e9, 8 * MIB),
        name="layer",
    )(outer_rows, live, own, other, outer, total, features, cotangent, w_self, w_neigh)


def outer_back_kernel(outer_rows, live, keep, got, came, outer, scaled, payload):
    peers, slots, part, block = payload.shape
    scaled[...] = (keep[1].astype(F32) + got[1].astype(F32) + came[...].astype(F32)).astype(BF16)

    def some(g, _):
        products = []
        for k in range(GROUP):
            n = g * GROUP + k
            products.append(dot(scaled[outer_rows[0, n]], outer[n]))
        for k in range(GROUP):
            n = g * GROUP + k
            alive = (n % slots < live[0, n // slots]).astype(F32)
            payload[n // slots, n % slots] = (products[k] * alive).astype(BF16)
        return 0

    lax.fori_loop(0, outer.shape[0] // GROUP, some, 0)


def outer_back(outer_rows, live, keep, got, came, outer, peers):
    loc, part, block = came.shape
    count = outer.shape[0]
    return pl.pallas_call(
        outer_back_kernel,
        out_shape=(
            jax.ShapeDtypeStruct((loc, part, block), BF16),
            jax.ShapeDtypeStruct((peers, count // peers, part, block), BF16),
        ),
        in_specs=[SCALARS, SCALARS, WHOLE, WHOLE, WHOLE, WHOLE],
        out_specs=(WHOLE, WHOLE),
        compiler_params=params(8 + count * block * (block + part) * 2 / MIB),
        cost_estimate=cost(count * block * block * part * 2, 2 * MIB),
        name="outer_back",
    )(outer_rows, live, keep, got, came, outer)


def inner_back_kernel(rows, cols, scaled, keep, got, came, a, total):
    step = pl.program_id(0)

    @pl.when(step == 0)
    def _():
        total[...] = (
            keep[1].astype(F32) + got[1].astype(F32) + came[...].astype(F32) + scaled[...].astype(F32)
        )

    count = a.shape[0]
    products = [dot(scaled[rows[0, step * count + k]], a[k]) for k in range(count)]
    for k in range(count):
        total[cols[0, step * count + k]] += products[k]


def inner_back(rows, cols, scaled, keep, got, came, values):
    count, block, _ = values.shape
    loc, part, _ = scaled.shape
    zero3 = lambda i: (0, 0, 0)
    zero4 = lambda i: (0, 0, 0, 0)
    group = 2 * GROUP
    return pl.pallas_call(
        inner_back_kernel,
        out_shape=jax.ShapeDtypeStruct((loc, part, block), F32),
        grid=(count // group,),
        in_specs=[
            SCALARS,
            SCALARS,
            pl.BlockSpec(scaled.shape, zero3),
            pl.BlockSpec(keep.shape, zero4),
            pl.BlockSpec(got.shape, zero4),
            pl.BlockSpec(came.shape, zero3),
            pl.BlockSpec((group, block, block), lambda i: (i, 0, 0)),
        ],
        out_specs=pl.BlockSpec((loc, part, block), zero3),
        compiler_params=params(8),
        cost_estimate=cost(count * block * block * part * 2, 3 * MIB),
        name="inner_back",
    )(rows, cols, scaled, keep, got, came, values)


def add_returned_kernel(targets, returned, total, out, summed):
    peers, slots, _, _ = returned.shape
    summed[...] = total[...]

    def some(q, _):
        for s in range(slots):
            summed[targets[q, s]] += returned[q, s].astype(F32)
        return 0

    lax.fori_loop(0, peers, some, 0)
    out[...] = summed[...].astype(BF16)


def add_returned(targets, returned, total):
    return pl.pallas_call(
        add_returned_kernel,
        out_shape=jax.ShapeDtypeStruct(total.shape, BF16),
        in_specs=[SCALARS, WHOLE, WHOLE],
        out_specs=WHOLE,
        scratch_shapes=[pltpu.VMEM(total.shape, F32)],
        compiler_params=params(8 + returned.size * 2 / MIB),
        cost_estimate=cost(total.size * 8, 2 * MIB),
        name="add_returned",
    )(targets, returned, total)


def turn_kernel(mine, across, beside, out):
    loc, part, block = mine.shape
    me = lax.axis_index("grp")
    feat_width = out.shape[1]
    row = lax.broadcasted_iota(jnp.int32, (feat_width, feat_width), 0)
    lane = lax.broadcasted_iota(jnp.int32, (feat_width, feat_width), 1)
    stacked = row // part
    away = jnp.where(stacked == 1, 2, jnp.where(stacked == 2, 1, stacked))
    order = (((me ^ away) * part + row % part) == lane).astype(BF16)
    for b in range(loc):
        stack = jnp.concatenate([mine[b], across[b], beside[0, b], beside[1, b]], axis=0)
        out[b * block : (b + 1) * block] = lax.dot_general(stack, order, ROWS_FIRST, preferred_element_type=F32)


def turn(mine, across, beside, feat_width):
    loc, part, block = mine.shape
    return pl.pallas_call(
        turn_kernel,
        out_shape=jax.ShapeDtypeStruct((loc * block, feat_width), F32),
        in_specs=[WHOLE, WHOLE, WHOLE],
        out_specs=WHOLE,
        compiler_params=params(8),
        cost_estimate=cost(loc * block * feat_width * feat_width * 2, 2 * MIB),
        name="turn",
    )(mine, across, beside)


def swap(x, axis, bit):
    return lax.ppermute(x, axis, [(i, i ^ bit) for i in range(lax.axis_size(axis))])


def shards(
    features,
    weight_self,
    weight_neigh,
    cotangent,
    inner_rows,
    inner_cols,
    inner_values,
    send_blocks,
    outer_rows,
    outer_values,
    live_count,
):
    peers = lax.axis_size("dom")
    feat_width = features.shape[1]
    inner_a, outer_a, targets = inner_values[0], outer_values[0], send_blocks[0]
    block = inner_a.shape[-1]

    outgoing = gather_halves(features, targets, block)
    own = lax.all_to_all(outgoing, "dom", split_axis=0, concat_axis=0, tiled=True)
    total = inner_sums(inner_rows, inner_cols, features, inner_a)
    other = swap(own, "grp", 1)
    layer_out, grads, send_n, keep_n, send_s, keep_s = layer(
        outer_rows, live_count, own, other, outer_a, total, features, cotangent, weight_self, weight_neigh
    )
    got_n = swap(send_n, "grp", 1)
    came_n = swap((keep_n[0].astype(F32) + got_n[0].astype(F32)).astype(BF16), "grp", 2)
    got_s = swap(send_s, "grp", 1)
    came_s = swap((keep_s[0].astype(F32) + got_s[0].astype(F32)).astype(BF16), "grp", 2)
    scaled, payload = outer_back(outer_rows, live_count, keep_n, got_n, came_n, outer_a, peers)
    returned = lax.all_to_all(payload, "dom", split_axis=0, concat_axis=0, tiled=True)
    bit = peers // 2
    while bit:
        grads = grads.astype(BF16)
        grads = grads.astype(F32) + swap(grads, "dom", bit).astype(F32)
        bit //= 2
    partial = inner_back(inner_rows, inner_cols, scaled, keep_s, got_s, came_s, inner_a)
    mine = add_returned(targets, returned, partial)
    across = swap(mine, "grp", 2)
    beside = swap(jnp.stack([mine, across]), "grp", 1)
    feature_grad = turn(mine, across, beside, feat_width)
    return layer_out, feature_grad, grads[:feat_width], grads[feat_width:]


def solution(mesh):
    placed = (
        P("dom", None),
        P(None, "grp"),
        P(None, "grp"),
        P("dom", "grp"),
        P("dom", None),
        P("dom", None),
        P("dom", None, None, None),
        P("dom", None, None),
        P("dom", None),
        P("dom", None, None, None),
        P("dom", None),
    )
    return jax.shard_map(
        shards,
        mesh=mesh,
        in_specs=placed,
        out_specs=(P("dom", "grp"), P("dom", None), P(None, "grp"), P(None, "grp")),
        check_vma=False,
    )
```

time: 239 us -> 81.8 us (0.34)
  waiting for transfers between devices: 126 us -> 13.3 us
  matrix products: 45.5 us -> 0 us
  Pallas kernels: 0 us -> 28.7 us
  local copies, waits for them, and re-layouts: 32.3 us -> 6.06 us
  blocking collectives: 0 us -> 19.4 us
  between operations: 15.7 us -> 0.84 us
  other arithmetic: 5.14 us -> 1.77 us
    psum x2 -> x0, waiting for transfers between devices: 126 us -> none  [the longest x1 73.3 us: shards(): grad_self, grad_neigh = lax.psum((grad_self, grad_neigh), 'dom')]
    dot_general x16 -> x0, matrix products: 45.5 us -> none  [the longest x4 18.6 us: block_segment(): jnp.dot(one_hot, products.reshape(count, -1), precision=lax.Precision.HIG...]
    pallas_call x0 -> x7, Pallas kernels: none -> 28.7 us  [the longest x1 13.8 us: gather_halves(): pl.pallas_call(functools.partial(gather_kernel, block // 2), out_shape=ja...]
    all_to_all x0 -> x1, blocking collectives: none -> 19.4 us  [shards(): lax.all_to_all(outgoing, 'dom', split_axis=0, concat_axis=0, tiled=True)]
    dot_general x3 -> x0, local copies, waits for them, and re-layouts: 14.3 us -> none  [the longest x1 5.66 us: shards(): jnp.einsum('nij,njf->nif', inner_a, feat_blocks[col_inner], preferred_ele...]
    ppermute x0 -> x10, waiting for transfers between devices: none -> 9.24 us  [swap(): lax.ppermute(x, axis, [(i, i ^ bit) for i in range(lax.axis_size(axis))])]
    all_to_all x2 -> x1, starting transfers between devices: 12.9 us -> 3.79 us  [shards(): lax.all_to_all(payload, 'dom', split_axis=0, concat_axis=0, tiled=True)]
    gather x4 -> x0, local copies, waits for them, and re-layouts: 8.45 us -> none  [the longest x1 2.6 us: shards(): outgoing = feat_blocks[targets]]
  transfers between devices with their start and end apart: 4 -> 11, of which waited for: 2 -> 5; matrix products, arithmetic and copies ran while one was open for 18% -> 3% of each run, Pallas kernels for 0% -> 9%
where the time goes in v1:
time: 81.8 us; the launch traced here: 81.3 us
  Pallas kernels  28.7 us (35%)
  blocking collectives  19.4 us (24%)
  waiting for transfers between devices  13.3 us (16%)
  starting transfers between devices  11.2 us (14%)
  local copies, waits for them, and re-layouts  6.06 us (7%)
  other arithmetic  1.77 us (2%)
  between operations  0.84 us (1%)
    all_to_all x1, blocking collectives, shards(): lax.all_to_all(outgoing, 'dom', split_axis=0, concat_axis=0, tiled=True)  19.4 us
    pallas_call x1, Pallas kernels, gather_halves(): pl.pallas_call(functools.partial(gather_kernel, block // 2), out_shape=ja...  13.8 us
    ppermute x10, waiting for transfers between devices, swap(): lax.ppermute(x, axis, [(i, i ^ bit) for i in range(lax.axis_size(axis))])  9.24 us
    ppermute x10, starting transfers between devices, swap(): lax.ppermute(x, axis, [(i, i ^ bit) for i in range(lax.axis_size(axis))])  7.46 us
    pallas_call x1, Pallas kernels, layer(): pl.pallas_call(functools.partial(layer_kernel, chunk), out_shape=(jax.Sha...  5.96 us
    all_to_all x1, waiting for transfers between devices, shards(): lax.all_to_all(payload, 'dom', split_axis=0, concat_axis=0, tiled=True)  4.06 us
    unnamed x30, local copies, waits for them, and re-layouts  4 us
    all_to_all x1, starting transfers between devices, shards(): lax.all_to_all(payload, 'dom', split_axis=0, concat_axis=0, tiled=True)  3.79 us
  transfers between devices with their start and end apart: 11, of which 5 were waited for; matrix products, arithmetic and copies ran while one was open for 3% of the time, Pallas kernels for 9%

profile of v1, /device:TPU:0, one launch (start us, length us, event | category | flops | bytes accessed | tf_op | source)
XLA Modules:
  0.0 81.3 jit_solution(2880460886794872160)
XLA Ops:
  0.6 1.3 %copy.17 = s32[1,8,3]{2,1,0:T(8,128)} copy(s32[1,8,3]{1,0,2:T(1,128)} %param.18) | data formatting | bytes 192 | tf_op jit(solution)/shard_map/squeeze | solution.py:379
  2.0 13.8 %gather_halves.1 = bf16[8,3,64,128]{3,2,1,0:T(8,128)(2,1)} custom-call(s32[8,3]{1,0:T(8,128)} %bitcast.15, bf16[2048,128]{1,0:T(8,128)(2,1)} %feat.5), custom_call_target="tpu_custom_call" | custom-call | tf_op jit(solution)/shard_map/gather_halves/pallas_call | solution.py:46
  15.7 19.4 %all_to_all.10.own = bf16[8,3,64,128]{3,2,1,0:T(8,128)(2,1)S(1)} all-to-all(bf16[8,3,64,128]{3,2,1,0:T(8,128)(2,1)} %gather_halves.1), channel_id=1, replica_groups=mesh['dom'=8,'grp'=4] {'dom'}, dimensions={0} | all-to-all | bytes 786432 | tf_op jit(solution)/shard_map/all_to_all | solution.py:383
  35.1 1.6 %copy-done = bf16[1,64,128,128]{3,2,1,0:T(8,128)(2,1)S(1)} copy-done((bf16[1,64,128,128]{3,2,1,0:T(8,128)(2,1)S(1)}, bf16[1,64,128,128]{3,2,1,0:T(8,128)(2,1)}, u32[]{:S(2)}) %copy-start) | copy-done | bytes 2097176
  36.7 1.0 %copy-done.2 = bf16[2048,128]{1,0:T(8,128)(2,1)S(1)} copy-done((bf16[2048,128]{1,0:T(8,128)(2,1)S(1)}, bf16[2048,128]{1,0:T(8,128)(2,1)}, u32[]{:S(2)}) %copy-start.2) | copy-done | bytes 524312
  37.7 0.7 copy-done.11
  39.1 3.4 %inner_sums.1.total = f32[16,128,256]{2,1,0:T(8,128)S(1)} custom-call(s32[1,64]{1,0:T(1,128)S(1)} %copy-done.11, s32[1,64]{1,0:T(1,128)S(1)} %copy-done.13, bf16[2048,128]{1,0:T(8,128)(2,1)S(1)} %copy-done.2, bf16[64,128,128]{2,1,0:T(8,128)(2,1)S(1)} %bitcast.9), custom_call_target="tpu_custom_call" | custom-call | flops 536870912 | bytes 6291456 | tf_op jit(solution)/shard_map/inner_sums/pallas_call | solution.py:79
  42.6 6.0 %layer.1 = (bf16[2048,256]{1,0:T(8,128)(2,1)}, bf16[256,256]{1,0:T(8,128)(2,1)S(1)}, bf16[2,16,32,128]{3,2,1,0:T(8,128)(2,1)S(1)}, bf16[2,16,32,128]{3,2,1,0:T(8...) custom-call(s32[1,24]{1,0:T(1,128)S(1)} %copy-done.9, s32[1,8]{1,0:T(1,128)S(1)} %copy-done.10, ...), custom_call_target="tpu_custom_call" | custom-call | flops 1200000000 | bytes 8388608 | tf_op jit(solution)/shard_map/layer/pallas_call | solution.py:195
  49.2 0.9 %collective-permute-start.7 = (bf16[256,256]{1,0:T(8,128)(2,1)S(1)}, bf16[256,256]{1,0:T(8,128)(2,1)S(1)}, u32[]{:S(2)}, u32[]{:S(2)}) collective-permute-start(bf16[256,256]{1,0:T(8,128)(2,1)S(1)} %get-tuple-element.19), channel_id=1, source_target_pairs={{0,16},{4,20},{8,24},{12,28},{16,0},{20,4},{24,8},{28,12},{1,17},{... | collective-permute-start | bytes 393224 | tf_op jit(solution)/shard_map/ppermute | solution.py:361
  50.3 1.6 %collective-permute-start.2 = (bf16[16,32,128]{2,1,0:T(8,128)(2,1)S(1)}, bf16[16,32,128]{2,1,0:T(8,128)(2,1)S(1)}, u32[]{:S(2)}, u32[]{:S(2)}) collective-permute-start(bf16[16,32,128]{2,1,0:T(8,128)(2,1)S(1)} %fusion), channel_id=1, source_target_pairs={{0,2},{1,3},{2,0},{3,1},{4,6},{5,7},{6,4},{7,5},{8,10},{9,11},{10,... | collective-permute-start | bytes 393224 | tf_op jit(solution)/shard_map/ppermute | solution.py:361
  52.6 4.2 %collective-permute-done.2.came = bf16[16,32,128]{2,1,0:T(8,128)(2,1)S(1)} collective-permute-done((bf16[16,32,128]{2,1,0:T(8,128)(2,1)S(1)}, bf16[16,32,128]{2,1,0:T(8,128)(2,1)S(1)}, u32[]{:S(2)}, u32[]{:S(2)}) %collective-permute-start.2) | collective-permute-done | bytes 131104 | tf_op jit(solution)/shard_map/ppermute | solution.py:361
  56.7 1.8 %outer_back.1 = (bf16[16,32,128]{2,1,0:T(8,128)(2,1)S(1)}, bf16[8,3,32,128]{3,2,1,0:T(8,128)(2,1)}) custom-call(s32[1,24]{1,0:T(1,128)S(1)} %copy-done.9, s32[1,8]{1,0:T(1,128)S(1)} %copy-done.10, bf16[2,16,32,128]{3,2,1,0:T(8,128)(2,1)S(1)} %get-tuple-element.13.keep, bf16[2,16,32,128]{3,2,1,0:T(8,128)(2,1)S(1)} %collective-permute-done.1.got, ...), custom_call_target="tpu_custom_call" | custom-call | flops 25165824 | bytes 2097152 | tf_op jit(solution)/shard_map/outer_back/pallas_call | solution.py:252
  58.6 3.8 %all-to-all-start.1 = ((bf16[8,3,32,128]{3,2,1,0:T(8,128)(2,1)}), bf16[8,3,32,128]{3,2,1,0:T(8,128)(2,1)S(1)}, u32[]{:S(2)}, u32[]{:S(2)}) async-start(bf16[8,3,32,128]{3,2,1,0:T(8,128)(2,1)} %get-tuple-element.15), calls=%async_computation.1 | async-start | bytes 393216 | tf_op jit(solution)/shard_map/all_to_all | solution.py:394
  62.4 0.7 add_convert_fusion.1
  63.1 2.0 %collective-permute-start.8 = (bf16[256,256]{1,0:T(8,128)(2,1)}, bf16[256,256]{1,0:T(8,128)(2,1)S(1)}, u32[]{:S(2)}, u32[]{:S(2)}) collective-permute-start(bf16[256,256]{1,0:T(8,128)(2,1)} %add_convert_fusion.1), channel_id=1, source_target_pairs={{0,8},{4,12},{8,0},{12,4},{16,24},{20,28},{24,16},{28,20},{1,9},{5... | collective-permute-start | bytes 393224 | tf_op jit(solution)/shard_map/ppermute | solution.py:361
  65.1 1.7 %inner_back.1.total = f32[16,32,128]{2,1,0:T(8,128)S(1)} custom-call(s32[1,64]{1,0:T(1,128)S(1)} %copy-done.12, s32[1,64]{1,0:T(1,128)S(1)} %copy-done.14, bf16[16,32,128]{2,1,0:T(8,128)(2,1)S(1)} %get-tuple-element.16.scaled, bf16[2,16,32,128]{3,2,1,0:T(8,128)(2,1)S(1)} %get-tuple-element.17.keep, bf16[2,16,32,128]{3,2,1,0:T(8,128)(2,1)S(1)} %collective-permute-done.3.got, ...), custom_call_target="tpu_custom_call" | custom-call | flops 67108864 | bytes 3145728 | tf_op jit(solution)/shard_map/inner_back/pallas_call | solution.py:287
  66.8 4.1 %all-to-all-done.1.returned = bf16[8,3,32,128]{3,2,1,0:T(8,128)(2,1)S(1)} async-done(((bf16[8,3,32,128]{3,2,1,0:T(8,128)(2,1)}), bf16[8,3,32,128]{3,2,1,0:T(8,128)(2,1)S(1)}, u32[]{:S(2)}, u32[]{:S(2)}) %all-to-all-start.1) | async-done | bytes 196640 | tf_op jit(solution)/shard_map/all_to_all | solution.py:394
  70.9 0.7 add_returned.1.mine
  71.6 1.6 %collective-permute-start.5 = (bf16[16,32,128]{2,1,0:T(8,128)(2,1)S(1)}, bf16[16,32,128]{2,1,0:T(8,128)(2,1)S(1)}, u32[]{:S(2)}, u32[]{:S(2)}) collective-permute-start(bf16[16,32,128]{2,1,0:T(8,128)(2,1)S(1)} %add_returned.1.mine), channel_id=1, source_target_pairs={{0,2},{1,3},{2,0},{3,1},{4,6},{5,7},{6,4},{7,5},{8,10},{9,11},{10,... | collective-permute-start | bytes 393224 | tf_op jit(solution)/shard_map/ppermute | solution.py:361
  73.2 0.9 %add_convert_fusion = bf16[256,256]{1,0:T(8,128)(2,1)S(1)} fusion(bf16[256,256]{1,0:T(8,128)(2,1)S(1)} %collective-permute-done.8, bf16[256,256]{1,0:T(8,128)(2,1)} %add_convert_fusion.1), kind=kLoop, calls=%fused_computation.2 | loop fusion | flops 262144 | bytes 393216 | tf_op jit(solution)/shard_map/convert_element_type | solution.py:397
  74.3 2.4 %collective-permute-done.5.across = bf16[16,32,128]{2,1,0:T(8,128)(2,1)S(1)} collective-permute-done((bf16[16,32,128]{2,1,0:T(8,128)(2,1)S(1)}, bf16[16,32,128]{2,1,0:T(8,128)(2,1)S(1)}, u32[]{:S(2)}, u32[]{:S(2)}) %collective-permute-start.5) | collective-permute-done | bytes 131104 | tf_op jit(solution)/shard_map/ppermute | solution.py:361
  76.8 2.4 %collective-permute-done.9 = bf16[256,256]{1,0:T(8,128)(2,1)S(1)} collective-permute-done((bf16[256,256]{1,0:T(8,128)(2,1)S(1)}, bf16[256,256]{1,0:T(8,128)(2,1)S(1)}, u32[]{:S(2)}, u32[]{:S(2)}) %collective-permute-start.9) | collective-permute-done | bytes 131104 | tf_op jit(solution)/shard_map/ppermute | solution.py:361
  79.2 0.7 fusion.2
  80.0 1.3 %turn.1 = f32[2048,128]{1,0:T(8,128)} custom-call(bf16[16,32,128]{2,1,0:T(8,128)(2,1)S(1)} %add_returned.1.mine, bf16[16,32,128]{2,1,0:T(8,128)(2,1)S(1)} %collective-permute-done.5.across, bf16[2,16,32,128]{3,2,1,0:T(8,128)(2,1)S(1)} %collective-permute-done.6.beside), custom_call_target="tpu_custom_call" | custom-call | flops 67108864 | bytes 2097152 | tf_op jit(solution)/shard_map/turn/pallas_call | solution.py:349
  (44 shorter events, 2.5 us)
Async XLA Ops:
  35.1 7.4 %collective-permute-start = (bf16[8,3,64,128]{3,2,1,0:T(8,128)(2,1)S(1)}, bf16[8,3,64,128]{3,2,1,0:T(8,128)(2,1)S(1)}, u32[]{:S(2)}, u32[]{:S(2)}) collective-permute-start(bf16[8,3,64,128]{3,2,1,0:T(8,128)(2,1)S(1)} %all_to_all.10.own), channel_id=1, source_target_pairs={{0,1},{1,0},{2,3},{3,2},{4,5},{5,4},{6,7},{7,6},{8,9},{9,8},{10,11... | collective-permute-start | bytes 1179656 | tf_op jit(solution)/shard_map/ppermute | solution.py:361
  35.1 1.6 %copy-start = (bf16[1,64,128,128]{3,2,1,0:T(8,128)(2,1)S(1)}, bf16[1,64,128,128]{3,2,1,0:T(8,128)(2,1)}, u32[]{:S(2)}) copy-start(bf16[1,64,128,128]{3,2,1,0:T(8,128)(2,1)} %param.17) | copy-start | bytes 6291460
  36.7 1.0 %copy-start.2 = (bf16[2048,128]{1,0:T(8,128)(2,1)S(1)}, bf16[2048,128]{1,0:T(8,128)(2,1)}, u32[]{:S(2)}) copy-start(bf16[2048,128]{1,0:T(8,128)(2,1)} %feat.5) | copy-start | bytes 1572868
  39.0 3.5 %copy-start.3 = (bf16[2048,128]{1,0:T(8,128)(2,1)S(1)}, bf16[2048,128]{1,0:T(8,128)(2,1)}, u32[]{:S(2)}) copy-start(bf16[2048,128]{1,0:T(8,128)(2,1)} %feat.5) | copy-start | bytes 1572868
  39.0 3.5 %copy-start.4 = (bf16[1,24,128,128]{3,2,1,0:T(8,128)(2,1)S(1)}, bf16[1,24,128,128]{3,2,1,0:T(8,128)(2,1)}, u32[]{:S(2)}) copy-start(bf16[1,24,128,128]{3,2,1,0:T(8,128)(2,1)} %param.20) | copy-start | bytes 2359300
  39.0 3.5 %copy-start.5 = (bf16[2048,256]{1,0:T(8,128)(2,1)S(1)}, bf16[2048,256]{1,0:T(8,128)(2,1)}, u32[]{:S(2)}) copy-start(bf16[2048,256]{1,0:T(8,128)(2,1)} %cot.1) | copy-start | bytes 3145732
  39.0 3.5 %copy-start.6 = (bf16[128,256]{1,0:T(8,128)(2,1)S(1)}, bf16[128,256]{1,0:T(8,128)(2,1)}, u32[]{:S(2)}) copy-start(bf16[128,256]{1,0:T(8,128)(2,1)} %w_self.1) | copy-start | bytes 196612
  39.1 3.5 %copy-start.7 = (bf16[128,256]{1,0:T(8,128)(2,1)S(1)}, bf16[128,256]{1,0:T(8,128)(2,1)}, u32[]{:S(2)}) copy-start(bf16[128,256]{1,0:T(8,128)(2,1)} %w_neigh.1) | copy-start | bytes 196612
  39.1 3.5 %copy-start.9 = (s32[1,24]{1,0:T(1,128)S(1)}, s32[1,24]{1,0:T(1,128)}, u32[]{:S(2)}) copy-start(s32[1,24]{1,0:T(1,128)} %outer_rows.3) | copy-start | bytes 292
  39.1 3.5 %copy-start.10 = (s32[1,8]{1,0:T(1,128)S(1)}, s32[1,8]{1,0:T(1,128)}, u32[]{:S(2)}) copy-start(s32[1,8]{1,0:T(1,128)} %live.3) | copy-start | bytes 100
  48.5 16.6 %copy-start.1 = (bf16[1,64,128,128]{3,2,1,0:T(8,128)(2,1)S(1)}, bf16[1,64,128,128]{3,2,1,0:T(8,128)(2,1)}, u32[]{:S(2)}) copy-start(bf16[1,64,128,128]{3,2,1,0:T(8,128)(2,1)} %param.17) | copy-start | bytes 6291460
  48.5 16.6 %copy-start.12 = (s32[1,64]{1,0:T(1,128)S(1)}, s32[1,64]{1,0:T(1,128)}, u32[]{:S(2)}) copy-start(s32[1,64]{1,0:T(1,128)} %rows.3) | copy-start | bytes 772
  48.6 16.5 %copy-start.14 = (s32[1,64]{1,0:T(1,128)S(1)}, s32[1,64]{1,0:T(1,128)}, u32[]{:S(2)}) copy-start(s32[1,64]{1,0:T(1,128)} %cols.3) | copy-start | bytes 772
  48.6 1.7 %collective-permute-start.1 = (bf16[2,16,32,128]{3,2,1,0:T(8,128)(2,1)S(1)}, bf16[2,16,32,128]{3,2,1,0:T(8,128)(2,1)S(1)}, u32[]{:S(2)}, u32[]{:S(2)}) collective-permute-start(bf16[2,16,32,128]{3,2,1,0:T(8,128)(2,1)S(1)} %get-tuple-element.14), channel_id=1, source_target_pairs={{0,1},{1,0},{2,3},{3,2},{4,5},{5,4},{6,7},{7,6},{8,9},{9,8},{10,11... | collective-permute-start | bytes 786440 | tf_op jit(solution)/shard_map/ppermute | solution.py:361
  49.1 2.8 %collective-permute-start.3 = (bf16[2,16,32,128]{3,2,1,0:T(8,128)(2,1)S(1)}, bf16[2,16,32,128]{3,2,1,0:T(8,128)(2,1)S(1)}, u32[]{:S(2)}, u32[]{:S(2)}) collective-permute-start(bf16[2,16,32,128]{3,2,1,0:T(8,128)(2,1)S(1)} %get-tuple-element.18), channel_id=1, source_target_pairs={{0,1},{1,0},{2,3},{3,2},{4,5},{5,4},{6,7},{7,6},{8,9},{9,8},{10,11... | collective-permute-start | bytes 786440 | tf_op jit(solution)/shard_map/ppermute | solution.py:361
  49.2 13.2 %collective-permute-start.7 = (bf16[256,256]{1,0:T(8,128)(2,1)S(1)}, bf16[256,256]{1,0:T(8,128)(2,1)S(1)}, u32[]{:S(2)}, u32[]{:S(2)}) collective-permute-start(bf16[256,256]{1,0:T(8,128)(2,1)S(1)} %get-tuple-element.19), channel_id=1, source_target_pairs={{0,16},{4,20},{8,24},{12,28},{16,0},{20,4},{24,8},{28,12},{1,17},{... | collective-permute-start | bytes 393224 | tf_op jit(solution)/shard_map/ppermute | solution.py:361
  50.3 6.4 %collective-permute-start.2 = (bf16[16,32,128]{2,1,0:T(8,128)(2,1)S(1)}, bf16[16,32,128]{2,1,0:T(8,128)(2,1)S(1)}, u32[]{:S(2)}, u32[]{:S(2)}) collective-permute-start(bf16[16,32,128]{2,1,0:T(8,128)(2,1)S(1)} %fusion), channel_id=1, source_target_pairs={{0,2},{1,3},{2,0},{3,1},{4,6},{5,7},{6,4},{7,5},{8,10},{9,11},{10,... | collective-permute-start | bytes 393224 | tf_op jit(solution)/shard_map/ppermute | solution.py:361
  52.0 13.1 %collective-permute-start.4 = (bf16[16,32,128]{2,1,0:T(8,128)(2,1)S(1)}, bf16[16,32,128]{2,1,0:T(8,128)(2,1)S(1)}, u32[]{:S(2)}, u32[]{:S(2)}) collective-permute-start(bf16[16,32,128]{2,1,0:T(8,128)(2,1)S(1)} %fusion.1), channel_id=1, source_target_pairs={{0,2},{1,3},{2,0},{3,1},{4,6},{5,7},{6,4},{7,5},{8,10},{9,11},{10,... | collective-permute-start | bytes 393224 | tf_op jit(solution)/shard_map/ppermute | solution.py:361
  58.6 12.3 %copy-start.8 = (s32[1,8,3]{2,1,0:T(8,128)S(1)}, s32[1,8,3]{2,1,0:T(8,128)}, u32[]{:S(2)}) copy-start(s32[1,8,3]{2,1,0:T(8,128)} %copy.17) | copy-start | bytes 292
  58.6 12.3 %all-to-all-start.1 = ((bf16[8,3,32,128]{3,2,1,0:T(8,128)(2,1)}), bf16[8,3,32,128]{3,2,1,0:T(8,128)(2,1)S(1)}, u32[]{:S(2)}, u32[]{:S(2)}) async-start(bf16[8,3,32,128]{3,2,1,0:T(8,128)(2,1)} %get-tuple-element.15), calls=%async_computation.1 | async-start | bytes 393216 | tf_op jit(solution)/shard_map/all_to_all | solution.py:394
  63.1 10.2 %collective-permute-start.8 = (bf16[256,256]{1,0:T(8,128)(2,1)}, bf16[256,256]{1,0:T(8,128)(2,1)S(1)}, u32[]{:S(2)}, u32[]{:S(2)}) collective-permute-start(bf16[256,256]{1,0:T(8,128)(2,1)} %add_convert_fusion.1), channel_id=1, source_target_pairs={{0,8},{4,12},{8,0},{12,4},{16,24},{20,28},{24,16},{28,20},{1,9},{5... | collective-permute-start | bytes 393224 | tf_op jit(solution)/shard_map/ppermute | solution.py:361
  71.6 5.0 %collective-permute-start.5 = (bf16[16,32,128]{2,1,0:T(8,128)(2,1)S(1)}, bf16[16,32,128]{2,1,0:T(8,128)(2,1)S(1)}, u32[]{:S(2)}, u32[]{:S(2)}) collective-permute-start(bf16[16,32,128]{2,1,0:T(8,128)(2,1)S(1)} %add_returned.1.mine), channel_id=1, source_target_pairs={{0,2},{1,3},{2,0},{3,1},{4,6},{5,7},{6,4},{7,5},{8,10},{9,11},{10,... | collective-permute-start | bytes 393224 | tf_op jit(solution)/shard_map/ppermute | solution.py:361
  74.2 5.0 %collective-permute-start.9 = (bf16[256,256]{1,0:T(8,128)(2,1)S(1)}, bf16[256,256]{1,0:T(8,128)(2,1)S(1)}, u32[]{:S(2)}, u32[]{:S(2)}) collective-permute-start(bf16[256,256]{1,0:T(8,128)(2,1)S(1)} %add_convert_fusion), channel_id=1, source_target_pairs={{0,4},{4,0},{8,12},{12,8},{16,20},{20,16},{24,28},{28,24},{1,5},{5... | collective-permute-start | bytes 393224 | tf_op jit(solution)/shard_map/ppermute | solution.py:361
  76.7 3.3 %collective-permute-start.6 = (bf16[2,16,32,128]{3,2,1,0:T(8,128)(2,1)S(1)}, bf16[2,16,32,128]{3,2,1,0:T(8,128)(2,1)S(1)}, u32[]{:S(2)}, u32[]{:S(2)}) collective-permute-start(bf16[2,16,32,128]{3,2,1,0:T(8,128)(2,1)S(1)} %pad_maximum_fusion), channel_id=1, source_target_pairs={{0,1},{1,0},{2,3},{3,2},{4,5},{5,4},{6,7},{7,6},{8,9},{9,8},{10,11... | collective-permute-start | bytes 786440 | tf_op jit(solution)/shard_map/ppermute | solution.py:361
  (2 other events, 1.3 us)

commit v2 on v1

--- a/solution.py
+++ b/solution.py
@@ -31,24 +31,25 @@
 
 
 def gather_kernel(half, targets, feat, out, sem):
-    peers, slots = targets.shape
+    slots, _, peers = targets.shape
     block = half * 2
     mine = lax.axis_index("grp") % 2
     for p in range(peers):
         for s in range(slots):
-            start = pl.multiple_of(targets[p, s] * block + mine * half, half)
+            start = pl.multiple_of(targets[s, 0, p] * block + mine * half, half)
             pltpu.make_async_copy(feat.at[pl.ds(start, half)], out.at[p, s], sem).start()
     pltpu.make_async_copy(out, out, sem).wait()
 
 
 def gather_halves(features, targets, block):
-    peers, slots = targets.shape
+    slots, _, peers = targets.shape
     return pl.pallas_call(
         functools.partial(gather_kernel, block // 2),
         out_shape=jax.ShapeDtypeStruct((peers, slots, block // 2, features.shape[1]), BF16),
         in_specs=[SCALARS, ANYWHERE],
-        out_specs=ANYWHERE,
+        out_specs=WHOLE,
         scratch_shapes=[pltpu.SemaphoreType.DMA],
+        compiler_params=params(2 + 6 * peers * slots * block * features.shape[1] / MIB),
         name="gather_halves",
     )(targets, features)
 
@@ -310,7 +311,7 @@
 
     def some(q, _):
         for s in range(slots):
-            summed[targets[q, s]] += returned[q, s].astype(F32)
+            summed[targets[s, 0, q]] += returned[q, s].astype(F32)
         return 0
 
     lax.fori_loop(0, peers, some, 0)
@@ -376,12 +377,13 @@
 ):
     peers = lax.axis_size("dom")
     feat_width = features.shape[1]
-    inner_a, outer_a, targets = inner_values[0], outer_values[0], send_blocks[0]
+    inner_a, outer_a = inner_values[0], outer_values[0]
+    targets = send_blocks.transpose(2, 0, 1)
     block = inner_a.shape[-1]
 
     outgoing = gather_halves(features, targets, block)
     own = lax.all_to_all(outgoing, "dom", split_axis=0, concat_axis=0, tiled=True)
-    total = inner_sums(inner_rows, inner_cols, features, inner_a)
+    own, total = lax.optimization_barrier((own, inner_sums(inner_rows, inner_cols, features, inner_a)))
     other = swap(own, "grp", 1)
     layer_out, grads, send_n, keep_n, send_s, keep_s = layer(
         outer_rows, live_count, own, other, outer_a, total, features, cotangent, weight_self, weight_neigh
@@ -392,11 +394,11 @@
     came_s = swap((keep_s[0].astype(F32) + got_s[0].astype(F32)).astype(BF16), "grp", 2)
     scaled, payload = outer_back(outer_rows, live_count, keep_n, got_n, came_n, outer_a, peers)
     returned = lax.all_to_all(payload, "dom", split_axis=0, concat_axis=0, tiled=True)
-    bit = peers // 2
-    while bit:
+    bit = 1
+    while bit < peers:
         grads = grads.astype(BF16)
         grads = grads.astype(F32) + swap(grads, "dom", bit).astype(F32)
-        bit //= 2
+        bit *= 2
     partial = inner_back(inner_rows, inner_cols, scaled, keep_s, got_s, came_s, inner_a)
     mine = add_returned(targets, returned, partial)
     across = swap(mine, "grp", 2)

time: 81.8 us -> 68.2 us (0.83)
  blocking collectives: 19.4 us -> 0 us
  Pallas kernels: 28.7 us -> 17.2 us
  starting transfers between devices: 11.2 us -> 19.9 us
  local copies, waits for them, and re-layouts: 6.06 us -> 11.2 us
  waiting for transfers between devices: 13.3 us -> 16.5 us
    all_to_all x1 -> x0, blocking collectives: 19.4 us -> none  [shards(): lax.all_to_all(outgoing, 'dom', split_axis=0, concat_axis=0, tiled=True)]
    pallas_call x1, Pallas kernels: 13.8 us -> 1.95 us  [gather_halves(): pl.pallas_call(functools.partial(gather_kernel, block // 2), out_shape=ja...]
    all_to_all x0 -> x1, starting transfers between devices: none -> 7.26 us  [shards(): lax.all_to_all(outgoing, 'dom', split_axis=0, concat_axis=0, tiled=True)]
    unnamed x30 -> x42, local copies, waits for them, and re-layouts: 4 us -> 10.5 us
    all_to_all x0 -> x1, waiting for transfers between devices: none -> 4.45 us  [shards(): lax.all_to_all(outgoing, 'dom', split_axis=0, concat_axis=0, tiled=True)]
    all_to_all x1, waiting for transfers between devices: 4.06 us -> 1.65 us  [shards(): lax.all_to_all(payload, 'dom', split_axis=0, concat_axis=0, tiled=True)]
    ppermute x10, starting transfers between devices: 7.46 us -> 9.06 us  [swap(): lax.ppermute(x, axis, [(i, i ^ bit) for i in range(lax.axis_size(axis))])]
    squeeze x1 -> x0, local copies, waits for them, and re-layouts: 1.35 us -> none  [shards(): send_blocks[0]]
  transfers between devices with their start and end apart: 11 -> 12, of which waited for: 5 -> 6; matrix products, arithmetic and copies ran while one was open for 3% -> 4% of each run, Pallas kernels for 9% -> 11%
where the time goes in v2:
time: 68.2 us; the launch traced here: 67.4 us
  starting transfers between devices  19.9 us (29%)
  Pallas kernels  17.2 us (25%)
  waiting for transfers between devices  16.5 us (24%)
  local copies, waits for them, and re-layouts  11.2 us (16%)
  other arithmetic  1.8 us (3%)
  between operations  0.82 us (1%)
    unnamed x42, local copies, waits for them, and re-layouts  10.5 us
    ppermute x10, waiting for transfers between devices, swap(): lax.ppermute(x, axis, [(i, i ^ bit) for i in range(lax.axis_size(axis))])  10.4 us
    ppermute x10, starting transfers between devices, swap(): lax.ppermute(x, axis, [(i, i ^ bit) for i in range(lax.axis_size(axis))])  9.06 us
    all_to_all x1, starting transfers between devices, shards(): lax.all_to_all(outgoing, 'dom', split_axis=0, concat_axis=0, tiled=True)  7.26 us
    pallas_call x1, Pallas kernels, layer(): pl.pallas_call(functools.partial(layer_kernel, chunk), out_shape=(jax.Sha...  6.38 us
    all_to_all x1, waiting for transfers between devices, shards(): lax.all_to_all(outgoing, 'dom', split_axis=0, concat_axis=0, tiled=True)  4.45 us
    all_to_all x1, starting transfers between devices, shards(): lax.all_to_all(payload, 'dom', split_axis=0, concat_axis=0, tiled=True)  3.58 us
    pallas_call x1, Pallas kernels, inner_sums(): pl.pallas_call(inner_kernel, out_shape=jax.ShapeDtypeStruct((loc, block,...  3.39 us
  transfers between devices with their start and end apart: 12, of which 6 were waited for; matrix products, arithmetic and copies ran while one was open for 4% of the time, Pallas kernels for 11%

profile of v2, /device:TPU:0, one launch (start us, length us, event | category | flops | bytes accessed | tf_op | source)
XLA Modules:
  0.0 67.4 jit_solution(16102852199555501792)
XLA Ops:
  0.6 1.0 %copy-done.2 = bf16[2048,128]{1,0:T(8,128)(2,1)S(1)} copy-done((bf16[2048,128]{1,0:T(8,128)(2,1)S(1)}, bf16[2048,128]{1,0:T(8,128)(2,1)}, u32[]{:S(2)}) %copy-start.2) | copy-done | bytes 524312
  2.4 2.0 %gather_halves.1 = bf16[8,3,64,128]{3,2,1,0:T(8,128)(2,1)} custom-call(s32[3,1,8]{2,1,0:T(1,128)S(1)} %bitcast.15, bf16[2048,128]{1,0:T(8,128)(2,1)S(1)} %copy-done.2), custom_call_target="tpu_custom_call" | custom-call | tf_op jit(solution)/shard_map/gather_halves/pallas_call | solution.py:46
  4.3 7.3 %all-to-all-start = ((bf16[8,3,64,128]{3,2,1,0:T(8,128)(2,1)}), bf16[8,3,64,128]{3,2,1,0:T(8,128)(2,1)}, u32[]{:S(2)}, u32[]{:S(2)}) async-start(bf16[8,3,64,128]{3,2,1,0:T(8,128)(2,1)} %gather_halves.1), calls=%async_computation | async-start | bytes 786432 | tf_op jit(solution)/shard_map/all_to_all | solution.py:385
  11.6 1.6 %copy-done = bf16[1,64,128,128]{3,2,1,0:T(8,128)(2,1)S(1)} copy-done((bf16[1,64,128,128]{3,2,1,0:T(8,128)(2,1)S(1)}, bf16[1,64,128,128]{3,2,1,0:T(8,128)(2,1)}, u32[]{:S(2)}) %copy-start) | copy-done | bytes 2097176
  13.2 1.0 %copy-done.3 = bf16[2048,128]{1,0:T(8,128)(2,1)S(1)} copy-done((bf16[2048,128]{1,0:T(8,128)(2,1)S(1)}, bf16[2048,128]{1,0:T(8,128)(2,1)}, u32[]{:S(2)}) %copy-start.3) | copy-done | bytes 524312
  15.5 3.4 %inner_sums.1.total = f32[16,128,256]{2,1,0:T(8,128)S(1)} custom-call(s32[1,64]{1,0:T(1,128)S(1)} %copy-done.17, s32[1,64]{1,0:T(1,128)S(1)} %copy-done.19, bf16[2048,128]{1,0:T(8,128)(2,1)S(1)} %copy-done.3, bf16[64,128,128]{2,1,0:T(8,128)(2,1)S(1)} %bitcast.9), custom_call_target="tpu_custom_call" | custom-call | flops 536870912 | bytes 6291456 | tf_op jit(solution)/shard_map/inner_sums/pallas_call | solution.py:80
  18.9 4.4 %all-to-all-done.own = bf16[8,3,64,128]{3,2,1,0:T(8,128)(2,1)} async-done(((bf16[8,3,64,128]{3,2,1,0:T(8,128)(2,1)}), bf16[8,3,64,128]{3,2,1,0:T(8,128)(2,1)}, u32[]{:S(2)}, u32[]{:S(2)}) %all-to-all-start) | async-done | bytes 393248 | tf_op jit(solution)/shard_map/all_to_all | solution.py:385
  23.4 1.9 %collective-permute-done.other = bf16[8,3,64,128]{3,2,1,0:T(8,128)(2,1)S(1)} collective-permute-done((bf16[8,3,64,128]{3,2,1,0:T(8,128)(2,1)}, bf16[8,3,64,128]{3,2,1,0:T(8,128)(2,1)S(1)}, u32[]{:S(2)}, u32[]{:S(2)}) %collective-permute-start) | collective-permute-done | bytes 393248 | tf_op jit(solution)/shard_map/ppermute | solution.py:362
  25.3 1.2 %copy-done.6 = bf16[2048,256]{1,0:T(8,128)(2,1)S(1)} copy-done((bf16[2048,256]{1,0:T(8,128)(2,1)S(1)}, bf16[2048,256]{1,0:T(8,128)(2,1)}, u32[]{:S(2)}) %copy-start.6) | copy-done | bytes 1048600
  28.2 6.4 %layer.1 = (bf16[2048,256]{1,0:T(8,128)(2,1)}, bf16[256,256]{1,0:T(8,128)(2,1)S(1)}, bf16[2,16,32,128]{3,2,1,0:T(8,128)(2,1)S(1)}, bf16[2,16,32,128]{3,2,1,0:T(8...) custom-call(s32[1,24]{1,0:T(1,128)S(1)} %copy-done.15, s32[1,8]{1,0:T(1,128)S(1)} %copy-done.16, ...), custom_call_target="tpu_custom_call" | custom-call | flops 1200000000 | bytes 8388608 | tf_op jit(solution)/shard_map/layer/pallas_call | solution.py:196
  35.3 1.4 %collective-permute-start.7 = (bf16[256,256]{1,0:T(8,128)(2,1)S(1)}, bf16[256,256]{1,0:T(8,128)(2,1)}, u32[]{:S(2)}, u32[]{:S(2)}) collective-permute-start(bf16[256,256]{1,0:T(8,128)(2,1)S(1)} %get-tuple-element.23), channel_id=1, source_target_pairs={{0,4},{4,0},{8,12},{12,8},{16,20},{20,16},{24,28},{28,24},{1,5},{5... | collective-permute-start | bytes 393224 | tf_op jit(solution)/shard_map/ppermute | solution.py:362
  36.7 1.6 %collective-permute-start.2 = (bf16[16,32,128]{2,1,0:T(8,128)(2,1)S(1)}, bf16[16,32,128]{2,1,0:T(8,128)(2,1)S(1)}, u32[]{:S(2)}, u32[]{:S(2)}) collective-permute-start(bf16[16,32,128]{2,1,0:T(8,128)(2,1)S(1)} %fusion), channel_id=1, source_target_pairs={{0,2},{1,3},{2,0},{3,1},{4,6},{5,7},{6,4},{7,5},{8,10},{9,11},{10,... | collective-permute-start | bytes 393224 | tf_op jit(solution)/shard_map/ppermute | solution.py:362
  39.6 3.1 %collective-permute-done.2.came = bf16[16,32,128]{2,1,0:T(8,128)(2,1)S(1)} collective-permute-done((bf16[16,32,128]{2,1,0:T(8,128)(2,1)S(1)}, bf16[16,32,128]{2,1,0:T(8,128)(2,1)S(1)}, u32[]{:S(2)}, u32[]{:S(2)}) %collective-permute-start.2) | collective-permute-done | bytes 131104 | tf_op jit(solution)/shard_map/ppermute | solution.py:362
  42.7 1.8 %outer_back.1 = (bf16[16,32,128]{2,1,0:T(8,128)(2,1)S(1)}, bf16[8,3,32,128]{3,2,1,0:T(8,128)(2,1)}) custom-call(s32[1,24]{1,0:T(1,128)S(1)} %copy-done.15, s32[1,8]{1,0:T(1,128)S(1)} %copy-done.16, bf16[2,16,32,128]{3,2,1,0:T(8,128)(2,1)S(1)} %get-tuple-element.17.keep, bf16[2,16,32,128]{3,2,1,0:T(8,128)(2,1)S(1)} %collective-permute-done.1.got, ...), custom_call_target="tpu_custom_call" | custom-call | flops 25165824 | bytes 2097152 | tf_op jit(solution)/shard_map/outer_back/pallas_call | solution.py:253
  44.5 3.6 %all-to-all-start.1 = ((bf16[8,3,32,128]{3,2,1,0:T(8,128)(2,1)}), bf16[8,3,32,128]{3,2,1,0:T(8,128)(2,1)S(1)}, u32[]{:S(2)}, u32[]{:S(2)}) async-start(bf16[8,3,32,128]{3,2,1,0:T(8,128)(2,1)} %get-tuple-element.19), calls=%async_computation.1 | async-start | bytes 393216 | tf_op jit(solution)/shard_map/all_to_all | solution.py:396
  49.0 2.1 %collective-permute-start.8 = (bf16[256,256]{1,0:T(8,128)(2,1)S(1)}, bf16[256,256]{1,0:T(8,128)(2,1)S(1)}, u32[]{:S(2)}, u32[]{:S(2)}) collective-permute-start(bf16[256,256]{1,0:T(8,128)(2,1)S(1)} %add_convert_fusion.1), channel_id=1, source_target_pairs={{0,8},{4,12},{8,0},{12,4},{16,24},{20,28},{24,16},{28,20},{1,9},{5... | collective-permute-start | bytes 393224 | tf_op jit(solution)/shard_map/ppermute | solution.py:362
  52.1 0.9 %copy-done.10 = bf16[2,16,32,128]{3,2,1,0:T(8,128)(2,1)S(1)} copy-done((bf16[2,16,32,128]{3,2,1,0:T(8,128)(2,1)S(1)}, bf16[2,16,32,128]{3,2,1,0:T(8,128)(2,1)}, u32[]{:S(2)}) %copy-start.10) | copy-done | bytes 262168
  53.0 1.7 %inner_back.1.total = f32[16,32,128]{2,1,0:T(8,128)S(1)} custom-call(s32[1,64]{1,0:T(1,128)S(1)} %copy-done.18, s32[1,64]{1,0:T(1,128)S(1)} %copy-done.20, bf16[16,32,128]{2,1,0:T(8,128)(2,1)S(1)} %get-tuple-element.20.scaled, bf16[2,16,32,128]{3,2,1,0:T(8,128)(2,1)S(1)} %copy-done.8, bf16[2,16,32,128]{3,2,1,0:T(8,128)(2,1)S(1)} %copy-done.10, ...), custom_call_target="tpu_custom_call" | custom-call | flops 67108864 | bytes 3145728 | tf_op jit(solution)/shard_map/inner_back/pallas_call | solution.py:288
  54.7 1.7 %all-to-all-done.1.returned = bf16[8,3,32,128]{3,2,1,0:T(8,128)(2,1)S(1)} async-done(((bf16[8,3,32,128]{3,2,1,0:T(8,128)(2,1)}), bf16[8,3,32,128]{3,2,1,0:T(8,128)(2,1)S(1)}, u32[]{:S(2)}, u32[]{:S(2)}) %all-to-all-start.1) | async-done | bytes 196640 | tf_op jit(solution)/shard_map/all_to_all | solution.py:396
  57.1 1.6 %collective-permute-start.5 = (bf16[16,32,128]{2,1,0:T(8,128)(2,1)S(1)}, bf16[16,32,128]{2,1,0:T(8,128)(2,1)S(1)}, u32[]{:S(2)}, u32[]{:S(2)}) collective-permute-start(bf16[16,32,128]{2,1,0:T(8,128)(2,1)S(1)} %add_returned.1.mine), channel_id=1, source_target_pairs={{0,2},{1,3},{2,0},{3,1},{4,6},{5,7},{6,4},{7,5},{8,10},{9,11},{10,... | collective-permute-start | bytes 393224 | tf_op jit(solution)/shard_map/ppermute | solution.py:362
  58.7 1.2 %collective-permute-start.9 = (bf16[256,256]{1,0:T(8,128)(2,1)S(1)}, bf16[256,256]{1,0:T(8,128)(2,1)S(1)}, u32[]{:S(2)}, u32[]{:S(2)}) collective-permute-start(bf16[256,256]{1,0:T(8,128)(2,1)S(1)} %add_convert_fusion), channel_id=1, source_target_pairs={{0,16},{4,20},{8,24},{12,28},{16,0},{20,4},{24,8},{28,12},{1,17},{... | collective-permute-start | bytes 393224 | tf_op jit(solution)/shard_map/ppermute | solution.py:362
  59.9 2.2 %collective-permute-done.5.across = bf16[16,32,128]{2,1,0:T(8,128)(2,1)S(1)} collective-permute-done((bf16[16,32,128]{2,1,0:T(8,128)(2,1)S(1)}, bf16[16,32,128]{2,1,0:T(8,128)(2,1)S(1)}, u32[]{:S(2)}, u32[]{:S(2)}) %collective-permute-start.5) | collective-permute-done | bytes 131104 | tf_op jit(solution)/shard_map/ppermute | solution.py:362
  62.2 3.2 %collective-permute-done.9 = bf16[256,256]{1,0:T(8,128)(2,1)S(1)} collective-permute-done((bf16[256,256]{1,0:T(8,128)(2,1)S(1)}, bf16[256,256]{1,0:T(8,128)(2,1)S(1)}, u32[]{:S(2)}, u32[]{:S(2)}) %collective-permute-start.9) | collective-permute-done | bytes 131104 | tf_op jit(solution)/shard_map/ppermute | solution.py:362
  66.1 1.3 %turn.1 = f32[2048,128]{1,0:T(8,128)} custom-call(bf16[16,32,128]{2,1,0:T(8,128)(2,1)S(1)} %add_returned.1.mine, bf16[16,32,128]{2,1,0:T(8,128)(2,1)S(1)} %collective-permute-done.5.across, bf16[2,16,32,128]{3,2,1,0:T(8,128)(2,1)S(1)} %collective-permute-done.6.beside), custom_call_target="tpu_custom_call" | custom-call | flops 67108864 | bytes 2097152 | tf_op jit(solution)/shard_map/turn/pallas_call | solution.py:350
  (56 shorter events, 9.1 us)
Async XLA Ops:
  4.3 19.1 %all-to-all-start = ((bf16[8,3,64,128]{3,2,1,0:T(8,128)(2,1)}), bf16[8,3,64,128]{3,2,1,0:T(8,128)(2,1)}, u32[]{:S(2)}, u32[]{:S(2)}) async-start(bf16[8,3,64,128]{3,2,1,0:T(8,128)(2,1)} %gather_halves.1), calls=%async_computation | async-start | bytes 786432 | tf_op jit(solution)/shard_map/all_to_all | solution.py:385
  11.6 1.6 %copy-start = (bf16[1,64,128,128]{3,2,1,0:T(8,128)(2,1)S(1)}, bf16[1,64,128,128]{3,2,1,0:T(8,128)(2,1)}, u32[]{:S(2)}) copy-start(bf16[1,64,128,128]{3,2,1,0:T(8,128)(2,1)} %param.17) | copy-start | bytes 6291460
  15.5 9.8 %copy-start.4 = (bf16[2048,128]{1,0:T(8,128)(2,1)S(1)}, bf16[2048,128]{1,0:T(8,128)(2,1)}, u32[]{:S(2)}) copy-start(bf16[2048,128]{1,0:T(8,128)(2,1)} %feat.5) | copy-start | bytes 1572868
  15.5 9.8 %copy-start.5 = (bf16[1,24,128,128]{3,2,1,0:T(8,128)(2,1)S(1)}, bf16[1,24,128,128]{3,2,1,0:T(8,128)(2,1)}, u32[]{:S(2)}) copy-start(bf16[1,24,128,128]{3,2,1,0:T(8,128)(2,1)} %param.20) | copy-start | bytes 2359300
  15.5 9.8 %copy-start.15 = (s32[1,24]{1,0:T(1,128)S(1)}, s32[1,24]{1,0:T(1,128)}, u32[]{:S(2)}) copy-start(s32[1,24]{1,0:T(1,128)} %outer_rows.3) | copy-start | bytes 292
  15.5 9.8 %copy-start.16 = (s32[1,8]{1,0:T(1,128)S(1)}, s32[1,8]{1,0:T(1,128)}, u32[]{:S(2)}) copy-start(s32[1,8]{1,0:T(1,128)} %live.3) | copy-start | bytes 100
  23.4 1.9 %collective-permute-start = (bf16[8,3,64,128]{3,2,1,0:T(8,128)(2,1)}, bf16[8,3,64,128]{3,2,1,0:T(8,128)(2,1)S(1)}, u32[]{:S(2)}, u32[]{:S(2)}) collective-permute-start(bf16[8,3,64,128]{3,2,1,0:T(8,128)(2,1)} %all-to-all-done.own), channel_id=1, source_target_pairs={{0,1},{1,0},{2,3},{3,2},{4,5},{5,4},{6,7},{7,6},{8,9},{9,8},{10,11... | collective-permute-start | bytes 1179656 | tf_op jit(solution)/shard_map/ppermute | solution.py:362
  25.3 1.2 %copy-start.6 = (bf16[2048,256]{1,0:T(8,128)(2,1)S(1)}, bf16[2048,256]{1,0:T(8,128)(2,1)}, u32[]{:S(2)}) copy-start(bf16[2048,256]{1,0:T(8,128)(2,1)} %cot.1) | copy-start | bytes 3145732
  34.6 9.9 %copy-start.7 = (bf16[2,16,32,128]{3,2,1,0:T(8,128)(2,1)}, bf16[2,16,32,128]{3,2,1,0:T(8,128)(2,1)S(1)}, u32[]{:S(2)}) copy-start(bf16[2,16,32,128]{3,2,1,0:T(8,128)(2,1)S(1)} %get-tuple-element.21.keep) | copy-start | bytes 786436
  34.6 16.5 %copy-start.1 = (bf16[1,64,128,128]{3,2,1,0:T(8,128)(2,1)S(1)}, bf16[1,64,128,128]{3,2,1,0:T(8,128)(2,1)}, u32[]{:S(2)}) copy-start(bf16[1,64,128,128]{3,2,1,0:T(8,128)(2,1)} %param.17) | copy-start | bytes 6291460
  34.6 16.5 %copy-start.18 = (s32[1,64]{1,0:T(1,128)S(1)}, s32[1,64]{1,0:T(1,128)}, u32[]{:S(2)}) copy-start(s32[1,64]{1,0:T(1,128)} %rows.3) | copy-start | bytes 772
  34.7 16.5 %copy-start.20 = (s32[1,64]{1,0:T(1,128)S(1)}, s32[1,64]{1,0:T(1,128)}, u32[]{:S(2)}) copy-start(s32[1,64]{1,0:T(1,128)} %cols.3) | copy-start | bytes 772
  34.7 2.0 %collective-permute-start.1 = (bf16[2,16,32,128]{3,2,1,0:T(8,128)(2,1)S(1)}, bf16[2,16,32,128]{3,2,1,0:T(8,128)(2,1)S(1)}, u32[]{:S(2)}, u32[]{:S(2)}) collective-permute-start(bf16[2,16,32,128]{3,2,1,0:T(8,128)(2,1)S(1)} %get-tuple-element.18), channel_id=1, source_target_pairs={{0,1},{1,0},{2,3},{3,2},{4,5},{5,4},{6,7},{7,6},{8,9},{9,8},{10,11... | collective-permute-start | bytes 786440 | tf_op jit(solution)/shard_map/ppermute | solution.py:362
  34.9 3.5 %collective-permute-start.3 = (bf16[2,16,32,128]{3,2,1,0:T(8,128)(2,1)S(1)}, bf16[2,16,32,128]{3,2,1,0:T(8,128)(2,1)S(1)}, u32[]{:S(2)}, u32[]{:S(2)}) collective-permute-start(bf16[2,16,32,128]{3,2,1,0:T(8,128)(2,1)S(1)} %get-tuple-element.22), channel_id=1, source_target_pairs={{0,1},{1,0},{2,3},{3,2},{4,5},{5,4},{6,7},{7,6},{8,9},{9,8},{10,11... | collective-permute-start | bytes 786440 | tf_op jit(solution)/shard_map/ppermute | solution.py:362
  35.3 12.8 %collective-permute-start.7 = (bf16[256,256]{1,0:T(8,128)(2,1)S(1)}, bf16[256,256]{1,0:T(8,128)(2,1)}, u32[]{:S(2)}, u32[]{:S(2)}) collective-permute-start(bf16[256,256]{1,0:T(8,128)(2,1)S(1)} %get-tuple-element.23), channel_id=1, source_target_pairs={{0,4},{4,0},{8,12},{12,8},{16,20},{20,16},{24,28},{28,24},{1,5},{5... | collective-permute-start | bytes 393224 | tf_op jit(solution)/shard_map/ppermute | solution.py:362
  36.7 5.9 %collective-permute-start.2 = (bf16[16,32,128]{2,1,0:T(8,128)(2,1)S(1)}, bf16[16,32,128]{2,1,0:T(8,128)(2,1)S(1)}, u32[]{:S(2)}, u32[]{:S(2)}) collective-permute-start(bf16[16,32,128]{2,1,0:T(8,128)(2,1)S(1)} %fusion), channel_id=1, source_target_pairs={{0,2},{1,3},{2,0},{3,1},{4,6},{5,7},{6,4},{7,5},{8,10},{9,11},{10,... | collective-permute-start | bytes 393224 | tf_op jit(solution)/shard_map/ppermute | solution.py:362
  38.3 12.8 %copy-start.9 = (bf16[2,16,32,128]{3,2,1,0:T(8,128)(2,1)}, bf16[2,16,32,128]{3,2,1,0:T(8,128)(2,1)S(1)}, u32[]{:S(2)}) copy-start(bf16[2,16,32,128]{3,2,1,0:T(8,128)(2,1)S(1)} %collective-permute-done.3.got) | copy-start | bytes 786436
  39.1 12.0 %collective-permute-start.4 = (bf16[16,32,128]{2,1,0:T(8,128)(2,1)}, bf16[16,32,128]{2,1,0:T(8,128)(2,1)S(1)}, u32[]{:S(2)}, u32[]{:S(2)}) collective-permute-start(bf16[16,32,128]{2,1,0:T(8,128)(2,1)} %fusion.1), channel_id=1, source_target_pairs={{0,2},{1,3},{2,0},{3,1},{4,6},{5,7},{6,4},{7,5},{8,10},{9,11},{10,... | collective-permute-start | bytes 393224 | tf_op jit(solution)/shard_map/ppermute | solution.py:362
  44.5 11.9 %copy-start.14 = (s32[1,8,3]{1,0,2:T(1,128)S(1)}, s32[1,8,3]{1,0,2:T(1,128)}, u32[]{:S(2)}) copy-start(s32[1,8,3]{1,0,2:T(1,128)} %param.18) | copy-start | bytes 292
  44.5 11.9 %all-to-all-start.1 = ((bf16[8,3,32,128]{3,2,1,0:T(8,128)(2,1)}), bf16[8,3,32,128]{3,2,1,0:T(8,128)(2,1)S(1)}, u32[]{:S(2)}, u32[]{:S(2)}) async-start(bf16[8,3,32,128]{3,2,1,0:T(8,128)(2,1)} %get-tuple-element.19), calls=%async_computation.1 | async-start | bytes 393216 | tf_op jit(solution)/shard_map/all_to_all | solution.py:396
  49.0 9.6 %collective-permute-start.8 = (bf16[256,256]{1,0:T(8,128)(2,1)S(1)}, bf16[256,256]{1,0:T(8,128)(2,1)S(1)}, u32[]{:S(2)}, u32[]{:S(2)}) collective-permute-start(bf16[256,256]{1,0:T(8,128)(2,1)S(1)} %add_convert_fusion.1), channel_id=1, source_target_pairs={{0,8},{4,12},{8,0},{12,4},{16,24},{20,28},{24,16},{28,20},{1,9},{5... | collective-permute-start | bytes 393224 | tf_op jit(solution)/shard_map/ppermute | solution.py:362
  57.1 5.0 %collective-permute-start.5 = (bf16[16,32,128]{2,1,0:T(8,128)(2,1)S(1)}, bf16[16,32,128]{2,1,0:T(8,128)(2,1)S(1)}, u32[]{:S(2)}, u32[]{:S(2)}) collective-permute-start(bf16[16,32,128]{2,1,0:T(8,128)(2,1)S(1)} %add_returned.1.mine), channel_id=1, source_target_pairs={{0,2},{1,3},{2,0},{3,1},{4,6},{5,7},{6,4},{7,5},{8,10},{9,11},{10,... | collective-permute-start | bytes 393224 | tf_op jit(solution)/shard_map/ppermute | solution.py:362
  58.7 6.7 %collective-permute-start.9 = (bf16[256,256]{1,0:T(8,128)(2,1)S(1)}, bf16[256,256]{1,0:T(8,128)(2,1)S(1)}, u32[]{:S(2)}, u32[]{:S(2)}) collective-permute-start(bf16[256,256]{1,0:T(8,128)(2,1)S(1)} %add_convert_fusion), channel_id=1, source_target_pairs={{0,16},{4,20},{8,24},{12,28},{16,0},{20,4},{24,8},{28,12},{1,17},{... | collective-permute-start | bytes 393224 | tf_op jit(solution)/shard_map/ppermute | solution.py:362
  62.1 4.0 %collective-permute-start.6 = (bf16[2,16,32,128]{3,2,1,0:T(8,128)(2,1)S(1)}, bf16[2,16,32,128]{3,2,1,0:T(8,128)(2,1)S(1)}, u32[]{:S(2)}, u32[]{:S(2)}) collective-permute-start(bf16[2,16,32,128]{3,2,1,0:T(8,128)(2,1)S(1)} %pad_maximum_fusion), channel_id=1, source_target_pairs={{0,1},{1,0},{2,3},{3,2},{4,5},{5,4},{6,7},{7,6},{8,9},{9,8},{10,11... | collective-permute-start | bytes 786440 | tf_op jit(solution)/shard_map/ppermute | solution.py:362
  (9 other events, 7.7 us)

commit v3 on v2

v3 whole, which is shorter than its diff:
```python
import functools

import jax
import jax.numpy as jnp
from jax import lax
from jax.experimental import pallas as pl
from jax.experimental.pallas import tpu as pltpu
from jax.sharding import PartitionSpec as P

F32 = jnp.float32
BF16 = jnp.bfloat16
MIB = 1 << 20
GROUP = 8
ROWS_LAST = (((1,), (1,)), ((), ()))
ROWS_FIRST = (((0,), (0,)), ((), ()))
WHOLE = pl.BlockSpec(memory_space=pltpu.VMEM)
SCALARS = pl.BlockSpec(memory_space=pltpu.SMEM)
FAR = pl.BlockSpec(memory_space=pltpu.HBM)


def dot(a, b):
    return jnp.dot(a, b, preferred_element_type=F32)


def far(*arrays):
    return [pltpu.with_memory_space_constraint(x, pltpu.HBM) for x in arrays]


def params(mib):
    return pltpu.CompilerParams(vmem_limit_bytes=int(mib * MIB))


def cost(flops, moved):
    return pl.CostEstimate(flops=int(flops), bytes_accessed=int(moved), transcendentals=0)


def gather_kernel(half, targets_far, feat_far, out, targets, feat, sems):
    fetches = [
        pltpu.make_async_copy(targets_far, targets, sems.at[0]),
        pltpu.make_async_copy(feat_far, feat, sems.at[1]),
    ]
    for fetch in fetches:
        fetch.start()
    for fetch in fetches:
        fetch.wait()
    slots, _, peers = targets.shape
    block = half * 2
    mine = lax.axis_index("grp") % 2
    for p in range(peers):
        for s in range(slots):
            start = pl.multiple_of(targets[s, 0, p] * block + mine * half, half)
            pltpu.make_async_copy(feat.at[pl.ds(start, half)], out.at[p, s], sems.at[2]).start()
    pltpu.make_async_copy(out, out, sems.at[2]).wait()


def gather_halves(features, targets, block):
    slots, _, peers = targets.shape
    return pl.pallas_call(
        functools.partial(gather_kernel, block // 2),
        out_shape=jax.ShapeDtypeStruct((peers, slots, block // 2, features.shape[1]), BF16),
        in_specs=[FAR, FAR],
        out_specs=FAR,
        scratch_shapes=[
            pltpu.SMEM(targets.shape, jnp.int32),
            pltpu.VMEM(features.shape, BF16),
            pltpu.SemaphoreType.DMA((3,)),
        ],
        compiler_params=params(4),
        name="gather_halves",
    )(*far(targets, features))


def inner_kernel(rows, cols, feat, a, total, wide):
    step = pl.program_id(0)
    loc, block, width = total.shape
    feat_width = width // 2

    @pl.when(step == 0)
    def _():
        x = feat[...].reshape(loc, block, feat_width)
        wide[:, :, :feat_width] = x
        wide[:, :, feat_width:] = jnp.ones((loc, block, feat_width), BF16)
        total[:, :, :feat_width] = x.astype(F32)
        total[:, :, feat_width:] = jnp.ones((loc, block, feat_width), F32)

    count = a.shape[0]
    products = [dot(a[k], wide[cols[0, step * count + k]]) for k in range(count)]
    for k in range(count):
        total[rows[0, step * count + k]] += products[k]


def inner_sums(rows, cols, features, values):
    count, block, _ = values.shape
    nodes, feat_width = features.shape
    loc = nodes // block
    return pl.pallas_call(
        inner_kernel,
        out_shape=jax.ShapeDtypeStruct((loc, block, 2 * feat_width), F32),
        grid=(count // GROUP,),
        in_specs=[
            SCALARS,
            SCALARS,
            pl.BlockSpec((nodes, feat_width), lambda i: (0, 0)),
            pl.BlockSpec((GROUP, block, block), lambda i: (i, 0, 0)),
        ],
        out_specs=pl.BlockSpec((loc, block, 2 * feat_width), lambda i: (0, 0, 0)),
        scratch_shapes=[pltpu.VMEM((loc, block, 2 * feat_width), BF16)],
        compiler_params=params(16),
        cost_estimate=cost(count * block * block * feat_width * 4, 6 * MIB),
        name="inner_sums",
    )(*far(rows, cols, features, values))


def layer_kernel(
    chunk_blocks,
    outer_rows_far, live_far, own, other, outer_far, total_in, feat_far, cot_far, w_self_far, w_neigh_far,
    layer_out, grads, send_n, keep_n, send_s, keep_s, total,
    outer_rows, live, outer, feat, cot, w_self, w_neigh, smooth, weights, turned, grad_sum, sems, chunk_sems, out_sems,
):
    del total_in
    peers, slots, half, feat_width = own.shape
    count, block, _ = outer.shape
    loc = total.shape[0]
    chunks = loc // chunk_blocks
    rows = chunk_blocks * block
    part = feat_width // lax.axis_size("grp")
    me = lax.axis_index("grp")
    mine = me % 2

    def place(chunk):
        return pl.ds(chunk * rows, rows)

    first = [
        pltpu.make_async_copy(outer_rows_far, outer_rows, sems.at[0]),
        pltpu.make_async_copy(live_far, live, sems.at[1]),
        pltpu.make_async_copy(outer_far, outer, sems.at[2]),
    ]
    second = [
        pltpu.make_async_copy(w_self_far, w_self, sems.at[3]),
        pltpu.make_async_copy(w_neigh_far, w_neigh, sems.at[4]),
    ]
    for c in range(chunks):
        second.append(pltpu.make_async_copy(feat_far.at[place(c)], feat.at[place(c)], chunk_sems.at[0, c]))
        second.append(pltpu.make_async_copy(cot_far.at[place(c)], cot.at[place(c)], chunk_sems.at[1, c]))
    for copy in first + second:
        copy.start()
    ones = jnp.ones((block, feat_width), BF16)
    for copy in first:
        copy.wait()

    def some(g, _):
        products = []
        for k in range(GROUP):
            n = g * GROUP + k
            near, away = own[n // slots, n % slots], other[n // slots, n % slots]
            x = jnp.concatenate([jnp.where(mine == 0, near, away), jnp.where(mine == 0, away, near)], axis=0)
            products.append(dot(outer[n], jnp.concatenate([x, ones], axis=1)))
        for k in range(GROUP):
            n = g * GROUP + k
            alive = (n % slots < live[0, n // slots]).astype(F32)
            total[outer_rows[0, n]] += products[k] * alive
        return 0

    lax.fori_loop(0, count // GROUP, some, 0)
    for copy in second:
        copy.wait()
    weights[:feat_width] = w_self[...] * 0.5
    weights[feat_width:] = w_neigh[...] * 0.5
    for spot, away in enumerate((3, 1, 2, 0)):
        start = pl.multiple_of((me ^ away) * part, part)
        turned[pl.ds(spot * part, part)] = w_self[pl.ds(start, part)] * 0.5
        turned[pl.ds(feat_width + spot * part, part)] = w_neigh[pl.ds(start, part)] * 0.5
    eye = lax.broadcasted_iota(jnp.int32, (feat_width, feat_width), 0) == lax.broadcasted_iota(
        jnp.int32, (feat_width, feat_width), 1
    )
    eye = eye.astype(BF16)
    leaving = []
    for c in range(chunks):
        here = total[pl.ds(c * chunk_blocks, chunk_blocks)].reshape(rows, 2 * feat_width)
        over = 1.0 / here[:, feat_width:]
        agg = (here[:, :feat_width] * over).astype(BF16)
        both = jnp.concatenate([feat[place(c)], agg], axis=1)
        pre = dot(both, weights[...])
        bent = jnp.tanh(pre)
        twice = 1.0 + bent
        silu = pre * twice
        smooth[place(c)] = silu.astype(BF16)
        leaving.append(pltpu.make_async_copy(smooth.at[place(c)], layer_out.at[place(c)], out_sems.at[c]))
        leaving[-1].start()
        grad_pre = (cot[place(c)].astype(F32) * (twice + silu * (1.0 - bent))).astype(BF16)
        grown = lax.dot_general(both, grad_pre, ROWS_FIRST, preferred_element_type=F32)
        if c == 0:
            grad_sum[...] = grown
        elif c < chunks - 1:
            grad_sum[...] += grown
        else:
            grads[...] = (0.5 * (grad_sum[...] + grown)).astype(BF16)
        self_t = lax.dot_general(turned[:feat_width], grad_pre, ROWS_LAST, preferred_element_type=F32).astype(BF16)
        neigh = lax.dot_general(grad_pre, turned[feat_width:], ROWS_LAST, preferred_element_type=F32)
        neigh = (neigh * over).astype(BF16)
        neigh_t = lax.dot_general(eye, neigh, ROWS_LAST, preferred_element_type=F32).astype(BF16)
        for b in range(chunk_blocks):
            lanes = slice(b * block, (b + 1) * block)
            at = c * chunk_blocks + b
            for y in range(2):
                send_n[y, at] = neigh_t[y * part : (y + 1) * part, lanes]
                keep_n[y, at] = neigh_t[(2 + y) * part : (3 + y) * part, lanes]
                send_s[y, at] = self_t[y * part : (y + 1) * part, lanes]
                keep_s[y, at] = self_t[(2 + y) * part : (3 + y) * part, lanes]
    for copy in leaving:
        copy.wait()


def layer(outer_rows, live, own, other, outer, total, features, cotangent, w_self, w_neigh):
    nodes, feat_width = features.shape
    hidden = cotangent.shape[1]
    loc, block, _ = total.shape
    count = outer.shape[0]
    chunk = 4
    part = feat_width // lax.axis_size("grp")
    piece = jax.ShapeDtypeStruct((2, loc, part, block), BF16)
    grads = (2 * feat_width, hidden)
    boundary_bytes = 2 * count * block * (block + 2 * feat_width)
    return pl.pallas_call(
        functools.partial(layer_kernel, chunk),
        out_shape=(
            jax.ShapeDtypeStruct((nodes, hidden), BF16),
            jax.ShapeDtypeStruct(grads, BF16),
            piece, piece, piece, piece,
            jax.ShapeDtypeStruct(total.shape, F32),
        ),
        in_specs=[FAR, FAR, WHOLE, WHOLE, FAR, WHOLE, FAR, FAR, FAR, FAR],
        out_specs=(FAR, WHOLE, WHOLE, WHOLE, WHOLE, WHOLE, WHOLE),
        input_output_aliases={5: 6},
        scratch_shapes=[
            pltpu.SMEM(outer_rows.shape, jnp.int32),
            pltpu.SMEM(live.shape, jnp.int32),
            pltpu.VMEM(outer.shape, BF16),
            pltpu.VMEM(features.shape, BF16),
            pltpu.VMEM(cotangent.shape, BF16),
            pltpu.VMEM(w_self.shape, BF16),
            pltpu.VMEM(w_neigh.shape, BF16),
            pltpu.VMEM(cotangent.shape, BF16),
            pltpu.VMEM(grads, BF16),
            pltpu.VMEM(grads, BF16),
            pltpu.VMEM(grads, F32),
            pltpu.SemaphoreType.DMA((5,)),
            pltpu.SemaphoreType.DMA((2, loc // chunk)),
            pltpu.SemaphoreType.DMA((loc // chunk,)),
        ],
        compiler_params=params(20 + boundary_bytes / MIB),
        cost_estimate=cost(1.2e9, 8 * MIB),
        name="layer",
    )(
        *far(outer_rows, live), own, other, *far(outer), total, *far(features, cotangent, w_self, w_neigh)
    )[:6]


def outer_back_kernel(outer_rows, live, keep, got, came, keep_s, got_s, outer, scaled, base, payload):
    peers, slots, part, block = payload.shape
    near = (keep[1].astype(F32) + got[1].astype(F32) + came[...].astype(F32)).astype(BF16)
    scaled[...] = near
    base[...] = near.astype(F32) + keep_s[1].astype(F32) + got_s[1].astype(F32)

    def some(g, _):
        products = []
        for k in range(GROUP):
            n = g * GROUP + k
            products.append(dot(scaled[outer_rows[0, n]], outer[n]))
        for k in range(GROUP):
            n = g * GROUP + k
            alive = (n % slots < live[0, n // slots]).astype(F32)
            payload[n // slots, n % slots] = (products[k] * alive).astype(BF16)
        return 0

    lax.fori_loop(0, outer.shape[0] // GROUP, some, 0)


def outer_back(outer_rows, live, keep, got, came, keep_s, got_s, outer, peers):
    loc, part, block = came.shape
    count = outer.shape[0]
    return pl.pallas_call(
        outer_back_kernel,
        out_shape=(
            jax.ShapeDtypeStruct((loc, part, block), BF16),
            jax.ShapeDtypeStruct((loc, part, block), F32),
            jax.ShapeDtypeStruct((peers, count // peers, part, block), BF16),
        ),
        in_specs=[SCALARS, SCALARS] + [WHOLE] * 6,
        out_specs=(WHOLE, WHOLE, WHOLE),
        compiler_params=params(8 + count * block * (block + part) * 2 / MIB),
        cost_estimate=cost(count * block * block * part * 2, 2 * MIB),
        name="outer_back",
    )(*far(outer_rows, live), keep, got, came, keep_s, got_s, outer)


def inner_back_kernel(rows, cols, scaled, base, came, a, total):
    step = pl.program_id(0)

    @pl.when(step == 0)
    def _():
        total[...] = base[...] + came[...].astype(F32)

    count = a.shape[0]
    products = [dot(scaled[rows[0, step * count + k]], a[k]) for k in range(count)]
    for k in range(count):
        total[cols[0, step * count + k]] += products[k]


def inner_back(rows, cols, scaled, base, came, values):
    count, block, _ = values.shape
    group = 2 * GROUP
    piece = pl.BlockSpec(scaled.shape, lambda i: (0, 0, 0))
    return pl.pallas_call(
        inner_back_kernel,
        out_shape=jax.ShapeDtypeStruct(base.shape, F32),
        grid=(count // group,),
        in_specs=[
            SCALARS,
            SCALARS,
            piece,
            piece,
            piece,
            pl.BlockSpec((group, block, block), lambda i: (i, 0, 0)),
        ],
        out_specs=piece,
        compiler_params=params(8),
        cost_estimate=cost(count * block * block * scaled.shape[1] * 2, 3 * MIB),
        name="inner_back",
    )(*far(rows, cols), scaled, base, came, *far(values))


def add_returned_kernel(targets, returned, total, out, summed):
    peers, slots, _, _ = returned.shape
    summed[...] = total[...]

    def some(q, _):
        for s in range(slots):
            summed[targets[s, 0, q]] += returned[q, s].astype(F32)
        return 0

    lax.fori_loop(0, peers, some, 0)
    out[...] = summed[...].astype(BF16)


def add_returned(targets, returned, total):
    return pl.pallas_call(
        add_returned_kernel,
        out_shape=jax.ShapeDtypeStruct(total.shape, BF16),
        in_specs=[SCALARS, WHOLE, WHOLE],
        out_specs=WHOLE,
        scratch_shapes=[pltpu.VMEM(total.shape, F32)],
        compiler_params=params(8 + returned.size * 2 / MIB),
        cost_estimate=cost(total.size * 8, 2 * MIB),
        name="add_returned",
    )(*far(targets), returned, total)


def pair_sum_kernel(a, b, out):
    out[...] = (a[...].astype(F32) + b[...].astype(F32)).astype(BF16)


def pair_sum(a, b):
    return pl.pallas_call(
        pair_sum_kernel,
        out_shape=jax.ShapeDtypeStruct(a.shape, BF16),
        in_specs=[WHOLE, WHOLE],
        out_specs=WHOLE,
        compiler_params=params(4),
        cost_estimate=cost(a.size * 2, a.size * 6),
        name="pair_sum",
    )(a, b)


def finish_kernel(mine, across, beside, opposite, grads, grads_came, out, self_grad, neigh_grad):
    loc, part, block = mine.shape
    me = lax.axis_index("grp")
    feat_width = out.shape[1]
    self_grad[...] = grads[:feat_width].astype(F32) + grads_came[:feat_width].astype(F32)
    neigh_grad[...] = grads[feat_width:].astype(F32) + grads_came[feat_width:].astype(F32)
    row = lax.broadcasted_iota(jnp.int32, (feat_width, feat_width), 0)
    lane = lax.broadcasted_iota(jnp.int32, (feat_width, feat_width), 1)
    stacked = row // part
    away = jnp.where(stacked == 1, 2, jnp.where(stacked == 2, 1, stacked))
    order = (((me ^ away) * part + row % part) == lane).astype(BF16)
    for b in range(loc):
        stack = jnp.concatenate([mine[b], across[b], beside[b], opposite[b]], axis=0)
        out[b * block : (b + 1) * block] = lax.dot_general(stack, order, ROWS_FIRST, preferred_element_type=F32)


def finish(mine, across, beside, opposite, grads, grads_came):
    loc, part, block = mine.shape
    feat_width = grads.shape[0] // 2
    weight = jax.ShapeDtypeStruct((feat_width, grads.shape[1]), F32)
    return pl.pallas_call(
        finish_kernel,
        out_shape=(jax.ShapeDtypeStruct((loc * block, feat_width), F32), weight, weight),
        in_specs=[WHOLE] * 6,
        out_specs=(WHOLE, WHOLE, WHOLE),
        compiler_params=params(8),
        cost_estimate=cost(loc * block * feat_width * feat_width * 2, 2 * MIB),
        name="finish",
    )(mine, across, beside, opposite, grads, grads_came)


def swap(x, axis, bit):
    return lax.ppermute(x, axis, [(i, i ^ bit) for i in range(lax.axis_size(axis))])


def shards(
    features,
    weight_self,
    weight_neigh,
    cotangent,
    inner_rows,
    inner_cols,
    inner_values,
    send_blocks,
    outer_rows,
    outer_values,
    live_count,
):
    peers = lax.axis_size("dom")
    feat_width = features.shape[1]
    inner_a, outer_a = inner_values[0], outer_values[0]
    targets = send_blocks.transpose(2, 0, 1)
    block = inner_a.shape[-1]

    outgoing = gather_halves(features, targets, block)
    own = lax.all_to_all(outgoing, "dom", split_axis=0, concat_axis=0, tiled=True)
    own, total = lax.optimization_barrier((own, inner_sums(inner_rows, inner_cols, features, inner_a)))
    other = swap(own, "grp", 1)
    layer_out, grads, send_n, keep_n, send_s, keep_s = layer(
        outer_rows, live_count, own, other, outer_a, total, features, cotangent, weight_self, weight_neigh
    )
    got_n = swap(send_n, "grp", 1)
    came_n = swap((keep_n[0].astype(F32) + got_n[0].astype(F32)).astype(BF16), "grp", 2)
    got_s = swap(send_s, "grp", 1)
    came_s = swap((keep_s[0].astype(F32) + got_s[0].astype(F32)).astype(BF16), "grp", 2)
    scaled, base, payload = outer_back(
        outer_rows, live_count, keep_n, got_n, came_n, keep_s, got_s, outer_a, peers
    )
    returned = lax.all_to_all(payload, "dom", split_axis=0, concat_axis=0, tiled=True)
    bit = peers // 2
    while bit > 2:
        grads = pair_sum(grads, swap(grads, "dom", bit))
        bit //= 2
    base, grads = lax.optimization_barrier((base, grads))
    partial = inner_back(inner_rows, inner_cols, scaled, base, came_s, inner_a)
    partial, grads = lax.optimization_barrier((partial, pair_sum(grads, swap(grads, "dom", 2))))
    mine = add_returned(targets, returned, partial)
    across = swap(mine, "grp", 2)
    beside = swap(mine, "grp", 1)
    opposite = swap(across, "grp", 1)
    feature_grad, self_grad, neigh_grad = finish(mine, across, beside, opposite, grads, swap(grads, "dom", 1))
    return layer_out, feature_grad, self_grad, neigh_grad


def solution(mesh):
    placed = (
        P("dom", None),
        P(None, "grp"),
        P(None, "grp"),
        P("dom", "grp"),
        P("dom", None),
        P("dom", None),
        P("dom", None, None, None),
        P("dom", None, None),
        P("dom", None),
        P("dom", None, None, None),
        P("dom", None),
    )
    return jax.shard_map(
        shards,
        mesh=mesh,
        in_specs=placed,
        out_specs=(P("dom", "grp"), P("dom", None), P(None, "grp"), P(None, "grp")),
        check_vma=False,
    )
```

time: 68.2 us -> 59.4 us (0.87)
  local copies, waits for them, and re-layouts: 11.2 us -> 0.01 us
  Pallas kernels: 17.2 us -> 20.3 us
  other arithmetic: 1.8 us -> 0.08 us
  waiting for transfers between devices: 16.5 us -> 17.6 us
    unnamed x42 -> x2, local copies, waits for them, and re-layouts: 10.5 us -> 0.01 us
    pallas_call x1, Pallas kernels: 3.39 us -> 5.93 us  [inner_sums(): pl.pallas_call(inner_kernel, out_shape=jax.ShapeDtypeStruct((loc, block,...]
    pallas_call x2 -> x4, Pallas kernels: 2.98 us -> 4.36 us  [the longest x1 2.96 us: inner_back(): pl.pallas_call(inner_back_kernel, out_shape=jax.ShapeDtypeStruct(base.sha...]
    all_to_all x1, waiting for transfers between devices: 1.65 us -> 0.31 us  [shards(): lax.all_to_all(payload, 'dom', split_axis=0, concat_axis=0, tiled=True)]
    all_to_all x1, waiting for transfers between devices: 4.45 us -> 5.75 us  [shards(): lax.all_to_all(outgoing, 'dom', split_axis=0, concat_axis=0, tiled=True)]
    ppermute x10 -> x11, waiting for transfers between devices: 10.4 us -> 11.5 us  [swap(): lax.ppermute(x, axis, [(i, i ^ bit) for i in range(lax.axis_size(axis))])]
    pallas_call x1, Pallas kernels: 6.38 us -> 5.33 us  [layer(): pl.pallas_call(functools.partial(layer_kernel, chunk), out_shape=(jax.Sha...]
    convert_element_type x2 -> x0, other arithmetic: 0.97 us -> none  [shards(): grads = grads.astype(BF16)]
  transfers between devices with their start and end apart: 12 -> 13, of which waited for: 6 -> 9; matrix products, arithmetic and copies ran while one was open for 4% -> 0% of each run, Pallas kernels for 11% -> 19%
where the time goes in v3:
time: 59.4 us; the launch traced here: 58.9 us
  Pallas kernels  20.3 us (34%)
  starting transfers between devices  20.3 us (34%)
  waiting for transfers between devices  17.6 us (30%)
  between operations  0.69 us (1%)
    ppermute x11, waiting for transfers between devices, swap(): lax.ppermute(x, axis, [(i, i ^ bit) for i in range(lax.axis_size(axis))])  11.5 us
    ppermute x11, starting transfers between devices, swap(): lax.ppermute(x, axis, [(i, i ^ bit) for i in range(lax.axis_size(axis))])  9.42 us
    all_to_all x1, starting transfers between devices, shards(): lax.all_to_all(outgoing, 'dom', split_axis=0, concat_axis=0, tiled=True)  7.26 us
    pallas_call x1, Pallas kernels, inner_sums(): pl.pallas_call(inner_kernel, out_shape=jax.ShapeDtypeStruct((loc, block,...  5.93 us
    all_to_all x1, waiting for transfers between devices, shards(): lax.all_to_all(outgoing, 'dom', split_axis=0, concat_axis=0, tiled=True)  5.75 us
    pallas_call x1, Pallas kernels, layer(): pl.pallas_call(functools.partial(layer_kernel, chunk), out_shape=(jax.Sha...  5.33 us
    all_to_all x1, starting transfers between devices, shards(): lax.all_to_all(payload, 'dom', split_axis=0, concat_axis=0, tiled=True)  3.63 us
    pallas_call x1, Pallas kernels, inner_back(): pl.pallas_call(inner_back_kernel, out_shape=jax.ShapeDtypeStruct(base.sha...  2.96 us
  transfers between devices with their start and end apart: 13, of which 9 were waited for; matrix products, arithmetic and copies ran while one was open for 0% of the time, Pallas kernels for 19%

profile of v3, /device:TPU:0, one launch (start us, length us, event | category | flops | bytes accessed | tf_op | source)
XLA Modules:
  0.0 58.9 jit_solution(7512219228741536118)
XLA Ops:
  0.6 1.8 %gather_halves.1 = bf16[8,3,64,128]{3,2,1,0:T(8,128)(2,1)} custom-call(s32[3,1,8]{2,1,0:T(1,128)} %bitcast.11, bf16[2048,128]{1,0:T(8,128)(2,1)} %feat_far.3), custom_call_target="tpu_custom_call" | custom-call | tf_op jit(solution)/shard_map/gather_halves/pallas_call | solution.py:58
  2.4 7.3 %all-to-all-start = ((bf16[8,3,64,128]{3,2,1,0:T(8,128)(2,1)}), bf16[8,3,64,128]{3,2,1,0:T(8,128)(2,1)S(1)}, u32[]{:S(2)}, u32[]{:S(2)}) async-start(bf16[8,3,64,128]{3,2,1,0:T(8,128)(2,1)} %gather_halves.1), calls=%async_computation | async-start | bytes 786432 | tf_op jit(solution)/shard_map/all_to_all | solution.py:430
  9.7 5.9 %inner_sums.1.total_in = f32[16,128,256]{2,1,0:T(8,128)S(1)} custom-call(s32[1,64]{1,0:T(1,128)} %rows.3, s32[1,64]{1,0:T(1,128)} %cols.3, bf16[2048,128]{1,0:T(8,128)(2,1)} %feat_far.3, bf16[64,128,128]{2,1,0:T(8,128)(2,1)} %bitcast.9), custom_call_target="tpu_custom_call" | custom-call | flops 536870912 | bytes 6291456 | tf_op jit(solution)/shard_map/inner_sums/pallas_call | solution.py:96
  15.6 5.8 %all-to-all-done.own = bf16[8,3,64,128]{3,2,1,0:T(8,128)(2,1)S(1)} async-done(((bf16[8,3,64,128]{3,2,1,0:T(8,128)(2,1)}), bf16[8,3,64,128]{3,2,1,0:T(8,128)(2,1)S(1)}, u32[]{:S(2)}, u32[]{:S(2)}) %all-to-all-start) | async-done | bytes 393248 | tf_op jit(solution)/shard_map/all_to_all | solution.py:430
  21.4 1.7 %collective-permute-done.other = bf16[8,3,64,128]{3,2,1,0:T(8,128)(2,1)S(1)} collective-permute-done((bf16[8,3,64,128]{3,2,1,0:T(8,128)(2,1)S(1)}, bf16[8,3,64,128]{3,2,1,0:T(8,128)(2,1)S(1)}, u32[]{:S(2)}, u32[]{:S(2)}) %collective-permute-start) | collective-permute-done | bytes 393248 | tf_op jit(solution)/shard_map/ppermute | solution.py:407
  23.1 5.3 %layer.1 = (bf16[2048,256]{1,0:T(8,128)(2,1)}, bf16[256,256]{1,0:T(8,128)(2,1)S(1)}, bf16[2,16,32,128]{3,2,1,0:T(8,128)(2,1)S(1)}, bf16[2,16,32,128]{3,2,1,0:T(8...) custom-call(s32[1,24]{1,0:T(1,128)} %outer_rows.1, ...), custom_call_target="tpu_custom_call", output_to_operand_aliasing={{6}: (5, {})} | custom-call | flops 1200000000 | bytes 8388608 | tf_op jit(solution)/shard_map/layer/pallas_call | solution.py:224
  28.7 0.4 collective-permute-start.3
  29.0 1.0 %collective-permute-done.1.got = bf16[2,16,32,128]{3,2,1,0:T(8,128)(2,1)S(1)} collective-permute-done((bf16[2,16,32,128]{3,2,1,0:T(8,128)(2,1)S(1)}, bf16[2,16,32,128]{3,2,1,0:T(8,128)(2,1)S(1)}, u32[]{:S(2)}, u32[]{:S(2)}) %collective-permute-start.1) | collective-permute-done | bytes 262176 | tf_op jit(solution)/shard_map/ppermute | solution.py:407
  30.1 1.6 %collective-permute-start.2 = (bf16[16,32,128]{2,1,0:T(8,128)(2,1)S(1)}, bf16[16,32,128]{2,1,0:T(8,128)(2,1)S(1)}, u32[]{:S(2)}, u32[]{:S(2)}) collective-permute-start(bf16[16,32,128]{2,1,0:T(8,128)(2,1)S(1)} %fusion), channel_id=1, source_target_pairs={{0,2},{1,3},{2,0},{3,1},{4,6},{5,7},{6,4},{7,5},{8,10},{9,11},{10,... | collective-permute-start | bytes 393224 | tf_op jit(solution)/shard_map/ppermute | solution.py:407
  31.7 0.8 %collective-permute-start.4 = (bf16[256,256]{1,0:T(8,128)(2,1)S(1)}, bf16[256,256]{1,0:T(8,128)(2,1)S(1)}, u32[]{:S(2)}, u32[]{:S(2)}) collective-permute-start(bf16[256,256]{1,0:T(8,128)(2,1)S(1)} %get-tuple-element.32.a), channel_id=1, source_target_pairs={{0,16},{4,20},{8,24},{12,28},{16,0},{20,4},{24,8},{28,12},{1,17},{... | collective-permute-start | bytes 393224 | tf_op jit(solution)/shard_map/ppermute | solution.py:407
  32.5 3.2 %collective-permute-done.2.came = bf16[16,32,128]{2,1,0:T(8,128)(2,1)S(1)} collective-permute-done((bf16[16,32,128]{2,1,0:T(8,128)(2,1)S(1)}, bf16[16,32,128]{2,1,0:T(8,128)(2,1)S(1)}, u32[]{:S(2)}, u32[]{:S(2)}) %collective-permute-start.2) | collective-permute-done | bytes 131104 | tf_op jit(solution)/shard_map/ppermute | solution.py:407
  35.7 2.0 %outer_back.1 = (bf16[16,32,128]{2,1,0:T(8,128)(2,1)S(1)}, f32[16,32,128]{2,1,0:T(8,128)S(1)}, bf16[8,3,32,128]{3,2,1,0:T(8,128)(2,1)}) custom-call(s32[1,24]{1,0:T(1,128)} %outer_rows.1, s32[1,8]{1,0:T(1,128)} %live.1, bf16[2,16,32,128]{3,2,1,0:T(8,128)(2,1)S(1)} %get-tuple-element.25.keep, bf16[2,16,32,128]{3,2,1,0:T(8,128)(2,1)S(1)} %collective-permute-done.1.got, ...), custom_call_target="tpu_custom_call" | custom-call | flops 25165824 | bytes 2097152 | tf_op jit(solution)/shard_map/outer_back/pallas_call | solution.py:282
  37.7 3.6 %all-to-all-start.1 = ((bf16[8,3,32,128]{3,2,1,0:T(8,128)(2,1)}), bf16[8,3,32,128]{3,2,1,0:T(8,128)(2,1)S(1)}, u32[]{:S(2)}, u32[]{:S(2)}) async-start(bf16[8,3,32,128]{3,2,1,0:T(8,128)(2,1)} %get-tuple-element.29), calls=%async_computation.1 | async-start | bytes 393216 | tf_op jit(solution)/shard_map/all_to_all | solution.py:443
  41.4 1.6 %collective-permute-start.5 = (bf16[16,32,128]{2,1,0:T(8,128)(2,1)S(1)}, bf16[16,32,128]{2,1,0:T(8,128)(2,1)S(1)}, u32[]{:S(2)}, u32[]{:S(2)}) collective-permute-start(bf16[16,32,128]{2,1,0:T(8,128)(2,1)S(1)} %fusion.1), channel_id=1, source_target_pairs={{0,2},{1,3},{2,0},{3,1},{4,6},{5,7},{6,4},{7,5},{8,10},{9,11},{10,... | collective-permute-start | bytes 393224 | tf_op jit(solution)/shard_map/ppermute | solution.py:407
  43.0 2.1 %collective-permute-start.6 = (bf16[256,256]{1,0:T(8,128)(2,1)S(1)}, bf16[256,256]{1,0:T(8,128)(2,1)S(1)}, u32[]{:S(2)}, u32[]{:S(2)}) collective-permute-start(bf16[256,256]{1,0:T(8,128)(2,1)S(1)} %pair_sum.2.a), channel_id=1, source_target_pairs={{0,8},{4,12},{8,0},{12,4},{16,24},{20,28},{24,16},{28,20},{1,9},{5... | collective-permute-start | bytes 393224 | tf_op jit(solution)/shard_map/ppermute | solution.py:407
  45.1 1.3 %collective-permute-done.5.came = bf16[16,32,128]{2,1,0:T(8,128)(2,1)S(1)} collective-permute-done((bf16[16,32,128]{2,1,0:T(8,128)(2,1)S(1)}, bf16[16,32,128]{2,1,0:T(8,128)(2,1)S(1)}, u32[]{:S(2)}, u32[]{:S(2)}) %collective-permute-start.5) | collective-permute-done | bytes 131104 | tf_op jit(solution)/shard_map/ppermute | solution.py:407
  46.4 3.0 %inner_back.1.total = f32[16,32,128]{2,1,0:T(8,128)S(1)} custom-call(s32[1,64]{1,0:T(1,128)} %rows.3, s32[1,64]{1,0:T(1,128)} %cols.3, bf16[16,32,128]{2,1,0:T(8,128)(2,1)S(1)} %get-tuple-element.30.scaled, f32[16,32,128]{2,1,0:T(8,128)S(1)} %get-tuple-element.33.base, bf16[16,32,128]{2,1,0:T(8,128)(2,1)S(1)} %collective-permute-done.5.came, ...), custom_call_target="tpu_custom_call" | custom-call | flops 67108864 | bytes 3145728 | tf_op jit(solution)/shard_map/inner_back/pallas_call | solution.py:314
  49.4 0.5 collective-permute-done.6.b
  50.3 0.8 %add_returned.1.mine = bf16[16,32,128]{2,1,0:T(8,128)(2,1)S(1)} custom-call(s32[3,1,8]{2,1,0:T(1,128)} %bitcast.12, bf16[8,3,32,128]{3,2,1,0:T(8,128)(2,1)S(1)} %all-to-all-done.1.returned, f32[16,32,128]{2,1,0:T(8,128)S(1)} %inner_back.1.total), custom_call_target="tpu_custom_call" | custom-call | flops 524288 | bytes 2097152 | tf_op jit(solution)/shard_map/add_returned/pallas_call | solution.py:347
  51.1 1.5 %collective-permute-start.7 = (bf16[16,32,128]{2,1,0:T(8,128)(2,1)S(1)}, bf16[16,32,128]{2,1,0:T(8,128)(2,1)S(1)}, u32[]{:S(2)}, u32[]{:S(2)}) collective-permute-start(bf16[16,32,128]{2,1,0:T(8,128)(2,1)S(1)} %add_returned.1.mine), channel_id=1, source_target_pairs={{0,2},{1,3},{2,0},{3,1},{4,6},{5,7},{6,4},{7,5},{8,10},{9,11},{10,... | collective-permute-start | bytes 393224 | tf_op jit(solution)/shard_map/ppermute | solution.py:407
  52.6 1.3 %collective-permute-start.10 = (bf16[256,256]{1,0:T(8,128)(2,1)S(1)}, bf16[256,256]{1,0:T(8,128)(2,1)S(1)}, u32[]{:S(2)}, u32[]{:S(2)}) collective-permute-start(bf16[256,256]{1,0:T(8,128)(2,1)S(1)} %pair_sum.3.grads), channel_id=1, source_target_pairs={{0,4},{4,0},{8,12},{12,8},{16,20},{20,16},{24,28},{28,24},{1,5},{5... | collective-permute-start | bytes 393224 | tf_op jit(solution)/shard_map/ppermute | solution.py:407
  53.9 2.3 %collective-permute-done.7.across = bf16[16,32,128]{2,1,0:T(8,128)(2,1)S(1)} collective-permute-done((bf16[16,32,128]{2,1,0:T(8,128)(2,1)S(1)}, bf16[16,32,128]{2,1,0:T(8,128)(2,1)S(1)}, u32[]{:S(2)}, u32[]{:S(2)}) %collective-permute-start.7) | collective-permute-done | bytes 131104 | tf_op jit(solution)/shard_map/ppermute | solution.py:407
  56.2 1.4 %collective-permute-done.10.grads_came = bf16[256,256]{1,0:T(8,128)(2,1)S(1)} collective-permute-done((bf16[256,256]{1,0:T(8,128)(2,1)S(1)}, bf16[256,256]{1,0:T(8,128)(2,1)S(1)}, u32[]{:S(2)}, u32[]{:S(2)}) %collective-permute-start.10) | collective-permute-done | bytes 131104 | tf_op jit(solution)/shard_map/ppermute | solution.py:407
  57.6 1.3 %finish.1 = (f32[2048,128]{1,0:T(8,128)}, f32[128,256]{1,0:T(8,128)}, f32[128,256]{1,0:T(8,128)}) custom-call(bf16[16,32,128]{2,1,0:T(8,128)(2,1)S(1)} %add_returned.1.mine, bf16[16,32,128]{2,1,0:T(8,128)(2,1)S(1)} %collective-permute-done.7.across, bf16[16,32,128]{2,1,0:T(8,128)(2,1)S(1)} %collective-permute-done.8.beside, ...), custom_call_target="tpu_custom_call" | custom-call | flops 67108864 | bytes 2097152 | tf_op jit(solution)/shard_map/finish/pallas_call | solution.py:395
  (15 shorter events, 0.7 us)
Async XLA Ops:
  2.4 19.0 %all-to-all-start = ((bf16[8,3,64,128]{3,2,1,0:T(8,128)(2,1)}), bf16[8,3,64,128]{3,2,1,0:T(8,128)(2,1)S(1)}, u32[]{:S(2)}, u32[]{:S(2)}) async-start(bf16[8,3,64,128]{3,2,1,0:T(8,128)(2,1)} %gather_halves.1), calls=%async_computation | async-start | bytes 786432 | tf_op jit(solution)/shard_map/all_to_all | solution.py:430
  21.4 1.7 %collective-permute-start = (bf16[8,3,64,128]{3,2,1,0:T(8,128)(2,1)S(1)}, bf16[8,3,64,128]{3,2,1,0:T(8,128)(2,1)S(1)}, u32[]{:S(2)}, u32[]{:S(2)}) collective-permute-start(bf16[8,3,64,128]{3,2,1,0:T(8,128)(2,1)S(1)} %all-to-all-done.own), channel_id=1, source_target_pairs={{0,1},{1,0},{2,3},{3,2},{4,5},{5,4},{6,7},{7,6},{8,9},{9,8},{10,11... | collective-permute-start | bytes 1179656 | tf_op jit(solution)/shard_map/ppermute | solution.py:407
  23.1 12.6 %copy-start = (bf16[1,24,128,128]{3,2,1,0:T(8,128)(2,1)S(1)}, bf16[1,24,128,128]{3,2,1,0:T(8,128)(2,1)}, u32[]{:S(2)}) copy-start(bf16[1,24,128,128]{3,2,1,0:T(8,128)(2,1)} %param.20) | copy-start | bytes 2359300
  28.5 1.6 %collective-permute-start.1 = (bf16[2,16,32,128]{3,2,1,0:T(8,128)(2,1)S(1)}, bf16[2,16,32,128]{3,2,1,0:T(8,128)(2,1)S(1)}, u32[]{:S(2)}, u32[]{:S(2)}) collective-permute-start(bf16[2,16,32,128]{3,2,1,0:T(8,128)(2,1)S(1)} %get-tuple-element.26), channel_id=1, source_target_pairs={{0,1},{1,0},{2,3},{3,2},{4,5},{5,4},{6,7},{7,6},{8,9},{9,8},{10,11... | collective-permute-start | bytes 786440 | tf_op jit(solution)/shard_map/ppermute | solution.py:407
  28.7 3.8 %collective-permute-start.3 = (bf16[2,16,32,128]{3,2,1,0:T(8,128)(2,1)S(1)}, bf16[2,16,32,128]{3,2,1,0:T(8,128)(2,1)S(1)}, u32[]{:S(2)}, u32[]{:S(2)}) collective-permute-start(bf16[2,16,32,128]{3,2,1,0:T(8,128)(2,1)S(1)} %get-tuple-element.28), channel_id=1, source_target_pairs={{0,1},{1,0},{2,3},{3,2},{4,5},{5,4},{6,7},{7,6},{8,9},{9,8},{10,11... | collective-permute-start | bytes 786440 | tf_op jit(solution)/shard_map/ppermute | solution.py:407
  30.1 5.6 %collective-permute-start.2 = (bf16[16,32,128]{2,1,0:T(8,128)(2,1)S(1)}, bf16[16,32,128]{2,1,0:T(8,128)(2,1)S(1)}, u32[]{:S(2)}, u32[]{:S(2)}) collective-permute-start(bf16[16,32,128]{2,1,0:T(8,128)(2,1)S(1)} %fusion), channel_id=1, source_target_pairs={{0,2},{1,3},{2,0},{3,1},{4,6},{5,7},{6,4},{7,5},{8,10},{9,11},{10,... | collective-permute-start | bytes 393224 | tf_op jit(solution)/shard_map/ppermute | solution.py:407
  31.7 11.3 %collective-permute-start.4 = (bf16[256,256]{1,0:T(8,128)(2,1)S(1)}, bf16[256,256]{1,0:T(8,128)(2,1)S(1)}, u32[]{:S(2)}, u32[]{:S(2)}) collective-permute-start(bf16[256,256]{1,0:T(8,128)(2,1)S(1)} %get-tuple-element.32.a), channel_id=1, source_target_pairs={{0,16},{4,20},{8,24},{12,28},{16,0},{20,4},{24,8},{28,12},{1,17},{... | collective-permute-start | bytes 393224 | tf_op jit(solution)/shard_map/ppermute | solution.py:407
  37.7 12.6 %all-to-all-start.1 = ((bf16[8,3,32,128]{3,2,1,0:T(8,128)(2,1)}), bf16[8,3,32,128]{3,2,1,0:T(8,128)(2,1)S(1)}, u32[]{:S(2)}, u32[]{:S(2)}) async-start(bf16[8,3,32,128]{3,2,1,0:T(8,128)(2,1)} %get-tuple-element.29), calls=%async_computation.1 | async-start | bytes 393216 | tf_op jit(solution)/shard_map/all_to_all | solution.py:443
  41.4 5.0 %collective-permute-start.5 = (bf16[16,32,128]{2,1,0:T(8,128)(2,1)S(1)}, bf16[16,32,128]{2,1,0:T(8,128)(2,1)S(1)}, u32[]{:S(2)}, u32[]{:S(2)}) collective-permute-start(bf16[16,32,128]{2,1,0:T(8,128)(2,1)S(1)} %fusion.1), channel_id=1, source_target_pairs={{0,2},{1,3},{2,0},{3,1},{4,6},{5,7},{6,4},{7,5},{8,10},{9,11},{10,... | collective-permute-start | bytes 393224 | tf_op jit(solution)/shard_map/ppermute | solution.py:407
  43.0 6.9 %collective-permute-start.6 = (bf16[256,256]{1,0:T(8,128)(2,1)S(1)}, bf16[256,256]{1,0:T(8,128)(2,1)S(1)}, u32[]{:S(2)}, u32[]{:S(2)}) collective-permute-start(bf16[256,256]{1,0:T(8,128)(2,1)S(1)} %pair_sum.2.a), channel_id=1, source_target_pairs={{0,8},{4,12},{8,0},{12,4},{16,24},{20,28},{24,16},{28,20},{1,9},{5... | collective-permute-start | bytes 393224 | tf_op jit(solution)/shard_map/ppermute | solution.py:407
  51.1 5.0 %collective-permute-start.7 = (bf16[16,32,128]{2,1,0:T(8,128)(2,1)S(1)}, bf16[16,32,128]{2,1,0:T(8,128)(2,1)S(1)}, u32[]{:S(2)}, u32[]{:S(2)}) collective-permute-start(bf16[16,32,128]{2,1,0:T(8,128)(2,1)S(1)} %add_returned.1.mine), channel_id=1, source_target_pairs={{0,2},{1,3},{2,0},{3,1},{4,6},{5,7},{6,4},{7,5},{8,10},{9,11},{10,... | collective-permute-start | bytes 393224 | tf_op jit(solution)/shard_map/ppermute | solution.py:407
  52.6 5.0 %collective-permute-start.10 = (bf16[256,256]{1,0:T(8,128)(2,1)S(1)}, bf16[256,256]{1,0:T(8,128)(2,1)S(1)}, u32[]{:S(2)}, u32[]{:S(2)}) collective-permute-start(bf16[256,256]{1,0:T(8,128)(2,1)S(1)} %pair_sum.3.grads), channel_id=1, source_target_pairs={{0,4},{4,0},{8,12},{12,8},{16,20},{20,16},{24,28},{28,24},{1,5},{5... | collective-permute-start | bytes 393224 | tf_op jit(solution)/shard_map/ppermute | solution.py:407
  53.9 3.7 %collective-permute-start.8 = (bf16[16,32,128]{2,1,0:T(8,128)(2,1)S(1)}, bf16[16,32,128]{2,1,0:T(8,128)(2,1)S(1)}, u32[]{:S(2)}, u32[]{:S(2)}) collective-permute-start(bf16[16,32,128]{2,1,0:T(8,128)(2,1)S(1)} %add_returned.1.mine), channel_id=1, source_target_pairs={{0,1},{1,0},{2,3},{3,2},{4,5},{5,4},{6,7},{7,6},{8,9},{9,8},{10,11... | collective-permute-start | bytes 393224 | tf_op jit(solution)/shard_map/ppermute | solution.py:407
  56.2 1.4 %collective-permute-start.9 = (bf16[16,32,128]{2,1,0:T(8,128)(2,1)S(1)}, bf16[16,32,128]{2,1,0:T(8,128)(2,1)S(1)}, u32[]{:S(2)}, u32[]{:S(2)}) collective-permute-start(bf16[16,32,128]{2,1,0:T(8,128)(2,1)S(1)} %collective-permute-done.7.across), channel_id=1, source_target_pairs={{0,1},{1,0},{2,3},{3,2},{4,5},{5,4},{6,7},{7,6},{8,9},{9,8},{10,11... | collective-permute-start | bytes 393224 | tf_op jit(solution)/shard_map/ppermute | solution.py:407

commit v4 on v3

v4 whole, which is shorter than its diff:
```python
import functools

import jax
import jax.numpy as jnp
from jax import lax
from jax.experimental import pallas as pl
from jax.experimental.pallas import tpu as pltpu
from jax.sharding import PartitionSpec as P

F32 = jnp.float32
BF16 = jnp.bfloat16
MIB = 1 << 20
GROUP = 8
ROWS_LAST = (((1,), (1,)), ((), ()))
ROWS_FIRST = (((0,), (0,)), ((), ()))
WHOLE = pl.BlockSpec(memory_space=pltpu.VMEM)
SCALARS = pl.BlockSpec(memory_space=pltpu.SMEM)
FAR = pl.BlockSpec(memory_space=pltpu.HBM)


def dot(a, b):
    return jnp.dot(a, b, preferred_element_type=F32)


def far(*arrays):
    return [pltpu.with_memory_space_constraint(x, pltpu.HBM) for x in arrays]


def params(mib):
    return pltpu.CompilerParams(vmem_limit_bytes=int(mib * MIB))


def cost(flops, moved):
    return pl.CostEstimate(flops=int(flops), bytes_accessed=int(moved), transcendentals=0)


def gather_kernel(half, targets_far, feat_far, out, targets, feat, sems):
    fetches = [
        pltpu.make_async_copy(targets_far, targets, sems.at[0]),
        pltpu.make_async_copy(feat_far, feat, sems.at[1]),
    ]
    for fetch in fetches:
        fetch.start()
    for fetch in fetches:
        fetch.wait()
    slots, _, peers = targets.shape
    block = half * 2
    mine = lax.axis_index("grp") % 2
    for p in range(peers):
        for s in range(slots):
            start = pl.multiple_of(targets[s, 0, p] * block + mine * half, half)
            pltpu.make_async_copy(feat.at[pl.ds(start, half)], out.at[p, s], sems.at[2]).start()
    pltpu.make_async_copy(out, out, sems.at[2]).wait()


def gather_halves(features, targets, block):
    slots, _, peers = targets.shape
    return pl.pallas_call(
        functools.partial(gather_kernel, block // 2),
        out_shape=jax.ShapeDtypeStruct((peers, slots, block // 2, features.shape[1]), BF16),
        in_specs=[FAR, FAR],
        out_specs=FAR,
        scratch_shapes=[
            pltpu.SMEM(targets.shape, jnp.int32),
            pltpu.VMEM(features.shape, BF16),
            pltpu.SemaphoreType.DMA((3,)),
        ],
        compiler_params=params(4),
        name="gather_halves",
    )(*far(targets, features))


def stage_kernel(
    rows_far, cols_far, outer_rows_far, live_far, targets_far, feat_far, inner_far, outer_far,
    rows, cols, outer_rows, live, targets, total, over, outer,
    feat, inner, wide, sems, inner_sems,
):
    loc, block, feat_width = total.shape
    count, outer_count = inner.shape[0], outer.shape[0]
    slots, _, peers = targets.shape
    scalars = [
        pltpu.make_async_copy(source, place, sems.at[k])
        for k, (source, place) in enumerate((
            (rows_far, rows), (cols_far, cols), (outer_rows_far, outer_rows), (live_far, live), (targets_far, targets),
        ))
    ]
    tables = [
        pltpu.make_async_copy(source, place, sems.at[5 + k])
        for k, (source, place) in enumerate((
            (feat_far, feat), (outer_far, outer),
        ))
    ]
    groups = count // GROUP
    blocks = [
        pltpu.make_async_copy(
            inner_far.at[pl.ds(g * GROUP, GROUP)], inner.at[pl.ds(g * GROUP, GROUP)], inner_sems.at[g]
        )
        for g in range(groups)
    ]
    for copy in scalars + tables[:1] + blocks + tables[1:]:
        copy.start()
    for copy in scalars + tables[:1]:
        copy.wait()
    x = feat[...].reshape(loc, block, feat_width)
    wide[:, :, :feat_width] = x
    wide[:, :, feat_width:] = jnp.ones((loc, block, feat_width), BF16)
    total[...] = x.astype(F32)
    over[...] = jnp.ones((loc, block, feat_width), F32)
    for g in range(groups):
        blocks[g].wait()
        products = [dot(inner[g * GROUP + k], wide[cols[0, g * GROUP + k]]) for k in range(GROUP)]
        for k in range(GROUP):
            r = rows[0, g * GROUP + k]
            total[r] += products[k][:, :feat_width]
            over[r] += products[k][:, feat_width:]
    for copy in tables[1:]:
        copy.wait()

    def some(g, _):
        ones = jnp.ones((block, feat_width), BF16)
        products = [dot(outer[g * GROUP + k], ones) for k in range(GROUP)]
        for k in range(GROUP):
            n = g * GROUP + k
            alive = (n % slots < live[0, n // slots]).astype(F32)
            over[outer_rows[0, n]] += products[k] * alive
        return 0

    lax.fori_loop(0, outer_count // GROUP, some, 0)
    over[...] = 1.0 / over[...]


def stage(rows, cols, outer_rows, live, targets, features, inner, outer):
    count, block, _ = inner.shape
    nodes, feat_width = features.shape
    loc = nodes // block
    scalars = (rows, cols, outer_rows, live, targets)
    sums = (loc, block, feat_width)
    return pl.pallas_call(
        stage_kernel,
        out_shape=tuple(pltpu.SMEM(x.shape, jnp.int32) for x in scalars)
        + (pltpu.VMEM(sums, F32), pltpu.VMEM(sums, F32), pltpu.VMEM(outer.shape, BF16)),
        in_specs=[FAR] * 8,
        out_specs=(SCALARS,) * 5 + (WHOLE,) * 3,
        scratch_shapes=[
            pltpu.VMEM(features.shape, BF16),
            pltpu.VMEM(inner.shape, BF16),
            pltpu.VMEM((loc, block, 2 * feat_width), BF16),
            pltpu.SemaphoreType.DMA((7,)),
            pltpu.SemaphoreType.DMA((count // GROUP,)),
        ],
        compiler_params=params(12 + outer.size * 2 / MIB),
        cost_estimate=cost(count * block * block * feat_width * 4, 6 * MIB),
        name="stage",
    )(*far(*scalars, features, inner, outer))


def layer_kernel(
    chunk_blocks,
    outer_rows, live, own, other, outer, total_in, over_all, feat_far, cot_far, self_far, neigh_far,
    layer_out, grads, send_n, keep_n, send_s, keep_s, total,
    feat, cot, w_self, w_neigh, smooth, weights, turned, grad_sum, sems, out_sems,
):
    del total_in
    peers, slots, half, feat_width = own.shape
    count, block, _ = outer.shape
    loc = total.shape[0]
    chunks = loc // chunk_blocks
    rows = chunk_blocks * block
    part = feat_width // lax.axis_size("grp")
    me = lax.axis_index("grp")
    mine = me % 2
    fetches = [
        pltpu.make_async_copy(source, place, sems.at[k])
        for k, (source, place) in enumerate((
            (self_far, w_self), (neigh_far, w_neigh), (feat_far, feat), (cot_far, cot),
        ))
    ]
    for fetch in fetches:
        fetch.start()

    def some(g, _):
        products = []
        for k in range(GROUP):
            n = g * GROUP + k
            near, away = own[n // slots, n % slots], other[n // slots, n % slots]
            x = jnp.concatenate([jnp.where(mine == 0, near, away), jnp.where(mine == 0, away, near)], axis=0)
            products.append(dot(outer[n], x))
        for k in range(GROUP):
            n = g * GROUP + k
            alive = (n % slots < live[0, n // slots]).astype(F32)
            total[outer_rows[0, n]] += products[k] * alive
        return 0

    lax.fori_loop(0, count // GROUP, some, 0)
    for fetch in fetches:
        fetch.wait()
    weights[:feat_width] = w_self[...] * 0.5
    weights[feat_width:] = w_neigh[...] * 0.5
    for spot, away in enumerate((3, 1, 2, 0)):
        start = pl.multiple_of((me ^ away) * part, part)
        turned[pl.ds(spot * part, part)] = w_self[pl.ds(start, part)] * 0.5
        turned[pl.ds(feat_width + spot * part, part)] = w_neigh[pl.ds(start, part)] * 0.5
    eye = lax.broadcasted_iota(jnp.int32, (feat_width, feat_width), 0) == lax.broadcasted_iota(
        jnp.int32, (feat_width, feat_width), 1
    )
    eye = eye.astype(BF16)
    leaving = []
    for c in range(chunks):
        place = pl.ds(c * rows, rows)
        here = pl.ds(c * chunk_blocks, chunk_blocks)
        over = over_all[here].reshape(rows, feat_width)
        agg = (total[here].reshape(rows, feat_width) * over).astype(BF16)
        both = jnp.concatenate([feat[place], agg], axis=1)
        pre = dot(both, weights[...])
        bent = jnp.tanh(pre)
        twice = 1.0 + bent
        silu = pre * twice
        smooth[place] = silu.astype(BF16)
        leaving.append(pltpu.make_async_copy(smooth.at[place], layer_out.at[place], out_sems.at[c]))
        leaving[-1].start()
        grad_pre = (cot[place].astype(F32) * (twice + silu * (1.0 - bent))).astype(BF16)
        grown = lax.dot_general(both, grad_pre, ROWS_FIRST, preferred_element_type=F32)
        if c == 0:
            grad_sum[...] = grown
        elif c < chunks - 1:
            grad_sum[...] += grown
        else:
            grads[...] = (0.5 * (grad_sum[...] + grown)).astype(BF16)
        self_t = lax.dot_general(turned[:feat_width], grad_pre, ROWS_LAST, preferred_element_type=F32).astype(BF16)
        neigh = lax.dot_general(grad_pre, turned[feat_width:], ROWS_LAST, preferred_element_type=F32)
        neigh = (neigh * over).astype(BF16)
        neigh_t = lax.dot_general(eye, neigh, ROWS_LAST, preferred_element_type=F32).astype(BF16)
        for b in range(chunk_blocks):
            lanes = slice(b * block, (b + 1) * block)
            at = c * chunk_blocks + b
            for y in range(2):
                send_n[y, at] = neigh_t[y * part : (y + 1) * part, lanes]
                keep_n[y, at] = neigh_t[(2 + y) * part : (3 + y) * part, lanes]
                send_s[y, at] = self_t[y * part : (y + 1) * part, lanes]
                keep_s[y, at] = self_t[(2 + y) * part : (3 + y) * part, lanes]
    for copy in leaving:
        copy.wait()


def layer(outer_rows, live, own, other, outer, total, over, features, cotangent, w_self, w_neigh):
    feat_width = features.shape[1]
    loc, block, _ = total.shape
    chunk = 4
    grads = (2 * feat_width, cotangent.shape[1])
    part = feat_width // lax.axis_size("grp")
    piece = pltpu.VMEM((2, loc, part, block), BF16)
    return pl.pallas_call(
        functools.partial(layer_kernel, chunk),
        out_shape=(
            jax.ShapeDtypeStruct(cotangent.shape, BF16),
            pltpu.VMEM(grads, BF16),
            piece, piece, piece, piece,
            pltpu.VMEM(total.shape, F32),
        ),
        in_specs=[SCALARS] * 2 + [WHOLE] * 5 + [FAR] * 4,
        out_specs=(FAR,) + (WHOLE,) * 6,
        input_output_aliases={5: 6},
        scratch_shapes=[
            pltpu.VMEM(features.shape, BF16),
            pltpu.VMEM(cotangent.shape, BF16),
            pltpu.VMEM(w_self.shape, BF16),
            pltpu.VMEM(w_neigh.shape, BF16),
            pltpu.VMEM(cotangent.shape, BF16),
            pltpu.VMEM(grads, BF16),
            pltpu.VMEM(grads, BF16),
            pltpu.VMEM(grads, F32),
            pltpu.SemaphoreType.DMA((4,)),
            pltpu.SemaphoreType.DMA((loc // chunk,)),
        ],
        compiler_params=params(16 + 4 * own.size * 2 / MIB),
        cost_estimate=cost(1.2e9, 8 * MIB),
        name="layer",
    )(outer_rows, live, own, other, outer, total, over, *far(features, cotangent, w_self, w_neigh))[:6]


def outer_back_kernel(outer_rows, live, keep, got, came, keep_s, got_s, outer, scaled, base, payload):
    peers, slots, part, block = payload.shape
    near = (keep[1].astype(F32) + got[1].astype(F32) + came[...].astype(F32)).astype(BF16)
    scaled[...] = near
    base[...] = near.astype(F32) + keep_s[1].astype(F32) + got_s[1].astype(F32)

    def some(g, _):
        products = []
        for k in range(GROUP):
            n = g * GROUP + k
            products.append(dot(scaled[outer_rows[0, n]], outer[n]))
        for k in range(GROUP):
            n = g * GROUP + k
            alive = (n % slots < live[0, n // slots]).astype(F32)
            payload[n // slots, n % slots] = (products[k] * alive).astype(BF16)
        return 0

    lax.fori_loop(0, outer.shape[0] // GROUP, some, 0)


def outer_back(outer_rows, live, keep, got, came, keep_s, got_s, outer, peers):
    loc, part, block = came.shape
    count = outer.shape[0]
    return pl.pallas_call(
        outer_back_kernel,
        out_shape=(
            pltpu.VMEM((loc, part, block), BF16),
            pltpu.VMEM((loc, part, block), F32),
            jax.ShapeDtypeStruct((peers, count // peers, part, block), BF16),
        ),
        in_specs=[SCALARS, SCALARS] + [WHOLE] * 6,
        out_specs=(WHOLE, WHOLE, WHOLE),
        compiler_params=params(8 + count * block * (block + part) * 2 / MIB),
        cost_estimate=cost(count * block * block * part * 2, 2 * MIB),
        name="outer_back",
    )(outer_rows, live, keep, got, came, keep_s, got_s, outer)


def inner_back_kernel(rows, cols, scaled, base, inner_far, grads, grads_came, total, grads_out, inner, sems):
    groups = inner.shape[0] // GROUP
    blocks = [
        pltpu.make_async_copy(inner_far.at[pl.ds(g * GROUP, GROUP)], inner.at[pl.ds(g * GROUP, GROUP)], sems.at[g])
        for g in range(groups)
    ]
    for copy in blocks:
        copy.start()
    total[...] = base[...]
    grads_out[...] = (grads[...].astype(F32) + grads_came[...].astype(F32)).astype(BF16)
    for g in range(groups):
        blocks[g].wait()
        products = [dot(scaled[rows[0, g * GROUP + k]], inner[g * GROUP + k]) for k in range(GROUP)]
        for k in range(GROUP):
            total[cols[0, g * GROUP + k]] += products[k]


def inner_back(rows, cols, scaled, base, inner, grads, grads_came):
    count, block, _ = inner.shape
    return pl.pallas_call(
        inner_back_kernel,
        out_shape=(pltpu.VMEM(base.shape, F32), pltpu.VMEM(grads.shape, BF16)),
        in_specs=[SCALARS, SCALARS, WHOLE, WHOLE, FAR, WHOLE, WHOLE],
        out_specs=(WHOLE, WHOLE),
        scratch_shapes=[pltpu.VMEM(inner.shape, BF16), pltpu.SemaphoreType.DMA((count // GROUP,))],
        compiler_params=params(8),
        cost_estimate=cost(count * block * block * scaled.shape[1] * 2, 3 * MIB),
        name="inner_back",
    )(rows, cols, scaled, base, *far(inner), grads, grads_came)


def add_returned_kernel(targets, returned, came, total, out, summed):
    peers, slots, _, _ = returned.shape
    summed[...] = total[...] + came[...].astype(F32)

    def some(q, _):
        for s in range(slots):
            summed[targets[s, 0, q]] += returned[q, s].astype(F32)
        return 0

    lax.fori_loop(0, peers, some, 0)
    out[...] = summed[...].astype(BF16)


def add_returned(targets, returned, came, total):
    return pl.pallas_call(
        add_returned_kernel,
        out_shape=pltpu.VMEM(total.shape, BF16),
        in_specs=[SCALARS, WHOLE, WHOLE, WHOLE],
        out_specs=WHOLE,
        scratch_shapes=[pltpu.VMEM(total.shape, F32)],
        compiler_params=params(8 + returned.size * 2 / MIB),
        cost_estimate=cost(total.size * 8, 2 * MIB),
        name="add_returned",
    )(targets, returned, came, total)


def pair_sum_kernel(a, b, out):
    out[...] = (a[...].astype(F32) + b[...].astype(F32)).astype(BF16)


def pair_sum(a, b):
    return pl.pallas_call(
        pair_sum_kernel,
        out_shape=jax.ShapeDtypeStruct(a.shape, BF16),
        in_specs=[WHOLE, WHOLE],
        out_specs=WHOLE,
        compiler_params=params(4),
        cost_estimate=cost(a.size * 2, a.size * 6),
        name="pair_sum",
    )(a, b)


def finish_kernel(mine, across, beside, opposite, grads, grads_came, out, self_out, neigh_out, turned, summed, sems):
    loc, part, block = mine.shape
    me = lax.axis_index("grp")
    feat_width = turned.shape[1]
    summed[...] = grads[...].astype(F32) + grads_came[...].astype(F32)
    copies = [
        pltpu.make_async_copy(summed.at[pl.ds(0, feat_width)], self_out, sems.at[0]),
        pltpu.make_async_copy(summed.at[pl.ds(feat_width, feat_width)], neigh_out, sems.at[1]),
    ]
    for copy in copies:
        copy.start()
    row = lax.broadcasted_iota(jnp.int32, (feat_width, feat_width), 0)
    lane = lax.broadcasted_iota(jnp.int32, (feat_width, feat_width), 1)
    stacked = row // part
    away = jnp.where(stacked == 1, 2, jnp.where(stacked == 2, 1, stacked))
    order = (((me ^ away) * part + row % part) == lane).astype(BF16)
    step = loc // 4
    for c in range(4):
        for b in range(c * step, (c + 1) * step):
            stack = jnp.concatenate([mine[b], across[b], beside[b], opposite[b]], axis=0)
            turned[b * block : (b + 1) * block] = lax.dot_general(stack, order, ROWS_FIRST, preferred_element_type=F32)
        place = pl.ds(c * step * block, step * block)
        copies.append(pltpu.make_async_copy(turned.at[place], out.at[place], sems.at[2 + c]))
        copies[-1].start()
    for copy in copies:
        copy.wait()


def finish(mine, across, beside, opposite, grads, grads_came):
    loc, part, block = mine.shape
    feat_width = grads.shape[0] // 2
    weight = jax.ShapeDtypeStruct((feat_width, grads.shape[1]), F32)
    return pl.pallas_call(
        finish_kernel,
        out_shape=(jax.ShapeDtypeStruct((loc * block, feat_width), F32), weight, weight),
        in_specs=[WHOLE] * 6,
        out_specs=(FAR, FAR, FAR),
        scratch_shapes=[
            pltpu.VMEM((loc * block, feat_width), F32),
            pltpu.VMEM(grads.shape, F32),
            pltpu.SemaphoreType.DMA((6,)),
        ],
        compiler_params=params(8),
        cost_estimate=cost(loc * block * feat_width * feat_width * 2, 2 * MIB),
        name="finish",
    )(mine, across, beside, opposite, grads, grads_came)


def swap(x, axis, bit):
    return lax.ppermute(x, axis, [(i, i ^ bit) for i in range(lax.axis_size(axis))])


def shards(
    features,
    weight_self,
    weight_neigh,
    cotangent,
    inner_rows,
    inner_cols,
    inner_values,
    send_blocks,
    outer_rows,
    outer_values,
    live_count,
):
    peers = lax.axis_size("dom")
    feat_width = features.shape[1]
    inner_a, outer_a = inner_values[0], outer_values[0]
    targets = send_blocks.transpose(2, 0, 1)
    block = inner_a.shape[-1]

    outgoing = gather_halves(features, targets, block)
    own = lax.all_to_all(outgoing, "dom", split_axis=0, concat_axis=0, tiled=True)
    rows, cols, outer_rows, live, targets, total, over, outer_a = stage(
        inner_rows, inner_cols, outer_rows, live_count, targets, features, inner_a, outer_a
    )
    own, total = lax.optimization_barrier((own, total))
    other = swap(own, "grp", 1)
    layer_out, grads, send_n, keep_n, send_s, keep_s = layer(
        outer_rows, live, own, other, outer_a, total, over, features, cotangent, weight_self, weight_neigh
    )
    got_n = swap(send_n, "grp", 1)
    came_n = swap((keep_n[0].astype(F32) + got_n[0].astype(F32)).astype(BF16), "grp", 2)
    got_s = swap(send_s, "grp", 1)
    came_s = swap((keep_s[0].astype(F32) + got_s[0].astype(F32)).astype(BF16), "grp", 2)
    scaled, base, payload = outer_back(outer_rows, live, keep_n, got_n, came_n, keep_s, got_s, outer_a, peers)
    returned = lax.all_to_all(payload, "dom", split_axis=0, concat_axis=0, tiled=True)
    bit = peers // 2
    while bit > 4:
        grads = pair_sum(grads, swap(grads, "dom", bit))
        bit //= 2
    partial, grads = inner_back(rows, cols, scaled, base, inner_a, grads, swap(grads, "dom", 4))
    grads = pair_sum(grads, swap(grads, "dom", 2))
    mine = add_returned(targets, returned, came_s, partial)
    across = swap(mine, "grp", 2)
    beside = swap(mine, "grp", 1)
    opposite = swap(across, "grp", 1)
    feature_grad, self_grad, neigh_grad = finish(mine, across, beside, opposite, grads, swap(grads, "dom", 1))
    return layer_out, feature_grad, self_grad, neigh_grad


def solution(mesh):
    placed = (
        P("dom", None),
        P(None, "grp"),
        P(None, "grp"),
        P("dom", "grp"),
        P("dom", None),
        P("dom", None),
        P("dom", None, None, None),
        P("dom", None, None),
        P("dom", None),
        P("dom", None, None, None),
        P("dom", None),
    )
    return jax.shard_map(
        shards,
        mesh=mesh,
        in_specs=placed,
        out_specs=(P("dom", "grp"), P("dom", None), P(None, "grp"), P(None, "grp")),
        check_vma=False,
    )
```

time: 59.4 us -> 57.3 us (0.965)
  Pallas kernels: 20.3 us -> 18.2 us
  waiting for transfers between devices: 17.6 us -> 16.6 us
  starting transfers between devices: 20.3 us -> 21.2 us
    ppermute x11, waiting for transfers between devices: 11.5 us -> 9.45 us  [swap(): lax.ppermute(x, axis, [(i, i ^ bit) for i in range(lax.axis_size(axis))])]
    pallas_call x4, Pallas kernels: 11.7 us -> 10 us  [the longest x1 5.13 us: stage(): pl.pallas_call(stage_kernel, out_shape=tuple((pltpu.SMEM(x.shape, jnp.int...]
    ppermute x11, starting transfers between devices: 9.42 us -> 10.4 us  [swap(): lax.ppermute(x, axis, [(i, i ^ bit) for i in range(lax.axis_size(axis))])]
    all_to_all x1, waiting for transfers between devices: 5.75 us -> 6.55 us  [shards(): lax.all_to_all(outgoing, 'dom', split_axis=0, concat_axis=0, tiled=True)]
  transfers between devices with their start and end apart: 13 -> 13, of which waited for: 9 -> 8; matrix products, arithmetic and copies ran while one was open for 0% -> 0% of each run, Pallas kernels for 19% -> 18%
where the time goes in v4:
time: 57.3 us; the launch traced here: 56.8 us
  starting transfers between devices  21.2 us (37%)
  Pallas kernels  18.2 us (32%)
  waiting for transfers between devices  16.6 us (29%)
  between operations  0.69 us (1%)
    ppermute x11, starting transfers between devices, swap(): lax.ppermute(x, axis, [(i, i ^ bit) for i in range(lax.axis_size(axis))])  10.4 us
    ppermute x11, waiting for transfers between devices, swap(): lax.ppermute(x, axis, [(i, i ^ bit) for i in range(lax.axis_size(axis))])  9.45 us
    all_to_all x1, starting transfers between devices, shards(): lax.all_to_all(outgoing, 'dom', split_axis=0, concat_axis=0, tiled=True)  7.26 us
    all_to_all x1, waiting for transfers between devices, shards(): lax.all_to_all(outgoing, 'dom', split_axis=0, concat_axis=0, tiled=True)  6.55 us
    pallas_call x1, Pallas kernels, stage(): pl.pallas_call(stage_kernel, out_shape=tuple((pltpu.SMEM(x.shape, jnp.int...  5.13 us
    pallas_call x1, Pallas kernels, layer(): pl.pallas_call(functools.partial(layer_kernel, chunk), out_shape=(jax.Sha...  5.02 us
    all_to_all x1, starting transfers between devices, shards(): lax.all_to_all(payload, 'dom', split_axis=0, concat_axis=0, tiled=True)  3.62 us
    pallas_call x1, Pallas kernels, inner_back(): pl.pallas_call(inner_back_kernel, out_shape=(pltpu.VMEM(base.shape, F32),...  3.44 us
  transfers between devices with their start and end apart: 13, of which 8 were waited for; matrix products, arithmetic and copies ran while one was open for 0% of the time, Pallas kernels for 18%

profile of v4, /device:TPU:0, one launch (start us, length us, event | category | flops | bytes accessed | tf_op | source)
XLA Modules:
  0.0 56.8 jit_solution(17520891554142663409)
XLA Ops:
  0.6 1.8 %gather_halves.1 = bf16[8,3,64,128]{3,2,1,0:T(8,128)(2,1)} custom-call(s32[3,1,8]{2,1,0:T(1,128)} %bitcast.10, bf16[2048,128]{1,0:T(8,128)(2,1)} %feat_far.5), custom_call_target="tpu_custom_call" | custom-call | tf_op jit(solution)/shard_map/gather_halves/pallas_call | solution.py:58
  2.4 7.3 %all-to-all-start = ((bf16[8,3,64,128]{3,2,1,0:T(8,128)(2,1)}), bf16[8,3,64,128]{3,2,1,0:T(8,128)(2,1)S(1)}, u32[]{:S(2)}, u32[]{:S(2)}) async-start(bf16[8,3,64,128]{3,2,1,0:T(8,128)(2,1)} %gather_halves.1), calls=%async_computation | async-start | bytes 786432 | tf_op jit(solution)/shard_map/all_to_all | solution.py:464
  9.7 5.1 %stage.1 = (s32[1,64]{1,0:T(1,128)S(4)}, s32[1,64]{1,0:T(1,128)S(4)}, s32[1,24]{1,0:T(1,128)S(4)}, s32[1,8]{1,0:T(1,128)S(4)}, s32[3,1,8]{2,1,0:T(1,128)S(4)}, /...) custom-call(s32[1,64]{1,0:T(1,128)} %rows_far.1, s32[1,64]{1,0:T(1,128)} %cols_far.1, ...), custom_call_target="tpu_custom_call" | custom-call | flops 536870912 | bytes 6291456 | tf_op jit(solution)/shard_map/stage/pallas_call | solution.py:138
  14.8 6.6 %all-to-all-done.own = bf16[8,3,64,128]{3,2,1,0:T(8,128)(2,1)S(1)} async-done(((bf16[8,3,64,128]{3,2,1,0:T(8,128)(2,1)}), bf16[8,3,64,128]{3,2,1,0:T(8,128)(2,1)S(1)}, u32[]{:S(2)}, u32[]{:S(2)}) %all-to-all-start) | async-done | bytes 393248 | tf_op jit(solution)/shard_map/all_to_all | solution.py:464
  21.4 1.7 %collective-permute-done.other = bf16[8,3,64,128]{3,2,1,0:T(8,128)(2,1)S(1)} collective-permute-done((bf16[8,3,64,128]{3,2,1,0:T(8,128)(2,1)S(1)}, bf16[8,3,64,128]{3,2,1,0:T(8,128)(2,1)S(1)}, u32[]{:S(2)}, u32[]{:S(2)}) %collective-permute-start) | collective-permute-done | bytes 393248 | tf_op jit(solution)/shard_map/ppermute | solution.py:441
  23.1 5.0 %layer.1 = (bf16[2048,256]{1,0:T(8,128)(2,1)}, bf16[256,256]{1,0:T(8,128)(2,1)}, bf16[2,16,32,128]{3,2,1,0:T(8,128)(2,1)S(1)}, bf16[2,16,32,128]{3,2,1,0:T(8,128...) custom-call(s32[1,24]{1,0:T(1,128)S(4)} %get-tuple-element.28.outer_, ...), custom_call_target="tpu_custom_call", output_to_operand_aliasing={{6}: (5, {})} | custom-call | flops 1200000000 | bytes 8388608 | tf_op jit(solution)/shard_map/layer/pallas_call | solution.py:252
  28.1 0.2 collective-permute-start.1
  28.3 0.4 collective-permute-start.3
  28.7 1.0 %collective-permute-done.1.got = bf16[2,16,32,128]{3,2,1,0:T(8,128)(2,1)S(1)} collective-permute-done((bf16[2,16,32,128]{3,2,1,0:T(8,128)(2,1)S(1)}, bf16[2,16,32,128]{3,2,1,0:T(8,128)(2,1)S(1)}, u32[]{:S(2)}, u32[]{:S(2)}) %collective-permute-start.1) | collective-permute-done | bytes 262176 | tf_op jit(solution)/shard_map/ppermute | solution.py:441
  29.8 1.6 %collective-permute-start.2 = (bf16[16,32,128]{2,1,0:T(8,128)(2,1)S(1)}, bf16[16,32,128]{2,1,0:T(8,128)(2,1)S(1)}, u32[]{:S(2)}, u32[]{:S(2)}) collective-permute-start(bf16[16,32,128]{2,1,0:T(8,128)(2,1)S(1)} %fusion), channel_id=1, source_target_pairs={{0,2},{1,3},{2,0},{3,1},{4,6},{5,7},{6,4},{7,5},{8,10},{9,11},{10,... | collective-permute-start | bytes 393224 | tf_op jit(solution)/shard_map/ppermute | solution.py:441
  31.4 0.8 %collective-permute-start.5 = (bf16[256,256]{1,0:T(8,128)(2,1)}, bf16[256,256]{1,0:T(8,128)(2,1)S(1)}, u32[]{:S(2)}, u32[]{:S(2)}) collective-permute-start(bf16[256,256]{1,0:T(8,128)(2,1)} %get-tuple-element.46.grads), channel_id=1, source_target_pairs={{0,16},{4,20},{8,24},{12,28},{16,0},{20,4},{24,8},{28,12},{1,17},{... | collective-permute-start | bytes 393224 | tf_op jit(solution)/shard_map/ppermute | solution.py:441
  32.2 3.2 %collective-permute-done.2.came = bf16[16,32,128]{2,1,0:T(8,128)(2,1)S(1)} collective-permute-done((bf16[16,32,128]{2,1,0:T(8,128)(2,1)S(1)}, bf16[16,32,128]{2,1,0:T(8,128)(2,1)S(1)}, u32[]{:S(2)}, u32[]{:S(2)}) %collective-permute-start.2) | collective-permute-done | bytes 131104 | tf_op jit(solution)/shard_map/ppermute | solution.py:441
  35.4 1.3 %outer_back.1 = (bf16[16,32,128]{2,1,0:T(8,128)(2,1)S(1)}, f32[16,32,128]{2,1,0:T(8,128)S(1)}, bf16[8,3,32,128]{3,2,1,0:T(8,128)(2,1)}) custom-call(s32[1,24]{1,0:T(1,128)S(4)} %get-tuple-element.28.outer_rows, s32[1,8]{1,0:T(1,128)S(4)} %get-tuple-element.29.live, bf16[2,16,32,128]{3,2,1,0:T(8,128)(2,1)S(1)} %get-tuple-element.37.keep, ...), custom_call_target="tpu_custom_call" | custom-call | flops 25165824 | bytes 2097152 | tf_op jit(solution)/shard_map/outer_back/pallas_call | solution.py:304
  36.7 3.6 %all-to-all-start.1 = ((bf16[8,3,32,128]{3,2,1,0:T(8,128)(2,1)}), bf16[8,3,32,128]{3,2,1,0:T(8,128)(2,1)S(1)}, u32[]{:S(2)}, u32[]{:S(2)}) async-start(bf16[8,3,32,128]{3,2,1,0:T(8,128)(2,1)} %get-tuple-element.41), calls=%async_computation.1 | async-start | bytes 393216 | tf_op jit(solution)/shard_map/all_to_all | solution.py:478
  40.4 1.6 %collective-permute-start.4 = (bf16[16,32,128]{2,1,0:T(8,128)(2,1)S(1)}, bf16[16,32,128]{2,1,0:T(8,128)(2,1)S(1)}, u32[]{:S(2)}, u32[]{:S(2)}) collective-permute-start(bf16[16,32,128]{2,1,0:T(8,128)(2,1)S(1)} %fusion.1), channel_id=1, source_target_pairs={{0,2},{1,3},{2,0},{3,1},{4,6},{5,7},{6,4},{7,5},{8,10},{9,11},{10,... | collective-permute-start | bytes 393224 | tf_op jit(solution)/shard_map/ppermute | solution.py:441
  42.0 3.4 %inner_back.1 = (f32[16,32,128]{2,1,0:T(8,128)S(1)}, bf16[256,256]{1,0:T(8,128)(2,1)S(1)}) custom-call(s32[1,64]{1,0:T(1,128)S(4)} %get-tuple-element.42.rows, s32[1,64]{1,0:T(1,128)S(4)} %get-tuple-element.43.cols, bf16[16,32,128]{2,1,0:T(8,128)(2,1)S(1)} %get-tuple-element.44.scaled, f32[16,32,128]{2,1,0:T(8,128)S(1)} %get-tuple-element.45.base, ...), custom_call_target="tpu_custom_call" | custom-call | flops 67108864 | bytes 3145728 | tf_op jit(solution)/shard_map/inner_back/pallas_call | solution.py:338
  45.4 2.1 %collective-permute-start.9 = (bf16[256,256]{1,0:T(8,128)(2,1)S(1)}, bf16[256,256]{1,0:T(8,128)(2,1)S(1)}, u32[]{:S(2)}, u32[]{:S(2)}) collective-permute-start(bf16[256,256]{1,0:T(8,128)(2,1)S(1)} %get-tuple-element.48.a), channel_id=1, source_target_pairs={{0,8},{4,12},{8,0},{12,4},{16,24},{20,28},{24,16},{28,20},{1,9},{5... | collective-permute-start | bytes 393224 | tf_op jit(solution)/shard_map/ppermute | solution.py:441
  47.5 0.6 %all-to-all-done.1.returned = bf16[8,3,32,128]{3,2,1,0:T(8,128)(2,1)S(1)} async-done(((bf16[8,3,32,128]{3,2,1,0:T(8,128)(2,1)}), bf16[8,3,32,128]{3,2,1,0:T(8,128)(2,1)S(1)}, u32[]{:S(2)}, u32[]{:S(2)}) %all-to-all-start.1) | async-done | bytes 196640 | tf_op jit(solution)/shard_map/all_to_all | solution.py:478
  48.3 1.6 %collective-permute-start.6 = (bf16[16,32,128]{2,1,0:T(8,128)(2,1)S(1)}, bf16[16,32,128]{2,1,0:T(8,128)(2,1)S(1)}, u32[]{:S(2)}, u32[]{:S(2)}) collective-permute-start(bf16[16,32,128]{2,1,0:T(8,128)(2,1)S(1)} %add_returned.1.mine), channel_id=1, source_target_pairs={{0,2},{1,3},{2,0},{3,1},{4,6},{5,7},{6,4},{7,5},{8,10},{9,11},{10,... | collective-permute-start | bytes 393224 | tf_op jit(solution)/shard_map/ppermute | solution.py:441
  49.9 0.5 collective-permute-done.9.b
  50.5 2.1 %collective-permute-start.10 = (bf16[256,256]{1,0:T(8,128)(2,1)S(1)}, bf16[256,256]{1,0:T(8,128)(2,1)S(1)}, u32[]{:S(2)}, u32[]{:S(2)}) collective-permute-start(bf16[256,256]{1,0:T(8,128)(2,1)S(1)} %pair_sum.1.grads), channel_id=1, source_target_pairs={{0,4},{4,0},{8,12},{12,8},{16,20},{20,16},{24,28},{28,24},{1,5},{5... | collective-permute-start | bytes 393224 | tf_op jit(solution)/shard_map/ppermute | solution.py:441
  52.6 0.7 %collective-permute-done.6.across = bf16[16,32,128]{2,1,0:T(8,128)(2,1)S(1)} collective-permute-done((bf16[16,32,128]{2,1,0:T(8,128)(2,1)S(1)}, bf16[16,32,128]{2,1,0:T(8,128)(2,1)S(1)}, u32[]{:S(2)}, u32[]{:S(2)}) %collective-permute-start.6) | collective-permute-done | bytes 131104 | tf_op jit(solution)/shard_map/ppermute | solution.py:441
  53.3 2.2 %collective-permute-done.10.grads_came = bf16[256,256]{1,0:T(8,128)(2,1)S(1)} collective-permute-done((bf16[256,256]{1,0:T(8,128)(2,1)S(1)}, bf16[256,256]{1,0:T(8,128)(2,1)S(1)}, u32[]{:S(2)}, u32[]{:S(2)}) %collective-permute-start.10) | collective-permute-done | bytes 131104 | tf_op jit(solution)/shard_map/ppermute | solution.py:441
  55.5 1.3 %finish.1 = (f32[2048,128]{1,0:T(8,128)}, f32[128,256]{1,0:T(8,128)}, f32[128,256]{1,0:T(8,128)}) custom-call(bf16[16,32,128]{2,1,0:T(8,128)(2,1)S(1)} %add_returned.1.mine, bf16[16,32,128]{2,1,0:T(8,128)(2,1)S(1)} %collective-permute-done.6.across, bf16[16,32,128]{2,1,0:T(8,128)(2,1)S(1)} %collective-permute-done.7.beside, ...), custom_call_target="tpu_custom_call" | custom-call | flops 67108864 | bytes 2097152 | tf_op jit(solution)/shard_map/finish/pallas_call | solution.py:424
  (12 shorter events, 0.3 us)
Async XLA Ops:
  2.4 19.0 %all-to-all-start = ((bf16[8,3,64,128]{3,2,1,0:T(8,128)(2,1)}), bf16[8,3,64,128]{3,2,1,0:T(8,128)(2,1)S(1)}, u32[]{:S(2)}, u32[]{:S(2)}) async-start(bf16[8,3,64,128]{3,2,1,0:T(8,128)(2,1)} %gather_halves.1), calls=%async_computation | async-start | bytes 786432 | tf_op jit(solution)/shard_map/all_to_all | solution.py:464
  21.4 1.7 %collective-permute-start = (bf16[8,3,64,128]{3,2,1,0:T(8,128)(2,1)S(1)}, bf16[8,3,64,128]{3,2,1,0:T(8,128)(2,1)S(1)}, u32[]{:S(2)}, u32[]{:S(2)}) collective-permute-start(bf16[8,3,64,128]{3,2,1,0:T(8,128)(2,1)S(1)} %all-to-all-done.own), channel_id=1, source_target_pairs={{0,1},{1,0},{2,3},{3,2},{4,5},{5,4},{6,7},{7,6},{8,9},{9,8},{10,11... | collective-permute-start | bytes 1179656 | tf_op jit(solution)/shard_map/ppermute | solution.py:441
  28.1 1.6 %collective-permute-start.1 = (bf16[2,16,32,128]{3,2,1,0:T(8,128)(2,1)S(1)}, bf16[2,16,32,128]{3,2,1,0:T(8,128)(2,1)S(1)}, u32[]{:S(2)}, u32[]{:S(2)}) collective-permute-start(bf16[2,16,32,128]{3,2,1,0:T(8,128)(2,1)S(1)} %get-tuple-element.38), channel_id=1, source_target_pairs={{0,1},{1,0},{2,3},{3,2},{4,5},{5,4},{6,7},{7,6},{8,9},{9,8},{10,11... | collective-permute-start | bytes 786440 | tf_op jit(solution)/shard_map/ppermute | solution.py:441
  28.3 3.8 %collective-permute-start.3 = (bf16[2,16,32,128]{3,2,1,0:T(8,128)(2,1)S(1)}, bf16[2,16,32,128]{3,2,1,0:T(8,128)(2,1)S(1)}, u32[]{:S(2)}, u32[]{:S(2)}) collective-permute-start(bf16[2,16,32,128]{3,2,1,0:T(8,128)(2,1)S(1)} %get-tuple-element.40), channel_id=1, source_target_pairs={{0,1},{1,0},{2,3},{3,2},{4,5},{5,4},{6,7},{7,6},{8,9},{9,8},{10,11... | collective-permute-start | bytes 786440 | tf_op jit(solution)/shard_map/ppermute | solution.py:441
  29.8 5.6 %collective-permute-start.2 = (bf16[16,32,128]{2,1,0:T(8,128)(2,1)S(1)}, bf16[16,32,128]{2,1,0:T(8,128)(2,1)S(1)}, u32[]{:S(2)}, u32[]{:S(2)}) collective-permute-start(bf16[16,32,128]{2,1,0:T(8,128)(2,1)S(1)} %fusion), channel_id=1, source_target_pairs={{0,2},{1,3},{2,0},{3,1},{4,6},{5,7},{6,4},{7,5},{8,10},{9,11},{10,... | collective-permute-start | bytes 393224 | tf_op jit(solution)/shard_map/ppermute | solution.py:441
  31.4 10.6 %collective-permute-start.5 = (bf16[256,256]{1,0:T(8,128)(2,1)}, bf16[256,256]{1,0:T(8,128)(2,1)S(1)}, u32[]{:S(2)}, u32[]{:S(2)}) collective-permute-start(bf16[256,256]{1,0:T(8,128)(2,1)} %get-tuple-element.46.grads), channel_id=1, source_target_pairs={{0,16},{4,20},{8,24},{12,28},{16,0},{20,4},{24,8},{28,12},{1,17},{... | collective-permute-start | bytes 393224 | tf_op jit(solution)/shard_map/ppermute | solution.py:441
  36.7 11.4 %all-to-all-start.1 = ((bf16[8,3,32,128]{3,2,1,0:T(8,128)(2,1)}), bf16[8,3,32,128]{3,2,1,0:T(8,128)(2,1)S(1)}, u32[]{:S(2)}, u32[]{:S(2)}) async-start(bf16[8,3,32,128]{3,2,1,0:T(8,128)(2,1)} %get-tuple-element.41), calls=%async_computation.1 | async-start | bytes 393216 | tf_op jit(solution)/shard_map/all_to_all | solution.py:478
  40.4 7.1 %collective-permute-start.4 = (bf16[16,32,128]{2,1,0:T(8,128)(2,1)S(1)}, bf16[16,32,128]{2,1,0:T(8,128)(2,1)S(1)}, u32[]{:S(2)}, u32[]{:S(2)}) collective-permute-start(bf16[16,32,128]{2,1,0:T(8,128)(2,1)S(1)} %fusion.1), channel_id=1, source_target_pairs={{0,2},{1,3},{2,0},{3,1},{4,6},{5,7},{6,4},{7,5},{8,10},{9,11},{10,... | collective-permute-start | bytes 393224 | tf_op jit(solution)/shard_map/ppermute | solution.py:441
  45.4 5.0 %collective-permute-start.9 = (bf16[256,256]{1,0:T(8,128)(2,1)S(1)}, bf16[256,256]{1,0:T(8,128)(2,1)S(1)}, u32[]{:S(2)}, u32[]{:S(2)}) collective-permute-start(bf16[256,256]{1,0:T(8,128)(2,1)S(1)} %get-tuple-element.48.a), channel_id=1, source_target_pairs={{0,8},{4,12},{8,0},{12,4},{16,24},{20,28},{24,16},{28,20},{1,9},{5... | collective-permute-start | bytes 393224 | tf_op jit(solution)/shard_map/ppermute | solution.py:441
  48.3 5.0 %collective-permute-start.6 = (bf16[16,32,128]{2,1,0:T(8,128)(2,1)S(1)}, bf16[16,32,128]{2,1,0:T(8,128)(2,1)S(1)}, u32[]{:S(2)}, u32[]{:S(2)}) collective-permute-start(bf16[16,32,128]{2,1,0:T(8,128)(2,1)S(1)} %add_returned.1.mine), channel_id=1, source_target_pairs={{0,2},{1,3},{2,0},{3,1},{4,6},{5,7},{6,4},{7,5},{8,10},{9,11},{10,... | collective-permute-start | bytes 393224 | tf_op jit(solution)/shard_map/ppermute | solution.py:441
  50.5 5.0 %collective-permute-start.10 = (bf16[256,256]{1,0:T(8,128)(2,1)S(1)}, bf16[256,256]{1,0:T(8,128)(2,1)S(1)}, u32[]{:S(2)}, u32[]{:S(2)}) collective-permute-start(bf16[256,256]{1,0:T(8,128)(2,1)S(1)} %pair_sum.1.grads), channel_id=1, source_target_pairs={{0,4},{4,0},{8,12},{12,8},{16,20},{20,16},{24,28},{28,24},{1,5},{5... | collective-permute-start | bytes 393224 | tf_op jit(solution)/shard_map/ppermute | solution.py:441
  52.6 3.0 %collective-permute-start.7 = (bf16[16,32,128]{2,1,0:T(8,128)(2,1)S(1)}, bf16[16,32,128]{2,1,0:T(8,128)(2,1)S(1)}, u32[]{:S(2)}, u32[]{:S(2)}) collective-permute-start(bf16[16,32,128]{2,1,0:T(8,128)(2,1)S(1)} %add_returned.1.mine), channel_id=1, source_target_pairs={{0,1},{1,0},{2,3},{3,2},{4,5},{5,4},{6,7},{7,6},{8,9},{9,8},{10,11... | collective-permute-start | bytes 393224 | tf_op jit(solution)/shard_map/ppermute | solution.py:441
  53.3 2.2 %collective-permute-start.8 = (bf16[16,32,128]{2,1,0:T(8,128)(2,1)S(1)}, bf16[16,32,128]{2,1,0:T(8,128)(2,1)S(1)}, u32[]{:S(2)}, u32[]{:S(2)}) collective-permute-start(bf16[16,32,128]{2,1,0:T(8,128)(2,1)S(1)} %collective-permute-done.6.across), channel_id=1, source_target_pairs={{0,1},{1,0},{2,3},{3,2},{4,5},{5,4},{6,7},{7,6},{8,9},{9,8},{10,11... | collective-permute-start | bytes 393224 | tf_op jit(solution)/shard_map/ppermute | solution.py:441

commit v5 on v4

--- a/solution.py
+++ b/solution.py
@@ -72,8 +72,8 @@
 
 def stage_kernel(
     rows_far, cols_far, outer_rows_far, live_far, targets_far, feat_far, inner_far, outer_far,
-    rows, cols, outer_rows, live, targets, total, over, outer,
-    feat, inner, wide, sems, inner_sems,
+    rows, cols, outer_rows, live, targets, total, over, over_rows,
+    feat, inner, outer, wide, degree_rows, sems, inner_sems,
 ):
     loc, block, feat_width = total.shape
     count, outer_count = inner.shape[0], outer.shape[0]
@@ -106,27 +106,38 @@
     wide[:, :, feat_width:] = jnp.ones((loc, block, feat_width), BF16)
     total[...] = x.astype(F32)
     over[...] = jnp.ones((loc, block, feat_width), F32)
+    degree_rows[...] = jnp.ones(degree_rows.shape, F32)
+    few = jnp.ones((degree_rows.shape[1], block), BF16)
     for g in range(groups):
         blocks[g].wait()
         products = [dot(inner[g * GROUP + k], wide[cols[0, g * GROUP + k]]) for k in range(GROUP)]
+        flat = [
+            lax.dot_general(few, inner[g * GROUP + k], ROWS_LAST, preferred_element_type=F32) for k in range(GROUP)
+        ]
         for k in range(GROUP):
             r = rows[0, g * GROUP + k]
             total[r] += products[k][:, :feat_width]
             over[r] += products[k][:, feat_width:]
+            degree_rows[r] += flat[k]
     for copy in tables[1:]:
         copy.wait()
 
     def some(g, _):
         ones = jnp.ones((block, feat_width), BF16)
         products = [dot(outer[g * GROUP + k], ones) for k in range(GROUP)]
+        flat = [
+            lax.dot_general(few, outer[g * GROUP + k], ROWS_LAST, preferred_element_type=F32) for k in range(GROUP)
+        ]
         for k in range(GROUP):
             n = g * GROUP + k
             alive = (n % slots < live[0, n // slots]).astype(F32)
             over[outer_rows[0, n]] += products[k] * alive
+            degree_rows[outer_rows[0, n]] += flat[k] * alive
         return 0
 
     lax.fori_loop(0, outer_count // GROUP, some, 0)
     over[...] = 1.0 / over[...]
+    over_rows[...] = 1.0 / degree_rows[...]
 
 
 def stage(rows, cols, outer_rows, live, targets, features, inner, outer):
@@ -138,13 +149,15 @@
     return pl.pallas_call(
         stage_kernel,
         out_shape=tuple(pltpu.SMEM(x.shape, jnp.int32) for x in scalars)
-        + (pltpu.VMEM(sums, F32), pltpu.VMEM(sums, F32), pltpu.VMEM(outer.shape, BF16)),
+        + (pltpu.VMEM(sums, F32), pltpu.VMEM(sums, F32), pltpu.VMEM((loc, 8, block), F32)),
         in_specs=[FAR] * 8,
         out_specs=(SCALARS,) * 5 + (WHOLE,) * 3,
         scratch_shapes=[
             pltpu.VMEM(features.shape, BF16),
             pltpu.VMEM(inner.shape, BF16),
+            pltpu.VMEM(outer.shape, BF16),
             pltpu.VMEM((loc, block, 2 * feat_width), BF16),
+            pltpu.VMEM((loc, 8, block), F32),
             pltpu.SemaphoreType.DMA((7,)),
             pltpu.SemaphoreType.DMA((count // GROUP,)),
         ],
@@ -154,11 +167,55 @@
     )(*far(*scalars, features, inner, outer))
 
 
+def fetch_kernel(
+    outer_far, feat_far, cot_far, self_far, neigh_far, outer, feat, cot, weights, turned, w_self, w_neigh, sems
+):
+    feat_width = feat.shape[1]
+    part = feat_width // lax.axis_size("grp")
+    me = lax.axis_index("grp")
+    fetches = [
+        pltpu.make_async_copy(source, place, sems.at[k])
+        for k, (source, place) in enumerate((
+            (self_far, w_self), (neigh_far, w_neigh), (outer_far, outer), (feat_far, feat), (cot_far, cot),
+        ))
+    ]
+    for fetch in fetches:
+        fetch.start()
+    for fetch in fetches[:2]:
+        fetch.wait()
+    weights[:feat_width] = w_self[...] * 0.5
+    weights[feat_width:] = w_neigh[...] * 0.5
+    for spot, away in enumerate((3, 1, 2, 0)):
+        start = pl.multiple_of((me ^ away) * part, part)
+        turned[pl.ds(spot * part, part)] = w_self[pl.ds(start, part)] * 0.5
+        turned[pl.ds(feat_width + spot * part, part)] = w_neigh[pl.ds(start, part)] * 0.5
+    for fetch in fetches[2:]:
+        fetch.wait()
+
+
+def fetch(outer, features, cotangent, w_self, w_neigh):
+    both = (2 * features.shape[1], w_self.shape[1])
+    return pl.pallas_call(
+        fetch_kernel,
+        out_shape=tuple(pltpu.VMEM(shape, BF16) for shape in (outer.shape, features.shape, cotangent.shape, both, both)),
+        in_specs=[FAR] * 5,
+        out_specs=(WHOLE,) * 5,
+        scratch_shapes=[
+            pltpu.VMEM(w_self.shape, BF16),
+            pltpu.VMEM(w_neigh.shape, BF16),
+            pltpu.SemaphoreType.DMA((5,)),
+        ],
+        compiler_params=params(8 + outer.size * 2 / MIB),
+        cost_estimate=cost(1e6, 3 * MIB),
+        name="fetch",
+    )(*far(outer, features, cotangent, w_self, w_neigh))
+
+
 def layer_kernel(
     chunk_blocks,
-    outer_rows, live, own, other, outer, total_in, over_all, feat_far, cot_far, self_far, neigh_far,
+    outer_rows, live, own, other, outer, total_in, over_all, over_rows, feat, cot, weights, turned,
     layer_out, grads, send_n, keep_n, send_s, keep_s, total,
-    feat, cot, w_self, w_neigh, smooth, weights, turned, grad_sum, sems, out_sems,
+    smooth, grad_sum, out_sems,
 ):
     del total_in
     peers, slots, half, feat_width = own.shape
@@ -167,16 +224,7 @@
     chunks = loc // chunk_blocks
     rows = chunk_blocks * block
     part = feat_width // lax.axis_size("grp")
-    me = lax.axis_index("grp")
-    mine = me % 2
-    fetches = [
-        pltpu.make_async_copy(source, place, sems.at[k])
-        for k, (source, place) in enumerate((
-            (self_far, w_self), (neigh_far, w_neigh), (feat_far, feat), (cot_far, cot),
-        ))
-    ]
-    for fetch in fetches:
-        fetch.start()
+    mine = lax.axis_index("grp") % 2
 
     def some(g, _):
         products = []
@@ -192,18 +240,6 @@
         return 0
 
     lax.fori_loop(0, count // GROUP, some, 0)
-    for fetch in fetches:
-        fetch.wait()
-    weights[:feat_width] = w_self[...] * 0.5
-    weights[feat_width:] = w_neigh[...] * 0.5
-    for spot, away in enumerate((3, 1, 2, 0)):
-        start = pl.multiple_of((me ^ away) * part, part)
-        turned[pl.ds(spot * part, part)] = w_self[pl.ds(start, part)] * 0.5
-        turned[pl.ds(feat_width + spot * part, part)] = w_neigh[pl.ds(start, part)] * 0.5
-    eye = lax.broadcasted_iota(jnp.int32, (feat_width, feat_width), 0) == lax.broadcasted_iota(
-        jnp.int32, (feat_width, feat_width), 1
-    )
-    eye = eye.astype(BF16)
     leaving = []
     for c in range(chunks):
         place = pl.ds(c * rows, rows)
@@ -226,27 +262,26 @@
             grad_sum[...] += grown
         else:
             grads[...] = (0.5 * (grad_sum[...] + grown)).astype(BF16)
-        self_t = lax.dot_general(turned[:feat_width], grad_pre, ROWS_LAST, preferred_element_type=F32).astype(BF16)
-        neigh = lax.dot_general(grad_pre, turned[feat_width:], ROWS_LAST, preferred_element_type=F32)
-        neigh = (neigh * over).astype(BF16)
-        neigh_t = lax.dot_general(eye, neigh, ROWS_LAST, preferred_element_type=F32).astype(BF16)
+        back = lax.dot_general(turned[...], grad_pre, ROWS_LAST, preferred_element_type=F32)
         for b in range(chunk_blocks):
+            at = c * chunk_blocks + b
             lanes = slice(b * block, (b + 1) * block)
-            at = c * chunk_blocks + b
+            self_t = back[:feat_width, lanes].astype(BF16)
+            neigh_t = (back[feat_width:, lanes] * over_rows[at, :1]).astype(BF16)
             for y in range(2):
-                send_n[y, at] = neigh_t[y * part : (y + 1) * part, lanes]
-                keep_n[y, at] = neigh_t[(2 + y) * part : (3 + y) * part, lanes]
-                send_s[y, at] = self_t[y * part : (y + 1) * part, lanes]
-                keep_s[y, at] = self_t[(2 + y) * part : (3 + y) * part, lanes]
+                send_n[y, at] = neigh_t[y * part : (y + 1) * part]
+                keep_n[y, at] = neigh_t[(2 + y) * part : (3 + y) * part]
+                send_s[y, at] = self_t[y * part : (y + 1) * part]
+                keep_s[y, at] = self_t[(2 + y) * part : (3 + y) * part]
     for copy in leaving:
         copy.wait()
 
 
-def layer(outer_rows, live, own, other, outer, total, over, features, cotangent, w_self, w_neigh):
+def layer(outer_rows, live, own, other, outer, total, over, over_rows, features, cotangent, weights, turned):
     feat_width = features.shape[1]
     loc, block, _ = total.shape
     chunk = 4
-    grads = (2 * feat_width, cotangent.shape[1])
+    grads = weights.shape
     part = feat_width // lax.axis_size("grp")
     piece = pltpu.VMEM((2, loc, part, block), BF16)
     return pl.pallas_call(
@@ -257,25 +292,18 @@
             piece, piece, piece, piece,
             pltpu.VMEM(total.shape, F32),
         ),
-        in_specs=[SCALARS] * 2 + [WHOLE] * 5 + [FAR] * 4,
+        in_specs=[SCALARS] * 2 + [WHOLE] * 10,
         out_specs=(FAR,) + (WHOLE,) * 6,
         input_output_aliases={5: 6},
         scratch_shapes=[
-            pltpu.VMEM(features.shape, BF16),
             pltpu.VMEM(cotangent.shape, BF16),
-            pltpu.VMEM(w_self.shape, BF16),
-            pltpu.VMEM(w_neigh.shape, BF16),
-            pltpu.VMEM(cotangent.shape, BF16),
-            pltpu.VMEM(grads, BF16),
-            pltpu.VMEM(grads, BF16),
             pltpu.VMEM(grads, F32),
-            pltpu.SemaphoreType.DMA((4,)),
             pltpu.SemaphoreType.DMA((loc // chunk,)),
         ],
         compiler_params=params(16 + 4 * own.size * 2 / MIB),
         cost_estimate=cost(1.2e9, 8 * MIB),
         name="layer",
-    )(outer_rows, live, own, other, outer, total, over, *far(features, cotangent, w_self, w_neigh))[:6]
+    )(outer_rows, live, own, other, outer, total, over, over_rows, features, cotangent, weights, turned)[:6]
 
 
 def outer_back_kernel(outer_rows, live, keep, got, came, keep_s, got_s, outer, scaled, base, payload):
@@ -316,7 +344,7 @@
     )(outer_rows, live, keep, got, came, keep_s, got_s, outer)
 
 
-def inner_back_kernel(rows, cols, scaled, base, inner_far, grads, grads_came, total, grads_out, inner, sems):
+def inner_back_kernel(rows, cols, scaled, base, inner_far, came, total, inner, sems):
     groups = inner.shape[0] // GROUP
     blocks = [
         pltpu.make_async_copy(inner_far.at[pl.ds(g * GROUP, GROUP)], inner.at[pl.ds(g * GROUP, GROUP)], sems.at[g])
@@ -324,8 +352,7 @@
     ]
     for copy in blocks:
         copy.start()
-    total[...] = base[...]
-    grads_out[...] = (grads[...].astype(F32) + grads_came[...].astype(F32)).astype(BF16)
+    total[...] = base[...] + came[...].astype(F32)
     for g in range(groups):
         blocks[g].wait()
         products = [dot(scaled[rows[0, g * GROUP + k]], inner[g * GROUP + k]) for k in range(GROUP)]
@@ -333,23 +360,23 @@
             total[cols[0, g * GROUP + k]] += products[k]
 
 
-def inner_back(rows, cols, scaled, base, inner, grads, grads_came):
+def inner_back(rows, cols, scaled, base, inner, came):
     count, block, _ = inner.shape
     return pl.pallas_call(
         inner_back_kernel,
-        out_shape=(pltpu.VMEM(base.shape, F32), pltpu.VMEM(grads.shape, BF16)),
-        in_specs=[SCALARS, SCALARS, WHOLE, WHOLE, FAR, WHOLE, WHOLE],
-        out_specs=(WHOLE, WHOLE),
+        out_shape=pltpu.VMEM(base.shape, F32),
+        in_specs=[SCALARS, SCALARS, WHOLE, WHOLE, FAR, WHOLE],
+        out_specs=WHOLE,
         scratch_shapes=[pltpu.VMEM(inner.shape, BF16), pltpu.SemaphoreType.DMA((count // GROUP,))],
         compiler_params=params(8),
         cost_estimate=cost(count * block * block * scaled.shape[1] * 2, 3 * MIB),
         name="inner_back",
-    )(rows, cols, scaled, base, *far(inner), grads, grads_came)
-
-
-def add_returned_kernel(targets, returned, came, total, out, summed):
+    )(rows, cols, scaled, base, *far(inner), came)
+
+
+def add_returned_kernel(targets, returned, total, out, summed):
     peers, slots, _, _ = returned.shape
-    summed[...] = total[...] + came[...].astype(F32)
+    summed[...] = total[...]
 
     def some(q, _):
         for s in range(slots):
@@ -360,17 +387,17 @@
     out[...] = summed[...].astype(BF16)
 
 
-def add_returned(targets, returned, came, total):
+def add_returned(targets, returned, total):
     return pl.pallas_call(
         add_returned_kernel,
         out_shape=pltpu.VMEM(total.shape, BF16),
-        in_specs=[SCALARS, WHOLE, WHOLE, WHOLE],
+        in_specs=[SCALARS, WHOLE, WHOLE],
         out_specs=WHOLE,
         scratch_shapes=[pltpu.VMEM(total.shape, F32)],
         compiler_params=params(8 + returned.size * 2 / MIB),
         cost_estimate=cost(total.size * 8, 2 * MIB),
         name="add_returned",
-    )(targets, returned, came, total)
+    )(targets, returned, total)
 
 
 def pair_sum_kernel(a, b, out):
@@ -462,13 +489,14 @@
 
     outgoing = gather_halves(features, targets, block)
     own = lax.all_to_all(outgoing, "dom", split_axis=0, concat_axis=0, tiled=True)
-    rows, cols, outer_rows, live, targets, total, over, outer_a = stage(
+    rows, cols, outer_rows, live, targets, total, over, over_rows = stage(
         inner_rows, inner_cols, outer_rows, live_count, targets, features, inner_a, outer_a
     )
-    own, total = lax.optimization_barrier((own, total))
+    own, total, outer_a = lax.optimization_barrier((own, total, outer_a))
     other = swap(own, "grp", 1)
+    outer_a, features, cotangent, weights, turned = fetch(outer_a, features, cotangent, weight_self, weight_neigh)
     layer_out, grads, send_n, keep_n, send_s, keep_s = layer(
-        outer_rows, live, own, other, outer_a, total, over, features, cotangent, weight_self, weight_neigh
+        outer_rows, live, own, other, outer_a, total, over, over_rows, features, cotangent, weights, turned
     )
     got_n = swap(send_n, "grp", 1)
     came_n = swap((keep_n[0].astype(F32) + got_n[0].astype(F32)).astype(BF16), "grp", 2)
@@ -477,12 +505,13 @@
     scaled, base, payload = outer_back(outer_rows, live, keep_n, got_n, came_n, keep_s, got_s, outer_a, peers)
     returned = lax.all_to_all(payload, "dom", split_axis=0, concat_axis=0, tiled=True)
     bit = peers // 2
-    while bit > 4:
+    while bit > 2:
         grads = pair_sum(grads, swap(grads, "dom", bit))
         bit //= 2
-    partial, grads = inner_back(rows, cols, scaled, base, inner_a, grads, swap(grads, "dom", 4))
+    base, grads = lax.optimization_barrier((base, grads))
+    partial = inner_back(rows, cols, scaled, base, inner_a, came_s)
     grads = pair_sum(grads, swap(grads, "dom", 2))
-    mine = add_returned(targets, returned, came_s, partial)
+    mine = add_returned(targets, returned, partial)
     across = swap(mine, "grp", 2)
     beside = swap(mine, "grp", 1)
     opposite = swap(across, "grp", 1)

time: 57.3 us -> 56.1 us (0.979)
  starting transfers between devices: 21.2 us -> 19.8 us
    pallas_call x1, Pallas kernels: 5.02 us -> 2.73 us  [layer(): pl.pallas_call(functools.partial(layer_kernel, chunk), out_shape=(jax.Sha...]
    ppermute x11, starting transfers between devices: 10.4 us -> 8.9 us  [swap(): lax.ppermute(x, axis, [(i, i ^ bit) for i in range(lax.axis_size(axis))])]
    all_to_all x1, waiting for transfers between devices: 6.55 us -> 5.36 us  [shards(): lax.all_to_all(outgoing, 'dom', split_axis=0, concat_axis=0, tiled=True)]
    pallas_call x1, Pallas kernels: 5.13 us -> 6.33 us  [stage(): pl.pallas_call(stage_kernel, out_shape=tuple((pltpu.SMEM(x.shape, jnp.int...]
    all_to_all x1, waiting for transfers between devices: 0.63 us -> 1.55 us  [shards(): lax.all_to_all(payload, 'dom', split_axis=0, concat_axis=0, tiled=True)]
    pallas_call x1 -> x2, Pallas kernels: 3.44 us -> 4.28 us  [the longest x1 2.54 us: inner_back(): pl.pallas_call(inner_back_kernel, out_shape=pltpu.VMEM(base.shape, F32),...]
    ppermute x11, waiting for transfers between devices: 9.45 us -> 10.2 us  [swap(): lax.ppermute(x, axis, [(i, i ^ bit) for i in range(lax.axis_size(axis))])]
  transfers between devices with their start and end apart: 13 -> 13, of which waited for: 8 -> 7; matrix products, arithmetic and copies ran while one was open for 0% -> 0% of each run, Pallas kernels for 18% -> 22%
where the time goes in v5:
time: 56.1 us; the launch traced here: 55.7 us
  starting transfers between devices  19.8 us (35%)
  Pallas kernels  18 us (32%)
  waiting for transfers between devices  17.1 us (30%)
  between operations  0.71 us (1%)
    ppermute x11, waiting for transfers between devices, swap(): lax.ppermute(x, axis, [(i, i ^ bit) for i in range(lax.axis_size(axis))])  10.2 us
    ppermute x11, starting transfers between devices, swap(): lax.ppermute(x, axis, [(i, i ^ bit) for i in range(lax.axis_size(axis))])  8.9 us
    all_to_all x1, starting transfers between devices, shards(): lax.all_to_all(outgoing, 'dom', split_axis=0, concat_axis=0, tiled=True)  7.26 us
    pallas_call x1, Pallas kernels, stage(): pl.pallas_call(stage_kernel, out_shape=tuple((pltpu.SMEM(x.shape, jnp.int...  6.33 us
    all_to_all x1, waiting for transfers between devices, shards(): lax.all_to_all(outgoing, 'dom', split_axis=0, concat_axis=0, tiled=True)  5.36 us
    all_to_all x1, starting transfers between devices, shards(): lax.all_to_all(payload, 'dom', split_axis=0, concat_axis=0, tiled=True)  3.62 us
    pallas_call x1, Pallas kernels, layer(): pl.pallas_call(functools.partial(layer_kernel, chunk), out_shape=(jax.Sha...  2.73 us
    pallas_call x1, Pallas kernels, inner_back(): pl.pallas_call(inner_back_kernel, out_shape=pltpu.VMEM(base.shape, F32),...  2.54 us
  transfers between devices with their start and end apart: 13, of which 7 were waited for; matrix products, arithmetic and copies ran while one was open for 0% of the time, Pallas kernels for 22%

profile of v5, /device:TPU:0, one launch (start us, length us, event | category | flops | bytes accessed | tf_op | source)
XLA Modules:
  0.0 55.7 jit_solution(11344372866957618612)
XLA Ops:
  0.6 1.8 %gather_halves.1 = bf16[8,3,64,128]{3,2,1,0:T(8,128)(2,1)} custom-call(s32[3,1,8]{2,1,0:T(1,128)} %bitcast.11, bf16[2048,128]{1,0:T(8,128)(2,1)} %feat_far.5), custom_call_target="tpu_custom_call" | custom-call | tf_op jit(solution)/shard_map/gather_halves/pallas_call | solution.py:58
  2.4 7.3 %all-to-all-start = ((bf16[8,3,64,128]{3,2,1,0:T(8,128)(2,1)}), bf16[8,3,64,128]{3,2,1,0:T(8,128)(2,1)S(1)}, u32[]{:S(2)}, u32[]{:S(2)}) async-start(bf16[8,3,64,128]{3,2,1,0:T(8,128)(2,1)} %gather_halves.1), calls=%async_computation | async-start | bytes 786432 | tf_op jit(solution)/shard_map/all_to_all | solution.py:491
  9.7 6.3 %stage.1 = (s32[1,64]{1,0:T(1,128)S(4)}, s32[1,64]{1,0:T(1,128)S(4)}, s32[1,24]{1,0:T(1,128)S(4)}, s32[1,8]{1,0:T(1,128)S(4)}, s32[3,1,8]{2,1,0:T(1,128)S(4)}, /...) custom-call(s32[1,64]{1,0:T(1,128)} %rows_far.1, s32[1,64]{1,0:T(1,128)} %cols_far.1, ...), custom_call_target="tpu_custom_call" | custom-call | flops 536870912 | bytes 6291456 | tf_op jit(solution)/shard_map/stage/pallas_call | solution.py:149
  16.0 5.4 %all-to-all-done.own = bf16[8,3,64,128]{3,2,1,0:T(8,128)(2,1)S(1)} async-done(((bf16[8,3,64,128]{3,2,1,0:T(8,128)(2,1)}), bf16[8,3,64,128]{3,2,1,0:T(8,128)(2,1)S(1)}, u32[]{:S(2)}, u32[]{:S(2)}) %all-to-all-start) | async-done | bytes 393248 | tf_op jit(solution)/shard_map/all_to_all | solution.py:491
  21.4 1.7 %fetch.1 = (bf16[24,128,128]{2,1,0:T(8,128)(2,1)S(1)}, bf16[2048,128]{1,0:T(8,128)(2,1)S(1)}, bf16[2048,256]{1,0:T(8,128)(2,1)S(1)}, bf16[256,256]{1,0:T(8,128)(2,1)S(1)}, bf16[256,256]{1,0:T(8,128)(2,1)S(1)}) custom-call(bf16[24,128,128]{2,1,0:T(8,128)(2,1)} %bitcast.10, bf16[2048,128]{1,0:T(8,128)(2,1)} %feat_far.5, bf16[2048,256]{1,0:T(8,128)(2,1)} %cot_far.1, ...), custom_call_target="tpu_custom_call" | custom-call | flops 1000000 | bytes 3145728 | tf_op jit(solution)/shard_map/fetch/pallas_call | solution.py:198
  23.2 2.7 %layer.1 = (bf16[2048,256]{1,0:T(8,128)(2,1)}, bf16[256,256]{1,0:T(8,128)(2,1)S(1)}, bf16[2,16,32,128]{3,2,1,0:T(8,128)(2,1)S(1)}, bf16[2,16,32,128]{3,2,1,0:T(8...) custom-call(s32[1,24]{1,0:T(1,128)S(4)} %get-tuple-element.34.outer_, ...), custom_call_target="tpu_custom_call", output_to_operand_aliasing={{6}: (5, {})} | custom-call | flops 1200000000 | bytes 8388608 | tf_op jit(solution)/shard_map/layer/pallas_call | solution.py:287
  25.9 0.6 %collective-permute-start.1 = (bf16[2,16,32,128]{3,2,1,0:T(8,128)(2,1)S(1)}, bf16[2,16,32,128]{3,2,1,0:T(8,128)(2,1)S(1)}, u32[]{:S(2)}, u32[]{:S(2)}) collective-permute-start(bf16[2,16,32,128]{3,2,1,0:T(8,128)(2,1)S(1)} %get-tuple-element.50), channel_id=1, source_target_pairs={{0,1},{1,0},{2,3},{3,2},{4,5},{5,4},{6,7},{7,6},{8,9},{9,8},{10,11... | collective-permute-start | bytes 786440 | tf_op jit(solution)/shard_map/ppermute | solution.py:468
  26.5 1.1 %collective-permute-done.1.got = bf16[2,16,32,128]{3,2,1,0:T(8,128)(2,1)S(1)} collective-permute-done((bf16[2,16,32,128]{3,2,1,0:T(8,128)(2,1)S(1)}, bf16[2,16,32,128]{3,2,1,0:T(8,128)(2,1)S(1)}, u32[]{:S(2)}, u32[]{:S(2)}) %collective-permute-start.1) | collective-permute-done | bytes 262176 | tf_op jit(solution)/shard_map/ppermute | solution.py:468
  27.7 1.6 %collective-permute-start.2 = (bf16[16,32,128]{2,1,0:T(8,128)(2,1)S(1)}, bf16[16,32,128]{2,1,0:T(8,128)(2,1)S(1)}, u32[]{:S(2)}, u32[]{:S(2)}) collective-permute-start(bf16[16,32,128]{2,1,0:T(8,128)(2,1)S(1)} %fusion), channel_id=1, source_target_pairs={{0,2},{1,3},{2,0},{3,1},{4,6},{5,7},{6,4},{7,5},{8,10},{9,11},{10,... | collective-permute-start | bytes 393224 | tf_op jit(solution)/shard_map/ppermute | solution.py:468
  29.3 0.8 %collective-permute-start.4 = (bf16[256,256]{1,0:T(8,128)(2,1)S(1)}, bf16[256,256]{1,0:T(8,128)(2,1)S(1)}, u32[]{:S(2)}, u32[]{:S(2)}) collective-permute-start(bf16[256,256]{1,0:T(8,128)(2,1)S(1)} %get-tuple-element.58.a), channel_id=1, source_target_pairs={{0,16},{4,20},{8,24},{12,28},{16,0},{20,4},{24,8},{28,12},{1,17},{... | collective-permute-start | bytes 393224 | tf_op jit(solution)/shard_map/ppermute | solution.py:468
  30.1 3.4 %collective-permute-done.2.came = bf16[16,32,128]{2,1,0:T(8,128)(2,1)S(1)} collective-permute-done((bf16[16,32,128]{2,1,0:T(8,128)(2,1)S(1)}, bf16[16,32,128]{2,1,0:T(8,128)(2,1)S(1)}, u32[]{:S(2)}, u32[]{:S(2)}) %collective-permute-start.2) | collective-permute-done | bytes 131104 | tf_op jit(solution)/shard_map/ppermute | solution.py:468
  33.5 1.3 %outer_back.1 = (bf16[16,32,128]{2,1,0:T(8,128)(2,1)S(1)}, f32[16,32,128]{2,1,0:T(8,128)S(1)}, bf16[8,3,32,128]{3,2,1,0:T(8,128)(2,1)}) custom-call(s32[1,24]{1,0:T(1,128)S(4)} %get-tuple-element.34.outer_rows, s32[1,8]{1,0:T(1,128)S(4)} %get-tuple-element.35.live, bf16[2,16,32,128]{3,2,1,0:T(8,128)(2,1)S(1)} %get-tuple-element.49.keep, ...), custom_call_target="tpu_custom_call" | custom-call | flops 25165824 | bytes 2097152 | tf_op jit(solution)/shard_map/outer_back/pallas_call | solution.py:332
  34.8 3.6 %all-to-all-start.1 = ((bf16[8,3,32,128]{3,2,1,0:T(8,128)(2,1)}), bf16[8,3,32,128]{3,2,1,0:T(8,128)(2,1)S(1)}, u32[]{:S(2)}, u32[]{:S(2)}) async-start(bf16[8,3,32,128]{3,2,1,0:T(8,128)(2,1)} %get-tuple-element.53), calls=%async_computation.1 | async-start | bytes 393216 | tf_op jit(solution)/shard_map/all_to_all | solution.py:506
  38.5 1.6 %collective-permute-start.5 = (bf16[16,32,128]{2,1,0:T(8,128)(2,1)S(1)}, bf16[16,32,128]{2,1,0:T(8,128)(2,1)S(1)}, u32[]{:S(2)}, u32[]{:S(2)}) collective-permute-start(bf16[16,32,128]{2,1,0:T(8,128)(2,1)S(1)} %fusion.1), channel_id=1, source_target_pairs={{0,2},{1,3},{2,0},{3,1},{4,6},{5,7},{6,4},{7,5},{8,10},{9,11},{10,... | collective-permute-start | bytes 393224 | tf_op jit(solution)/shard_map/ppermute | solution.py:468
  40.1 2.1 %collective-permute-start.9 = (bf16[256,256]{1,0:T(8,128)(2,1)S(1)}, bf16[256,256]{1,0:T(8,128)(2,1)S(1)}, u32[]{:S(2)}, u32[]{:S(2)}) collective-permute-start(bf16[256,256]{1,0:T(8,128)(2,1)S(1)} %pair_sum.2.a), channel_id=1, source_target_pairs={{0,8},{4,12},{8,0},{12,4},{16,24},{20,28},{24,16},{28,20},{1,9},{5... | collective-permute-start | bytes 393224 | tf_op jit(solution)/shard_map/ppermute | solution.py:468
  42.2 1.3 %collective-permute-done.5.came = bf16[16,32,128]{2,1,0:T(8,128)(2,1)S(1)} collective-permute-done((bf16[16,32,128]{2,1,0:T(8,128)(2,1)S(1)}, bf16[16,32,128]{2,1,0:T(8,128)(2,1)S(1)}, u32[]{:S(2)}, u32[]{:S(2)}) %collective-permute-start.5) | collective-permute-done | bytes 131104 | tf_op jit(solution)/shard_map/ppermute | solution.py:468
  43.5 2.5 %inner_back.1.total = f32[16,32,128]{2,1,0:T(8,128)S(1)} custom-call(s32[1,64]{1,0:T(1,128)S(4)} %get-tuple-element.54.rows, s32[1,64]{1,0:T(1,128)S(4)} %get-tuple-element.55.cols, bf16[16,32,128]{2,1,0:T(8,128)(2,1)S(1)} %get-tuple-element.56.scaled, f32[16,32,128]{2,1,0:T(8,128)S(1)} %get-tuple-element.59.base, bf16[64,128,128]{2,1,0:T(8,128)(2,1)} %bitcast.8, ...), custom_call_target="tpu_custom_call" | custom-call | flops 67108864 | bytes 3145728 | tf_op jit(solution)/shard_map/inner_back/pallas_call | solution.py:365
  46.1 1.6 %all-to-all-done.1.returned = bf16[8,3,32,128]{3,2,1,0:T(8,128)(2,1)S(1)} async-done(((bf16[8,3,32,128]{3,2,1,0:T(8,128)(2,1)}), bf16[8,3,32,128]{3,2,1,0:T(8,128)(2,1)S(1)}, u32[]{:S(2)}, u32[]{:S(2)}) %all-to-all-start.1) | async-done | bytes 196640 | tf_op jit(solution)/shard_map/all_to_all | solution.py:506
  47.6 0.1 add_returned.1.mine
  47.8 1.5 %collective-permute-start.6 = (bf16[16,32,128]{2,1,0:T(8,128)(2,1)S(1)}, bf16[16,32,128]{2,1,0:T(8,128)(2,1)S(1)}, u32[]{:S(2)}, u32[]{:S(2)}) collective-permute-start(bf16[16,32,128]{2,1,0:T(8,128)(2,1)S(1)} %add_returned.1.mine), channel_id=1, source_target_pairs={{0,2},{1,3},{2,0},{3,1},{4,6},{5,7},{6,4},{7,5},{8,10},{9,11},{10,... | collective-permute-start | bytes 393224 | tf_op jit(solution)/shard_map/ppermute | solution.py:468
  49.3 0.7 %collective-permute-start.10 = (bf16[256,256]{1,0:T(8,128)(2,1)S(1)}, bf16[256,256]{1,0:T(8,128)(2,1)S(1)}, u32[]{:S(2)}, u32[]{:S(2)}) collective-permute-start(bf16[256,256]{1,0:T(8,128)(2,1)S(1)} %pair_sum.3.grads), channel_id=1, source_target_pairs={{0,4},{4,0},{8,12},{12,8},{16,20},{20,16},{24,28},{28,24},{1,5},{5... | collective-permute-start | bytes 393224 | tf_op jit(solution)/shard_map/ppermute | solution.py:468
  50.0 2.8 %collective-permute-done.6.across = bf16[16,32,128]{2,1,0:T(8,128)(2,1)S(1)} collective-permute-done((bf16[16,32,128]{2,1,0:T(8,128)(2,1)S(1)}, bf16[16,32,128]{2,1,0:T(8,128)(2,1)S(1)}, u32[]{:S(2)}, u32[]{:S(2)}) %collective-permute-start.6) | collective-permute-done | bytes 131104 | tf_op jit(solution)/shard_map/ppermute | solution.py:468
  52.8 1.5 %collective-permute-done.10.grads_came = bf16[256,256]{1,0:T(8,128)(2,1)S(1)} collective-permute-done((bf16[256,256]{1,0:T(8,128)(2,1)S(1)}, bf16[256,256]{1,0:T(8,128)(2,1)S(1)}, u32[]{:S(2)}, u32[]{:S(2)}) %collective-permute-start.10) | collective-permute-done | bytes 131104 | tf_op jit(solution)/shard_map/ppermute | solution.py:468
  54.4 1.3 %finish.1 = (f32[2048,128]{1,0:T(8,128)}, f32[128,256]{1,0:T(8,128)}, f32[128,256]{1,0:T(8,128)}) custom-call(bf16[16,32,128]{2,1,0:T(8,128)(2,1)S(1)} %add_returned.1.mine, bf16[16,32,128]{2,1,0:T(8,128)(2,1)S(1)} %collective-permute-done.6.across, bf16[16,32,128]{2,1,0:T(8,128)(2,1)S(1)} %collective-permute-done.7.beside, ...), custom_call_target="tpu_custom_call" | custom-call | flops 67108864 | bytes 2097152 | tf_op jit(solution)/shard_map/finish/pallas_call | solution.py:451
  (14 shorter events, 0.2 us)
Async XLA Ops:
  2.4 19.0 %all-to-all-start = ((bf16[8,3,64,128]{3,2,1,0:T(8,128)(2,1)}), bf16[8,3,64,128]{3,2,1,0:T(8,128)(2,1)S(1)}, u32[]{:S(2)}, u32[]{:S(2)}) async-start(bf16[8,3,64,128]{3,2,1,0:T(8,128)(2,1)} %gather_halves.1), calls=%async_computation | async-start | bytes 786432 | tf_op jit(solution)/shard_map/all_to_all | solution.py:491
  21.4 1.8 %collective-permute-start = (bf16[8,3,64,128]{3,2,1,0:T(8,128)(2,1)S(1)}, bf16[8,3,64,128]{3,2,1,0:T(8,128)(2,1)S(1)}, u32[]{:S(2)}, u32[]{:S(2)}) collective-permute-start(bf16[8,3,64,128]{3,2,1,0:T(8,128)(2,1)S(1)} %all-to-all-done.own), channel_id=1, source_target_pairs={{0,1},{1,0},{2,3},{3,2},{4,5},{5,4},{6,7},{7,6},{8,9},{9,8},{10,11... | collective-permute-start | bytes 1179656 | tf_op jit(solution)/shard_map/ppermute | solution.py:468
  25.9 1.7 %collective-permute-start.1 = (bf16[2,16,32,128]{3,2,1,0:T(8,128)(2,1)S(1)}, bf16[2,16,32,128]{3,2,1,0:T(8,128)(2,1)S(1)}, u32[]{:S(2)}, u32[]{:S(2)}) collective-permute-start(bf16[2,16,32,128]{3,2,1,0:T(8,128)(2,1)S(1)} %get-tuple-element.50), channel_id=1, source_target_pairs={{0,1},{1,0},{2,3},{3,2},{4,5},{5,4},{6,7},{7,6},{8,9},{9,8},{10,11... | collective-permute-start | bytes 786440 | tf_op jit(solution)/shard_map/ppermute | solution.py:468
  26.5 3.6 %collective-permute-start.3 = (bf16[2,16,32,128]{3,2,1,0:T(8,128)(2,1)S(1)}, bf16[2,16,32,128]{3,2,1,0:T(8,128)(2,1)S(1)}, u32[]{:S(2)}, u32[]{:S(2)}) collective-permute-start(bf16[2,16,32,128]{3,2,1,0:T(8,128)(2,1)S(1)} %get-tuple-element.52), channel_id=1, source_target_pairs={{0,1},{1,0},{2,3},{3,2},{4,5},{5,4},{6,7},{7,6},{8,9},{9,8},{10,11... | collective-permute-start | bytes 786440 | tf_op jit(solution)/shard_map/ppermute | solution.py:468
  27.7 5.8 %collective-permute-start.2 = (bf16[16,32,128]{2,1,0:T(8,128)(2,1)S(1)}, bf16[16,32,128]{2,1,0:T(8,128)(2,1)S(1)}, u32[]{:S(2)}, u32[]{:S(2)}) collective-permute-start(bf16[16,32,128]{2,1,0:T(8,128)(2,1)S(1)} %fusion), channel_id=1, source_target_pairs={{0,2},{1,3},{2,0},{3,1},{4,6},{5,7},{6,4},{7,5},{8,10},{9,11},{10,... | collective-permute-start | bytes 393224 | tf_op jit(solution)/shard_map/ppermute | solution.py:468
  29.3 10.8 %collective-permute-start.4 = (bf16[256,256]{1,0:T(8,128)(2,1)S(1)}, bf16[256,256]{1,0:T(8,128)(2,1)S(1)}, u32[]{:S(2)}, u32[]{:S(2)}) collective-permute-start(bf16[256,256]{1,0:T(8,128)(2,1)S(1)} %get-tuple-element.58.a), channel_id=1, source_target_pairs={{0,16},{4,20},{8,24},{12,28},{16,0},{20,4},{24,8},{28,12},{1,17},{... | collective-permute-start | bytes 393224 | tf_op jit(solution)/shard_map/ppermute | solution.py:468
  34.8 12.8 %all-to-all-start.1 = ((bf16[8,3,32,128]{3,2,1,0:T(8,128)(2,1)}), bf16[8,3,32,128]{3,2,1,0:T(8,128)(2,1)S(1)}, u32[]{:S(2)}, u32[]{:S(2)}) async-start(bf16[8,3,32,128]{3,2,1,0:T(8,128)(2,1)} %get-tuple-element.53), calls=%async_computation.1 | async-start | bytes 393216 | tf_op jit(solution)/shard_map/all_to_all | solution.py:506
  38.5 5.0 %collective-permute-start.5 = (bf16[16,32,128]{2,1,0:T(8,128)(2,1)S(1)}, bf16[16,32,128]{2,1,0:T(8,128)(2,1)S(1)}, u32[]{:S(2)}, u32[]{:S(2)}) collective-permute-start(bf16[16,32,128]{2,1,0:T(8,128)(2,1)S(1)} %fusion.1), channel_id=1, source_target_pairs={{0,2},{1,3},{2,0},{3,1},{4,6},{5,7},{6,4},{7,5},{8,10},{9,11},{10,... | collective-permute-start | bytes 393224 | tf_op jit(solution)/shard_map/ppermute | solution.py:468
  40.1 9.1 %collective-permute-start.9 = (bf16[256,256]{1,0:T(8,128)(2,1)S(1)}, bf16[256,256]{1,0:T(8,128)(2,1)S(1)}, u32[]{:S(2)}, u32[]{:S(2)}) collective-permute-start(bf16[256,256]{1,0:T(8,128)(2,1)S(1)} %pair_sum.2.a), channel_id=1, source_target_pairs={{0,8},{4,12},{8,0},{12,4},{16,24},{20,28},{24,16},{28,20},{1,9},{5... | collective-permute-start | bytes 393224 | tf_op jit(solution)/shard_map/ppermute | solution.py:468
  47.8 5.0 %collective-permute-start.6 = (bf16[16,32,128]{2,1,0:T(8,128)(2,1)S(1)}, bf16[16,32,128]{2,1,0:T(8,128)(2,1)S(1)}, u32[]{:S(2)}, u32[]{:S(2)}) collective-permute-start(bf16[16,32,128]{2,1,0:T(8,128)(2,1)S(1)} %add_returned.1.mine), channel_id=1, source_target_pairs={{0,2},{1,3},{2,0},{3,1},{4,6},{5,7},{6,4},{7,5},{8,10},{9,11},{10,... | collective-permute-start | bytes 393224 | tf_op jit(solution)/shard_map/ppermute | solution.py:468
  49.3 5.0 %collective-permute-start.10 = (bf16[256,256]{1,0:T(8,128)(2,1)S(1)}, bf16[256,256]{1,0:T(8,128)(2,1)S(1)}, u32[]{:S(2)}, u32[]{:S(2)}) collective-permute-start(bf16[256,256]{1,0:T(8,128)(2,1)S(1)} %pair_sum.3.grads), channel_id=1, source_target_pairs={{0,4},{4,0},{8,12},{12,8},{16,20},{20,16},{24,28},{28,24},{1,5},{5... | collective-permute-start | bytes 393224 | tf_op jit(solution)/shard_map/ppermute | solution.py:468
  50.0 4.4 %collective-permute-start.7 = (bf16[16,32,128]{2,1,0:T(8,128)(2,1)S(1)}, bf16[16,32,128]{2,1,0:T(8,128)(2,1)S(1)}, u32[]{:S(2)}, u32[]{:S(2)}) collective-permute-start(bf16[16,32,128]{2,1,0:T(8,128)(2,1)S(1)} %add_returned.1.mine), channel_id=1, source_target_pairs={{0,1},{1,0},{2,3},{3,2},{4,5},{5,4},{6,7},{7,6},{8,9},{9,8},{10,11... | collective-permute-start | bytes 393224 | tf_op jit(solution)/shard_map/ppermute | solution.py:468
  52.8 1.5 %collective-permute-start.8 = (bf16[16,32,128]{2,1,0:T(8,128)(2,1)S(1)}, bf16[16,32,128]{2,1,0:T(8,128)(2,1)S(1)}, u32[]{:S(2)}, u32[]{:S(2)}) collective-permute-start(bf16[16,32,128]{2,1,0:T(8,128)(2,1)S(1)} %collective-permute-done.6.across), channel_id=1, source_target_pairs={{0,1},{1,0},{2,3},{3,2},{4,5},{5,4},{6,7},{7,6},{8,9},{9,8},{10,11... | collective-permute-start | bytes 393224 | tf_op jit(solution)/shard_map/ppermute | solution.py:468

commit v6 on v5

--- a/solution.py
+++ b/solution.py
@@ -26,6 +26,17 @@
     return [pltpu.with_memory_space_constraint(x, pltpu.HBM) for x in arrays]
 
 
+def group_of(count, slots):
+    return slots * max(k for k in range(1, 9) if count // slots % k == 0)
+
+
+def for_groups(count, body):
+    if count == 1:
+        body(0, 0)
+    else:
+        lax.fori_loop(0, count, body, 0)
+
+
 def params(mib):
     return pltpu.CompilerParams(vmem_limit_bytes=int(mib * MIB))
 
@@ -34,40 +45,45 @@
     return pl.CostEstimate(flops=int(flops), bytes_accessed=int(moved), transcendentals=0)
 
 
-def gather_kernel(half, targets_far, feat_far, out, targets, feat, sems):
-    fetches = [
-        pltpu.make_async_copy(targets_far, targets, sems.at[0]),
-        pltpu.make_async_copy(feat_far, feat, sems.at[1]),
-    ]
+def gather_kernel(targets_far, feat_far, out, targets, feat, outgoing, sems, out_sem):
+    pieces = sems.shape[0] - 1
+    step = feat.shape[0] // pieces
+    mine = lax.axis_index("grp") % 2
+    fetches = [pltpu.make_async_copy(targets_far, targets, sems.at[pieces])]
+    for k in range(pieces):
+        place = pl.ds(k * step, step)
+        fetches.append(pltpu.make_async_copy(feat_far.at[place, pl.ds(mine, 1)], feat.at[place], sems.at[k]))
     for fetch in fetches:
         fetch.start()
     for fetch in fetches:
         fetch.wait()
     slots, _, peers = targets.shape
-    block = half * 2
-    mine = lax.axis_index("grp") % 2
     for p in range(peers):
         for s in range(slots):
-            start = pl.multiple_of(targets[s, 0, p] * block + mine * half, half)
-            pltpu.make_async_copy(feat.at[pl.ds(start, half)], out.at[p, s], sems.at[2]).start()
-    pltpu.make_async_copy(out, out, sems.at[2]).wait()
+            outgoing[p, s] = feat[targets[s, 0, p], 0]
+        pltpu.make_async_copy(outgoing.at[p], out.at[p], out_sem).start()
+    pltpu.make_async_copy(outgoing, out, out_sem).wait()
 
 
 def gather_halves(features, targets, block):
+    nodes, feat_width = features.shape
+    loc, half = nodes // block, block // 2
     slots, _, peers = targets.shape
     return pl.pallas_call(
-        functools.partial(gather_kernel, block // 2),
-        out_shape=jax.ShapeDtypeStruct((peers, slots, block // 2, features.shape[1]), BF16),
+        gather_kernel,
+        out_shape=jax.ShapeDtypeStruct((peers, slots, half, feat_width), BF16),
         in_specs=[FAR, FAR],
         out_specs=FAR,
         scratch_shapes=[
             pltpu.SMEM(targets.shape, jnp.int32),
-            pltpu.VMEM(features.shape, BF16),
-            pltpu.SemaphoreType.DMA((3,)),
+            pltpu.VMEM((loc, 1, half, feat_width), BF16),
+            pltpu.VMEM((peers, slots, half, feat_width), BF16),
+            pltpu.SemaphoreType.DMA((5,)),
+            pltpu.SemaphoreType.DMA,
         ],
-        compiler_params=params(4),
+        compiler_params=params(4 + 2 * peers * slots * half * feat_width / MIB),
         name="gather_halves",
-    )(*far(targets, features))
+    )(*far(targets, features.reshape(loc, 2, half, feat_width)))
 
 
 def stage_kernel(
@@ -214,8 +230,7 @@
 def layer_kernel(
     chunk_blocks,
     outer_rows, live, own, other, outer, total_in, over_all, over_rows, feat, cot, weights, turned,
-    layer_out, grads, send_n, keep_n, send_s, keep_s, total,
-    smooth, grad_sum, out_sems,
+    smooth, grad_pre_all, both_all, send_n, keep_n, send_s, keep_s, total,
 ):
     del total_in
     peers, slots, half, feat_width = own.shape
@@ -225,22 +240,22 @@
     rows = chunk_blocks * block
     part = feat_width // lax.axis_size("grp")
     mine = lax.axis_index("grp") % 2
+    group = group_of(count, slots)
 
     def some(g, _):
         products = []
-        for k in range(GROUP):
-            n = g * GROUP + k
+        for k in range(group):
+            n = g * group + k
             near, away = own[n // slots, n % slots], other[n // slots, n % slots]
             x = jnp.concatenate([jnp.where(mine == 0, near, away), jnp.where(mine == 0, away, near)], axis=0)
             products.append(dot(outer[n], x))
-        for k in range(GROUP):
-            n = g * GROUP + k
+        for k in range(group):
+            n = g * group + k
             alive = (n % slots < live[0, n // slots]).astype(F32)
             total[outer_rows[0, n]] += products[k] * alive
         return 0
 
-    lax.fori_loop(0, count // GROUP, some, 0)
-    leaving = []
+    for_groups(count // group, some)
     for c in range(chunks):
         place = pl.ds(c * rows, rows)
         here = pl.ds(c * chunk_blocks, chunk_blocks)
@@ -252,16 +267,9 @@
         twice = 1.0 + bent
         silu = pre * twice
         smooth[place] = silu.astype(BF16)
-        leaving.append(pltpu.make_async_copy(smooth.at[place], layer_out.at[place], out_sems.at[c]))
-        leaving[-1].start()
         grad_pre = (cot[place].astype(F32) * (twice + silu * (1.0 - bent))).astype(BF16)
-        grown = lax.dot_general(both, grad_pre, ROWS_FIRST, preferred_element_type=F32)
-        if c == 0:
-            grad_sum[...] = grown
-        elif c < chunks - 1:
-            grad_sum[...] += grown
-        else:
-            grads[...] = (0.5 * (grad_sum[...] + grown)).astype(BF16)
+        grad_pre_all[place] = grad_pre
+        both_all[place] = both
         back = lax.dot_general(turned[...], grad_pre, ROWS_LAST, preferred_element_type=F32)
         for b in range(chunk_blocks):
             at = c * chunk_blocks + b
@@ -273,57 +281,88 @@
                 keep_n[y, at] = neigh_t[(2 + y) * part : (3 + y) * part]
                 send_s[y, at] = self_t[y * part : (y + 1) * part]
                 keep_s[y, at] = self_t[(2 + y) * part : (3 + y) * part]
-    for copy in leaving:
-        copy.wait()
 
 
 def layer(outer_rows, live, own, other, outer, total, over, over_rows, features, cotangent, weights, turned):
     feat_width = features.shape[1]
     loc, block, _ = total.shape
     chunk = 4
-    grads = weights.shape
     part = feat_width // lax.axis_size("grp")
     piece = pltpu.VMEM((2, loc, part, block), BF16)
     return pl.pallas_call(
         functools.partial(layer_kernel, chunk),
         out_shape=(
-            jax.ShapeDtypeStruct(cotangent.shape, BF16),
-            pltpu.VMEM(grads, BF16),
+            pltpu.VMEM(cotangent.shape, BF16),
+            pltpu.VMEM(cotangent.shape, BF16),
+            pltpu.VMEM((cotangent.shape[0], 2 * feat_width), BF16),
             piece, piece, piece, piece,
             pltpu.VMEM(total.shape, F32),
         ),
         in_specs=[SCALARS] * 2 + [WHOLE] * 10,
-        out_specs=(FAR,) + (WHOLE,) * 6,
-        input_output_aliases={5: 6},
-        scratch_shapes=[
-            pltpu.VMEM(cotangent.shape, BF16),
-            pltpu.VMEM(grads, F32),
-            pltpu.SemaphoreType.DMA((loc // chunk,)),
-        ],
+        out_specs=(WHOLE,) * 8,
+        input_output_aliases={5: 7},
         compiler_params=params(16 + 4 * own.size * 2 / MIB),
         cost_estimate=cost(1.2e9, 8 * MIB),
         name="layer",
-    )(outer_rows, live, own, other, outer, total, over, over_rows, features, cotangent, weights, turned)[:6]
-
-
-def outer_back_kernel(outer_rows, live, keep, got, came, keep_s, got_s, outer, scaled, base, payload):
+    )(outer_rows, live, own, other, outer, total, over, over_rows, features, cotangent, weights, turned)[:7]
+
+
+def weight_grads_kernel(smooth, grad_pre, both, layer_out, grads, sems):
+    pieces = sems.shape[0]
+    rows = smooth.shape[0] // pieces
+    copies = [
+        pltpu.make_async_copy(smooth.at[pl.ds(c * rows, rows)], layer_out.at[pl.ds(c * rows, rows)], sems.at[c])
+        for c in range(pieces)
+    ]
+    for copy in copies:
+        copy.start()
+    grown = lax.dot_general(both[...], grad_pre[...], ROWS_FIRST, preferred_element_type=F32)
+    grads[...] = (0.5 * grown).astype(BF16)
+    for copy in copies:
+        copy.wait()
+
+
+def weight_grads(smooth, grad_pre, both):
+    return pl.pallas_call(
+        weight_grads_kernel,
+        out_shape=(
+            jax.ShapeDtypeStruct(smooth.shape, BF16),
+            pltpu.VMEM((both.shape[1], grad_pre.shape[1]), BF16),
+        ),
+        in_specs=[WHOLE] * 3,
+        out_specs=(FAR, WHOLE),
+        scratch_shapes=[pltpu.SemaphoreType.DMA((4,))],
+        compiler_params=params(12),
+        cost_estimate=cost(2 * grad_pre.size * both.shape[1], 4 * MIB),
+        name="weight_grads",
+    )(smooth, grad_pre, both)
+
+
+def outer_back_kernel(
+    outer_rows, live, keep, got, came, keep_s, got_s, outer, scaled, base, payload_far, payload, sem
+):
     peers, slots, part, block = payload.shape
     near = (keep[1].astype(F32) + got[1].astype(F32) + came[...].astype(F32)).astype(BF16)
     scaled[...] = near
     base[...] = near.astype(F32) + keep_s[1].astype(F32) + got_s[1].astype(F32)
+    group = group_of(outer.shape[0], slots)
 
     def some(g, _):
         products = []
-        for k in range(GROUP):
-            n = g * GROUP + k
+        for k in range(group):
+            n = g * group + k
             products.append(dot(scaled[outer_rows[0, n]], outer[n]))
-        for k in range(GROUP):
-            n = g * GROUP + k
+        for k in range(group):
+            n = g * group + k
             alive = (n % slots < live[0, n // slots]).astype(F32)
-            payload[n // slots, n % slots] = (products[k] * alive).astype(BF16)
+            p = n // slots
+            payload[p, n % slots] = (products[k] * alive).astype(BF16)
+            if k % slots == slots - 1:
+                pltpu.make_async_copy(payload.at[p], payload_far.at[p], sem).start()
         return 0
 
-    lax.fori_loop(0, outer.shape[0] // GROUP, some, 0)
+    for_groups(outer.shape[0] // group, some)
+    pltpu.make_async_copy(payload, payload_far, sem).wait()
 
 
 def outer_back(outer_rows, live, keep, got, came, keep_s, got_s, outer, peers):
@@ -337,24 +376,41 @@
             jax.ShapeDtypeStruct((peers, count // peers, part, block), BF16),
         ),
         in_specs=[SCALARS, SCALARS] + [WHOLE] * 6,
-        out_specs=(WHOLE, WHOLE, WHOLE),
+        out_specs=(WHOLE, WHOLE, FAR),
+        scratch_shapes=[pltpu.VMEM((peers, count // peers, part, block), BF16), pltpu.SemaphoreType.DMA],
         compiler_params=params(8 + count * block * (block + part) * 2 / MIB),
         cost_estimate=cost(count * block * block * part * 2, 2 * MIB),
         name="outer_back",
     )(outer_rows, live, keep, got, came, keep_s, got_s, outer)
 
 
-def inner_back_kernel(rows, cols, scaled, base, inner_far, came, total, inner, sems):
-    groups = inner.shape[0] // GROUP
-    blocks = [
+def fetch_inner_kernel(inner_far, inner, sems):
+    copies = [
         pltpu.make_async_copy(inner_far.at[pl.ds(g * GROUP, GROUP)], inner.at[pl.ds(g * GROUP, GROUP)], sems.at[g])
-        for g in range(groups)
+        for g in range(sems.shape[0])
     ]
-    for copy in blocks:
+    for copy in copies:
         copy.start()
+    for copy in copies:
+        copy.wait()
+
+
+def fetch_inner(inner):
+    return pl.pallas_call(
+        fetch_inner_kernel,
+        out_shape=pltpu.VMEM(inner.shape, BF16),
+        in_specs=[FAR],
+        out_specs=WHOLE,
+        scratch_shapes=[pltpu.SemaphoreType.DMA((inner.shape[0] // GROUP,))],
+        compiler_params=params(4),
+        cost_estimate=cost(1e6, 2 * MIB),
+        name="fetch_inner",
+    )(*far(inner))
+
+
+def inner_back_kernel(rows, cols, scaled, base, inner, came, total):
     total[...] = base[...] + came[...].astype(F32)
-    for g in range(groups):
-        blocks[g].wait()
+    for g in range(inner.shape[0] // GROUP):
         products = [dot(scaled[rows[0, g * GROUP + k]], inner[g * GROUP + k]) for k in range(GROUP)]
         for k in range(GROUP):
             total[cols[0, g * GROUP + k]] += products[k]
@@ -365,13 +421,12 @@
     return pl.pallas_call(
         inner_back_kernel,
         out_shape=pltpu.VMEM(base.shape, F32),
-        in_specs=[SCALARS, SCALARS, WHOLE, WHOLE, FAR, WHOLE],
+        in_specs=[SCALARS, SCALARS, WHOLE, WHOLE, WHOLE, WHOLE],
         out_specs=WHOLE,
-        scratch_shapes=[pltpu.VMEM(inner.shape, BF16), pltpu.SemaphoreType.DMA((count // GROUP,))],
         compiler_params=params(8),
         cost_estimate=cost(count * block * block * scaled.shape[1] * 2, 3 * MIB),
         name="inner_back",
-    )(rows, cols, scaled, base, *far(inner), came)
+    )(rows, cols, scaled, base, inner, came)
 
 
 def add_returned_kernel(targets, returned, total, out, summed):
@@ -495,11 +550,16 @@
     own, total, outer_a = lax.optimization_barrier((own, total, outer_a))
     other = swap(own, "grp", 1)
     outer_a, features, cotangent, weights, turned = fetch(outer_a, features, cotangent, weight_self, weight_neigh)
-    layer_out, grads, send_n, keep_n, send_s, keep_s = layer(
+    smooth, grad_pre, both, send_n, keep_n, send_s, keep_s = layer(
         outer_rows, live, own, other, outer_a, total, over, over_rows, features, cotangent, weights, turned
     )
+    layer_out, grads = weight_grads(smooth, grad_pre, both)
     got_n = swap(send_n, "grp", 1)
-    came_n = swap((keep_n[0].astype(F32) + got_n[0].astype(F32)).astype(BF16), "grp", 2)
+    got_n, grads = lax.optimization_barrier((got_n, grads))
+    pass_n, inner_a = lax.optimization_barrier(
+        ((keep_n[0].astype(F32) + got_n[0].astype(F32)).astype(BF16), inner_a)
+    )
+    came_n, inner_a = lax.optimization_barrier((swap(pass_n, "grp", 2), fetch_inner(inner_a)))
     got_s = swap(send_s, "grp", 1)
     came_s = swap((keep_s[0].astype(F32) + got_s[0].astype(F32)).astype(BF16), "grp", 2)
     scaled, base, payload = outer_back(outer_rows, live, keep_n, got_n, came_n, keep_s, got_s, outer_a, peers)
@@ -510,12 +570,12 @@
         bit //= 2
     base, grads = lax.optimization_barrier((base, grads))
     partial = inner_back(rows, cols, scaled, base, inner_a, came_s)
-    grads = pair_sum(grads, swap(grads, "dom", 2))
+    grads = pair_sum(grads, swap(grads, "dom", 1))
     mine = add_returned(targets, returned, partial)
     across = swap(mine, "grp", 2)
     beside = swap(mine, "grp", 1)
     opposite = swap(across, "grp", 1)
-    feature_grad, self_grad, neigh_grad = finish(mine, across, beside, opposite, grads, swap(grads, "dom", 1))
+    feature_grad, self_grad, neigh_grad = finish(mine, across, beside, opposite, grads, swap(grads, "dom", 2))
     return layer_out, feature_grad, self_grad, neigh_grad
 
 

time: 56.1 us -> 53.3 us (0.950)
  waiting for transfers between devices: 17.1 us -> 15.5 us
  Pallas kernels: 18 us -> 17.1 us
    ppermute x11, waiting for transfers between devices: 10.2 us -> 8.01 us  [swap(): lax.ppermute(x, axis, [(i, i ^ bit) for i in range(lax.axis_size(axis))])]
    pallas_call x1, Pallas kernels: 2.54 us -> 0.66 us  [inner_back(): pl.pallas_call(inner_back_kernel, out_shape=pltpu.VMEM(base.shape, F32),...]
    pallas_call x2 -> x4, Pallas kernels: 4.52 us -> 5.85 us  [the longest x1 1.73 us: gather_halves(): pl.pallas_call(gather_kernel, out_shape=jax.ShapeDtypeStruct((peers, slot...]
    all_to_all x1, waiting for transfers between devices: 1.55 us -> 2.15 us  [shards(): lax.all_to_all(payload, 'dom', split_axis=0, concat_axis=0, tiled=True)]
  transfers between devices with their start and end apart: 13 -> 13, of which waited for: 7 -> 7; matrix products, arithmetic and copies ran while one was open for 0% -> 0% of each run, Pallas kernels for 22% -> 24%
where the time goes in v6:
time: 53.3 us; the launch traced here: 52.8 us
  starting transfers between devices  19.4 us (36%)
  Pallas kernels  17.1 us (32%)
  waiting for transfers between devices  15.5 us (29%)
  between operations  0.72 us (1%)
    ppermute x11, starting transfers between devices, swap(): lax.ppermute(x, axis, [(i, i ^ bit) for i in range(lax.axis_size(axis))])  8.48 us
    ppermute x11, waiting for transfers between devices, swap(): lax.ppermute(x, axis, [(i, i ^ bit) for i in range(lax.axis_size(axis))])  8.01 us
    all_to_all x1, starting transfers between devices, shards(): lax.all_to_all(outgoing, 'dom', split_axis=0, concat_axis=0, tiled=True)  7.26 us
    pallas_call x1, Pallas kernels, stage(): pl.pallas_call(stage_kernel, out_shape=tuple((pltpu.SMEM(x.shape, jnp.int...  6.33 us
    all_to_all x1, waiting for transfers between devices, shards(): lax.all_to_all(outgoing, 'dom', split_axis=0, concat_axis=0, tiled=True)  5.36 us
    all_to_all x1, starting transfers between devices, shards(): lax.all_to_all(payload, 'dom', split_axis=0, concat_axis=0, tiled=True)  3.64 us
    all_to_all x1, waiting for transfers between devices, shards(): lax.all_to_all(payload, 'dom', split_axis=0, concat_axis=0, tiled=True)  2.15 us
    pallas_call x1, Pallas kernels, fetch(): pl.pallas_call(fetch_kernel, out_shape=tuple((pltpu.VMEM(shape, BF16) for...  1.74 us
  transfers between devices with their start and end apart: 13, of which 7 were waited for; matrix products, arithmetic and copies ran while one was open for 0% of the time, Pallas kernels for 24%

profile of v6, /device:TPU:0, one launch (start us, length us, event | category | flops | bytes accessed | tf_op | source)
XLA Modules:
  0.0 52.8 jit_solution(12641280226928875776)
XLA Ops:
  0.6 1.7 %gather_halves.1 = bf16[8,3,64,128]{3,2,1,0:T(8,128)(2,1)} custom-call(s32[3,1,8]{2,1,0:T(1,128)} %bitcast.13, bf16[16,2,64,128]{3,2,1,0:T(8,128)(2,1)} %bitcast.10), custom_call_target="tpu_custom_call" | custom-call | tf_op jit(solution)/shard_map/gather_halves/pallas_call | solution.py:72
  2.4 7.3 %all-to-all-start = ((bf16[8,3,64,128]{3,2,1,0:T(8,128)(2,1)}), bf16[8,3,64,128]{3,2,1,0:T(8,128)(2,1)S(1)}, u32[]{:S(2)}, u32[]{:S(2)}) async-start(bf16[8,3,64,128]{3,2,1,0:T(8,128)(2,1)} %gather_halves.1), calls=%async_computation | async-start | bytes 786432 | tf_op jit(solution)/shard_map/all_to_all | solution.py:546
  9.6 6.3 %stage.1 = (s32[1,64]{1,0:T(1,128)S(4)}, s32[1,64]{1,0:T(1,128)S(4)}, s32[1,24]{1,0:T(1,128)S(4)}, s32[1,8]{1,0:T(1,128)S(4)}, s32[3,1,8]{2,1,0:T(1,128)S(4)}, /...) custom-call(s32[1,64]{1,0:T(1,128)} %rows_far.1, s32[1,64]{1,0:T(1,128)} %cols_far.1, ...), custom_call_target="tpu_custom_call" | custom-call | flops 536870912 | bytes 6291456 | tf_op jit(solution)/shard_map/stage/pallas_call | solution.py:165
  16.0 5.4 %all-to-all-done.own = bf16[8,3,64,128]{3,2,1,0:T(8,128)(2,1)S(1)} async-done(((bf16[8,3,64,128]{3,2,1,0:T(8,128)(2,1)}), bf16[8,3,64,128]{3,2,1,0:T(8,128)(2,1)S(1)}, u32[]{:S(2)}, u32[]{:S(2)}) %all-to-all-start) | async-done | bytes 393248 | tf_op jit(solution)/shard_map/all_to_all | solution.py:546
  21.3 1.7 %fetch.1 = (bf16[24,128,128]{2,1,0:T(8,128)(2,1)S(1)}, bf16[2048,128]{1,0:T(8,128)(2,1)S(1)}, bf16[2048,256]{1,0:T(8,128)(2,1)S(1)}, bf16[256,256]{1,0:T(8,128)(2,1)S(1)}, bf16[256,256]{1,0:T(8,128)(2,1)S(1)}) custom-call(bf16[24,128,128]{2,1,0:T(8,128)(2,1)} %bitcast.12, bf16[2048,128]{1,0:T(8,128)(2,1)} %feat_far.3, bf16[2048,256]{1,0:T(8,128)(2,1)} %cot_far.1, ...), custom_call_target="tpu_custom_call" | custom-call | flops 1000000 | bytes 3145728 | tf_op jit(solution)/shard_map/fetch/pallas_call | solution.py:214
  23.1 1.5 %layer.1 = (bf16[2048,256]{1,0:T(8,128)(2,1)S(1)}, bf16[2048,256]{1,0:T(8,128)(2,1)S(1)}, bf16[2048,256]{1,0:T(8,128)(2,1)S(1)}, bf16[2,16,32,128]{3,2,1,0:T(8,1...) custom-call(s32[1,24]{1,0:T(1,128)S(4)} %get-tuple-element.43.outer_, ...), custom_call_target="tpu_custom_call", output_to_operand_aliasing={{7}: (5, {})} | custom-call | flops 1200000000 | bytes 8388608 | tf_op jit(solution)/shard_map/layer/pallas_call | solution.py:292
  24.6 0.6 %collective-permute-start.1 = (bf16[2,16,32,128]{3,2,1,0:T(8,128)(2,1)S(1)}, bf16[2,16,32,128]{3,2,1,0:T(8,128)(2,1)S(1)}, u32[]{:S(2)}, u32[]{:S(2)}) collective-permute-start(bf16[2,16,32,128]{3,2,1,0:T(8,128)(2,1)S(1)} %get-tuple-element.62), channel_id=1, source_target_pairs={{0,1},{1,0},{2,3},{3,2},{4,5},{5,4},{6,7},{7,6},{8,9},{9,8},{10,11... | collective-permute-start | bytes 786440 | tf_op jit(solution)/shard_map/ppermute | solution.py:523
  25.3 1.0 %weight_grads.1 = (bf16[2048,256]{1,0:T(8,128)(2,1)}, bf16[256,256]{1,0:T(8,128)(2,1)S(1)}) custom-call(bf16[2048,256]{1,0:T(8,128)(2,1)S(1)} %get-tuple-element.56.smooth, bf16[2048,256]{1,0:T(8,128)(2,1)S(1)} %get-tuple-element.57.grad_pre, bf16[2048,256]{1,0:T(8,128)(2,1)S(1)} %get-tuple-element.58.both), custom_call_target="tpu_custom_call" | custom-call | flops 268435456 | bytes 4194304 | tf_op jit(solution)/shard_map/weight_grads/pallas_call | solution.py:326
  26.4 1.6 %collective-permute-start.2 = (bf16[16,32,128]{2,1,0:T(8,128)(2,1)S(1)}, bf16[16,32,128]{2,1,0:T(8,128)(2,1)S(1)}, u32[]{:S(2)}, u32[]{:S(2)}) collective-permute-start(bf16[16,32,128]{2,1,0:T(8,128)(2,1)S(1)} %fusion), channel_id=1, source_target_pairs={{0,2},{1,3},{2,0},{3,1},{4,6},{5,7},{6,4},{7,5},{8,10},{9,11},{10,... | collective-permute-start | bytes 393224 | tf_op jit(solution)/shard_map/ppermute | solution.py:523
  28.0 0.8 %collective-permute-start.4 = (bf16[256,256]{1,0:T(8,128)(2,1)S(1)}, bf16[256,256]{1,0:T(8,128)(2,1)S(1)}, u32[]{:S(2)}, u32[]{:S(2)}) collective-permute-start(bf16[256,256]{1,0:T(8,128)(2,1)S(1)} %get-tuple-element.75.a), channel_id=1, source_target_pairs={{0,16},{4,20},{8,24},{12,28},{16,0},{20,4},{24,8},{28,12},{1,17},{... | collective-permute-start | bytes 393224 | tf_op jit(solution)/shard_map/ppermute | solution.py:523
  28.8 1.6 %fetch_inner.1.inner = bf16[64,128,128]{2,1,0:T(8,128)(2,1)S(1)} custom-call(bf16[64,128,128]{2,1,0:T(8,128)(2,1)} %bitcast.9), custom_call_target="tpu_custom_call" | custom-call | flops 1000000 | bytes 2097152 | tf_op jit(solution)/shard_map/fetch_inner/pallas_call | solution.py:399
  30.4 1.9 %collective-permute-done.2.came = bf16[16,32,128]{2,1,0:T(8,128)(2,1)S(1)} collective-permute-done((bf16[16,32,128]{2,1,0:T(8,128)(2,1)S(1)}, bf16[16,32,128]{2,1,0:T(8,128)(2,1)S(1)}, u32[]{:S(2)}, u32[]{:S(2)}) %collective-permute-start.2) | collective-permute-done | bytes 131104 | tf_op jit(solution)/shard_map/ppermute | solution.py:523
  32.3 1.0 %outer_back.1 = (bf16[16,32,128]{2,1,0:T(8,128)(2,1)S(1)}, f32[16,32,128]{2,1,0:T(8,128)S(1)}, bf16[8,3,32,128]{3,2,1,0:T(8,128)(2,1)}) custom-call(s32[1,24]{1,0:T(1,128)S(4)} %get-tuple-element.43.outer_rows, s32[1,8]{1,0:T(1,128)S(4)} %get-tuple-element.44.live, bf16[2,16,32,128]{3,2,1,0:T(8,128)(2,1)S(1)} %get-tuple-element.61.keep, ...), custom_call_target="tpu_custom_call" | custom-call | flops 25165824 | bytes 2097152 | tf_op jit(solution)/shard_map/outer_back/pallas_call | solution.py:371
  33.3 3.6 %all-to-all-start.1 = ((bf16[8,3,32,128]{3,2,1,0:T(8,128)(2,1)}), bf16[8,3,32,128]{3,2,1,0:T(8,128)(2,1)S(1)}, u32[]{:S(2)}, u32[]{:S(2)}) async-start(bf16[8,3,32,128]{3,2,1,0:T(8,128)(2,1)} %get-tuple-element.70), calls=%async_computation.1 | async-start | bytes 393216 | tf_op jit(solution)/shard_map/all_to_all | solution.py:566
  37.0 1.6 %collective-permute-start.5 = (bf16[16,32,128]{2,1,0:T(8,128)(2,1)S(1)}, bf16[16,32,128]{2,1,0:T(8,128)(2,1)S(1)}, u32[]{:S(2)}, u32[]{:S(2)}) collective-permute-start(bf16[16,32,128]{2,1,0:T(8,128)(2,1)S(1)} %fusion.1), channel_id=1, source_target_pairs={{0,2},{1,3},{2,0},{3,1},{4,6},{5,7},{6,4},{7,5},{8,10},{9,11},{10,... | collective-permute-start | bytes 393224 | tf_op jit(solution)/shard_map/ppermute | solution.py:523
  38.6 2.1 %collective-permute-start.9 = (bf16[256,256]{1,0:T(8,128)(2,1)S(1)}, bf16[256,256]{1,0:T(8,128)(2,1)S(1)}, u32[]{:S(2)}, u32[]{:S(2)}) collective-permute-start(bf16[256,256]{1,0:T(8,128)(2,1)S(1)} %pair_sum.2.a), channel_id=1, source_target_pairs={{0,4},{4,0},{8,12},{12,8},{16,20},{20,16},{24,28},{28,24},{1,5},{5... | collective-permute-start | bytes 393224 | tf_op jit(solution)/shard_map/ppermute | solution.py:523
  40.7 1.3 %collective-permute-done.5.came = bf16[16,32,128]{2,1,0:T(8,128)(2,1)S(1)} collective-permute-done((bf16[16,32,128]{2,1,0:T(8,128)(2,1)S(1)}, bf16[16,32,128]{2,1,0:T(8,128)(2,1)S(1)}, u32[]{:S(2)}, u32[]{:S(2)}) %collective-permute-start.5) | collective-permute-done | bytes 131104 | tf_op jit(solution)/shard_map/ppermute | solution.py:523
  42.0 0.7 %inner_back.1.total = f32[16,32,128]{2,1,0:T(8,128)S(1)} custom-call(s32[1,64]{1,0:T(1,128)S(4)} %get-tuple-element.71.rows, s32[1,64]{1,0:T(1,128)S(4)} %get-tuple-element.72.cols, bf16[16,32,128]{2,1,0:T(8,128)(2,1)S(1)} %get-tuple-element.73.scaled, f32[16,32,128]{2,1,0:T(8,128)S(1)} %get-tuple-element.76.base, ...), custom_call_target="tpu_custom_call" | custom-call | flops 67108864 | bytes 3145728 | tf_op jit(solution)/shard_map/inner_back/pallas_call | solution.py:421
  42.7 2.2 %all-to-all-done.1.returned = bf16[8,3,32,128]{3,2,1,0:T(8,128)(2,1)S(1)} async-done(((bf16[8,3,32,128]{3,2,1,0:T(8,128)(2,1)}), bf16[8,3,32,128]{3,2,1,0:T(8,128)(2,1)S(1)}, u32[]{:S(2)}, u32[]{:S(2)}) %all-to-all-start.1) | async-done | bytes 196640 | tf_op jit(solution)/shard_map/all_to_all | solution.py:566
  45.0 1.5 %collective-permute-start.6 = (bf16[16,32,128]{2,1,0:T(8,128)(2,1)S(1)}, bf16[16,32,128]{2,1,0:T(8,128)(2,1)S(1)}, u32[]{:S(2)}, u32[]{:S(2)}) collective-permute-start(bf16[16,32,128]{2,1,0:T(8,128)(2,1)S(1)} %add_returned.1.mine), channel_id=1, source_target_pairs={{0,2},{1,3},{2,0},{3,1},{4,6},{5,7},{6,4},{7,5},{8,10},{9,11},{10,... | collective-permute-start | bytes 393224 | tf_op jit(solution)/shard_map/ppermute | solution.py:523
  46.5 0.3 collective-permute-start.10
  46.8 3.2 %collective-permute-done.6.across = bf16[16,32,128]{2,1,0:T(8,128)(2,1)S(1)} collective-permute-done((bf16[16,32,128]{2,1,0:T(8,128)(2,1)S(1)}, bf16[16,32,128]{2,1,0:T(8,128)(2,1)S(1)}, u32[]{:S(2)}, u32[]{:S(2)}) %collective-permute-start.6) | collective-permute-done | bytes 131104 | tf_op jit(solution)/shard_map/ppermute | solution.py:523
  50.0 1.5 %collective-permute-done.10.grads_came = bf16[256,256]{1,0:T(8,128)(2,1)S(1)} collective-permute-done((bf16[256,256]{1,0:T(8,128)(2,1)S(1)}, bf16[256,256]{1,0:T(8,128)(2,1)S(1)}, u32[]{:S(2)}, u32[]{:S(2)}) %collective-permute-start.10) | collective-permute-done | bytes 131104 | tf_op jit(solution)/shard_map/ppermute | solution.py:523
  51.5 1.3 %finish.1 = (f32[2048,128]{1,0:T(8,128)}, f32[128,256]{1,0:T(8,128)}, f32[128,256]{1,0:T(8,128)}) custom-call(bf16[16,32,128]{2,1,0:T(8,128)(2,1)S(1)} %add_returned.1.mine, bf16[16,32,128]{2,1,0:T(8,128)(2,1)S(1)} %collective-permute-done.6.across, bf16[16,32,128]{2,1,0:T(8,128)(2,1)S(1)} %collective-permute-done.7.beside, ...), custom_call_target="tpu_custom_call" | custom-call | flops 67108864 | bytes 2097152 | tf_op jit(solution)/shard_map/finish/pallas_call | solution.py:506
  (16 shorter events, 0.5 us)
Async XLA Ops:
  2.4 19.0 %all-to-all-start = ((bf16[8,3,64,128]{3,2,1,0:T(8,128)(2,1)}), bf16[8,3,64,128]{3,2,1,0:T(8,128)(2,1)S(1)}, u32[]{:S(2)}, u32[]{:S(2)}) async-start(bf16[8,3,64,128]{3,2,1,0:T(8,128)(2,1)} %gather_halves.1), calls=%async_computation | async-start | bytes 786432 | tf_op jit(solution)/shard_map/all_to_all | solution.py:546
  21.3 1.8 %collective-permute-start = (bf16[8,3,64,128]{3,2,1,0:T(8,128)(2,1)S(1)}, bf16[8,3,64,128]{3,2,1,0:T(8,128)(2,1)S(1)}, u32[]{:S(2)}, u32[]{:S(2)}) collective-permute-start(bf16[8,3,64,128]{3,2,1,0:T(8,128)(2,1)S(1)} %all-to-all-done.own), channel_id=1, source_target_pairs={{0,1},{1,0},{2,3},{3,2},{4,5},{5,4},{6,7},{7,6},{8,9},{9,8},{10,11... | collective-permute-start | bytes 1179656 | tf_op jit(solution)/shard_map/ppermute | solution.py:523
  24.6 1.7 %collective-permute-start.1 = (bf16[2,16,32,128]{3,2,1,0:T(8,128)(2,1)S(1)}, bf16[2,16,32,128]{3,2,1,0:T(8,128)(2,1)S(1)}, u32[]{:S(2)}, u32[]{:S(2)}) collective-permute-start(bf16[2,16,32,128]{3,2,1,0:T(8,128)(2,1)S(1)} %get-tuple-element.62), channel_id=1, source_target_pairs={{0,1},{1,0},{2,3},{3,2},{4,5},{5,4},{6,7},{7,6},{8,9},{9,8},{10,11... | collective-permute-start | bytes 786440 | tf_op jit(solution)/shard_map/ppermute | solution.py:523
  25.2 7.1 %collective-permute-start.3 = (bf16[2,16,32,128]{3,2,1,0:T(8,128)(2,1)S(1)}, bf16[2,16,32,128]{3,2,1,0:T(8,128)(2,1)S(1)}, u32[]{:S(2)}, u32[]{:S(2)}) collective-permute-start(bf16[2,16,32,128]{3,2,1,0:T(8,128)(2,1)S(1)} %get-tuple-element.69), channel_id=1, source_target_pairs={{0,1},{1,0},{2,3},{3,2},{4,5},{5,4},{6,7},{7,6},{8,9},{9,8},{10,11... | collective-permute-start | bytes 786440 | tf_op jit(solution)/shard_map/ppermute | solution.py:523
  26.4 5.9 %collective-permute-start.2 = (bf16[16,32,128]{2,1,0:T(8,128)(2,1)S(1)}, bf16[16,32,128]{2,1,0:T(8,128)(2,1)S(1)}, u32[]{:S(2)}, u32[]{:S(2)}) collective-permute-start(bf16[16,32,128]{2,1,0:T(8,128)(2,1)S(1)} %fusion), channel_id=1, source_target_pairs={{0,2},{1,3},{2,0},{3,1},{4,6},{5,7},{6,4},{7,5},{8,10},{9,11},{10,... | collective-permute-start | bytes 393224 | tf_op jit(solution)/shard_map/ppermute | solution.py:523
  28.0 10.5 %collective-permute-start.4 = (bf16[256,256]{1,0:T(8,128)(2,1)S(1)}, bf16[256,256]{1,0:T(8,128)(2,1)S(1)}, u32[]{:S(2)}, u32[]{:S(2)}) collective-permute-start(bf16[256,256]{1,0:T(8,128)(2,1)S(1)} %get-tuple-element.75.a), channel_id=1, source_target_pairs={{0,16},{4,20},{8,24},{12,28},{16,0},{20,4},{24,8},{28,12},{1,17},{... | collective-permute-start | bytes 393224 | tf_op jit(solution)/shard_map/ppermute | solution.py:523
  33.3 11.5 %all-to-all-start.1 = ((bf16[8,3,32,128]{3,2,1,0:T(8,128)(2,1)}), bf16[8,3,32,128]{3,2,1,0:T(8,128)(2,1)S(1)}, u32[]{:S(2)}, u32[]{:S(2)}) async-start(bf16[8,3,32,128]{3,2,1,0:T(8,128)(2,1)} %get-tuple-element.70), calls=%async_computation.1 | async-start | bytes 393216 | tf_op jit(solution)/shard_map/all_to_all | solution.py:566
  37.0 5.0 %collective-permute-start.5 = (bf16[16,32,128]{2,1,0:T(8,128)(2,1)S(1)}, bf16[16,32,128]{2,1,0:T(8,128)(2,1)S(1)}, u32[]{:S(2)}, u32[]{:S(2)}) collective-permute-start(bf16[16,32,128]{2,1,0:T(8,128)(2,1)S(1)} %fusion.1), channel_id=1, source_target_pairs={{0,2},{1,3},{2,0},{3,1},{4,6},{5,7},{6,4},{7,5},{8,10},{9,11},{10,... | collective-permute-start | bytes 393224 | tf_op jit(solution)/shard_map/ppermute | solution.py:523
  38.6 7.9 %collective-permute-start.9 = (bf16[256,256]{1,0:T(8,128)(2,1)S(1)}, bf16[256,256]{1,0:T(8,128)(2,1)S(1)}, u32[]{:S(2)}, u32[]{:S(2)}) collective-permute-start(bf16[256,256]{1,0:T(8,128)(2,1)S(1)} %pair_sum.2.a), channel_id=1, source_target_pairs={{0,4},{4,0},{8,12},{12,8},{16,20},{20,16},{24,28},{28,24},{1,5},{5... | collective-permute-start | bytes 393224 | tf_op jit(solution)/shard_map/ppermute | solution.py:523
  45.0 5.0 %collective-permute-start.6 = (bf16[16,32,128]{2,1,0:T(8,128)(2,1)S(1)}, bf16[16,32,128]{2,1,0:T(8,128)(2,1)S(1)}, u32[]{:S(2)}, u32[]{:S(2)}) collective-permute-start(bf16[16,32,128]{2,1,0:T(8,128)(2,1)S(1)} %add_returned.1.mine), channel_id=1, source_target_pairs={{0,2},{1,3},{2,0},{3,1},{4,6},{5,7},{6,4},{7,5},{8,10},{9,11},{10,... | collective-permute-start | bytes 393224 | tf_op jit(solution)/shard_map/ppermute | solution.py:523
  46.5 5.0 %collective-permute-start.10 = (bf16[256,256]{1,0:T(8,128)(2,1)S(1)}, bf16[256,256]{1,0:T(8,128)(2,1)S(1)}, u32[]{:S(2)}, u32[]{:S(2)}) collective-permute-start(bf16[256,256]{1,0:T(8,128)(2,1)S(1)} %pair_sum.3.grads), channel_id=1, source_target_pairs={{0,8},{4,12},{8,0},{12,4},{16,24},{20,28},{24,16},{28,20},{1,9},{5... | collective-permute-start | bytes 393224 | tf_op jit(solution)/shard_map/ppermute | solution.py:523
  46.7 4.8 %collective-permute-start.7 = (bf16[16,32,128]{2,1,0:T(8,128)(2,1)S(1)}, bf16[16,32,128]{2,1,0:T(8,128)(2,1)S(1)}, u32[]{:S(2)}, u32[]{:S(2)}) collective-permute-start(bf16[16,32,128]{2,1,0:T(8,128)(2,1)S(1)} %add_returned.1.mine), channel_id=1, source_target_pairs={{0,1},{1,0},{2,3},{3,2},{4,5},{5,4},{6,7},{7,6},{8,9},{9,8},{10,11... | collective-permute-start | bytes 393224 | tf_op jit(solution)/shard_map/ppermute | solution.py:523
  50.0 1.5 %collective-permute-start.8 = (bf16[16,32,128]{2,1,0:T(8,128)(2,1)S(1)}, bf16[16,32,128]{2,1,0:T(8,128)(2,1)S(1)}, u32[]{:S(2)}, u32[]{:S(2)}) collective-permute-start(bf16[16,32,128]{2,1,0:T(8,128)(2,1)S(1)} %collective-permute-done.6.across), channel_id=1, source_target_pairs={{0,1},{1,0},{2,3},{3,2},{4,5},{5,4},{6,7},{7,6},{8,9},{9,8},{10,11... | collective-permute-start | bytes 393224 | tf_op jit(solution)/shard_map/ppermute | solution.py:523

commit v7 on v6

--- a/solution.py
+++ b/solution.py
@@ -26,15 +26,33 @@
     return [pltpu.with_memory_space_constraint(x, pltpu.HBM) for x in arrays]
 
 
-def group_of(count, slots):
-    return slots * max(k for k in range(1, 9) if count // slots % k == 0)
-
-
-def for_groups(count, body):
-    if count == 1:
-        body(0, 0)
+OUT_ORDER = (5, 7, 1, 4, 6, 3, 0, 2)
+BACK_ORDER = (5, 7, 1, 4, 6, 3, 0, 2)
+
+
+def order_of(order, peers):
+    return order if len(order) == peers else tuple((j + peers // 2) % peers for j in range(peers))
+
+
+def peer_at(order, j):
+    return order[j] if isinstance(j, int) else lax.rem(j + len(order) // 2, len(order))
+
+
+def exchange(x, order):
+    return lax.all_to_all(x, "dom", split_axis=0, concat_axis=0, tiled=True, axis_index_groups=[list(order)])
+
+
+def for_places(peers, body):
+    together = max(k for k in range(1, 9) if peers % k == 0)
+    if together == peers:
+        body(range(peers))
     else:
-        lax.fori_loop(0, count, body, 0)
+
+        def some(g, _):
+            body([g * together + k for k in range(together)])
+            return 0
+
+        lax.fori_loop(0, peers // together, some, 0)
 
 
 def params(mib):
@@ -45,7 +63,7 @@
     return pl.CostEstimate(flops=int(flops), bytes_accessed=int(moved), transcendentals=0)
 
 
-def gather_kernel(targets_far, feat_far, out, targets, feat, outgoing, sems, out_sem):
+def gather_kernel(order, targets_far, feat_far, out, targets, feat, outgoing, sems, out_sem):
     pieces = sems.shape[0] - 1
     step = feat.shape[0] // pieces
     mine = lax.axis_index("grp") % 2
@@ -57,20 +75,20 @@
         fetch.start()
     for fetch in fetches:
         fetch.wait()
-    slots, _, peers = targets.shape
-    for p in range(peers):
+    slots = targets.shape[0]
+    for j, p in enumerate(order):
         for s in range(slots):
-            outgoing[p, s] = feat[targets[s, 0, p], 0]
-        pltpu.make_async_copy(outgoing.at[p], out.at[p], out_sem).start()
+            outgoing[j, s] = feat[targets[s, 0, p], 0]
+        pltpu.make_async_copy(outgoing.at[j], out.at[j], out_sem).start()
     pltpu.make_async_copy(outgoing, out, out_sem).wait()
 
 
-def gather_halves(features, targets, block):
+def gather_halves(features, targets, block, order):
     nodes, feat_width = features.shape
     loc, half = nodes // block, block // 2
     slots, _, peers = targets.shape
     return pl.pallas_call(
-        gather_kernel,
+        functools.partial(gather_kernel, order),
         out_shape=jax.ShapeDtypeStruct((peers, slots, half, feat_width), BF16),
         in_specs=[FAR, FAR],
         out_specs=FAR,
@@ -228,7 +246,7 @@
 
 
 def layer_kernel(
-    chunk_blocks,
+    chunk_blocks, order,
     outer_rows, live, own, other, outer, total_in, over_all, over_rows, feat, cot, weights, turned,
     smooth, grad_pre_all, both_all, send_n, keep_n, send_s, keep_s, total,
 ):
@@ -240,22 +258,19 @@
     rows = chunk_blocks * block
     part = feat_width // lax.axis_size("grp")
     mine = lax.axis_index("grp") % 2
-    group = group_of(count, slots)
-
-    def some(g, _):
+
+    def some(places):
+        blocks = [(j, k, peer_at(order, j) * slots + k) for j in places for k in range(slots)]
         products = []
-        for k in range(group):
-            n = g * group + k
-            near, away = own[n // slots, n % slots], other[n // slots, n % slots]
+        for j, k, n in blocks:
+            near, away = own[j, k], other[j, k]
             x = jnp.concatenate([jnp.where(mine == 0, near, away), jnp.where(mine == 0, away, near)], axis=0)
             products.append(dot(outer[n], x))
-        for k in range(group):
-            n = g * group + k
-            alive = (n % slots < live[0, n // slots]).astype(F32)
-            total[outer_rows[0, n]] += products[k] * alive
-        return 0
-
-    for_groups(count // group, some)
+        for (j, k, n), product in zip(blocks, products):
+            alive = (k < live[0, peer_at(order, j)]).astype(F32)
+            total[outer_rows[0, n]] += product * alive
+
+    for_places(peers, some)
     for c in range(chunks):
         place = pl.ds(c * rows, rows)
         here = pl.ds(c * chunk_blocks, chunk_blocks)
@@ -283,14 +298,14 @@
                 keep_s[y, at] = self_t[(2 + y) * part : (3 + y) * part]
 
 
-def layer(outer_rows, live, own, other, outer, total, over, over_rows, features, cotangent, weights, turned):
+def layer(outer_rows, live, own, other, outer, total, over, over_rows, features, cotangent, weights, turned, order):
     feat_width = features.shape[1]
     loc, block, _ = total.shape
     chunk = 4
     part = feat_width // lax.axis_size("grp")
     piece = pltpu.VMEM((2, loc, part, block), BF16)
     return pl.pallas_call(
-        functools.partial(layer_kernel, chunk),
+        functools.partial(layer_kernel, chunk, order),
         out_shape=(
             pltpu.VMEM(cotangent.shape, BF16),
             pltpu.VMEM(cotangent.shape, BF16),
@@ -339,37 +354,31 @@
 
 
 def outer_back_kernel(
-    outer_rows, live, keep, got, came, keep_s, got_s, outer, scaled, base, payload_far, payload, sem
+    order, outer_rows, live, keep, got, came, keep_s, got_s, outer, scaled, base, payload_far, payload, sem
 ):
     peers, slots, part, block = payload.shape
     near = (keep[1].astype(F32) + got[1].astype(F32) + came[...].astype(F32)).astype(BF16)
     scaled[...] = near
     base[...] = near.astype(F32) + keep_s[1].astype(F32) + got_s[1].astype(F32)
-    group = group_of(outer.shape[0], slots)
-
-    def some(g, _):
-        products = []
-        for k in range(group):
-            n = g * group + k
-            products.append(dot(scaled[outer_rows[0, n]], outer[n]))
-        for k in range(group):
-            n = g * group + k
-            alive = (n % slots < live[0, n // slots]).astype(F32)
-            p = n // slots
-            payload[p, n % slots] = (products[k] * alive).astype(BF16)
-            if k % slots == slots - 1:
-                pltpu.make_async_copy(payload.at[p], payload_far.at[p], sem).start()
-        return 0
-
-    for_groups(outer.shape[0] // group, some)
+
+    def some(places):
+        blocks = [(j, k, peer_at(order, j) * slots + k) for j in places for k in range(slots)]
+        products = [dot(scaled[outer_rows[0, n]], outer[n]) for _, _, n in blocks]
+        for (j, k, n), product in zip(blocks, products):
+            alive = (k < live[0, peer_at(order, j)]).astype(F32)
+            payload[j, k] = (product * alive).astype(BF16)
+            if k == slots - 1:
+                pltpu.make_async_copy(payload.at[j], payload_far.at[j], sem).start()
+
+    for_places(peers, some)
     pltpu.make_async_copy(payload, payload_far, sem).wait()
 
 
-def outer_back(outer_rows, live, keep, got, came, keep_s, got_s, outer, peers):
+def outer_back(outer_rows, live, keep, got, came, keep_s, got_s, outer, order):
     loc, part, block = came.shape
-    count = outer.shape[0]
-    return pl.pallas_call(
-        outer_back_kernel,
+    count, peers = outer.shape[0], len(order)
+    return pl.pallas_call(
+        functools.partial(outer_back_kernel, order),
         out_shape=(
             pltpu.VMEM((loc, part, block), BF16),
             pltpu.VMEM((loc, part, block), F32),
@@ -384,67 +393,68 @@
     )(outer_rows, live, keep, got, came, keep_s, got_s, outer)
 
 
-def fetch_inner_kernel(inner_far, inner, sems):
-    copies = [
+def inner_back_kernel(rows, cols, scaled, base, inner_far, total, inner, sems):
+    groups = inner.shape[0] // GROUP
+    blocks = [
         pltpu.make_async_copy(inner_far.at[pl.ds(g * GROUP, GROUP)], inner.at[pl.ds(g * GROUP, GROUP)], sems.at[g])
-        for g in range(sems.shape[0])
+        for g in range(groups)
     ]
-    for copy in copies:
+    for copy in blocks:
         copy.start()
-    for copy in copies:
-        copy.wait()
-
-
-def fetch_inner(inner):
-    return pl.pallas_call(
-        fetch_inner_kernel,
-        out_shape=pltpu.VMEM(inner.shape, BF16),
-        in_specs=[FAR],
-        out_specs=WHOLE,
-        scratch_shapes=[pltpu.SemaphoreType.DMA((inner.shape[0] // GROUP,))],
-        compiler_params=params(4),
-        cost_estimate=cost(1e6, 2 * MIB),
-        name="fetch_inner",
-    )(*far(inner))
-
-
-def inner_back_kernel(rows, cols, scaled, base, inner, came, total):
-    total[...] = base[...] + came[...].astype(F32)
-    for g in range(inner.shape[0] // GROUP):
+    total[...] = base[...]
+    for g in range(groups):
+        blocks[g].wait()
         products = [dot(scaled[rows[0, g * GROUP + k]], inner[g * GROUP + k]) for k in range(GROUP)]
         for k in range(GROUP):
             total[cols[0, g * GROUP + k]] += products[k]
 
 
-def inner_back(rows, cols, scaled, base, inner, came):
+def inner_back(rows, cols, scaled, base, inner):
     count, block, _ = inner.shape
     return pl.pallas_call(
         inner_back_kernel,
         out_shape=pltpu.VMEM(base.shape, F32),
-        in_specs=[SCALARS, SCALARS, WHOLE, WHOLE, WHOLE, WHOLE],
+        in_specs=[SCALARS, SCALARS, WHOLE, WHOLE, FAR],
         out_specs=WHOLE,
+        scratch_shapes=[pltpu.VMEM(inner.shape, BF16), pltpu.SemaphoreType.DMA((count // GROUP,))],
         compiler_params=params(8),
         cost_estimate=cost(count * block * block * scaled.shape[1] * 2, 3 * MIB),
         name="inner_back",
-    )(rows, cols, scaled, base, inner, came)
-
-
-def add_returned_kernel(targets, returned, total, out, summed):
+    )(rows, cols, scaled, base, *far(inner))
+
+
+def add_came_kernel(total, came, out):
+    out[...] = total[...] + came[...].astype(F32)
+
+
+def add_came(total, came):
+    return pl.pallas_call(
+        add_came_kernel,
+        out_shape=pltpu.VMEM(total.shape, F32),
+        in_specs=[WHOLE, WHOLE],
+        out_specs=WHOLE,
+        compiler_params=params(4),
+        cost_estimate=cost(total.size, total.size * 10),
+        name="add_came",
+    )(total, came)
+
+
+def add_returned_kernel(order, targets, returned, total, out, summed):
     peers, slots, _, _ = returned.shape
     summed[...] = total[...]
 
-    def some(q, _):
-        for s in range(slots):
-            summed[targets[s, 0, q]] += returned[q, s].astype(F32)
-        return 0
-
-    lax.fori_loop(0, peers, some, 0)
+    def some(places):
+        for j in places:
+            for k in range(slots):
+                summed[targets[k, 0, peer_at(order, j)]] += returned[j, k].astype(F32)
+
+    for_places(peers, some)
     out[...] = summed[...].astype(BF16)
 
 
-def add_returned(targets, returned, total):
-    return pl.pallas_call(
-        add_returned_kernel,
+def add_returned(targets, returned, total, order):
+    return pl.pallas_call(
+        functools.partial(add_returned_kernel, order),
         out_shape=pltpu.VMEM(total.shape, BF16),
         in_specs=[SCALARS, WHOLE, WHOLE],
         out_specs=WHOLE,
@@ -542,8 +552,8 @@
     targets = send_blocks.transpose(2, 0, 1)
     block = inner_a.shape[-1]
 
-    outgoing = gather_halves(features, targets, block)
-    own = lax.all_to_all(outgoing, "dom", split_axis=0, concat_axis=0, tiled=True)
+    out_order, back_order = order_of(OUT_ORDER, peers), order_of(BACK_ORDER, peers)
+    own = exchange(gather_halves(features, targets, block, out_order), out_order)
     rows, cols, outer_rows, live, targets, total, over, over_rows = stage(
         inner_rows, inner_cols, outer_rows, live_count, targets, features, inner_a, outer_a
     )
@@ -551,27 +561,24 @@
     other = swap(own, "grp", 1)
     outer_a, features, cotangent, weights, turned = fetch(outer_a, features, cotangent, weight_self, weight_neigh)
     smooth, grad_pre, both, send_n, keep_n, send_s, keep_s = layer(
-        outer_rows, live, own, other, outer_a, total, over, over_rows, features, cotangent, weights, turned
+        outer_rows, live, own, other, outer_a, total, over, over_rows, features, cotangent, weights, turned, out_order
     )
     layer_out, grads = weight_grads(smooth, grad_pre, both)
     got_n = swap(send_n, "grp", 1)
     got_n, grads = lax.optimization_barrier((got_n, grads))
-    pass_n, inner_a = lax.optimization_barrier(
-        ((keep_n[0].astype(F32) + got_n[0].astype(F32)).astype(BF16), inner_a)
-    )
-    came_n, inner_a = lax.optimization_barrier((swap(pass_n, "grp", 2), fetch_inner(inner_a)))
+    came_n = swap((keep_n[0].astype(F32) + got_n[0].astype(F32)).astype(BF16), "grp", 2)
     got_s = swap(send_s, "grp", 1)
     came_s = swap((keep_s[0].astype(F32) + got_s[0].astype(F32)).astype(BF16), "grp", 2)
-    scaled, base, payload = outer_back(outer_rows, live, keep_n, got_n, came_n, keep_s, got_s, outer_a, peers)
-    returned = lax.all_to_all(payload, "dom", split_axis=0, concat_axis=0, tiled=True)
+    scaled, base, payload = outer_back(outer_rows, live, keep_n, got_n, came_n, keep_s, got_s, outer_a, back_order)
+    returned = exchange(payload, back_order)
     bit = peers // 2
     while bit > 2:
         grads = pair_sum(grads, swap(grads, "dom", bit))
         bit //= 2
     base, grads = lax.optimization_barrier((base, grads))
-    partial = inner_back(rows, cols, scaled, base, inner_a, came_s)
+    partial = add_came(inner_back(rows, cols, scaled, base, inner_a), came_s)
     grads = pair_sum(grads, swap(grads, "dom", 1))
-    mine = add_returned(targets, returned, partial)
+    mine = add_returned(targets, returned, partial, back_order)
     across = swap(mine, "grp", 2)
     beside = swap(mine, "grp", 1)
     opposite = swap(across, "grp", 1)

time: 53.3 us -> 51.2 us (0.961)
  waiting for transfers between devices: 15.5 us -> 8.51 us
  starting transfers between devices: 19.4 us -> 24 us
    all_to_all x2, waiting for transfers between devices: 7.51 us -> 2.2 us  [exchange(): lax.all_to_all(x, 'dom', split_axis=0, concat_axis=0, tiled=True, axis_in...]
    all_to_all x2, starting transfers between devices: 10.9 us -> 14.7 us  [exchange(): lax.all_to_all(x, 'dom', split_axis=0, concat_axis=0, tiled=True, axis_in...]
    pallas_call x1, Pallas kernels: 0.66 us -> 2.53 us  [inner_back(): pl.pallas_call(inner_back_kernel, out_shape=pltpu.VMEM(base.shape, F32),...]
    ppermute x11, waiting for transfers between devices: 8.01 us -> 6.31 us  [swap(): lax.ppermute(x, axis, [(i, i ^ bit) for i in range(lax.axis_size(axis))])]
    pallas_call x5, Pallas kernels: 6 us -> 4.45 us  [the longest x1 1.73 us: gather_halves(): pl.pallas_call(functools.partial(gather_kernel, order), out_shape=jax.Sha...]
    ppermute x11, starting transfers between devices: 8.48 us -> 9.33 us  [swap(): lax.ppermute(x, axis, [(i, i ^ bit) for i in range(lax.axis_size(axis))])]
  transfers between devices with their start and end apart: 13 -> 13, of which waited for: 7 -> 6; matrix products, arithmetic and copies ran while one was open for 0% -> 0% of each run, Pallas kernels for 24% -> 25%
where the time goes in v7:
time: 51.2 us; the launch traced here: 50.8 us
  starting transfers between devices  24 us (47%)
  Pallas kernels  17.4 us (34%)
  waiting for transfers between devices  8.51 us (17%)
  between operations  0.73 us (1%)
    all_to_all x2, starting transfers between devices, exchange(): lax.all_to_all(x, 'dom', split_axis=0, concat_axis=0, tiled=True, axis_in...  14.7 us
    ppermute x11, starting transfers between devices, swap(): lax.ppermute(x, axis, [(i, i ^ bit) for i in range(lax.axis_size(axis))])  9.33 us
    pallas_call x1, Pallas kernels, stage(): pl.pallas_call(stage_kernel, out_shape=tuple((pltpu.SMEM(x.shape, jnp.int...  6.32 us
    ppermute x11, waiting for transfers between devices, swap(): lax.ppermute(x, axis, [(i, i ^ bit) for i in range(lax.axis_size(axis))])  6.31 us
    pallas_call x1, Pallas kernels, inner_back(): pl.pallas_call(inner_back_kernel, out_shape=pltpu.VMEM(base.shape, F32),...  2.53 us
    all_to_all x2, waiting for transfers between devices, exchange(): lax.all_to_all(x, 'dom', split_axis=0, concat_axis=0, tiled=True, axis_in...  2.2 us
    pallas_call x1, Pallas kernels, fetch(): pl.pallas_call(fetch_kernel, out_shape=tuple((pltpu.VMEM(shape, BF16) for...  1.74 us
    pallas_call x1, Pallas kernels, gather_halves(): pl.pallas_call(functools.partial(gather_kernel, order), out_shape=jax.Sha...  1.73 us
  transfers between devices with their start and end apart: 13, of which 6 were waited for; matrix products, arithmetic and copies ran while one was open for 0% of the time, Pallas kernels for 25%

profile of v7, /device:TPU:0, one launch (start us, length us, event | category | flops | bytes accessed | tf_op | source)
XLA Modules:
  0.0 50.8 jit_solution(13977259702707064483)
XLA Ops:
  0.6 1.7 %gather_halves.1 = bf16[8,3,64,128]{3,2,1,0:T(8,128)(2,1)} custom-call(s32[3,1,8]{2,1,0:T(1,128)} %bitcast.13, bf16[16,2,64,128]{3,2,1,0:T(8,128)(2,1)} %bitcast.10), custom_call_target="tpu_custom_call" | custom-call | tf_op jit(solution)/shard_map/gather_halves/pallas_call | solution.py:90
  2.4 8.4 %all-to-all-start = ((bf16[8,3,64,128]{3,2,1,0:T(8,128)(2,1)}), bf16[8,3,64,128]{3,2,1,0:T(8,128)(2,1)S(1)}, u32[]{:S(2)}, u32[]{:S(2)}) async-start(bf16[8,3,64,128]{3,2,1,0:T(8,128)(2,1)} %gather_halves.1), calls=%async_computation | async-start | bytes 786432 | tf_op jit(solution)/shard_map/all_to_all | solution.py:42
  10.7 6.3 %stage.1 = (s32[1,64]{1,0:T(1,128)S(4)}, s32[1,64]{1,0:T(1,128)S(4)}, s32[1,24]{1,0:T(1,128)S(4)}, s32[1,8]{1,0:T(1,128)S(4)}, s32[3,1,8]{2,1,0:T(1,128)S(4)}, /...) custom-call(s32[1,64]{1,0:T(1,128)} %rows_far.1, s32[1,64]{1,0:T(1,128)} %cols_far.1, ...), custom_call_target="tpu_custom_call" | custom-call | flops 536870912 | bytes 6291456 | tf_op jit(solution)/shard_map/stage/pallas_call | solution.py:183
  17.1 2.2 %all-to-all-done.own = bf16[8,3,64,128]{3,2,1,0:T(8,128)(2,1)S(1)} async-done(((bf16[8,3,64,128]{3,2,1,0:T(8,128)(2,1)}), bf16[8,3,64,128]{3,2,1,0:T(8,128)(2,1)S(1)}, u32[]{:S(2)}, u32[]{:S(2)}) %all-to-all-start) | async-done | bytes 393248 | tf_op jit(solution)/shard_map/all_to_all | solution.py:42
  19.3 1.7 %fetch.1 = (bf16[24,128,128]{2,1,0:T(8,128)(2,1)S(1)}, bf16[2048,128]{1,0:T(8,128)(2,1)S(1)}, bf16[2048,256]{1,0:T(8,128)(2,1)S(1)}, bf16[256,256]{1,0:T(8,128)(2,1)S(1)}, bf16[256,256]{1,0:T(8,128)(2,1)S(1)}) custom-call(bf16[24,128,128]{2,1,0:T(8,128)(2,1)} %bitcast.12, bf16[2048,128]{1,0:T(8,128)(2,1)} %feat_far.3, bf16[2048,256]{1,0:T(8,128)(2,1)} %cot_far.1, ...), custom_call_target="tpu_custom_call" | custom-call | flops 1000000 | bytes 3145728 | tf_op jit(solution)/shard_map/fetch/pallas_call | solution.py:232
  21.0 1.5 %layer.1 = (bf16[2048,256]{1,0:T(8,128)(2,1)S(1)}, bf16[2048,256]{1,0:T(8,128)(2,1)S(1)}, bf16[2048,256]{1,0:T(8,128)(2,1)S(1)}, bf16[2,16,32,128]{3,2,1,0:T(8,1...) custom-call(s32[1,24]{1,0:T(1,128)S(4)} %get-tuple-element.39.outer_, ...), custom_call_target="tpu_custom_call", output_to_operand_aliasing={{7}: (5, {})} | custom-call | flops 1200000000 | bytes 8388608 | tf_op jit(solution)/shard_map/layer/pallas_call | solution.py:307
  22.6 0.6 %collective-permute-start.1 = (bf16[2,16,32,128]{3,2,1,0:T(8,128)(2,1)S(1)}, bf16[2,16,32,128]{3,2,1,0:T(8,128)(2,1)S(1)}, u32[]{:S(2)}, u32[]{:S(2)}) collective-permute-start(bf16[2,16,32,128]{3,2,1,0:T(8,128)(2,1)S(1)} %get-tuple-element.58), channel_id=1, source_target_pairs={{0,1},{1,0},{2,3},{3,2},{4,5},{5,4},{6,7},{7,6},{8,9},{9,8},{10,11... | collective-permute-start | bytes 786440 | tf_op jit(solution)/shard_map/ppermute | solution.py:533
  23.1 0.1 collective-permute-start.3
  23.2 1.0 %weight_grads.1 = (bf16[2048,256]{1,0:T(8,128)(2,1)}, bf16[256,256]{1,0:T(8,128)(2,1)S(1)}) custom-call(bf16[2048,256]{1,0:T(8,128)(2,1)S(1)} %get-tuple-element.52.smooth, bf16[2048,256]{1,0:T(8,128)(2,1)S(1)} %get-tuple-element.53.grad_pre, bf16[2048,256]{1,0:T(8,128)(2,1)S(1)} %get-tuple-element.54.both), custom_call_target="tpu_custom_call" | custom-call | flops 268435456 | bytes 4194304 | tf_op jit(solution)/shard_map/weight_grads/pallas_call | solution.py:341
  24.3 1.6 %collective-permute-start.2 = (bf16[16,32,128]{2,1,0:T(8,128)(2,1)S(1)}, bf16[16,32,128]{2,1,0:T(8,128)(2,1)S(1)}, u32[]{:S(2)}, u32[]{:S(2)}) collective-permute-start(bf16[16,32,128]{2,1,0:T(8,128)(2,1)S(1)} %fusion), channel_id=1, source_target_pairs={{0,2},{1,3},{2,0},{3,1},{4,6},{5,7},{6,4},{7,5},{8,10},{9,11},{10,... | collective-permute-start | bytes 393224 | tf_op jit(solution)/shard_map/ppermute | solution.py:533
  25.9 2.6 %collective-permute-start.4 = (bf16[256,256]{1,0:T(8,128)(2,1)S(1)}, bf16[256,256]{1,0:T(8,128)(2,1)S(1)}, u32[]{:S(2)}, u32[]{:S(2)}) collective-permute-start(bf16[256,256]{1,0:T(8,128)(2,1)S(1)} %get-tuple-element.68.a), channel_id=1, source_target_pairs={{0,16},{4,20},{8,24},{12,28},{16,0},{20,4},{24,8},{28,12},{1,17},{... | collective-permute-start | bytes 393224 | tf_op jit(solution)/shard_map/ppermute | solution.py:533
  28.5 1.7 %collective-permute-done.2.came = bf16[16,32,128]{2,1,0:T(8,128)(2,1)S(1)} collective-permute-done((bf16[16,32,128]{2,1,0:T(8,128)(2,1)S(1)}, bf16[16,32,128]{2,1,0:T(8,128)(2,1)S(1)}, u32[]{:S(2)}, u32[]{:S(2)}) %collective-permute-start.2) | collective-permute-done | bytes 131104 | tf_op jit(solution)/shard_map/ppermute | solution.py:533
  30.2 1.0 %outer_back.1 = (bf16[16,32,128]{2,1,0:T(8,128)(2,1)S(1)}, f32[16,32,128]{2,1,0:T(8,128)S(1)}, bf16[8,3,32,128]{3,2,1,0:T(8,128)(2,1)}) custom-call(s32[1,24]{1,0:T(1,128)S(4)} %get-tuple-element.39.outer_rows, s32[1,8]{1,0:T(1,128)S(4)} %get-tuple-element.40.live, bf16[2,16,32,128]{3,2,1,0:T(8,128)(2,1)S(1)} %get-tuple-element.57.keep, ...), custom_call_target="tpu_custom_call" | custom-call | flops 25165824 | bytes 2097152 | tf_op jit(solution)/shard_map/outer_back/pallas_call | solution.py:380
  31.2 6.3 %all-to-all-start.1 = ((bf16[8,3,32,128]{3,2,1,0:T(8,128)(2,1)}), bf16[8,3,32,128]{3,2,1,0:T(8,128)(2,1)S(1)}, u32[]{:S(2)}, u32[]{:S(2)}) async-start(bf16[8,3,32,128]{3,2,1,0:T(8,128)(2,1)} %get-tuple-element.63), calls=%async_computation.1 | async-start | bytes 393216 | tf_op jit(solution)/shard_map/all_to_all | solution.py:42
  37.6 1.6 %collective-permute-start.5 = (bf16[16,32,128]{2,1,0:T(8,128)(2,1)S(1)}, bf16[16,32,128]{2,1,0:T(8,128)(2,1)S(1)}, u32[]{:S(2)}, u32[]{:S(2)}) collective-permute-start(bf16[16,32,128]{2,1,0:T(8,128)(2,1)S(1)} %fusion.1), channel_id=1, source_target_pairs={{0,2},{1,3},{2,0},{3,1},{4,6},{5,7},{6,4},{7,5},{8,10},{9,11},{10,... | collective-permute-start | bytes 393224 | tf_op jit(solution)/shard_map/ppermute | solution.py:533
  39.2 0.6 %collective-permute-start.9 = (bf16[256,256]{1,0:T(8,128)(2,1)S(1)}, bf16[256,256]{1,0:T(8,128)(2,1)S(1)}, u32[]{:S(2)}, u32[]{:S(2)}) collective-permute-start(bf16[256,256]{1,0:T(8,128)(2,1)S(1)} %pair_sum.2.a), channel_id=1, source_target_pairs={{0,4},{4,0},{8,12},{12,8},{16,20},{20,16},{24,28},{28,24},{1,5},{5... | collective-permute-start | bytes 393224 | tf_op jit(solution)/shard_map/ppermute | solution.py:533
  39.8 2.5 %inner_back.1.total = f32[16,32,128]{2,1,0:T(8,128)S(1)} custom-call(s32[1,64]{1,0:T(1,128)S(4)} %get-tuple-element.64.rows, s32[1,64]{1,0:T(1,128)S(4)} %get-tuple-element.65.cols, bf16[16,32,128]{2,1,0:T(8,128)(2,1)S(1)} %get-tuple-element.66.scaled, f32[16,32,128]{2,1,0:T(8,128)S(1)} %get-tuple-element.69.base, bf16[64,128,128]{2,1,0:T(8,128)(2,1)} %bitcast.9), custom_call_target="tpu_custom_call" | custom-call | flops 67108864 | bytes 3145728 | tf_op jit(solution)/shard_map/inner_back/pallas_call | solution.py:414
  42.3 0.3 collective-permute-done.5.came
  42.6 0.1 add_returned.1.mine
  42.8 1.6 %collective-permute-start.6 = (bf16[16,32,128]{2,1,0:T(8,128)(2,1)S(1)}, bf16[16,32,128]{2,1,0:T(8,128)(2,1)S(1)}, u32[]{:S(2)}, u32[]{:S(2)}) collective-permute-start(bf16[16,32,128]{2,1,0:T(8,128)(2,1)S(1)} %add_returned.1.mine), channel_id=1, source_target_pairs={{0,2},{1,3},{2,0},{3,1},{4,6},{5,7},{6,4},{7,5},{8,10},{9,11},{10,... | collective-permute-start | bytes 393224 | tf_op jit(solution)/shard_map/ppermute | solution.py:533
  44.4 0.7 %collective-permute-start.10 = (bf16[256,256]{1,0:T(8,128)(2,1)S(1)}, bf16[256,256]{1,0:T(8,128)(2,1)S(1)}, u32[]{:S(2)}, u32[]{:S(2)}) collective-permute-start(bf16[256,256]{1,0:T(8,128)(2,1)S(1)} %pair_sum.3.grads), channel_id=1, source_target_pairs={{0,8},{4,12},{8,0},{12,4},{16,24},{20,28},{24,16},{28,20},{1,9},{5... | collective-permute-start | bytes 393224 | tf_op jit(solution)/shard_map/ppermute | solution.py:533
  45.1 2.7 %collective-permute-done.6.across = bf16[16,32,128]{2,1,0:T(8,128)(2,1)S(1)} collective-permute-done((bf16[16,32,128]{2,1,0:T(8,128)(2,1)S(1)}, bf16[16,32,128]{2,1,0:T(8,128)(2,1)S(1)}, u32[]{:S(2)}, u32[]{:S(2)}) %collective-permute-start.6) | collective-permute-done | bytes 131104 | tf_op jit(solution)/shard_map/ppermute | solution.py:533
  47.8 1.6 %collective-permute-done.10.grads_came = bf16[256,256]{1,0:T(8,128)(2,1)S(1)} collective-permute-done((bf16[256,256]{1,0:T(8,128)(2,1)S(1)}, bf16[256,256]{1,0:T(8,128)(2,1)S(1)}, u32[]{:S(2)}, u32[]{:S(2)}) %collective-permute-start.10) | collective-permute-done | bytes 131104 | tf_op jit(solution)/shard_map/ppermute | solution.py:533
  49.4 1.3 %finish.1 = (f32[2048,128]{1,0:T(8,128)}, f32[128,256]{1,0:T(8,128)}, f32[128,256]{1,0:T(8,128)}) custom-call(bf16[16,32,128]{2,1,0:T(8,128)(2,1)S(1)} %add_returned.1.mine, bf16[16,32,128]{2,1,0:T(8,128)(2,1)S(1)} %collective-permute-done.6.across, bf16[16,32,128]{2,1,0:T(8,128)(2,1)S(1)} %collective-permute-done.7.beside, ...), custom_call_target="tpu_custom_call" | custom-call | flops 67108864 | bytes 2097152 | tf_op jit(solution)/shard_map/finish/pallas_call | solution.py:516
  (16 shorter events, 0.3 us)
Async XLA Ops:
  2.4 16.9 %all-to-all-start = ((bf16[8,3,64,128]{3,2,1,0:T(8,128)(2,1)}), bf16[8,3,64,128]{3,2,1,0:T(8,128)(2,1)S(1)}, u32[]{:S(2)}, u32[]{:S(2)}) async-start(bf16[8,3,64,128]{3,2,1,0:T(8,128)(2,1)} %gather_halves.1), calls=%async_computation | async-start | bytes 786432 | tf_op jit(solution)/shard_map/all_to_all | solution.py:42
  19.3 1.8 %collective-permute-start = (bf16[8,3,64,128]{3,2,1,0:T(8,128)(2,1)S(1)}, bf16[8,3,64,128]{3,2,1,0:T(8,128)(2,1)S(1)}, u32[]{:S(2)}, u32[]{:S(2)}) collective-permute-start(bf16[8,3,64,128]{3,2,1,0:T(8,128)(2,1)S(1)} %all-to-all-done.own), channel_id=1, source_target_pairs={{0,1},{1,0},{2,3},{3,2},{4,5},{5,4},{6,7},{7,6},{8,9},{9,8},{10,11... | collective-permute-start | bytes 1179656 | tf_op jit(solution)/shard_map/ppermute | solution.py:533
  22.6 1.7 %collective-permute-start.1 = (bf16[2,16,32,128]{3,2,1,0:T(8,128)(2,1)S(1)}, bf16[2,16,32,128]{3,2,1,0:T(8,128)(2,1)S(1)}, u32[]{:S(2)}, u32[]{:S(2)}) collective-permute-start(bf16[2,16,32,128]{3,2,1,0:T(8,128)(2,1)S(1)} %get-tuple-element.58), channel_id=1, source_target_pairs={{0,1},{1,0},{2,3},{3,2},{4,5},{5,4},{6,7},{7,6},{8,9},{9,8},{10,11... | collective-permute-start | bytes 786440 | tf_op jit(solution)/shard_map/ppermute | solution.py:533
  23.1 5.4 %collective-permute-start.3 = (bf16[2,16,32,128]{3,2,1,0:T(8,128)(2,1)S(1)}, bf16[2,16,32,128]{3,2,1,0:T(8,128)(2,1)S(1)}, u32[]{:S(2)}, u32[]{:S(2)}) collective-permute-start(bf16[2,16,32,128]{3,2,1,0:T(8,128)(2,1)S(1)} %get-tuple-element.62), channel_id=1, source_target_pairs={{0,1},{1,0},{2,3},{3,2},{4,5},{5,4},{6,7},{7,6},{8,9},{9,8},{10,11... | collective-permute-start | bytes 786440 | tf_op jit(solution)/shard_map/ppermute | solution.py:533
  24.3 5.9 %collective-permute-start.2 = (bf16[16,32,128]{2,1,0:T(8,128)(2,1)S(1)}, bf16[16,32,128]{2,1,0:T(8,128)(2,1)S(1)}, u32[]{:S(2)}, u32[]{:S(2)}) collective-permute-start(bf16[16,32,128]{2,1,0:T(8,128)(2,1)S(1)} %fusion), channel_id=1, source_target_pairs={{0,2},{1,3},{2,0},{3,1},{4,6},{5,7},{6,4},{7,5},{8,10},{9,11},{10,... | collective-permute-start | bytes 393224 | tf_op jit(solution)/shard_map/ppermute | solution.py:533
  25.9 13.2 %collective-permute-start.4 = (bf16[256,256]{1,0:T(8,128)(2,1)S(1)}, bf16[256,256]{1,0:T(8,128)(2,1)S(1)}, u32[]{:S(2)}, u32[]{:S(2)}) collective-permute-start(bf16[256,256]{1,0:T(8,128)(2,1)S(1)} %get-tuple-element.68.a), channel_id=1, source_target_pairs={{0,16},{4,20},{8,24},{12,28},{16,0},{20,4},{24,8},{28,12},{1,17},{... | collective-permute-start | bytes 393224 | tf_op jit(solution)/shard_map/ppermute | solution.py:533
  31.2 11.4 %all-to-all-start.1 = ((bf16[8,3,32,128]{3,2,1,0:T(8,128)(2,1)}), bf16[8,3,32,128]{3,2,1,0:T(8,128)(2,1)S(1)}, u32[]{:S(2)}, u32[]{:S(2)}) async-start(bf16[8,3,32,128]{3,2,1,0:T(8,128)(2,1)} %get-tuple-element.63), calls=%async_computation.1 | async-start | bytes 393216 | tf_op jit(solution)/shard_map/all_to_all | solution.py:42
  37.6 5.0 %collective-permute-start.5 = (bf16[16,32,128]{2,1,0:T(8,128)(2,1)S(1)}, bf16[16,32,128]{2,1,0:T(8,128)(2,1)S(1)}, u32[]{:S(2)}, u32[]{:S(2)}) collective-permute-start(bf16[16,32,128]{2,1,0:T(8,128)(2,1)S(1)} %fusion.1), channel_id=1, source_target_pairs={{0,2},{1,3},{2,0},{3,1},{4,6},{5,7},{6,4},{7,5},{8,10},{9,11},{10,... | collective-permute-start | bytes 393224 | tf_op jit(solution)/shard_map/ppermute | solution.py:533
  39.2 5.2 %collective-permute-start.9 = (bf16[256,256]{1,0:T(8,128)(2,1)S(1)}, bf16[256,256]{1,0:T(8,128)(2,1)S(1)}, u32[]{:S(2)}, u32[]{:S(2)}) collective-permute-start(bf16[256,256]{1,0:T(8,128)(2,1)S(1)} %pair_sum.2.a), channel_id=1, source_target_pairs={{0,4},{4,0},{8,12},{12,8},{16,20},{20,16},{24,28},{28,24},{1,5},{5... | collective-permute-start | bytes 393224 | tf_op jit(solution)/shard_map/ppermute | solution.py:533
  42.8 5.0 %collective-permute-start.6 = (bf16[16,32,128]{2,1,0:T(8,128)(2,1)S(1)}, bf16[16,32,128]{2,1,0:T(8,128)(2,1)S(1)}, u32[]{:S(2)}, u32[]{:S(2)}) collective-permute-start(bf16[16,32,128]{2,1,0:T(8,128)(2,1)S(1)} %add_returned.1.mine), channel_id=1, source_target_pairs={{0,2},{1,3},{2,0},{3,1},{4,6},{5,7},{6,4},{7,5},{8,10},{9,11},{10,... | collective-permute-start | bytes 393224 | tf_op jit(solution)/shard_map/ppermute | solution.py:533
  44.4 5.0 %collective-permute-start.10 = (bf16[256,256]{1,0:T(8,128)(2,1)S(1)}, bf16[256,256]{1,0:T(8,128)(2,1)S(1)}, u32[]{:S(2)}, u32[]{:S(2)}) collective-permute-start(bf16[256,256]{1,0:T(8,128)(2,1)S(1)} %pair_sum.3.grads), channel_id=1, source_target_pairs={{0,8},{4,12},{8,0},{12,4},{16,24},{20,28},{24,16},{28,20},{1,9},{5... | collective-permute-start | bytes 393224 | tf_op jit(solution)/shard_map/ppermute | solution.py:533
  45.1 4.3 %collective-permute-start.7 = (bf16[16,32,128]{2,1,0:T(8,128)(2,1)S(1)}, bf16[16,32,128]{2,1,0:T(8,128)(2,1)S(1)}, u32[]{:S(2)}, u32[]{:S(2)}) collective-permute-start(bf16[16,32,128]{2,1,0:T(8,128)(2,1)S(1)} %add_returned.1.mine), channel_id=1, source_target_pairs={{0,1},{1,0},{2,3},{3,2},{4,5},{5,4},{6,7},{7,6},{8,9},{9,8},{10,11... | collective-permute-start | bytes 393224 | tf_op jit(solution)/shard_map/ppermute | solution.py:533
  47.8 1.6 %collective-permute-start.8 = (bf16[16,32,128]{2,1,0:T(8,128)(2,1)S(1)}, bf16[16,32,128]{2,1,0:T(8,128)(2,1)S(1)}, u32[]{:S(2)}, u32[]{:S(2)}) collective-permute-start(bf16[16,32,128]{2,1,0:T(8,128)(2,1)S(1)} %collective-permute-done.6.across), channel_id=1, source_target_pairs={{0,1},{1,0},{2,3},{3,2},{4,5},{5,4},{6,7},{7,6},{8,9},{9,8},{10,11... | collective-permute-start | bytes 393224 | tf_op jit(solution)/shard_map/ppermute | solution.py:533

commit v8 on v7

--- a/solution.py
+++ b/solution.py
@@ -26,8 +26,8 @@
     return [pltpu.with_memory_space_constraint(x, pltpu.HBM) for x in arrays]
 
 
-OUT_ORDER = (5, 7, 1, 4, 6, 3, 0, 2)
-BACK_ORDER = (5, 7, 1, 4, 6, 3, 0, 2)
+OUT_ORDER = (4, 7, 1, 5, 6, 3, 0, 2)
+BACK_ORDER = (4, 2, 5, 3, 1, 0, 7, 6)
 
 
 def order_of(order, peers):
@@ -573,7 +573,8 @@
     returned = exchange(payload, back_order)
     bit = peers // 2
     while bit > 2:
-        grads = pair_sum(grads, swap(grads, "dom", bit))
+        came, came_s = lax.optimization_barrier((swap(grads, "dom", bit), came_s))
+        grads = (grads.astype(F32) + came.astype(F32)).astype(BF16)
         bit //= 2
     base, grads = lax.optimization_barrier((base, grads))
     partial = add_came(inner_back(rows, cols, scaled, base, inner_a), came_s)

time: 51.2 us -> 50.2 us (0.980)
  starting transfers between devices: 24 us -> 22.4 us
  waiting for transfers between devices: 8.51 us -> 9.11 us
    all_to_all x2, starting transfers between devices: 14.7 us -> 13.4 us  [exchange(): lax.all_to_all(x, 'dom', split_axis=0, concat_axis=0, tiled=True, axis_in...]
    all_to_all x2, waiting for transfers between devices: 2.2 us -> 3.19 us  [exchange(): lax.all_to_all(x, 'dom', split_axis=0, concat_axis=0, tiled=True, axis_in...]
  transfers between devices with their start and end apart: 13 -> 13, of which waited for: 6 -> 6; matrix products, arithmetic and copies ran while one was open for 0% -> 0% of each run, Pallas kernels for 25% -> 26%
where the time goes in v8:
time: 50.2 us; the launch traced here: 49.7 us
  starting transfers between devices  22.4 us (45%)
  Pallas kernels  17.4 us (35%)
  waiting for transfers between devices  9.11 us (18%)
  between operations  0.74 us (1%)
    all_to_all x2, starting transfers between devices, exchange(): lax.all_to_all(x, 'dom', split_axis=0, concat_axis=0, tiled=True, axis_in...  13.4 us
    ppermute x11, starting transfers between devices, swap(): lax.ppermute(x, axis, [(i, i ^ bit) for i in range(lax.axis_size(axis))])  8.98 us
    pallas_call x1, Pallas kernels, stage(): pl.pallas_call(stage_kernel, out_shape=tuple((pltpu.SMEM(x.shape, jnp.int...  6.32 us
    ppermute x11, waiting for transfers between devices, swap(): lax.ppermute(x, axis, [(i, i ^ bit) for i in range(lax.axis_size(axis))])  5.92 us
    all_to_all x2, waiting for transfers between devices, exchange(): lax.all_to_all(x, 'dom', split_axis=0, concat_axis=0, tiled=True, axis_in...  3.19 us
    pallas_call x1, Pallas kernels, inner_back(): pl.pallas_call(inner_back_kernel, out_shape=pltpu.VMEM(base.shape, F32),...  2.53 us
    pallas_call x1, Pallas kernels, fetch(): pl.pallas_call(fetch_kernel, out_shape=tuple((pltpu.VMEM(shape, BF16) for...  1.74 us
    pallas_call x1, Pallas kernels, gather_halves(): pl.pallas_call(functools.partial(gather_kernel, order), out_shape=jax.Sha...  1.73 us
  transfers between devices with their start and end apart: 13, of which 6 were waited for; matrix products, arithmetic and copies ran while one was open for 0% of the time, Pallas kernels for 26%

profile of v8, /device:TPU:0, one launch (start us, length us, event | category | flops | bytes accessed | tf_op | source)
XLA Modules:
  0.0 49.7 jit_solution(8710277876274532673)
XLA Ops:
  0.6 1.7 %gather_halves.1 = bf16[8,3,64,128]{3,2,1,0:T(8,128)(2,1)} custom-call(s32[3,1,8]{2,1,0:T(1,128)} %bitcast.13, bf16[16,2,64,128]{3,2,1,0:T(8,128)(2,1)} %bitcast.10), custom_call_target="tpu_custom_call" | custom-call | tf_op jit(solution)/shard_map/gather_halves/pallas_call | solution.py:90
  2.4 7.8 %all-to-all-start = ((bf16[8,3,64,128]{3,2,1,0:T(8,128)(2,1)}), bf16[8,3,64,128]{3,2,1,0:T(8,128)(2,1)S(1)}, u32[]{:S(2)}, u32[]{:S(2)}) async-start(bf16[8,3,64,128]{3,2,1,0:T(8,128)(2,1)} %gather_halves.1), calls=%async_computation | async-start | bytes 786432 | tf_op jit(solution)/shard_map/all_to_all | solution.py:42
  10.2 6.3 %stage.1 = (s32[1,64]{1,0:T(1,128)S(4)}, s32[1,64]{1,0:T(1,128)S(4)}, s32[1,24]{1,0:T(1,128)S(4)}, s32[1,8]{1,0:T(1,128)S(4)}, s32[3,1,8]{2,1,0:T(1,128)S(4)}, /...) custom-call(s32[1,64]{1,0:T(1,128)} %rows_far.1, s32[1,64]{1,0:T(1,128)} %cols_far.1, ...), custom_call_target="tpu_custom_call" | custom-call | flops 536870912 | bytes 6291456 | tf_op jit(solution)/shard_map/stage/pallas_call | solution.py:183
  16.5 2.8 %all-to-all-done.own = bf16[8,3,64,128]{3,2,1,0:T(8,128)(2,1)S(1)} async-done(((bf16[8,3,64,128]{3,2,1,0:T(8,128)(2,1)}), bf16[8,3,64,128]{3,2,1,0:T(8,128)(2,1)S(1)}, u32[]{:S(2)}, u32[]{:S(2)}) %all-to-all-start) | async-done | bytes 393248 | tf_op jit(solution)/shard_map/all_to_all | solution.py:42
  19.4 1.7 %fetch.1 = (bf16[24,128,128]{2,1,0:T(8,128)(2,1)S(1)}, bf16[2048,128]{1,0:T(8,128)(2,1)S(1)}, bf16[2048,256]{1,0:T(8,128)(2,1)S(1)}, bf16[256,256]{1,0:T(8,128)(2,1)S(1)}, bf16[256,256]{1,0:T(8,128)(2,1)S(1)}) custom-call(bf16[24,128,128]{2,1,0:T(8,128)(2,1)} %bitcast.12, bf16[2048,128]{1,0:T(8,128)(2,1)} %feat_far.3, bf16[2048,256]{1,0:T(8,128)(2,1)} %cot_far.1, ...), custom_call_target="tpu_custom_call" | custom-call | flops 1000000 | bytes 3145728 | tf_op jit(solution)/shard_map/fetch/pallas_call | solution.py:232
  21.1 1.5 %layer.1 = (bf16[2048,256]{1,0:T(8,128)(2,1)S(1)}, bf16[2048,256]{1,0:T(8,128)(2,1)S(1)}, bf16[2048,256]{1,0:T(8,128)(2,1)S(1)}, bf16[2,16,32,128]{3,2,1,0:T(8,1...) custom-call(s32[1,24]{1,0:T(1,128)S(4)} %get-tuple-element.41.outer_, ...), custom_call_target="tpu_custom_call", output_to_operand_aliasing={{7}: (5, {})} | custom-call | flops 1200000000 | bytes 8388608 | tf_op jit(solution)/shard_map/layer/pallas_call | solution.py:307
  22.7 0.6 %collective-permute-start.1 = (bf16[2,16,32,128]{3,2,1,0:T(8,128)(2,1)S(1)}, bf16[2,16,32,128]{3,2,1,0:T(8,128)(2,1)S(1)}, u32[]{:S(2)}, u32[]{:S(2)}) collective-permute-start(bf16[2,16,32,128]{3,2,1,0:T(8,128)(2,1)S(1)} %get-tuple-element.60), channel_id=1, source_target_pairs={{0,1},{1,0},{2,3},{3,2},{4,5},{5,4},{6,7},{7,6},{8,9},{9,8},{10,11... | collective-permute-start | bytes 786440 | tf_op jit(solution)/shard_map/ppermute | solution.py:533
  23.2 0.1 collective-permute-start.3
  23.3 1.0 %weight_grads.1 = (bf16[2048,256]{1,0:T(8,128)(2,1)}, bf16[256,256]{1,0:T(8,128)(2,1)S(1)}) custom-call(bf16[2048,256]{1,0:T(8,128)(2,1)S(1)} %get-tuple-element.54.smooth, bf16[2048,256]{1,0:T(8,128)(2,1)S(1)} %get-tuple-element.55.grad_pre, bf16[2048,256]{1,0:T(8,128)(2,1)S(1)} %get-tuple-element.56.both), custom_call_target="tpu_custom_call" | custom-call | flops 268435456 | bytes 4194304 | tf_op jit(solution)/shard_map/weight_grads/pallas_call | solution.py:341
  24.4 1.6 %collective-permute-start.2 = (bf16[16,32,128]{2,1,0:T(8,128)(2,1)S(1)}, bf16[16,32,128]{2,1,0:T(8,128)(2,1)S(1)}, u32[]{:S(2)}, u32[]{:S(2)}) collective-permute-start(bf16[16,32,128]{2,1,0:T(8,128)(2,1)S(1)} %fusion), channel_id=1, source_target_pairs={{0,2},{1,3},{2,0},{3,1},{4,6},{5,7},{6,4},{7,5},{8,10},{9,11},{10,... | collective-permute-start | bytes 393224 | tf_op jit(solution)/shard_map/ppermute | solution.py:533
  26.0 1.5 %collective-permute-start.4 = (bf16[256,256]{1,0:T(8,128)(2,1)S(1)}, bf16[256,256]{1,0:T(8,128)(2,1)S(1)}, u32[]{:S(2)}, u32[]{:S(2)}) collective-permute-start(bf16[256,256]{1,0:T(8,128)(2,1)S(1)} %get-tuple-element.70), channel_id=1, source_target_pairs={{0,16},{4,20},{8,24},{12,28},{16,0},{20,4},{24,8},{28,12},{1,17},{... | collective-permute-start | bytes 393224 | tf_op jit(solution)/shard_map/ppermute | solution.py:533
  27.5 0.6 %collective-permute-start.5 = (bf16[16,32,128]{2,1,0:T(8,128)(2,1)S(1)}, bf16[16,32,128]{2,1,0:T(8,128)(2,1)S(1)}, u32[]{:S(2)}, u32[]{:S(2)}) collective-permute-start(bf16[16,32,128]{2,1,0:T(8,128)(2,1)S(1)} %fusion.1), channel_id=1, source_target_pairs={{0,2},{1,3},{2,0},{3,1},{4,6},{5,7},{6,4},{7,5},{8,10},{9,11},{10,... | collective-permute-start | bytes 393224 | tf_op jit(solution)/shard_map/ppermute | solution.py:533
  28.1 2.4 %collective-permute-done.2.came = bf16[16,32,128]{2,1,0:T(8,128)(2,1)S(1)} collective-permute-done((bf16[16,32,128]{2,1,0:T(8,128)(2,1)S(1)}, bf16[16,32,128]{2,1,0:T(8,128)(2,1)S(1)}, u32[]{:S(2)}, u32[]{:S(2)}) %collective-permute-start.2) | collective-permute-done | bytes 131104 | tf_op jit(solution)/shard_map/ppermute | solution.py:533
  30.5 1.0 %outer_back.1 = (bf16[16,32,128]{2,1,0:T(8,128)(2,1)S(1)}, f32[16,32,128]{2,1,0:T(8,128)S(1)}, bf16[8,3,32,128]{3,2,1,0:T(8,128)(2,1)}) custom-call(s32[1,24]{1,0:T(1,128)S(4)} %get-tuple-element.41.outer_rows, s32[1,8]{1,0:T(1,128)S(4)} %get-tuple-element.42.live, bf16[2,16,32,128]{3,2,1,0:T(8,128)(2,1)S(1)} %get-tuple-element.59.keep, ...), custom_call_target="tpu_custom_call" | custom-call | flops 25165824 | bytes 2097152 | tf_op jit(solution)/shard_map/outer_back/pallas_call | solution.py:380
  31.5 5.6 %all-to-all-start.1 = ((bf16[8,3,32,128]{3,2,1,0:T(8,128)(2,1)}), bf16[8,3,32,128]{3,2,1,0:T(8,128)(2,1)S(1)}, u32[]{:S(2)}, u32[]{:S(2)}) async-start(bf16[8,3,32,128]{3,2,1,0:T(8,128)(2,1)} %get-tuple-element.65), calls=%async_computation.1 | async-start | bytes 393216 | tf_op jit(solution)/shard_map/all_to_all | solution.py:42
  37.2 1.5 %collective-permute-start.9 = (bf16[256,256]{1,0:T(8,128)(2,1)S(1)}, bf16[256,256]{1,0:T(8,128)(2,1)S(1)}, u32[]{:S(2)}, u32[]{:S(2)}) collective-permute-start(bf16[256,256]{1,0:T(8,128)(2,1)S(1)} %add_convert_fusion.a), channel_id=1, source_target_pairs={{0,4},{4,0},{8,12},{12,8},{16,20},{20,16},{24,28},{28,24},{1,5},{5... | collective-permute-start | bytes 393224 | tf_op jit(solution)/shard_map/ppermute | solution.py:533
  38.7 2.5 %inner_back.1.total = f32[16,32,128]{2,1,0:T(8,128)S(1)} custom-call(s32[1,64]{1,0:T(1,128)S(4)} %get-tuple-element.66.rows, s32[1,64]{1,0:T(1,128)S(4)} %get-tuple-element.67.cols, bf16[16,32,128]{2,1,0:T(8,128)(2,1)S(1)} %get-tuple-element.68.scaled, f32[16,32,128]{2,1,0:T(8,128)S(1)} %get-tuple-element.72.base, bf16[64,128,128]{2,1,0:T(8,128)(2,1)} %bitcast.9), custom_call_target="tpu_custom_call" | custom-call | flops 67108864 | bytes 3145728 | tf_op jit(solution)/shard_map/inner_back/pallas_call | solution.py:414
  41.3 0.3 all-to-all-done.1.returned
  41.6 0.1 add_returned.1.mine
  41.8 1.6 %collective-permute-start.6 = (bf16[16,32,128]{2,1,0:T(8,128)(2,1)S(1)}, bf16[16,32,128]{2,1,0:T(8,128)(2,1)S(1)}, u32[]{:S(2)}, u32[]{:S(2)}) collective-permute-start(bf16[16,32,128]{2,1,0:T(8,128)(2,1)S(1)} %add_returned.1.mine), channel_id=1, source_target_pairs={{0,2},{1,3},{2,0},{3,1},{4,6},{5,7},{6,4},{7,5},{8,10},{9,11},{10,... | collective-permute-start | bytes 393224 | tf_op jit(solution)/shard_map/ppermute | solution.py:533
  43.4 1.6 %collective-permute-start.10 = (bf16[256,256]{1,0:T(8,128)(2,1)S(1)}, bf16[256,256]{1,0:T(8,128)(2,1)S(1)}, u32[]{:S(2)}, u32[]{:S(2)}) collective-permute-start(bf16[256,256]{1,0:T(8,128)(2,1)S(1)} %pair_sum.1.grads), channel_id=1, source_target_pairs={{0,8},{4,12},{8,0},{12,4},{16,24},{20,28},{24,16},{28,20},{1,9},{5... | collective-permute-start | bytes 393224 | tf_op jit(solution)/shard_map/ppermute | solution.py:533
  45.0 1.8 %collective-permute-done.6.across = bf16[16,32,128]{2,1,0:T(8,128)(2,1)S(1)} collective-permute-done((bf16[16,32,128]{2,1,0:T(8,128)(2,1)S(1)}, bf16[16,32,128]{2,1,0:T(8,128)(2,1)S(1)}, u32[]{:S(2)}, u32[]{:S(2)}) %collective-permute-start.6) | collective-permute-done | bytes 131104 | tf_op jit(solution)/shard_map/ppermute | solution.py:533
  46.8 1.6 %collective-permute-done.10.grads_came = bf16[256,256]{1,0:T(8,128)(2,1)S(1)} collective-permute-done((bf16[256,256]{1,0:T(8,128)(2,1)S(1)}, bf16[256,256]{1,0:T(8,128)(2,1)S(1)}, u32[]{:S(2)}, u32[]{:S(2)}) %collective-permute-start.10) | collective-permute-done | bytes 131104 | tf_op jit(solution)/shard_map/ppermute | solution.py:533
  48.4 1.3 %finish.1 = (f32[2048,128]{1,0:T(8,128)}, f32[128,256]{1,0:T(8,128)}, f32[128,256]{1,0:T(8,128)}) custom-call(bf16[16,32,128]{2,1,0:T(8,128)(2,1)S(1)} %add_returned.1.mine, bf16[16,32,128]{2,1,0:T(8,128)(2,1)S(1)} %collective-permute-done.6.across, bf16[16,32,128]{2,1,0:T(8,128)(2,1)S(1)} %collective-permute-done.7.beside, ...), custom_call_target="tpu_custom_call" | custom-call | flops 67108864 | bytes 2097152 | tf_op jit(solution)/shard_map/finish/pallas_call | solution.py:516
  (16 shorter events, 0.3 us)
Async XLA Ops:
  2.4 17.0 %all-to-all-start = ((bf16[8,3,64,128]{3,2,1,0:T(8,128)(2,1)}), bf16[8,3,64,128]{3,2,1,0:T(8,128)(2,1)S(1)}, u32[]{:S(2)}, u32[]{:S(2)}) async-start(bf16[8,3,64,128]{3,2,1,0:T(8,128)(2,1)} %gather_halves.1), calls=%async_computation | async-start | bytes 786432 | tf_op jit(solution)/shard_map/all_to_all | solution.py:42
  19.4 1.8 %collective-permute-start = (bf16[8,3,64,128]{3,2,1,0:T(8,128)(2,1)S(1)}, bf16[8,3,64,128]{3,2,1,0:T(8,128)(2,1)S(1)}, u32[]{:S(2)}, u32[]{:S(2)}) collective-permute-start(bf16[8,3,64,128]{3,2,1,0:T(8,128)(2,1)S(1)} %all-to-all-done.own), channel_id=1, source_target_pairs={{0,1},{1,0},{2,3},{3,2},{4,5},{5,4},{6,7},{7,6},{8,9},{9,8},{10,11... | collective-permute-start | bytes 1179656 | tf_op jit(solution)/shard_map/ppermute | solution.py:533
  22.7 1.7 %collective-permute-start.1 = (bf16[2,16,32,128]{3,2,1,0:T(8,128)(2,1)S(1)}, bf16[2,16,32,128]{3,2,1,0:T(8,128)(2,1)S(1)}, u32[]{:S(2)}, u32[]{:S(2)}) collective-permute-start(bf16[2,16,32,128]{3,2,1,0:T(8,128)(2,1)S(1)} %get-tuple-element.60), channel_id=1, source_target_pairs={{0,1},{1,0},{2,3},{3,2},{4,5},{5,4},{6,7},{7,6},{8,9},{9,8},{10,11... | collective-permute-start | bytes 786440 | tf_op jit(solution)/shard_map/ppermute | solution.py:533
  23.2 4.3 %collective-permute-start.3 = (bf16[2,16,32,128]{3,2,1,0:T(8,128)(2,1)S(1)}, bf16[2,16,32,128]{3,2,1,0:T(8,128)(2,1)S(1)}, u32[]{:S(2)}, u32[]{:S(2)}) collective-permute-start(bf16[2,16,32,128]{3,2,1,0:T(8,128)(2,1)S(1)} %get-tuple-element.64), channel_id=1, source_target_pairs={{0,1},{1,0},{2,3},{3,2},{4,5},{5,4},{6,7},{7,6},{8,9},{9,8},{10,11... | collective-permute-start | bytes 786440 | tf_op jit(solution)/shard_map/ppermute | solution.py:533
  24.4 6.1 %collective-permute-start.2 = (bf16[16,32,128]{2,1,0:T(8,128)(2,1)S(1)}, bf16[16,32,128]{2,1,0:T(8,128)(2,1)S(1)}, u32[]{:S(2)}, u32[]{:S(2)}) collective-permute-start(bf16[16,32,128]{2,1,0:T(8,128)(2,1)S(1)} %fusion), channel_id=1, source_target_pairs={{0,2},{1,3},{2,0},{3,1},{4,6},{5,7},{6,4},{7,5},{8,10},{9,11},{10,... | collective-permute-start | bytes 393224 | tf_op jit(solution)/shard_map/ppermute | solution.py:533
  26.0 11.1 %collective-permute-start.4 = (bf16[256,256]{1,0:T(8,128)(2,1)S(1)}, bf16[256,256]{1,0:T(8,128)(2,1)S(1)}, u32[]{:S(2)}, u32[]{:S(2)}) collective-permute-start(bf16[256,256]{1,0:T(8,128)(2,1)S(1)} %get-tuple-element.70), channel_id=1, source_target_pairs={{0,16},{4,20},{8,24},{12,28},{16,0},{20,4},{24,8},{28,12},{1,17},{... | collective-permute-start | bytes 393224 | tf_op jit(solution)/shard_map/ppermute | solution.py:533
  27.5 9.6 %collective-permute-start.5 = (bf16[16,32,128]{2,1,0:T(8,128)(2,1)S(1)}, bf16[16,32,128]{2,1,0:T(8,128)(2,1)S(1)}, u32[]{:S(2)}, u32[]{:S(2)}) collective-permute-start(bf16[16,32,128]{2,1,0:T(8,128)(2,1)S(1)} %fusion.1), channel_id=1, source_target_pairs={{0,2},{1,3},{2,0},{3,1},{4,6},{5,7},{6,4},{7,5},{8,10},{9,11},{10,... | collective-permute-start | bytes 393224 | tf_op jit(solution)/shard_map/ppermute | solution.py:533
  31.5 10.1 %all-to-all-start.1 = ((bf16[8,3,32,128]{3,2,1,0:T(8,128)(2,1)}), bf16[8,3,32,128]{3,2,1,0:T(8,128)(2,1)S(1)}, u32[]{:S(2)}, u32[]{:S(2)}) async-start(bf16[8,3,32,128]{3,2,1,0:T(8,128)(2,1)} %get-tuple-element.65), calls=%async_computation.1 | async-start | bytes 393216 | tf_op jit(solution)/shard_map/all_to_all | solution.py:42
  37.2 6.2 %collective-permute-start.9 = (bf16[256,256]{1,0:T(8,128)(2,1)S(1)}, bf16[256,256]{1,0:T(8,128)(2,1)S(1)}, u32[]{:S(2)}, u32[]{:S(2)}) collective-permute-start(bf16[256,256]{1,0:T(8,128)(2,1)S(1)} %add_convert_fusion.a), channel_id=1, source_target_pairs={{0,4},{4,0},{8,12},{12,8},{16,20},{20,16},{24,28},{28,24},{1,5},{5... | collective-permute-start | bytes 393224 | tf_op jit(solution)/shard_map/ppermute | solution.py:533
  41.8 5.0 %collective-permute-start.6 = (bf16[16,32,128]{2,1,0:T(8,128)(2,1)S(1)}, bf16[16,32,128]{2,1,0:T(8,128)(2,1)S(1)}, u32[]{:S(2)}, u32[]{:S(2)}) collective-permute-start(bf16[16,32,128]{2,1,0:T(8,128)(2,1)S(1)} %add_returned.1.mine), channel_id=1, source_target_pairs={{0,2},{1,3},{2,0},{3,1},{4,6},{5,7},{6,4},{7,5},{8,10},{9,11},{10,... | collective-permute-start | bytes 393224 | tf_op jit(solution)/shard_map/ppermute | solution.py:533
  43.4 5.0 %collective-permute-start.10 = (bf16[256,256]{1,0:T(8,128)(2,1)S(1)}, bf16[256,256]{1,0:T(8,128)(2,1)S(1)}, u32[]{:S(2)}, u32[]{:S(2)}) collective-permute-start(bf16[256,256]{1,0:T(8,128)(2,1)S(1)} %pair_sum.1.grads), channel_id=1, source_target_pairs={{0,8},{4,12},{8,0},{12,4},{16,24},{20,28},{24,16},{28,20},{1,9},{5... | collective-permute-start | bytes 393224 | tf_op jit(solution)/shard_map/ppermute | solution.py:533
  45.0 3.5 %collective-permute-start.7 = (bf16[16,32,128]{2,1,0:T(8,128)(2,1)S(1)}, bf16[16,32,128]{2,1,0:T(8,128)(2,1)S(1)}, u32[]{:S(2)}, u32[]{:S(2)}) collective-permute-start(bf16[16,32,128]{2,1,0:T(8,128)(2,1)S(1)} %add_returned.1.mine), channel_id=1, source_target_pairs={{0,1},{1,0},{2,3},{3,2},{4,5},{5,4},{6,7},{7,6},{8,9},{9,8},{10,11... | collective-permute-start | bytes 393224 | tf_op jit(solution)/shard_map/ppermute | solution.py:533
  46.8 1.6 %collective-permute-start.8 = (bf16[16,32,128]{2,1,0:T(8,128)(2,1)S(1)}, bf16[16,32,128]{2,1,0:T(8,128)(2,1)S(1)}, u32[]{:S(2)}, u32[]{:S(2)}) collective-permute-start(bf16[16,32,128]{2,1,0:T(8,128)(2,1)S(1)} %collective-permute-done.6.across), channel_id=1, source_target_pairs={{0,1},{1,0},{2,3},{3,2},{4,5},{5,4},{6,7},{7,6},{8,9},{9,8},{10,11... | collective-permute-start | bytes 393224 | tf_op jit(solution)/shard_map/ppermute | solution.py:533

commit v9 on v8

--- a/solution.py
+++ b/solution.py
@@ -10,7 +10,8 @@
 F32 = jnp.float32
 BF16 = jnp.bfloat16
 MIB = 1 << 20
-GROUP = 8
+GROUP = 16
+OUTER_GROUP = 8
 ROWS_LAST = (((1,), (1,)), ((), ()))
 ROWS_FIRST = (((0,), (0,)), ((), ()))
 WHOLE = pl.BlockSpec(memory_space=pltpu.VMEM)
@@ -26,7 +27,7 @@
     return [pltpu.with_memory_space_constraint(x, pltpu.HBM) for x in arrays]
 
 
-OUT_ORDER = (4, 7, 1, 5, 6, 3, 0, 2)
+OUT_ORDER = (4, 7, 3, 5, 2, 1, 0, 6)
 BACK_ORDER = (4, 2, 5, 3, 1, 0, 7, 6)
 
 
@@ -158,18 +159,18 @@
 
     def some(g, _):
         ones = jnp.ones((block, feat_width), BF16)
-        products = [dot(outer[g * GROUP + k], ones) for k in range(GROUP)]
+        products = [dot(outer[g * OUTER_GROUP + k], ones) for k in range(OUTER_GROUP)]
         flat = [
-            lax.dot_general(few, outer[g * GROUP + k], ROWS_LAST, preferred_element_type=F32) for k in range(GROUP)
+            lax.dot_general(few, outer[g * OUTER_GROUP + k], ROWS_LAST, preferred_element_type=F32) for k in range(OUTER_GROUP)
         ]
-        for k in range(GROUP):
-            n = g * GROUP + k
+        for k in range(OUTER_GROUP):
+            n = g * OUTER_GROUP + k
             alive = (n % slots < live[0, n // slots]).astype(F32)
             over[outer_rows[0, n]] += products[k] * alive
             degree_rows[outer_rows[0, n]] += flat[k] * alive
         return 0
 
-    lax.fori_loop(0, outer_count // GROUP, some, 0)
+    lax.fori_loop(0, outer_count // OUTER_GROUP, some, 0)
     over[...] = 1.0 / over[...]
     over_rows[...] = 1.0 / degree_rows[...]
 

time: 50.2 us -> 50 us (level)
  Pallas kernels: 17.4 us -> 16.3 us
  waiting for transfers between devices: 9.11 us -> 9.95 us
    all_to_all x2, waiting for transfers between devices: 3.19 us -> 4.38 us  [exchange(): lax.all_to_all(x, 'dom', split_axis=0, concat_axis=0, tiled=True, axis_in...]
    pallas_call x1, Pallas kernels: 6.32 us -> 5.63 us  [stage(): pl.pallas_call(stage_kernel, out_shape=tuple((pltpu.SMEM(x.shape, jnp.int...]
  transfers between devices with their start and end apart: 13 -> 13, of which waited for: 6 -> 6; matrix products, arithmetic and copies ran while one was open for 0% -> 0% of each run, Pallas kernels for 26% -> 24%
where the time goes in v9:
time: 50 us; the launch traced here: 49.6 us
  starting transfers between devices  22.5 us (45%)
  Pallas kernels  16.3 us (33%)
  waiting for transfers between devices  9.95 us (20%)
  between operations  0.74 us (1%)
    all_to_all x2, starting transfers between devices, exchange(): lax.all_to_all(x, 'dom', split_axis=0, concat_axis=0, tiled=True, axis_in...  13.2 us
    ppermute x11, starting transfers between devices, swap(): lax.ppermute(x, axis, [(i, i ^ bit) for i in range(lax.axis_size(axis))])  9.25 us
    pallas_call x1, Pallas kernels, stage(): pl.pallas_call(stage_kernel, out_shape=tuple((pltpu.SMEM(x.shape, jnp.int...  5.63 us
    ppermute x11, waiting for transfers between devices, swap(): lax.ppermute(x, axis, [(i, i ^ bit) for i in range(lax.axis_size(axis))])  5.57 us
    all_to_all x2, waiting for transfers between devices, exchange(): lax.all_to_all(x, 'dom', split_axis=0, concat_axis=0, tiled=True, axis_in...  4.38 us
    pallas_call x1, Pallas kernels, inner_back(): pl.pallas_call(inner_back_kernel, out_shape=pltpu.VMEM(base.shape, F32),...  2.11 us
    pallas_call x1, Pallas kernels, fetch(): pl.pallas_call(fetch_kernel, out_shape=tuple((pltpu.VMEM(shape, BF16) for...  1.74 us
    pallas_call x1, Pallas kernels, gather_halves(): pl.pallas_call(functools.partial(gather_kernel, order), out_shape=jax.Sha...  1.73 us
  transfers between devices with their start and end apart: 13, of which 6 were waited for; matrix products, arithmetic and copies ran while one was open for 0% of the time, Pallas kernels for 24%

profile of v9, /device:TPU:0, one launch (start us, length us, event | category | flops | bytes accessed | tf_op | source)
XLA Modules:
  0.0 49.6 jit_solution(13168719841013614584)
XLA Ops:
  0.6 1.7 %gather_halves.1 = bf16[8,3,64,128]{3,2,1,0:T(8,128)(2,1)} custom-call(s32[3,1,8]{2,1,0:T(1,128)} %bitcast.13, bf16[16,2,64,128]{3,2,1,0:T(8,128)(2,1)} %bitcast.10), custom_call_target="tpu_custom_call" | custom-call | tf_op jit(solution)/shard_map/gather_halves/pallas_call | solution.py:91
  2.4 7.8 %all-to-all-start = ((bf16[8,3,64,128]{3,2,1,0:T(8,128)(2,1)}), bf16[8,3,64,128]{3,2,1,0:T(8,128)(2,1)S(1)}, u32[]{:S(2)}, u32[]{:S(2)}) async-start(bf16[8,3,64,128]{3,2,1,0:T(8,128)(2,1)} %gather_halves.1), calls=%async_computation | async-start | bytes 786432 | tf_op jit(solution)/shard_map/all_to_all | solution.py:43
  10.2 5.6 %stage.1 = (s32[1,64]{1,0:T(1,128)S(4)}, s32[1,64]{1,0:T(1,128)S(4)}, s32[1,24]{1,0:T(1,128)S(4)}, s32[1,8]{1,0:T(1,128)S(4)}, s32[3,1,8]{2,1,0:T(1,128)S(4)}, /...) custom-call(s32[1,64]{1,0:T(1,128)} %rows_far.1, s32[1,64]{1,0:T(1,128)} %cols_far.1, ...), custom_call_target="tpu_custom_call" | custom-call | flops 536870912 | bytes 6291456 | tf_op jit(solution)/shard_map/stage/pallas_call | solution.py:184
  15.8 3.5 %all-to-all-done.own = bf16[8,3,64,128]{3,2,1,0:T(8,128)(2,1)S(1)} async-done(((bf16[8,3,64,128]{3,2,1,0:T(8,128)(2,1)}), bf16[8,3,64,128]{3,2,1,0:T(8,128)(2,1)S(1)}, u32[]{:S(2)}, u32[]{:S(2)}) %all-to-all-start) | async-done | bytes 393248 | tf_op jit(solution)/shard_map/all_to_all | solution.py:43
  19.4 1.7 %fetch.1 = (bf16[24,128,128]{2,1,0:T(8,128)(2,1)S(1)}, bf16[2048,128]{1,0:T(8,128)(2,1)S(1)}, bf16[2048,256]{1,0:T(8,128)(2,1)S(1)}, bf16[256,256]{1,0:T(8,128)(2,1)S(1)}, bf16[256,256]{1,0:T(8,128)(2,1)S(1)}) custom-call(bf16[24,128,128]{2,1,0:T(8,128)(2,1)} %bitcast.12, bf16[2048,128]{1,0:T(8,128)(2,1)} %feat_far.3, bf16[2048,256]{1,0:T(8,128)(2,1)} %cot_far.1, ...), custom_call_target="tpu_custom_call" | custom-call | flops 1000000 | bytes 3145728 | tf_op jit(solution)/shard_map/fetch/pallas_call | solution.py:233
  21.1 1.5 %layer.1 = (bf16[2048,256]{1,0:T(8,128)(2,1)S(1)}, bf16[2048,256]{1,0:T(8,128)(2,1)S(1)}, bf16[2048,256]{1,0:T(8,128)(2,1)S(1)}, bf16[2,16,32,128]{3,2,1,0:T(8,1...) custom-call(s32[1,24]{1,0:T(1,128)S(4)} %get-tuple-element.41.outer_, ...), custom_call_target="tpu_custom_call", output_to_operand_aliasing={{7}: (5, {})} | custom-call | flops 1200000000 | bytes 8388608 | tf_op jit(solution)/shard_map/layer/pallas_call | solution.py:308
  22.7 0.6 %collective-permute-start.1 = (bf16[2,16,32,128]{3,2,1,0:T(8,128)(2,1)S(1)}, bf16[2,16,32,128]{3,2,1,0:T(8,128)(2,1)S(1)}, u32[]{:S(2)}, u32[]{:S(2)}) collective-permute-start(bf16[2,16,32,128]{3,2,1,0:T(8,128)(2,1)S(1)} %get-tuple-element.60), channel_id=1, source_target_pairs={{0,1},{1,0},{2,3},{3,2},{4,5},{5,4},{6,7},{7,6},{8,9},{9,8},{10,11... | collective-permute-start | bytes 786440 | tf_op jit(solution)/shard_map/ppermute | solution.py:534
  23.2 0.1 collective-permute-start.3
  23.3 1.0 %weight_grads.1 = (bf16[2048,256]{1,0:T(8,128)(2,1)}, bf16[256,256]{1,0:T(8,128)(2,1)S(1)}) custom-call(bf16[2048,256]{1,0:T(8,128)(2,1)S(1)} %get-tuple-element.54.smooth, bf16[2048,256]{1,0:T(8,128)(2,1)S(1)} %get-tuple-element.55.grad_pre, bf16[2048,256]{1,0:T(8,128)(2,1)S(1)} %get-tuple-element.56.both), custom_call_target="tpu_custom_call" | custom-call | flops 268435456 | bytes 4194304 | tf_op jit(solution)/shard_map/weight_grads/pallas_call | solution.py:342
  24.4 1.6 %collective-permute-start.2 = (bf16[16,32,128]{2,1,0:T(8,128)(2,1)S(1)}, bf16[16,32,128]{2,1,0:T(8,128)(2,1)S(1)}, u32[]{:S(2)}, u32[]{:S(2)}) collective-permute-start(bf16[16,32,128]{2,1,0:T(8,128)(2,1)S(1)} %fusion), channel_id=1, source_target_pairs={{0,2},{1,3},{2,0},{3,1},{4,6},{5,7},{6,4},{7,5},{8,10},{9,11},{10,... | collective-permute-start | bytes 393224 | tf_op jit(solution)/shard_map/ppermute | solution.py:534
  26.0 1.7 %collective-permute-start.4 = (bf16[256,256]{1,0:T(8,128)(2,1)S(1)}, bf16[256,256]{1,0:T(8,128)(2,1)S(1)}, u32[]{:S(2)}, u32[]{:S(2)}) collective-permute-start(bf16[256,256]{1,0:T(8,128)(2,1)S(1)} %get-tuple-element.70), channel_id=1, source_target_pairs={{0,16},{4,20},{8,24},{12,28},{16,0},{20,4},{24,8},{28,12},{1,17},{... | collective-permute-start | bytes 393224 | tf_op jit(solution)/shard_map/ppermute | solution.py:534
  27.8 0.6 %collective-permute-start.5 = (bf16[16,32,128]{2,1,0:T(8,128)(2,1)S(1)}, bf16[16,32,128]{2,1,0:T(8,128)(2,1)S(1)}, u32[]{:S(2)}, u32[]{:S(2)}) collective-permute-start(bf16[16,32,128]{2,1,0:T(8,128)(2,1)S(1)} %fusion.1), channel_id=1, source_target_pairs={{0,2},{1,3},{2,0},{3,1},{4,6},{5,7},{6,4},{7,5},{8,10},{9,11},{10,... | collective-permute-start | bytes 393224 | tf_op jit(solution)/shard_map/ppermute | solution.py:534
  28.3 2.0 %collective-permute-done.2.came = bf16[16,32,128]{2,1,0:T(8,128)(2,1)S(1)} collective-permute-done((bf16[16,32,128]{2,1,0:T(8,128)(2,1)S(1)}, bf16[16,32,128]{2,1,0:T(8,128)(2,1)S(1)}, u32[]{:S(2)}, u32[]{:S(2)}) %collective-permute-start.2) | collective-permute-done | bytes 131104 | tf_op jit(solution)/shard_map/ppermute | solution.py:534
  30.3 1.0 %outer_back.1 = (bf16[16,32,128]{2,1,0:T(8,128)(2,1)S(1)}, f32[16,32,128]{2,1,0:T(8,128)S(1)}, bf16[8,3,32,128]{3,2,1,0:T(8,128)(2,1)}) custom-call(s32[1,24]{1,0:T(1,128)S(4)} %get-tuple-element.41.outer_rows, s32[1,8]{1,0:T(1,128)S(4)} %get-tuple-element.42.live, bf16[2,16,32,128]{3,2,1,0:T(8,128)(2,1)S(1)} %get-tuple-element.59.keep, ...), custom_call_target="tpu_custom_call" | custom-call | flops 25165824 | bytes 2097152 | tf_op jit(solution)/shard_map/outer_back/pallas_call | solution.py:381
  31.3 5.4 %all-to-all-start.1 = ((bf16[8,3,32,128]{3,2,1,0:T(8,128)(2,1)}), bf16[8,3,32,128]{3,2,1,0:T(8,128)(2,1)S(1)}, u32[]{:S(2)}, u32[]{:S(2)}) async-start(bf16[8,3,32,128]{3,2,1,0:T(8,128)(2,1)} %get-tuple-element.65), calls=%async_computation.1 | async-start | bytes 393216 | tf_op jit(solution)/shard_map/all_to_all | solution.py:43
  36.8 1.5 %collective-permute-start.9 = (bf16[256,256]{1,0:T(8,128)(2,1)S(1)}, bf16[256,256]{1,0:T(8,128)(2,1)S(1)}, u32[]{:S(2)}, u32[]{:S(2)}) collective-permute-start(bf16[256,256]{1,0:T(8,128)(2,1)S(1)} %add_convert_fusion.a), channel_id=1, source_target_pairs={{0,4},{4,0},{8,12},{12,8},{16,20},{20,16},{24,28},{28,24},{1,5},{5... | collective-permute-start | bytes 393224 | tf_op jit(solution)/shard_map/ppermute | solution.py:534
  38.3 2.1 %inner_back.1.total = f32[16,32,128]{2,1,0:T(8,128)S(1)} custom-call(s32[1,64]{1,0:T(1,128)S(4)} %get-tuple-element.66.rows, s32[1,64]{1,0:T(1,128)S(4)} %get-tuple-element.67.cols, bf16[16,32,128]{2,1,0:T(8,128)(2,1)S(1)} %get-tuple-element.68.scaled, f32[16,32,128]{2,1,0:T(8,128)S(1)} %get-tuple-element.72.base, bf16[64,128,128]{2,1,0:T(8,128)(2,1)} %bitcast.9), custom_call_target="tpu_custom_call" | custom-call | flops 67108864 | bytes 3145728 | tf_op jit(solution)/shard_map/inner_back/pallas_call | solution.py:415
  40.5 0.9 %all-to-all-done.1.returned = bf16[8,3,32,128]{3,2,1,0:T(8,128)(2,1)S(1)} async-done(((bf16[8,3,32,128]{3,2,1,0:T(8,128)(2,1)}), bf16[8,3,32,128]{3,2,1,0:T(8,128)(2,1)S(1)}, u32[]{:S(2)}, u32[]{:S(2)}) %all-to-all-start.1) | async-done | bytes 196640 | tf_op jit(solution)/shard_map/all_to_all | solution.py:43
  41.3 0.1 add_returned.1.mine
  41.5 1.7 %collective-permute-start.6 = (bf16[16,32,128]{2,1,0:T(8,128)(2,1)S(1)}, bf16[16,32,128]{2,1,0:T(8,128)(2,1)S(1)}, u32[]{:S(2)}, u32[]{:S(2)}) collective-permute-start(bf16[16,32,128]{2,1,0:T(8,128)(2,1)S(1)} %add_returned.1.mine), channel_id=1, source_target_pairs={{0,2},{1,3},{2,0},{3,1},{4,6},{5,7},{6,4},{7,5},{8,10},{9,11},{10,... | collective-permute-start | bytes 393224 | tf_op jit(solution)/shard_map/ppermute | solution.py:534
  43.2 1.5 %collective-permute-start.10 = (bf16[256,256]{1,0:T(8,128)(2,1)S(1)}, bf16[256,256]{1,0:T(8,128)(2,1)S(1)}, u32[]{:S(2)}, u32[]{:S(2)}) collective-permute-start(bf16[256,256]{1,0:T(8,128)(2,1)S(1)} %pair_sum.1.grads), channel_id=1, source_target_pairs={{0,8},{4,12},{8,0},{12,4},{16,24},{20,28},{24,16},{28,20},{1,9},{5... | collective-permute-start | bytes 393224 | tf_op jit(solution)/shard_map/ppermute | solution.py:534
  44.7 1.8 %collective-permute-done.6.across = bf16[16,32,128]{2,1,0:T(8,128)(2,1)S(1)} collective-permute-done((bf16[16,32,128]{2,1,0:T(8,128)(2,1)S(1)}, bf16[16,32,128]{2,1,0:T(8,128)(2,1)S(1)}, u32[]{:S(2)}, u32[]{:S(2)}) %collective-permute-start.6) | collective-permute-done | bytes 131104 | tf_op jit(solution)/shard_map/ppermute | solution.py:534
  46.5 1.8 %collective-permute-done.10.grads_came = bf16[256,256]{1,0:T(8,128)(2,1)S(1)} collective-permute-done((bf16[256,256]{1,0:T(8,128)(2,1)S(1)}, bf16[256,256]{1,0:T(8,128)(2,1)S(1)}, u32[]{:S(2)}, u32[]{:S(2)}) %collective-permute-start.10) | collective-permute-done | bytes 131104 | tf_op jit(solution)/shard_map/ppermute | solution.py:534
  48.3 1.3 %finish.1 = (f32[2048,128]{1,0:T(8,128)}, f32[128,256]{1,0:T(8,128)}, f32[128,256]{1,0:T(8,128)}) custom-call(bf16[16,32,128]{2,1,0:T(8,128)(2,1)S(1)} %add_returned.1.mine, bf16[16,32,128]{2,1,0:T(8,128)(2,1)S(1)} %collective-permute-done.6.across, bf16[16,32,128]{2,1,0:T(8,128)(2,1)S(1)} %collective-permute-done.7.beside, ...), custom_call_target="tpu_custom_call" | custom-call | flops 67108864 | bytes 2097152 | tf_op jit(solution)/shard_map/finish/pallas_call | solution.py:517
  (16 shorter events, 0.3 us)
Async XLA Ops:
  2.4 17.0 %all-to-all-start = ((bf16[8,3,64,128]{3,2,1,0:T(8,128)(2,1)}), bf16[8,3,64,128]{3,2,1,0:T(8,128)(2,1)S(1)}, u32[]{:S(2)}, u32[]{:S(2)}) async-start(bf16[8,3,64,128]{3,2,1,0:T(8,128)(2,1)} %gather_halves.1), calls=%async_computation | async-start | bytes 786432 | tf_op jit(solution)/shard_map/all_to_all | solution.py:43
  19.4 1.8 %collective-permute-start = (bf16[8,3,64,128]{3,2,1,0:T(8,128)(2,1)S(1)}, bf16[8,3,64,128]{3,2,1,0:T(8,128)(2,1)S(1)}, u32[]{:S(2)}, u32[]{:S(2)}) collective-permute-start(bf16[8,3,64,128]{3,2,1,0:T(8,128)(2,1)S(1)} %all-to-all-done.own), channel_id=1, source_target_pairs={{0,1},{1,0},{2,3},{3,2},{4,5},{5,4},{6,7},{7,6},{8,9},{9,8},{10,11... | collective-permute-start | bytes 1179656 | tf_op jit(solution)/shard_map/ppermute | solution.py:534
  22.7 1.7 %collective-permute-start.1 = (bf16[2,16,32,128]{3,2,1,0:T(8,128)(2,1)S(1)}, bf16[2,16,32,128]{3,2,1,0:T(8,128)(2,1)S(1)}, u32[]{:S(2)}, u32[]{:S(2)}) collective-permute-start(bf16[2,16,32,128]{3,2,1,0:T(8,128)(2,1)S(1)} %get-tuple-element.60), channel_id=1, source_target_pairs={{0,1},{1,0},{2,3},{3,2},{4,5},{5,4},{6,7},{7,6},{8,9},{9,8},{10,11... | collective-permute-start | bytes 786440 | tf_op jit(solution)/shard_map/ppermute | solution.py:534
  23.2 4.5 %collective-permute-start.3 = (bf16[2,16,32,128]{3,2,1,0:T(8,128)(2,1)S(1)}, bf16[2,16,32,128]{3,2,1,0:T(8,128)(2,1)S(1)}, u32[]{:S(2)}, u32[]{:S(2)}) collective-permute-start(bf16[2,16,32,128]{3,2,1,0:T(8,128)(2,1)S(1)} %get-tuple-element.64), channel_id=1, source_target_pairs={{0,1},{1,0},{2,3},{3,2},{4,5},{5,4},{6,7},{7,6},{8,9},{9,8},{10,11... | collective-permute-start | bytes 786440 | tf_op jit(solution)/shard_map/ppermute | solution.py:534
  24.4 5.9 %collective-permute-start.2 = (bf16[16,32,128]{2,1,0:T(8,128)(2,1)S(1)}, bf16[16,32,128]{2,1,0:T(8,128)(2,1)S(1)}, u32[]{:S(2)}, u32[]{:S(2)}) collective-permute-start(bf16[16,32,128]{2,1,0:T(8,128)(2,1)S(1)} %fusion), channel_id=1, source_target_pairs={{0,2},{1,3},{2,0},{3,1},{4,6},{5,7},{6,4},{7,5},{8,10},{9,11},{10,... | collective-permute-start | bytes 393224 | tf_op jit(solution)/shard_map/ppermute | solution.py:534
  26.0 10.7 %collective-permute-start.4 = (bf16[256,256]{1,0:T(8,128)(2,1)S(1)}, bf16[256,256]{1,0:T(8,128)(2,1)S(1)}, u32[]{:S(2)}, u32[]{:S(2)}) collective-permute-start(bf16[256,256]{1,0:T(8,128)(2,1)S(1)} %get-tuple-element.70), channel_id=1, source_target_pairs={{0,16},{4,20},{8,24},{12,28},{16,0},{20,4},{24,8},{28,12},{1,17},{... | collective-permute-start | bytes 393224 | tf_op jit(solution)/shard_map/ppermute | solution.py:534
  27.8 9.0 %collective-permute-start.5 = (bf16[16,32,128]{2,1,0:T(8,128)(2,1)S(1)}, bf16[16,32,128]{2,1,0:T(8,128)(2,1)S(1)}, u32[]{:S(2)}, u32[]{:S(2)}) collective-permute-start(bf16[16,32,128]{2,1,0:T(8,128)(2,1)S(1)} %fusion.1), channel_id=1, source_target_pairs={{0,2},{1,3},{2,0},{3,1},{4,6},{5,7},{6,4},{7,5},{8,10},{9,11},{10,... | collective-permute-start | bytes 393224 | tf_op jit(solution)/shard_map/ppermute | solution.py:534
  31.3 10.0 %all-to-all-start.1 = ((bf16[8,3,32,128]{3,2,1,0:T(8,128)(2,1)}), bf16[8,3,32,128]{3,2,1,0:T(8,128)(2,1)S(1)}, u32[]{:S(2)}, u32[]{:S(2)}) async-start(bf16[8,3,32,128]{3,2,1,0:T(8,128)(2,1)} %get-tuple-element.65), calls=%async_computation.1 | async-start | bytes 393216 | tf_op jit(solution)/shard_map/all_to_all | solution.py:43
  36.8 6.4 %collective-permute-start.9 = (bf16[256,256]{1,0:T(8,128)(2,1)S(1)}, bf16[256,256]{1,0:T(8,128)(2,1)S(1)}, u32[]{:S(2)}, u32[]{:S(2)}) collective-permute-start(bf16[256,256]{1,0:T(8,128)(2,1)S(1)} %add_convert_fusion.a), channel_id=1, source_target_pairs={{0,4},{4,0},{8,12},{12,8},{16,20},{20,16},{24,28},{28,24},{1,5},{5... | collective-permute-start | bytes 393224 | tf_op jit(solution)/shard_map/ppermute | solution.py:534
  41.5 5.0 %collective-permute-start.6 = (bf16[16,32,128]{2,1,0:T(8,128)(2,1)S(1)}, bf16[16,32,128]{2,1,0:T(8,128)(2,1)S(1)}, u32[]{:S(2)}, u32[]{:S(2)}) collective-permute-start(bf16[16,32,128]{2,1,0:T(8,128)(2,1)S(1)} %add_returned.1.mine), channel_id=1, source_target_pairs={{0,2},{1,3},{2,0},{3,1},{4,6},{5,7},{6,4},{7,5},{8,10},{9,11},{10,... | collective-permute-start | bytes 393224 | tf_op jit(solution)/shard_map/ppermute | solution.py:534
  43.2 5.0 %collective-permute-start.10 = (bf16[256,256]{1,0:T(8,128)(2,1)S(1)}, bf16[256,256]{1,0:T(8,128)(2,1)S(1)}, u32[]{:S(2)}, u32[]{:S(2)}) collective-permute-start(bf16[256,256]{1,0:T(8,128)(2,1)S(1)} %pair_sum.1.grads), channel_id=1, source_target_pairs={{0,8},{4,12},{8,0},{12,4},{16,24},{20,28},{24,16},{28,20},{1,9},{5... | collective-permute-start | bytes 393224 | tf_op jit(solution)/shard_map/ppermute | solution.py:534
  44.7 3.5 %collective-permute-start.7 = (bf16[16,32,128]{2,1,0:T(8,128)(2,1)S(1)}, bf16[16,32,128]{2,1,0:T(8,128)(2,1)S(1)}, u32[]{:S(2)}, u32[]{:S(2)}) collective-permute-start(bf16[16,32,128]{2,1,0:T(8,128)(2,1)S(1)} %add_returned.1.mine), channel_id=1, source_target_pairs={{0,1},{1,0},{2,3},{3,2},{4,5},{5,4},{6,7},{7,6},{8,9},{9,8},{10,11... | collective-permute-start | bytes 393224 | tf_op jit(solution)/shard_map/ppermute | solution.py:534
  46.5 1.8 %collective-permute-start.8 = (bf16[16,32,128]{2,1,0:T(8,128)(2,1)S(1)}, bf16[16,32,128]{2,1,0:T(8,128)(2,1)S(1)}, u32[]{:S(2)}, u32[]{:S(2)}) collective-permute-start(bf16[16,32,128]{2,1,0:T(8,128)(2,1)S(1)} %collective-permute-done.6.across), channel_id=1, source_target_pairs={{0,1},{1,0},{2,3},{3,2},{4,5},{5,4},{6,7},{7,6},{8,9},{9,8},{10,11... | collective-permute-start | bytes 393224 | tf_op jit(solution)/shard_map/ppermute | solution.py:534

commit v10 on v9

--- a/solution.py
+++ b/solution.py
@@ -27,7 +27,7 @@
     return [pltpu.with_memory_space_constraint(x, pltpu.HBM) for x in arrays]
 
 
-OUT_ORDER = (4, 7, 3, 5, 2, 1, 0, 6)
+OUT_ORDER = (4, 7, 3, 2, 0, 1, 5, 6)
 BACK_ORDER = (4, 2, 5, 3, 1, 0, 7, 6)
 
 
@@ -107,8 +107,8 @@
 
 def stage_kernel(
     rows_far, cols_far, outer_rows_far, live_far, targets_far, feat_far, inner_far, outer_far,
-    rows, cols, outer_rows, live, targets, total, over, over_rows,
-    feat, inner, outer, wide, degree_rows, sems, inner_sems,
+    rows, cols, outer_rows, live, targets, total, over, over_rows, feat,
+    inner, outer, wide, degree_rows, sems, inner_sems,
 ):
     loc, block, feat_width = total.shape
     count, outer_count = inner.shape[0], outer.shape[0]
@@ -184,11 +184,11 @@
     return pl.pallas_call(
         stage_kernel,
         out_shape=tuple(pltpu.SMEM(x.shape, jnp.int32) for x in scalars)
-        + (pltpu.VMEM(sums, F32), pltpu.VMEM(sums, F32), pltpu.VMEM((loc, 8, block), F32)),
+        + (pltpu.VMEM(sums, F32), pltpu.VMEM(sums, F32), pltpu.VMEM((loc, 8, block), F32))
+        + (pltpu.VMEM(features.shape, BF16),),
         in_specs=[FAR] * 8,
-        out_specs=(SCALARS,) * 5 + (WHOLE,) * 3,
+        out_specs=(SCALARS,) * 5 + (WHOLE,) * 4,
         scratch_shapes=[
-            pltpu.VMEM(features.shape, BF16),
             pltpu.VMEM(inner.shape, BF16),
             pltpu.VMEM(outer.shape, BF16),
             pltpu.VMEM((loc, block, 2 * feat_width), BF16),
@@ -203,15 +203,15 @@
 
 
 def fetch_kernel(
-    outer_far, feat_far, cot_far, self_far, neigh_far, outer, feat, cot, weights, turned, w_self, w_neigh, sems
+    outer_far, cot_far, self_far, neigh_far, outer, cot, weights, turned, w_self, w_neigh, sems
 ):
-    feat_width = feat.shape[1]
+    feat_width = w_self.shape[0]
     part = feat_width // lax.axis_size("grp")
     me = lax.axis_index("grp")
     fetches = [
         pltpu.make_async_copy(source, place, sems.at[k])
         for k, (source, place) in enumerate((
-            (self_far, w_self), (neigh_far, w_neigh), (outer_far, outer), (feat_far, feat), (cot_far, cot),
+            (self_far, w_self), (neigh_far, w_neigh), (outer_far, outer), (cot_far, cot),
         ))
     ]
     for fetch in fetches:
@@ -228,22 +228,22 @@
         fetch.wait()
 
 
-def fetch(outer, features, cotangent, w_self, w_neigh):
-    both = (2 * features.shape[1], w_self.shape[1])
+def fetch(outer, cotangent, w_self, w_neigh):
+    both = (2 * w_self.shape[0], w_self.shape[1])
     return pl.pallas_call(
         fetch_kernel,
-        out_shape=tuple(pltpu.VMEM(shape, BF16) for shape in (outer.shape, features.shape, cotangent.shape, both, both)),
-        in_specs=[FAR] * 5,
-        out_specs=(WHOLE,) * 5,
+        out_shape=tuple(pltpu.VMEM(shape, BF16) for shape in (outer.shape, cotangent.shape, both, both)),
+        in_specs=[FAR] * 4,
+        out_specs=(WHOLE,) * 4,
         scratch_shapes=[
             pltpu.VMEM(w_self.shape, BF16),
             pltpu.VMEM(w_neigh.shape, BF16),
-            pltpu.SemaphoreType.DMA((5,)),
+            pltpu.SemaphoreType.DMA((4,)),
         ],
         compiler_params=params(8 + outer.size * 2 / MIB),
         cost_estimate=cost(1e6, 3 * MIB),
         name="fetch",
-    )(*far(outer, features, cotangent, w_self, w_neigh))
+    )(*far(outer, cotangent, w_self, w_neigh))
 
 
 def layer_kernel(
@@ -555,12 +555,12 @@
 
     out_order, back_order = order_of(OUT_ORDER, peers), order_of(BACK_ORDER, peers)
     own = exchange(gather_halves(features, targets, block, out_order), out_order)
-    rows, cols, outer_rows, live, targets, total, over, over_rows = stage(
+    rows, cols, outer_rows, live, targets, total, over, over_rows, features = stage(
         inner_rows, inner_cols, outer_rows, live_count, targets, features, inner_a, outer_a
     )
     own, total, outer_a = lax.optimization_barrier((own, total, outer_a))
     other = swap(own, "grp", 1)
-    outer_a, features, cotangent, weights, turned = fetch(outer_a, features, cotangent, weight_self, weight_neigh)
+    outer_a, cotangent, weights, turned = fetch(outer_a, cotangent, weight_self, weight_neigh)
     smooth, grad_pre, both, send_n, keep_n, send_s, keep_s = layer(
         outer_rows, live, own, other, outer_a, total, over, over_rows, features, cotangent, weights, turned, out_order
     )

time: 50 us -> 49.7 us (level)
  starting transfers between devices: 22.5 us -> 21.8 us
  waiting for transfers between devices: 9.95 us -> 10.5 us
    ppermute x11, waiting for transfers between devices: 5.57 us -> 6.09 us  [swap(): lax.ppermute(x, axis, [(i, i ^ bit) for i in range(lax.axis_size(axis))])]
  transfers between devices with their start and end apart: 13 -> 13, of which waited for: 6 -> 6; matrix products, arithmetic and copies ran while one was open for 0% -> 0% of each run, Pallas kernels for 24% -> 23%
where the time goes in v10:
time: 49.7 us; the launch traced here: 49.2 us
  starting transfers between devices  21.8 us (44%)
  Pallas kernels  16.1 us (32%)
  waiting for transfers between devices  10.5 us (21%)
  between operations  0.73 us (1%)
    all_to_all x2, starting transfers between devices, exchange(): lax.all_to_all(x, 'dom', split_axis=0, concat_axis=0, tiled=True, axis_in...  12.9 us
    ppermute x11, starting transfers between devices, swap(): lax.ppermute(x, axis, [(i, i ^ bit) for i in range(lax.axis_size(axis))])  8.88 us
    ppermute x11, waiting for transfers between devices, swap(): lax.ppermute(x, axis, [(i, i ^ bit) for i in range(lax.axis_size(axis))])  6.09 us
    pallas_call x1, Pallas kernels, stage(): pl.pallas_call(stage_kernel, out_shape=tuple((pltpu.SMEM(x.shape, jnp.int...  5.63 us
    all_to_all x2, waiting for transfers between devices, exchange(): lax.all_to_all(x, 'dom', split_axis=0, concat_axis=0, tiled=True, axis_in...  4.43 us
    pallas_call x1, Pallas kernels, inner_back(): pl.pallas_call(inner_back_kernel, out_shape=pltpu.VMEM(base.shape, F32),...  2.11 us
    pallas_call x1, Pallas kernels, gather_halves(): pl.pallas_call(functools.partial(gather_kernel, order), out_shape=jax.Sha...  1.73 us
    pallas_call x1, Pallas kernels, fetch(): pl.pallas_call(fetch_kernel, out_shape=tuple((pltpu.VMEM(shape, BF16) for...  1.57 us
  transfers between devices with their start and end apart: 13, of which 6 were waited for; matrix products, arithmetic and copies ran while one was open for 0% of the time, Pallas kernels for 23%

profile of v10, /device:TPU:0, one launch (start us, length us, event | category | flops | bytes accessed | tf_op | source)
XLA Modules:
  0.0 49.2 jit_solution(6122853053779984135)
XLA Ops:
  0.6 1.7 %gather_halves.1 = bf16[8,3,64,128]{3,2,1,0:T(8,128)(2,1)} custom-call(s32[3,1,8]{2,1,0:T(1,128)} %bitcast.13, bf16[16,2,64,128]{3,2,1,0:T(8,128)(2,1)} %bitcast.12), custom_call_target="tpu_custom_call" | custom-call | tf_op jit(solution)/shard_map/gather_halves/pallas_call | solution.py:91
  2.4 7.8 %all-to-all-start = ((bf16[8,3,64,128]{3,2,1,0:T(8,128)(2,1)}), bf16[8,3,64,128]{3,2,1,0:T(8,128)(2,1)S(1)}, u32[]{:S(2)}, u32[]{:S(2)}) async-start(bf16[8,3,64,128]{3,2,1,0:T(8,128)(2,1)} %gather_halves.1), calls=%async_computation | async-start | bytes 786432 | tf_op jit(solution)/shard_map/all_to_all | solution.py:43
  10.2 5.6 %stage.1 = (s32[1,64]{1,0:T(1,128)S(4)}, s32[1,64]{1,0:T(1,128)S(4)}, s32[1,24]{1,0:T(1,128)S(4)}, s32[1,8]{1,0:T(1,128)S(4)}, s32[3,1,8]{2,1,0:T(1,128)S(4)}, /...) custom-call(s32[1,64]{1,0:T(1,128)} %rows_far.1, ...), custom_call_target="tpu_custom_call" | custom-call | flops 536870912 | bytes 6291456 | tf_op jit(solution)/shard_map/stage/pallas_call | solution.py:184
  15.8 3.6 %all-to-all-done.own = bf16[8,3,64,128]{3,2,1,0:T(8,128)(2,1)S(1)} async-done(((bf16[8,3,64,128]{3,2,1,0:T(8,128)(2,1)}), bf16[8,3,64,128]{3,2,1,0:T(8,128)(2,1)S(1)}, u32[]{:S(2)}, u32[]{:S(2)}) %all-to-all-start) | async-done | bytes 393248 | tf_op jit(solution)/shard_map/all_to_all | solution.py:43
  19.4 1.6 %fetch.1 = (bf16[24,128,128]{2,1,0:T(8,128)(2,1)S(1)}, bf16[2048,256]{1,0:T(8,128)(2,1)S(1)}, bf16[256,256]{1,0:T(8,128)(2,1)S(1)}, bf16[256,256]{1,0:T(8,128)(2,1)S(1)}) custom-call(bf16[24,128,128]{2,1,0:T(8,128)(2,1)} %bitcast.11, bf16[2048,256]{1,0:T(8,128)(2,1)} %cot_far.1, bf16[128,256]{1,0:T(8,128)(2,1)} %self_far.1, bf16[128,256]{1,0:T(8,128)(2,1)} %neigh_far.1), custom_call_target="tpu_custom_call" | custom-call | flops 1000000 | bytes 3145728 | tf_op jit(solution)/shard_map/fetch/pallas_call | solution.py:233
  21.0 0.1 collective-permute-done.other
  21.1 1.5 %layer.1 = (bf16[2048,256]{1,0:T(8,128)(2,1)S(1)}, bf16[2048,256]{1,0:T(8,128)(2,1)S(1)}, bf16[2048,256]{1,0:T(8,128)(2,1)S(1)}, bf16[2,16,32,128]{3,2,1,0:T(8,1...) custom-call(s32[1,24]{1,0:T(1,128)S(4)} %get-tuple-element.41.outer_, ...), custom_call_target="tpu_custom_call", output_to_operand_aliasing={{7}: (5, {})} | custom-call | flops 1200000000 | bytes 8388608 | tf_op jit(solution)/shard_map/layer/pallas_call | solution.py:308
  22.7 0.5 collective-permute-start.1
  23.2 1.0 %weight_grads.1 = (bf16[2048,256]{1,0:T(8,128)(2,1)}, bf16[256,256]{1,0:T(8,128)(2,1)S(1)}) custom-call(bf16[2048,256]{1,0:T(8,128)(2,1)S(1)} %get-tuple-element.54.smooth, bf16[2048,256]{1,0:T(8,128)(2,1)S(1)} %get-tuple-element.55.grad_pre, bf16[2048,256]{1,0:T(8,128)(2,1)S(1)} %get-tuple-element.56.both), custom_call_target="tpu_custom_call" | custom-call | flops 268435456 | bytes 4194304 | tf_op jit(solution)/shard_map/weight_grads/pallas_call | solution.py:342
  24.3 1.6 %collective-permute-start.2 = (bf16[16,32,128]{2,1,0:T(8,128)(2,1)S(1)}, bf16[16,32,128]{2,1,0:T(8,128)(2,1)S(1)}, u32[]{:S(2)}, u32[]{:S(2)}) collective-permute-start(bf16[16,32,128]{2,1,0:T(8,128)(2,1)S(1)} %fusion), channel_id=1, source_target_pairs={{0,2},{1,3},{2,0},{3,1},{4,6},{5,7},{6,4},{7,5},{8,10},{9,11},{10,... | collective-permute-start | bytes 393224 | tf_op jit(solution)/shard_map/ppermute | solution.py:534
  25.9 1.5 %collective-permute-start.4 = (bf16[256,256]{1,0:T(8,128)(2,1)S(1)}, bf16[256,256]{1,0:T(8,128)(2,1)S(1)}, u32[]{:S(2)}, u32[]{:S(2)}) collective-permute-start(bf16[256,256]{1,0:T(8,128)(2,1)S(1)} %get-tuple-element.70), channel_id=1, source_target_pairs={{0,16},{4,20},{8,24},{12,28},{16,0},{20,4},{24,8},{28,12},{1,17},{... | collective-permute-start | bytes 393224 | tf_op jit(solution)/shard_map/ppermute | solution.py:534
  27.4 0.6 %collective-permute-start.5 = (bf16[16,32,128]{2,1,0:T(8,128)(2,1)S(1)}, bf16[16,32,128]{2,1,0:T(8,128)(2,1)S(1)}, u32[]{:S(2)}, u32[]{:S(2)}) collective-permute-start(bf16[16,32,128]{2,1,0:T(8,128)(2,1)S(1)} %fusion.1), channel_id=1, source_target_pairs={{0,2},{1,3},{2,0},{3,1},{4,6},{5,7},{6,4},{7,5},{8,10},{9,11},{10,... | collective-permute-start | bytes 393224 | tf_op jit(solution)/shard_map/ppermute | solution.py:534
  28.0 2.4 %collective-permute-done.2.came = bf16[16,32,128]{2,1,0:T(8,128)(2,1)S(1)} collective-permute-done((bf16[16,32,128]{2,1,0:T(8,128)(2,1)S(1)}, bf16[16,32,128]{2,1,0:T(8,128)(2,1)S(1)}, u32[]{:S(2)}, u32[]{:S(2)}) %collective-permute-start.2) | collective-permute-done | bytes 131104 | tf_op jit(solution)/shard_map/ppermute | solution.py:534
  30.4 1.0 %outer_back.1 = (bf16[16,32,128]{2,1,0:T(8,128)(2,1)S(1)}, f32[16,32,128]{2,1,0:T(8,128)S(1)}, bf16[8,3,32,128]{3,2,1,0:T(8,128)(2,1)}) custom-call(s32[1,24]{1,0:T(1,128)S(4)} %get-tuple-element.41.outer_rows, s32[1,8]{1,0:T(1,128)S(4)} %get-tuple-element.42.live, bf16[2,16,32,128]{3,2,1,0:T(8,128)(2,1)S(1)} %get-tuple-element.59.keep, ...), custom_call_target="tpu_custom_call" | custom-call | flops 25165824 | bytes 2097152 | tf_op jit(solution)/shard_map/outer_back/pallas_call | solution.py:381
  31.4 5.1 %all-to-all-start.1 = ((bf16[8,3,32,128]{3,2,1,0:T(8,128)(2,1)}), bf16[8,3,32,128]{3,2,1,0:T(8,128)(2,1)S(1)}, u32[]{:S(2)}, u32[]{:S(2)}) async-start(bf16[8,3,32,128]{3,2,1,0:T(8,128)(2,1)} %get-tuple-element.65), calls=%async_computation.1 | async-start | bytes 393216 | tf_op jit(solution)/shard_map/all_to_all | solution.py:43
  36.5 1.5 %collective-permute-start.9 = (bf16[256,256]{1,0:T(8,128)(2,1)S(1)}, bf16[256,256]{1,0:T(8,128)(2,1)S(1)}, u32[]{:S(2)}, u32[]{:S(2)}) collective-permute-start(bf16[256,256]{1,0:T(8,128)(2,1)S(1)} %add_convert_fusion.a), channel_id=1, source_target_pairs={{0,4},{4,0},{8,12},{12,8},{16,20},{20,16},{24,28},{28,24},{1,5},{5... | collective-permute-start | bytes 393224 | tf_op jit(solution)/shard_map/ppermute | solution.py:534
  38.1 2.1 %inner_back.1.total = f32[16,32,128]{2,1,0:T(8,128)S(1)} custom-call(s32[1,64]{1,0:T(1,128)S(4)} %get-tuple-element.66.rows, s32[1,64]{1,0:T(1,128)S(4)} %get-tuple-element.67.cols, bf16[16,32,128]{2,1,0:T(8,128)(2,1)S(1)} %get-tuple-element.68.scaled, f32[16,32,128]{2,1,0:T(8,128)S(1)} %get-tuple-element.72.base, bf16[64,128,128]{2,1,0:T(8,128)(2,1)} %bitcast.9), custom_call_target="tpu_custom_call" | custom-call | flops 67108864 | bytes 3145728 | tf_op jit(solution)/shard_map/inner_back/pallas_call | solution.py:415
  40.2 0.9 %all-to-all-done.1.returned = bf16[8,3,32,128]{3,2,1,0:T(8,128)(2,1)S(1)} async-done(((bf16[8,3,32,128]{3,2,1,0:T(8,128)(2,1)}), bf16[8,3,32,128]{3,2,1,0:T(8,128)(2,1)S(1)}, u32[]{:S(2)}, u32[]{:S(2)}) %all-to-all-start.1) | async-done | bytes 196640 | tf_op jit(solution)/shard_map/all_to_all | solution.py:43
  41.1 0.1 add_returned.1.mine
  41.2 1.6 %collective-permute-start.6 = (bf16[16,32,128]{2,1,0:T(8,128)(2,1)S(1)}, bf16[16,32,128]{2,1,0:T(8,128)(2,1)S(1)}, u32[]{:S(2)}, u32[]{:S(2)}) collective-permute-start(bf16[16,32,128]{2,1,0:T(8,128)(2,1)S(1)} %add_returned.1.mine), channel_id=1, source_target_pairs={{0,2},{1,3},{2,0},{3,1},{4,6},{5,7},{6,4},{7,5},{8,10},{9,11},{10,... | collective-permute-start | bytes 393224 | tf_op jit(solution)/shard_map/ppermute | solution.py:534
  42.9 1.5 %collective-permute-start.10 = (bf16[256,256]{1,0:T(8,128)(2,1)S(1)}, bf16[256,256]{1,0:T(8,128)(2,1)S(1)}, u32[]{:S(2)}, u32[]{:S(2)}) collective-permute-start(bf16[256,256]{1,0:T(8,128)(2,1)S(1)} %pair_sum.1.grads), channel_id=1, source_target_pairs={{0,8},{4,12},{8,0},{12,4},{16,24},{20,28},{24,16},{28,20},{1,9},{5... | collective-permute-start | bytes 393224 | tf_op jit(solution)/shard_map/ppermute | solution.py:534
  44.4 1.8 %collective-permute-done.6.across = bf16[16,32,128]{2,1,0:T(8,128)(2,1)S(1)} collective-permute-done((bf16[16,32,128]{2,1,0:T(8,128)(2,1)S(1)}, bf16[16,32,128]{2,1,0:T(8,128)(2,1)S(1)}, u32[]{:S(2)}, u32[]{:S(2)}) %collective-permute-start.6) | collective-permute-done | bytes 131104 | tf_op jit(solution)/shard_map/ppermute | solution.py:534
  46.2 1.7 %collective-permute-done.10.grads_came = bf16[256,256]{1,0:T(8,128)(2,1)S(1)} collective-permute-done((bf16[256,256]{1,0:T(8,128)(2,1)S(1)}, bf16[256,256]{1,0:T(8,128)(2,1)S(1)}, u32[]{:S(2)}, u32[]{:S(2)}) %collective-permute-start.10) | collective-permute-done | bytes 131104 | tf_op jit(solution)/shard_map/ppermute | solution.py:534
  47.9 1.3 %finish.1 = (f32[2048,128]{1,0:T(8,128)}, f32[128,256]{1,0:T(8,128)}, f32[128,256]{1,0:T(8,128)}) custom-call(bf16[16,32,128]{2,1,0:T(8,128)(2,1)S(1)} %add_returned.1.mine, bf16[16,32,128]{2,1,0:T(8,128)(2,1)S(1)} %collective-permute-done.6.across, bf16[16,32,128]{2,1,0:T(8,128)(2,1)S(1)} %collective-permute-done.7.beside, ...), custom_call_target="tpu_custom_call" | custom-call | flops 67108864 | bytes 2097152 | tf_op jit(solution)/shard_map/finish/pallas_call | solution.py:517
  (16 shorter events, 0.3 us)
Async XLA Ops:
  2.4 17.0 %all-to-all-start = ((bf16[8,3,64,128]{3,2,1,0:T(8,128)(2,1)}), bf16[8,3,64,128]{3,2,1,0:T(8,128)(2,1)S(1)}, u32[]{:S(2)}, u32[]{:S(2)}) async-start(bf16[8,3,64,128]{3,2,1,0:T(8,128)(2,1)} %gather_halves.1), calls=%async_computation | async-start | bytes 786432 | tf_op jit(solution)/shard_map/all_to_all | solution.py:43
  19.4 1.7 %collective-permute-start = (bf16[8,3,64,128]{3,2,1,0:T(8,128)(2,1)S(1)}, bf16[8,3,64,128]{3,2,1,0:T(8,128)(2,1)S(1)}, u32[]{:S(2)}, u32[]{:S(2)}) collective-permute-start(bf16[8,3,64,128]{3,2,1,0:T(8,128)(2,1)S(1)} %all-to-all-done.own), channel_id=1, source_target_pairs={{0,1},{1,0},{2,3},{3,2},{4,5},{5,4},{6,7},{7,6},{8,9},{9,8},{10,11... | collective-permute-start | bytes 1179656 | tf_op jit(solution)/shard_map/ppermute | solution.py:534
  22.7 1.6 %collective-permute-start.1 = (bf16[2,16,32,128]{3,2,1,0:T(8,128)(2,1)S(1)}, bf16[2,16,32,128]{3,2,1,0:T(8,128)(2,1)S(1)}, u32[]{:S(2)}, u32[]{:S(2)}) collective-permute-start(bf16[2,16,32,128]{3,2,1,0:T(8,128)(2,1)S(1)} %get-tuple-element.60), channel_id=1, source_target_pairs={{0,1},{1,0},{2,3},{3,2},{4,5},{5,4},{6,7},{7,6},{8,9},{9,8},{10,11... | collective-permute-start | bytes 786440 | tf_op jit(solution)/shard_map/ppermute | solution.py:534
  23.1 4.3 %collective-permute-start.3 = (bf16[2,16,32,128]{3,2,1,0:T(8,128)(2,1)S(1)}, bf16[2,16,32,128]{3,2,1,0:T(8,128)(2,1)S(1)}, u32[]{:S(2)}, u32[]{:S(2)}) collective-permute-start(bf16[2,16,32,128]{3,2,1,0:T(8,128)(2,1)S(1)} %get-tuple-element.64), channel_id=1, source_target_pairs={{0,1},{1,0},{2,3},{3,2},{4,5},{5,4},{6,7},{7,6},{8,9},{9,8},{10,11... | collective-permute-start | bytes 786440 | tf_op jit(solution)/shard_map/ppermute | solution.py:534
  24.3 6.1 %collective-permute-start.2 = (bf16[16,32,128]{2,1,0:T(8,128)(2,1)S(1)}, bf16[16,32,128]{2,1,0:T(8,128)(2,1)S(1)}, u32[]{:S(2)}, u32[]{:S(2)}) collective-permute-start(bf16[16,32,128]{2,1,0:T(8,128)(2,1)S(1)} %fusion), channel_id=1, source_target_pairs={{0,2},{1,3},{2,0},{3,1},{4,6},{5,7},{6,4},{7,5},{8,10},{9,11},{10,... | collective-permute-start | bytes 393224 | tf_op jit(solution)/shard_map/ppermute | solution.py:534
  25.9 10.5 %collective-permute-start.4 = (bf16[256,256]{1,0:T(8,128)(2,1)S(1)}, bf16[256,256]{1,0:T(8,128)(2,1)S(1)}, u32[]{:S(2)}, u32[]{:S(2)}) collective-permute-start(bf16[256,256]{1,0:T(8,128)(2,1)S(1)} %get-tuple-element.70), channel_id=1, source_target_pairs={{0,16},{4,20},{8,24},{12,28},{16,0},{20,4},{24,8},{28,12},{1,17},{... | collective-permute-start | bytes 393224 | tf_op jit(solution)/shard_map/ppermute | solution.py:534
  27.4 9.1 %collective-permute-start.5 = (bf16[16,32,128]{2,1,0:T(8,128)(2,1)S(1)}, bf16[16,32,128]{2,1,0:T(8,128)(2,1)S(1)}, u32[]{:S(2)}, u32[]{:S(2)}) collective-permute-start(bf16[16,32,128]{2,1,0:T(8,128)(2,1)S(1)} %fusion.1), channel_id=1, source_target_pairs={{0,2},{1,3},{2,0},{3,1},{4,6},{5,7},{6,4},{7,5},{8,10},{9,11},{10,... | collective-permute-start | bytes 393224 | tf_op jit(solution)/shard_map/ppermute | solution.py:534
  31.4 9.6 %all-to-all-start.1 = ((bf16[8,3,32,128]{3,2,1,0:T(8,128)(2,1)}), bf16[8,3,32,128]{3,2,1,0:T(8,128)(2,1)S(1)}, u32[]{:S(2)}, u32[]{:S(2)}) async-start(bf16[8,3,32,128]{3,2,1,0:T(8,128)(2,1)} %get-tuple-element.65), calls=%async_computation.1 | async-start | bytes 393216 | tf_op jit(solution)/shard_map/all_to_all | solution.py:43
  36.5 6.3 %collective-permute-start.9 = (bf16[256,256]{1,0:T(8,128)(2,1)S(1)}, bf16[256,256]{1,0:T(8,128)(2,1)S(1)}, u32[]{:S(2)}, u32[]{:S(2)}) collective-permute-start(bf16[256,256]{1,0:T(8,128)(2,1)S(1)} %add_convert_fusion.a), channel_id=1, source_target_pairs={{0,4},{4,0},{8,12},{12,8},{16,20},{20,16},{24,28},{28,24},{1,5},{5... | collective-permute-start | bytes 393224 | tf_op jit(solution)/shard_map/ppermute | solution.py:534
  41.2 5.0 %collective-permute-start.6 = (bf16[16,32,128]{2,1,0:T(8,128)(2,1)S(1)}, bf16[16,32,128]{2,1,0:T(8,128)(2,1)S(1)}, u32[]{:S(2)}, u32[]{:S(2)}) collective-permute-start(bf16[16,32,128]{2,1,0:T(8,128)(2,1)S(1)} %add_returned.1.mine), channel_id=1, source_target_pairs={{0,2},{1,3},{2,0},{3,1},{4,6},{5,7},{6,4},{7,5},{8,10},{9,11},{10,... | collective-permute-start | bytes 393224 | tf_op jit(solution)/shard_map/ppermute | solution.py:534
  42.9 5.0 %collective-permute-start.10 = (bf16[256,256]{1,0:T(8,128)(2,1)S(1)}, bf16[256,256]{1,0:T(8,128)(2,1)S(1)}, u32[]{:S(2)}, u32[]{:S(2)}) collective-permute-start(bf16[256,256]{1,0:T(8,128)(2,1)S(1)} %pair_sum.1.grads), channel_id=1, source_target_pairs={{0,8},{4,12},{8,0},{12,4},{16,24},{20,28},{24,16},{28,20},{1,9},{5... | collective-permute-start | bytes 393224 | tf_op jit(solution)/shard_map/ppermute | solution.py:534
  44.4 3.5 %collective-permute-start.7 = (bf16[16,32,128]{2,1,0:T(8,128)(2,1)S(1)}, bf16[16,32,128]{2,1,0:T(8,128)(2,1)S(1)}, u32[]{:S(2)}, u32[]{:S(2)}) collective-permute-start(bf16[16,32,128]{2,1,0:T(8,128)(2,1)S(1)} %add_returned.1.mine), channel_id=1, source_target_pairs={{0,1},{1,0},{2,3},{3,2},{4,5},{5,4},{6,7},{7,6},{8,9},{9,8},{10,11... | collective-permute-start | bytes 393224 | tf_op jit(solution)/shard_map/ppermute | solution.py:534
  46.2 1.7 %collective-permute-start.8 = (bf16[16,32,128]{2,1,0:T(8,128)(2,1)S(1)}, bf16[16,32,128]{2,1,0:T(8,128)(2,1)S(1)}, u32[]{:S(2)}, u32[]{:S(2)}) collective-permute-start(bf16[16,32,128]{2,1,0:T(8,128)(2,1)S(1)} %collective-permute-done.6.across), channel_id=1, source_target_pairs={{0,1},{1,0},{2,3},{3,2},{4,5},{5,4},{6,7},{7,6},{8,9},{9,8},{10,11... | collective-permute-start | bytes 393224 | tf_op jit(solution)/shard_map/ppermute | solution.py:534

commit v11 on v10

--- a/solution.py
+++ b/solution.py
@@ -211,9 +211,13 @@
     fetches = [
         pltpu.make_async_copy(source, place, sems.at[k])
         for k, (source, place) in enumerate((
-            (self_far, w_self), (neigh_far, w_neigh), (outer_far, outer), (cot_far, cot),
+            (self_far, w_self), (neigh_far, w_neigh), (outer_far, outer),
         ))
     ]
+    rows = cot.shape[0] // 4
+    for k in range(4):
+        place = pl.ds(k * rows, rows)
+        fetches.append(pltpu.make_async_copy(cot_far.at[place], cot.at[place], sems.at[3 + k]))
     for fetch in fetches:
         fetch.start()
     for fetch in fetches[:2]:
@@ -238,7 +242,7 @@
         scratch_shapes=[
             pltpu.VMEM(w_self.shape, BF16),
             pltpu.VMEM(w_neigh.shape, BF16),
-            pltpu.SemaphoreType.DMA((4,)),
+            pltpu.SemaphoreType.DMA((7,)),
         ],
         compiler_params=params(8 + outer.size * 2 / MIB),
         cost_estimate=cost(1e6, 3 * MIB),

time: 49.7 us -> 49.6 us (level)
  no operation moved by 1% of the time
where the time goes in v11:
time: 49.6 us; the launch traced here: 49.2 us
  starting transfers between devices  21.8 us (44%)
  Pallas kernels  16.1 us (32%)
  waiting for transfers between devices  10.5 us (21%)
  between operations  0.74 us (1%)
    all_to_all x2, starting transfers between devices, exchange(): lax.all_to_all(x, 'dom', split_axis=0, concat_axis=0, tiled=True, axis_in...  12.9 us
    ppermute x11, starting transfers between devices, swap(): lax.ppermute(x, axis, [(i, i ^ bit) for i in range(lax.axis_size(axis))])  8.88 us
    ppermute x11, waiting for transfers between devices, swap(): lax.ppermute(x, axis, [(i, i ^ bit) for i in range(lax.axis_size(axis))])  6.06 us
    pallas_call x1, Pallas kernels, stage(): pl.pallas_call(stage_kernel, out_shape=tuple((pltpu.SMEM(x.shape, jnp.int...  5.64 us
    all_to_all x2, waiting for transfers between devices, exchange(): lax.all_to_all(x, 'dom', split_axis=0, concat_axis=0, tiled=True, axis_in...  4.43 us
    pallas_call x1, Pallas kernels, inner_back(): pl.pallas_call(inner_back_kernel, out_shape=pltpu.VMEM(base.shape, F32),...  2.11 us
    pallas_call x1, Pallas kernels, gather_halves(): pl.pallas_call(functools.partial(gather_kernel, order), out_shape=jax.Sha...  1.73 us
    pallas_call x1, Pallas kernels, fetch(): pl.pallas_call(fetch_kernel, out_shape=tuple((pltpu.VMEM(shape, BF16) for...  1.56 us
  transfers between devices with their start and end apart: 13, of which 6 were waited for; matrix products, arithmetic and copies ran while one was open for 0% of the time, Pallas kernels for 23%

profile of v11, /device:TPU:0, one launch (start us, length us, event | category | flops | bytes accessed | tf_op | source)
XLA Modules:
  0.0 49.2 jit_solution(10084048160319855737)
XLA Ops:
  0.6 1.7 %gather_halves.1 = bf16[8,3,64,128]{3,2,1,0:T(8,128)(2,1)} custom-call(s32[3,1,8]{2,1,0:T(1,128)} %bitcast.13, bf16[16,2,64,128]{3,2,1,0:T(8,128)(2,1)} %bitcast.12), custom_call_target="tpu_custom_call" | custom-call | tf_op jit(solution)/shard_map/gather_halves/pallas_call | solution.py:91
  2.4 7.8 %all-to-all-start = ((bf16[8,3,64,128]{3,2,1,0:T(8,128)(2,1)}), bf16[8,3,64,128]{3,2,1,0:T(8,128)(2,1)S(1)}, u32[]{:S(2)}, u32[]{:S(2)}) async-start(bf16[8,3,64,128]{3,2,1,0:T(8,128)(2,1)} %gather_halves.1), calls=%async_computation | async-start | bytes 786432 | tf_op jit(solution)/shard_map/all_to_all | solution.py:43
  10.2 5.6 %stage.1 = (s32[1,64]{1,0:T(1,128)S(4)}, s32[1,64]{1,0:T(1,128)S(4)}, s32[1,24]{1,0:T(1,128)S(4)}, s32[1,8]{1,0:T(1,128)S(4)}, s32[3,1,8]{2,1,0:T(1,128)S(4)}, /...) custom-call(s32[1,64]{1,0:T(1,128)} %rows_far.1, ...), custom_call_target="tpu_custom_call" | custom-call | flops 536870912 | bytes 6291456 | tf_op jit(solution)/shard_map/stage/pallas_call | solution.py:184
  15.8 3.6 %all-to-all-done.own = bf16[8,3,64,128]{3,2,1,0:T(8,128)(2,1)S(1)} async-done(((bf16[8,3,64,128]{3,2,1,0:T(8,128)(2,1)}), bf16[8,3,64,128]{3,2,1,0:T(8,128)(2,1)S(1)}, u32[]{:S(2)}, u32[]{:S(2)}) %all-to-all-start) | async-done | bytes 393248 | tf_op jit(solution)/shard_map/all_to_all | solution.py:43
  19.4 1.6 %fetch.1 = (bf16[24,128,128]{2,1,0:T(8,128)(2,1)S(1)}, bf16[2048,256]{1,0:T(8,128)(2,1)S(1)}, bf16[256,256]{1,0:T(8,128)(2,1)S(1)}, bf16[256,256]{1,0:T(8,128)(2,1)S(1)}) custom-call(bf16[24,128,128]{2,1,0:T(8,128)(2,1)} %bitcast.11, bf16[2048,256]{1,0:T(8,128)(2,1)} %cot_far.1, bf16[128,256]{1,0:T(8,128)(2,1)} %self_far.1, bf16[128,256]{1,0:T(8,128)(2,1)} %neigh_far.1), custom_call_target="tpu_custom_call" | custom-call | flops 1000000 | bytes 3145728 | tf_op jit(solution)/shard_map/fetch/pallas_call | solution.py:237
  21.0 0.2 collective-permute-done.other
  21.1 1.5 %layer.1 = (bf16[2048,256]{1,0:T(8,128)(2,1)S(1)}, bf16[2048,256]{1,0:T(8,128)(2,1)S(1)}, bf16[2048,256]{1,0:T(8,128)(2,1)S(1)}, bf16[2,16,32,128]{3,2,1,0:T(8,1...) custom-call(s32[1,24]{1,0:T(1,128)S(4)} %get-tuple-element.41.outer_, ...), custom_call_target="tpu_custom_call", output_to_operand_aliasing={{7}: (5, {})} | custom-call | flops 1200000000 | bytes 8388608 | tf_op jit(solution)/shard_map/layer/pallas_call | solution.py:312
  22.7 0.4 collective-permute-start.1
  23.2 1.0 %weight_grads.1 = (bf16[2048,256]{1,0:T(8,128)(2,1)}, bf16[256,256]{1,0:T(8,128)(2,1)S(1)}) custom-call(bf16[2048,256]{1,0:T(8,128)(2,1)S(1)} %get-tuple-element.54.smooth, bf16[2048,256]{1,0:T(8,128)(2,1)S(1)} %get-tuple-element.55.grad_pre, bf16[2048,256]{1,0:T(8,128)(2,1)S(1)} %get-tuple-element.56.both), custom_call_target="tpu_custom_call" | custom-call | flops 268435456 | bytes 4194304 | tf_op jit(solution)/shard_map/weight_grads/pallas_call | solution.py:346
  24.3 1.6 %collective-permute-start.2 = (bf16[16,32,128]{2,1,0:T(8,128)(2,1)S(1)}, bf16[16,32,128]{2,1,0:T(8,128)(2,1)S(1)}, u32[]{:S(2)}, u32[]{:S(2)}) collective-permute-start(bf16[16,32,128]{2,1,0:T(8,128)(2,1)S(1)} %fusion), channel_id=1, source_target_pairs={{0,2},{1,3},{2,0},{3,1},{4,6},{5,7},{6,4},{7,5},{8,10},{9,11},{10,... | collective-permute-start | bytes 393224 | tf_op jit(solution)/shard_map/ppermute | solution.py:538
  25.9 1.5 %collective-permute-start.4 = (bf16[256,256]{1,0:T(8,128)(2,1)S(1)}, bf16[256,256]{1,0:T(8,128)(2,1)S(1)}, u32[]{:S(2)}, u32[]{:S(2)}) collective-permute-start(bf16[256,256]{1,0:T(8,128)(2,1)S(1)} %get-tuple-element.70), channel_id=1, source_target_pairs={{0,16},{4,20},{8,24},{12,28},{16,0},{20,4},{24,8},{28,12},{1,17},{... | collective-permute-start | bytes 393224 | tf_op jit(solution)/shard_map/ppermute | solution.py:538
  27.4 0.6 %collective-permute-start.5 = (bf16[16,32,128]{2,1,0:T(8,128)(2,1)S(1)}, bf16[16,32,128]{2,1,0:T(8,128)(2,1)S(1)}, u32[]{:S(2)}, u32[]{:S(2)}) collective-permute-start(bf16[16,32,128]{2,1,0:T(8,128)(2,1)S(1)} %fusion.1), channel_id=1, source_target_pairs={{0,2},{1,3},{2,0},{3,1},{4,6},{5,7},{6,4},{7,5},{8,10},{9,11},{10,... | collective-permute-start | bytes 393224 | tf_op jit(solution)/shard_map/ppermute | solution.py:538
  28.0 2.4 %collective-permute-done.2.came = bf16[16,32,128]{2,1,0:T(8,128)(2,1)S(1)} collective-permute-done((bf16[16,32,128]{2,1,0:T(8,128)(2,1)S(1)}, bf16[16,32,128]{2,1,0:T(8,128)(2,1)S(1)}, u32[]{:S(2)}, u32[]{:S(2)}) %collective-permute-start.2) | collective-permute-done | bytes 131104 | tf_op jit(solution)/shard_map/ppermute | solution.py:538
  30.4 1.0 %outer_back.1 = (bf16[16,32,128]{2,1,0:T(8,128)(2,1)S(1)}, f32[16,32,128]{2,1,0:T(8,128)S(1)}, bf16[8,3,32,128]{3,2,1,0:T(8,128)(2,1)}) custom-call(s32[1,24]{1,0:T(1,128)S(4)} %get-tuple-element.41.outer_rows, s32[1,8]{1,0:T(1,128)S(4)} %get-tuple-element.42.live, bf16[2,16,32,128]{3,2,1,0:T(8,128)(2,1)S(1)} %get-tuple-element.59.keep, ...), custom_call_target="tpu_custom_call" | custom-call | flops 25165824 | bytes 2097152 | tf_op jit(solution)/shard_map/outer_back/pallas_call | solution.py:385
  31.4 5.1 %all-to-all-start.1 = ((bf16[8,3,32,128]{3,2,1,0:T(8,128)(2,1)}), bf16[8,3,32,128]{3,2,1,0:T(8,128)(2,1)S(1)}, u32[]{:S(2)}, u32[]{:S(2)}) async-start(bf16[8,3,32,128]{3,2,1,0:T(8,128)(2,1)} %get-tuple-element.65), calls=%async_computation.1 | async-start | bytes 393216 | tf_op jit(solution)/shard_map/all_to_all | solution.py:43
  36.5 1.5 %collective-permute-start.9 = (bf16[256,256]{1,0:T(8,128)(2,1)S(1)}, bf16[256,256]{1,0:T(8,128)(2,1)S(1)}, u32[]{:S(2)}, u32[]{:S(2)}) collective-permute-start(bf16[256,256]{1,0:T(8,128)(2,1)S(1)} %add_convert_fusion.a), channel_id=1, source_target_pairs={{0,4},{4,0},{8,12},{12,8},{16,20},{20,16},{24,28},{28,24},{1,5},{5... | collective-permute-start | bytes 393224 | tf_op jit(solution)/shard_map/ppermute | solution.py:538
  38.1 2.1 %inner_back.1.total = f32[16,32,128]{2,1,0:T(8,128)S(1)} custom-call(s32[1,64]{1,0:T(1,128)S(4)} %get-tuple-element.66.rows, s32[1,64]{1,0:T(1,128)S(4)} %get-tuple-element.67.cols, bf16[16,32,128]{2,1,0:T(8,128)(2,1)S(1)} %get-tuple-element.68.scaled, f32[16,32,128]{2,1,0:T(8,128)S(1)} %get-tuple-element.72.base, bf16[64,128,128]{2,1,0:T(8,128)(2,1)} %bitcast.9), custom_call_target="tpu_custom_call" | custom-call | flops 67108864 | bytes 3145728 | tf_op jit(solution)/shard_map/inner_back/pallas_call | solution.py:419
  40.2 0.9 %all-to-all-done.1.returned = bf16[8,3,32,128]{3,2,1,0:T(8,128)(2,1)S(1)} async-done(((bf16[8,3,32,128]{3,2,1,0:T(8,128)(2,1)}), bf16[8,3,32,128]{3,2,1,0:T(8,128)(2,1)S(1)}, u32[]{:S(2)}, u32[]{:S(2)}) %all-to-all-start.1) | async-done | bytes 196640 | tf_op jit(solution)/shard_map/all_to_all | solution.py:43
  41.1 0.1 add_returned.1.mine
  41.2 1.6 %collective-permute-start.6 = (bf16[16,32,128]{2,1,0:T(8,128)(2,1)S(1)}, bf16[16,32,128]{2,1,0:T(8,128)(2,1)S(1)}, u32[]{:S(2)}, u32[]{:S(2)}) collective-permute-start(bf16[16,32,128]{2,1,0:T(8,128)(2,1)S(1)} %add_returned.1.mine), channel_id=1, source_target_pairs={{0,2},{1,3},{2,0},{3,1},{4,6},{5,7},{6,4},{7,5},{8,10},{9,11},{10,... | collective-permute-start | bytes 393224 | tf_op jit(solution)/shard_map/ppermute | solution.py:538
  42.9 1.5 %collective-permute-start.10 = (bf16[256,256]{1,0:T(8,128)(2,1)S(1)}, bf16[256,256]{1,0:T(8,128)(2,1)S(1)}, u32[]{:S(2)}, u32[]{:S(2)}) collective-permute-start(bf16[256,256]{1,0:T(8,128)(2,1)S(1)} %pair_sum.1.grads), channel_id=1, source_target_pairs={{0,8},{4,12},{8,0},{12,4},{16,24},{20,28},{24,16},{28,20},{1,9},{5... | collective-permute-start | bytes 393224 | tf_op jit(solution)/shard_map/ppermute | solution.py:538
  44.4 1.9 %collective-permute-done.6.across = bf16[16,32,128]{2,1,0:T(8,128)(2,1)S(1)} collective-permute-done((bf16[16,32,128]{2,1,0:T(8,128)(2,1)S(1)}, bf16[16,32,128]{2,1,0:T(8,128)(2,1)S(1)}, u32[]{:S(2)}, u32[]{:S(2)}) %collective-permute-start.6) | collective-permute-done | bytes 131104 | tf_op jit(solution)/shard_map/ppermute | solution.py:538
  46.2 1.7 %collective-permute-done.10.grads_came = bf16[256,256]{1,0:T(8,128)(2,1)S(1)} collective-permute-done((bf16[256,256]{1,0:T(8,128)(2,1)S(1)}, bf16[256,256]{1,0:T(8,128)(2,1)S(1)}, u32[]{:S(2)}, u32[]{:S(2)}) %collective-permute-start.10) | collective-permute-done | bytes 131104 | tf_op jit(solution)/shard_map/ppermute | solution.py:538
  47.9 1.3 %finish.1 = (f32[2048,128]{1,0:T(8,128)}, f32[128,256]{1,0:T(8,128)}, f32[128,256]{1,0:T(8,128)}) custom-call(bf16[16,32,128]{2,1,0:T(8,128)(2,1)S(1)} %add_returned.1.mine, bf16[16,32,128]{2,1,0:T(8,128)(2,1)S(1)} %collective-permute-done.6.across, bf16[16,32,128]{2,1,0:T(8,128)(2,1)S(1)} %collective-permute-done.7.beside, ...), custom_call_target="tpu_custom_call" | custom-call | flops 67108864 | bytes 2097152 | tf_op jit(solution)/shard_map/finish/pallas_call | solution.py:521
  (16 shorter events, 0.3 us)
Async XLA Ops:
  2.4 17.0 %all-to-all-start = ((bf16[8,3,64,128]{3,2,1,0:T(8,128)(2,1)}), bf16[8,3,64,128]{3,2,1,0:T(8,128)(2,1)S(1)}, u32[]{:S(2)}, u32[]{:S(2)}) async-start(bf16[8,3,64,128]{3,2,1,0:T(8,128)(2,1)} %gather_halves.1), calls=%async_computation | async-start | bytes 786432 | tf_op jit(solution)/shard_map/all_to_all | solution.py:43
  19.4 1.7 %collective-permute-start = (bf16[8,3,64,128]{3,2,1,0:T(8,128)(2,1)S(1)}, bf16[8,3,64,128]{3,2,1,0:T(8,128)(2,1)S(1)}, u32[]{:S(2)}, u32[]{:S(2)}) collective-permute-start(bf16[8,3,64,128]{3,2,1,0:T(8,128)(2,1)S(1)} %all-to-all-done.own), channel_id=1, source_target_pairs={{0,1},{1,0},{2,3},{3,2},{4,5},{5,4},{6,7},{7,6},{8,9},{9,8},{10,11... | collective-permute-start | bytes 1179656 | tf_op jit(solution)/shard_map/ppermute | solution.py:538
  22.7 1.6 %collective-permute-start.1 = (bf16[2,16,32,128]{3,2,1,0:T(8,128)(2,1)S(1)}, bf16[2,16,32,128]{3,2,1,0:T(8,128)(2,1)S(1)}, u32[]{:S(2)}, u32[]{:S(2)}) collective-permute-start(bf16[2,16,32,128]{3,2,1,0:T(8,128)(2,1)S(1)} %get-tuple-element.60), channel_id=1, source_target_pairs={{0,1},{1,0},{2,3},{3,2},{4,5},{5,4},{6,7},{7,6},{8,9},{9,8},{10,11... | collective-permute-start | bytes 786440 | tf_op jit(solution)/shard_map/ppermute | solution.py:538
  23.1 4.3 %collective-permute-start.3 = (bf16[2,16,32,128]{3,2,1,0:T(8,128)(2,1)S(1)}, bf16[2,16,32,128]{3,2,1,0:T(8,128)(2,1)S(1)}, u32[]{:S(2)}, u32[]{:S(2)}) collective-permute-start(bf16[2,16,32,128]{3,2,1,0:T(8,128)(2,1)S(1)} %get-tuple-element.64), channel_id=1, source_target_pairs={{0,1},{1,0},{2,3},{3,2},{4,5},{5,4},{6,7},{7,6},{8,9},{9,8},{10,11... | collective-permute-start | bytes 786440 | tf_op jit(solution)/shard_map/ppermute | solution.py:538
  24.3 6.1 %collective-permute-start.2 = (bf16[16,32,128]{2,1,0:T(8,128)(2,1)S(1)}, bf16[16,32,128]{2,1,0:T(8,128)(2,1)S(1)}, u32[]{:S(2)}, u32[]{:S(2)}) collective-permute-start(bf16[16,32,128]{2,1,0:T(8,128)(2,1)S(1)} %fusion), channel_id=1, source_target_pairs={{0,2},{1,3},{2,0},{3,1},{4,6},{5,7},{6,4},{7,5},{8,10},{9,11},{10,... | collective-permute-start | bytes 393224 | tf_op jit(solution)/shard_map/ppermute | solution.py:538
  25.9 10.6 %collective-permute-start.4 = (bf16[256,256]{1,0:T(8,128)(2,1)S(1)}, bf16[256,256]{1,0:T(8,128)(2,1)S(1)}, u32[]{:S(2)}, u32[]{:S(2)}) collective-permute-start(bf16[256,256]{1,0:T(8,128)(2,1)S(1)} %get-tuple-element.70), channel_id=1, source_target_pairs={{0,16},{4,20},{8,24},{12,28},{16,0},{20,4},{24,8},{28,12},{1,17},{... | collective-permute-start | bytes 393224 | tf_op jit(solution)/shard_map/ppermute | solution.py:538
  27.4 9.1 %collective-permute-start.5 = (bf16[16,32,128]{2,1,0:T(8,128)(2,1)S(1)}, bf16[16,32,128]{2,1,0:T(8,128)(2,1)S(1)}, u32[]{:S(2)}, u32[]{:S(2)}) collective-permute-start(bf16[16,32,128]{2,1,0:T(8,128)(2,1)S(1)} %fusion.1), channel_id=1, source_target_pairs={{0,2},{1,3},{2,0},{3,1},{4,6},{5,7},{6,4},{7,5},{8,10},{9,11},{10,... | collective-permute-start | bytes 393224 | tf_op jit(solution)/shard_map/ppermute | solution.py:538
  31.4 9.7 %all-to-all-start.1 = ((bf16[8,3,32,128]{3,2,1,0:T(8,128)(2,1)}), bf16[8,3,32,128]{3,2,1,0:T(8,128)(2,1)S(1)}, u32[]{:S(2)}, u32[]{:S(2)}) async-start(bf16[8,3,32,128]{3,2,1,0:T(8,128)(2,1)} %get-tuple-element.65), calls=%async_computation.1 | async-start | bytes 393216 | tf_op jit(solution)/shard_map/all_to_all | solution.py:43
  36.5 6.3 %collective-permute-start.9 = (bf16[256,256]{1,0:T(8,128)(2,1)S(1)}, bf16[256,256]{1,0:T(8,128)(2,1)S(1)}, u32[]{:S(2)}, u32[]{:S(2)}) collective-permute-start(bf16[256,256]{1,0:T(8,128)(2,1)S(1)} %add_convert_fusion.a), channel_id=1, source_target_pairs={{0,4},{4,0},{8,12},{12,8},{16,20},{20,16},{24,28},{28,24},{1,5},{5... | collective-permute-start | bytes 393224 | tf_op jit(solution)/shard_map/ppermute | solution.py:538
  41.2 5.0 %collective-permute-start.6 = (bf16[16,32,128]{2,1,0:T(8,128)(2,1)S(1)}, bf16[16,32,128]{2,1,0:T(8,128)(2,1)S(1)}, u32[]{:S(2)}, u32[]{:S(2)}) collective-permute-start(bf16[16,32,128]{2,1,0:T(8,128)(2,1)S(1)} %add_returned.1.mine), channel_id=1, source_target_pairs={{0,2},{1,3},{2,0},{3,1},{4,6},{5,7},{6,4},{7,5},{8,10},{9,11},{10,... | collective-permute-start | bytes 393224 | tf_op jit(solution)/shard_map/ppermute | solution.py:538
  42.9 5.0 %collective-permute-start.10 = (bf16[256,256]{1,0:T(8,128)(2,1)S(1)}, bf16[256,256]{1,0:T(8,128)(2,1)S(1)}, u32[]{:S(2)}, u32[]{:S(2)}) collective-permute-start(bf16[256,256]{1,0:T(8,128)(2,1)S(1)} %pair_sum.1.grads), channel_id=1, source_target_pairs={{0,8},{4,12},{8,0},{12,4},{16,24},{20,28},{24,16},{28,20},{1,9},{5... | collective-permute-start | bytes 393224 | tf_op jit(solution)/shard_map/ppermute | solution.py:538
  44.4 3.5 %collective-permute-start.7 = (bf16[16,32,128]{2,1,0:T(8,128)(2,1)S(1)}, bf16[16,32,128]{2,1,0:T(8,128)(2,1)S(1)}, u32[]{:S(2)}, u32[]{:S(2)}) collective-permute-start(bf16[16,32,128]{2,1,0:T(8,128)(2,1)S(1)} %add_returned.1.mine), channel_id=1, source_target_pairs={{0,1},{1,0},{2,3},{3,2},{4,5},{5,4},{6,7},{7,6},{8,9},{9,8},{10,11... | collective-permute-start | bytes 393224 | tf_op jit(solution)/shard_map/ppermute | solution.py:538
  46.2 1.7 %collective-permute-start.8 = (bf16[16,32,128]{2,1,0:T(8,128)(2,1)S(1)}, bf16[16,32,128]{2,1,0:T(8,128)(2,1)S(1)}, u32[]{:S(2)}, u32[]{:S(2)}) collective-permute-start(bf16[16,32,128]{2,1,0:T(8,128)(2,1)S(1)} %collective-permute-done.6.across), channel_id=1, source_target_pairs={{0,1},{1,0},{2,3},{3,2},{4,5},{5,4},{6,7},{7,6},{8,9},{9,8},{10,11... | collective-permute-start | bytes 393224 | tf_op jit(solution)/shard_map/ppermute | solution.py:538
